TPU v7x, 32 devices: a whole 2x2x4 slice. The times are simulated.
32 devices in a mesh: zone: 8 (over z, y), ja: 4 (over x, core).
Axes of the slice: x: 2, y: 2, z: 4, core: 2. Of those that a mesh axis runs over, the one named last changes fastest.
Arguments:
- flow_state: float32 [8, 32, 5, 16, 128], P('zone', 'ja'), may hold values from -3 to 3
- forcing: float32 [8, 32, 5, 16, 128], P('zone', 'ja'), may hold values from -6 to 6
- diag_block: float32 [8, 32, 5, 5, 16, 128], P('zone', 'ja'), may hold values from -0.4 to 7.2
- lower_jac: float32 [8, 32, 5, 5, 16, 128], P('zone', 'ja'), may hold values from -4.9 to 0.2
- upper_jac: float32 [8, 32, 5, 5, 16, 128], P('zone', 'ja'), may hold values from -4.9 to 0.2
- block_inv: float32 [8, 32, 5, 5, 16, 128], P('zone', 'ja'), may hold values from -0.03 to 0.21
- east_zone: int32 [8], replicated, may hold values from 0 to 7, each once
- zone_depth: int32 [8], replicated, may hold values from 4 to 16, as said below
Outputs:
- new_state: float32 [8, 32, 5, 16, 128], P('zone', 'ja')
- last_residual: float32 [8, 32, 5, 16, 128], P('zone', 'ja')
Inputs may be any that keep to these rules, and one draw needn't show every extreme that they name: `east_zone`: a permutation of the zones. `zone_depth`: some zone has all 16 planes live.
All inputs are finite; a program needn't handle non-finite values.
Results may differ from a plain program's by a relative error of at most 0.0003.
Values sent between devices are 32-bit elements; how exact they have to be, the bound alone decides.
No kernel may reach another device: no remote copies, remote signals or barrier semaphores. Data moves between devices by JAX's collectives and lax.ppermute only.
A program may use at most 64 MiB of HBM per device.

v0:
```python
import functools

import jax
import jax.numpy as jnp
from jax import lax
from jax.experimental import pallas as pl
from jax.experimental.pallas import tpu as pltpu
from jax.sharding import PartitionSpec as P

ITERS = 2
OMEGA = 1.2
COUPLE = 0.25

VMEM = pl.BlockSpec(memory_space=pltpu.VMEM)
SMEM = pl.BlockSpec(memory_space=pltpu.SMEM)


def call(kernel, shapes, scratch=(), flops=10**6):
    moved = sum(4 * functools.reduce(lambda a, b: a * b, s, 1) for s in shapes)

    def run(*arrays):
        total = moved + sum(a.size * 4 for a in arrays)
        return pl.pallas_call(
            kernel,
            out_shape=[jax.ShapeDtypeStruct(s, jnp.float32) for s in shapes],
            in_specs=[VMEM if a.dtype == jnp.float32 else SMEM for a in arrays],
            out_specs=[VMEM] * len(shapes),
            scratch_shapes=list(scratch),
            compiler_params=pltpu.CompilerParams(vmem_limit_bytes=10 * 2**20),
            cost_estimate=pl.CostEstimate(flops=flops, bytes_accessed=total, transcendentals=0),
        )(*arrays)

    return run


def iota(dim):
    return lax.broadcasted_iota(jnp.int32, (16, 128), dim)


def matvec(matrix, vector):
    n = len(vector)
    out = []
    for r in range(n):
        acc = matrix[r][0] * vector[0]
        for c in range(1, n):
            acc = acc + matrix[r][c] * vector[c]
        out.append(acc)
    return out


def block(ref, *lead):
    return [[ref[(*lead, r, c)] for c in range(5)] for r in range(5)]


def cell(ref, *lead):
    return [ref[(*lead, v)] for v in range(5)]


def put(ref, values, *lead):
    for v, value in enumerate(values):
        ref[(*lead, v)] = value


def add(a, b):
    return [x + y for x, y in zip(a, b)]


def pack_faces(load, planes, tile_ref):
    lane = iota(1)
    tile = jnp.zeros((16, 128), jnp.float32)
    for j in range(planes):
        for v in range(5):
            q = 2 * (j * 5 + v)
            here = (lane == q) | (lane == (q - 1) % 128)
            x = load(j, v)
            tile = jnp.where(here, pltpu.roll(x, q, 1) if q else x, tile)
    for w in range(tile_ref.shape[0]):
        tile_ref[w] = tile


def live_rows(depth_ref):
    return iota(0) < depth_ref[lax.axis_index("zone")]


def pack_kernel(depth_ref, flow_ref, tile_ref):
    live = live_rows(depth_ref)
    pack_faces(lambda j, v: jnp.where(live, flow_ref[j, v], 0.0), flow_ref.shape[0], tile_ref)


def matrix_kernel(inv_ref, low_ref, up_ref, e_ref, f_ref, mats_ref, y_ref):
    planes = inv_ref.shape[0]
    for h in range(2):
        rows = pl.ds(8 * h, 8)

        def col(ref, q, j):
            return [ref[j, r, q, rows] for r in range(5)]

        def put_col(ref, values, q, j):
            for r in range(5):
                ref[j, r, q, rows] = values[r]

        def mat(ref, j):
            return [[ref[j, r, c, rows] for c in range(5)] for r in range(5)]

        def product(ref_out, j, jac_ref):
            inv = mat(inv_ref, j)
            for q in range(5):
                put_col(ref_out, [OMEGA * x for x in matvec(inv, col(jac_ref, q, j))], q, j)

        def forward(j, carry):
            product(e_ref, j, low_ref)
            e = mat(e_ref, j)
            for q in range(5):
                put_col(y_ref, matvec(e, col(y_ref, q, j - 1)), q, j)
            return carry

        product(e_ref, 0, low_ref)
        for q in range(5):
            put_col(y_ref, col(e_ref, q, 0), q, 0)
        lax.fori_loop(1, planes, forward, 0)

        def backward(step, carry):
            j = planes - 2 - step
            product(f_ref, j, up_ref)
            f = mat(f_ref, j)
            for q in range(5):
                put_col(mats_ref, add(col(y_ref, q, j), matvec(f, col(mats_ref, q, 1))), q, 1)
                put_col(mats_ref, matvec(f, col(mats_ref, q, 2)), q, 2)
            return carry

        last = planes - 1
        product(f_ref, last, up_ref)
        for q in range(5):
            put_col(mats_ref, col(y_ref, q, last), q, 0)
            put_col(mats_ref, col(y_ref, q, last), q, 1)
            put_col(mats_ref, col(f_ref, q, last), q, 2)
        lax.fori_loop(0, planes - 1, backward, 0)


def by_place(mine_refs, other_refs, run):
    odd = lax.axis_index("ja") % 2

    @pl.when(odd == 0)
    def _():
        run(*mine_refs, *other_refs)

    @pl.when(odd == 1)
    def _():
        run(*other_refs, *mine_refs)


def beta_kernel(mine_ref, other_ref, beta_ref):
    def run(lo, hi):
        d_hi, n_lo = block(hi, 1), block(lo, 2)
        for q in range(5):
            m_col = [lo[0, r, q] for r in range(5)]
            d_col = [lo[1, r, q] for r in range(5)]
            out = add(d_col, matvec(n_lo, matvec(d_hi, m_col)))
            for r in range(5):
                beta_ref[r, q] = out[r]

    by_place([mine_ref], [other_ref], run)


def local_kernel(
    depth_ref, east_ref, cur_ref, force_ref, diag_ref, low_ref, up_ref, inv_ref, e_ref, f_ref,
    below_ref, above_ref, tiles_ref, res_ref, s_ref, ends_ref, y_ref,
):
    planes = cur_ref.shape[0]
    zone = lax.axis_index("zone")
    live = live_rows(depth_ref)
    lane, row = iota(1), iota(0)
    east = east_ref[zone]
    west = jnp.int32(0)
    for w in range(tiles_ref.shape[0]):
        west = west + jnp.where(east_ref[w] == zone, w, 0)
    ghosts = jnp.where(
        lane % 2 == 0, pltpu.roll(tiles_ref[west], 1, 1), pltpu.roll(tiles_ref[east], 127, 1)
    )

    def state(j):
        source = below_ref if j < 0 else above_ref if j >= planes else cur_ref.at[j]
        return [jnp.where(live, source[v], 0.0) for v in range(5)]

    value = None
    for j in range(planes):
        here = state(j)
        own = matvec(block(diag_ref, j), here)
        lower = matvec(block(low_ref, j), state(j - 1))
        upper = matvec(block(up_ref, j), state(j + 1))
        res = []
        for v in range(5):
            x = here[v]
            q = 2 * (j * 5 + v)
            ghost = pltpu.roll(ghosts, 128 - q, 1) if q else ghosts
            sides = jnp.where(lane == 0, ghost, pltpu.roll(x, 1, 1))
            sides = sides + jnp.where(lane == 127, ghost, pltpu.roll(x, 127, 1))
            sides = sides + jnp.where(row == 0, 0.0, pltpu.roll(x, 1, 0))
            sides = sides + jnp.where(row == 15, 0.0, pltpu.roll(x, 15, 0))
            applied = own[v] - lower[v] - upper[v] - COUPLE * sides
            res.append(jnp.where(live, force_ref[j, v] - applied, 0.0))
        put(res_ref, res, j)
        s = matvec(block(inv_ref, j), res)
        put(s_ref, s, j)
        value = s if j == 0 else add(s, matvec(block(e_ref, j), value))
        put(y_ref, value, j)
    put(ends_ref, value, 0)
    for j in range(planes - 2, -1, -1):
        value = add(cell(y_ref, j), matvec(block(f_ref, j), value))
    put(ends_ref, value, 1)


def mid_kernel(ends_ref, ends_other_ref, mats_ref, mats_other_ref, out_ref):
    def run(ends_lo, mats_lo, ends_hi, mats_hi):
        c_lo = cell(ends_lo, 0)

        @pl.when(lax.axis_index("ja") < 2)
        def _():
            put(out_ref, add(cell(ends_hi, 0), matvec(block(mats_hi, 0), c_lo)))

        @pl.when(lax.axis_index("ja") >= 2)
        def _():
            turned = add(cell(ends_hi, 1), matvec(block(mats_hi, 1), c_lo))
            put(out_ref, add(cell(ends_lo, 1), matvec(block(mats_lo, 2), turned)))

    by_place([ends_ref, mats_ref], [ends_other_ref, mats_other_ref], run)


def final_kernel(
    depth_ref, cur_ref, s_ref, e_ref, f_ref, below_ref, above_ref, f_below_ref,
    ends_ref, ends_other_ref, mats_ref, mats_other_ref, pair_ref, pair_other_ref, beta_ref,
    new_ref, *more,
):
    y_ref, inflow_ref = more[-2:]
    planes = cur_ref.shape[0]
    ja = lax.axis_index("ja")
    live = live_rows(depth_ref)

    def far(a, alpha):
        return add(cell(alpha), matvec(block(beta_ref), cell(a)))

    @pl.when(ja == 0)
    def _():
        put(inflow_ref, [jnp.zeros((16, 128), jnp.float32)] * 5, 0)
        b = add(cell(ends_other_ref, 1), matvec(block(mats_other_ref, 1), cell(ends_ref, 0)))
        b = add(b, matvec(block(mats_other_ref, 2), far(pair_ref, pair_other_ref)))
        put(inflow_ref, b, 1)

    @pl.when(ja == 1)
    def _():
        put(inflow_ref, cell(ends_other_ref, 0), 0)
        put(inflow_ref, far(pair_ref, pair_other_ref), 1)

    @pl.when(ja == 2)
    def _():
        a = cell(pair_other_ref)
        put(inflow_ref, a, 0)
        a = add(cell(ends_ref, 0), matvec(block(mats_ref, 0), a))
        b = add(cell(ends_other_ref, 1), matvec(block(mats_other_ref, 1), a))
        put(inflow_ref, b, 1)

    @pl.when(ja == 3)
    def _():
        a = add(cell(ends_other_ref, 0), matvec(block(mats_other_ref, 0), cell(pair_other_ref)))
        put(inflow_ref, a, 0)
        put(inflow_ref, [jnp.zeros((16, 128), jnp.float32)] * 5, 1)

    value = cell(inflow_ref, 0)
    for j in range(planes):
        value = add(cell(s_ref, j), matvec(block(e_ref, j), value))
        put(y_ref, value, j)
    value = cell(inflow_ref, 1)
    for j in range(planes - 1, -1, -1):
        value = add(cell(y_ref, j), matvec(block(f_ref, j), value))
        put(new_ref, [jnp.where(live, cur_ref[j, v], 0.0) + value[v] for v in range(5)], j)
    if len(more) > 2:
        below_new_ref, above_new_ref, tile_ref = more[:3]
        before = add(cell(inflow_ref, 0), matvec(block(f_below_ref), value))
        put(below_new_ref, add([jnp.where(live, below_ref[v], 0.0) for v in range(5)], before))
        after = cell(inflow_ref, 1)
        put(above_new_ref, add([jnp.where(live, above_ref[v], 0.0) for v in range(5)], after))
        pack_faces(lambda j, v: new_ref[j, v], planes, tile_ref)


def per_device(
    flow_state, forcing, diag_block, lower_jac, upper_jac, block_inv, east_zone, zone_depth
):
    zones, parts = lax.axis_size("zone"), lax.axis_size("ja")
    assert parts == 4
    current, force, diag, low, up, inv = (
        x[0] for x in (flow_state, forcing, diag_block, lower_jac, upper_jac, block_inv)
    )
    state = current.shape
    plane, blocks, tiles = state[1:], diag.shape, (zones, *state[2:])
    matrix = blocks[1:]

    def swap(x, bit):
        return lax.ppermute(x, "ja", [(p, p ^ bit) for p in range(parts)])

    def faces(x):
        return lax.all_to_all(x, "zone", 0, 0, tiled=True)

    got = faces(call(pack_kernel, [tiles])(zone_depth, current)[0])
    above = lax.ppermute(current[0], "ja", [(p + 1, p) for p in range(parts - 1)])
    e, f, mats = call(
        matrix_kernel, [blocks, blocks, (3, *matrix)], [pltpu.VMEM(blocks, jnp.float32)]
    )(inv, low, up)
    edge = jnp.concatenate([current[-1].reshape(1, *plane), f[-1]], axis=0)
    edge = lax.ppermute(edge, "ja", [(p, p + 1) for p in range(parts - 1)])
    below, f_below = edge[0], edge[1:]
    mats_other = swap(mats, 1)
    beta = call(beta_kernel, [matrix])(mats, mats_other)[0]
    beta = lax.ppermute(beta, "ja", [(2, 0), (3, 1)])

    for iteration in range(ITERS):
        last = iteration == ITERS - 1
        residual, s, ends = call(
            local_kernel, [state, state, (2, *plane)], [pltpu.VMEM(state, jnp.float32)]
        )(zone_depth, east_zone, current, force, diag, low, up, inv, e, f, below, above, got)
        ends_other = swap(ends, 1)
        pair = call(mid_kernel, [plane])(ends, ends_other, mats, mats_other)[0]
        pair_other = swap(pair, 2)
        current, *more = call(
            final_kernel,
            [state] if last else [state, plane, plane, tiles],
            [pltpu.VMEM(state, jnp.float32), pltpu.VMEM((2, *plane), jnp.float32)],
        )(
            zone_depth, current, s, e, f, below, above, f_below,
            ends, ends_other, mats, mats_other, pair, pair_other, beta,
        )
        if not last:
            below, above, got = more[0], more[1], faces(more[2])
    return (current[None], residual[None])


def solution(mesh):
    state = P("zone", "ja", None, None, None)
    blocks = P("zone", "ja", None, None, None, None)
    return jax.shard_map(
        per_device,
        mesh=mesh,
        in_specs=(state, state, blocks, blocks, blocks, blocks, P(), P()),
        out_specs=(state, state),
        check_vma=False,
    )
```

profile of v0, /device:TPU:0, one launch (start us, length us, event | category | flops | bytes accessed | tf_op | source)
XLA Modules:
  0.0 73.0 jit_solution(6255710876721217139)
XLA Ops:
  0.6 0.0 copy-start
  0.6 1.4 %copy-done = f32[1,8,5,5,16,128]{5,4,3,2,1,0:T(8,128)S(1)} copy-done((f32[1,8,5,5,16,128]{5,4,3,2,1,0:T(8,128)S(1)}, f32[1,8,5,5,16,128]{5,4,3,2,1,0:T(8,128)}, u32[]{:S(2)}) %copy-start) | copy-done | bytes 1638424
  2.1 0.0 copy-start.2
  2.1 1.4 %copy-done.2 = f32[1,8,5,5,16,128]{5,4,3,2,1,0:T(8,128)S(1)} copy-done((f32[1,8,5,5,16,128]{5,4,3,2,1,0:T(8,128)S(1)}, f32[1,8,5,5,16,128]{5,4,3,2,1,0:T(8,128)}, u32[]{:S(2)}) %copy-start.2) | copy-done | bytes 1638424
  3.5 0.0 copy-start.5
  3.5 1.4 %copy-done.5 = f32[1,8,5,5,16,128]{5,4,3,2,1,0:T(8,128)S(1)} copy-done((f32[1,8,5,5,16,128]{5,4,3,2,1,0:T(8,128)S(1)}, f32[1,8,5,5,16,128]{5,4,3,2,1,0:T(8,128)}, u32[]{:S(2)}) %copy-start.5) | copy-done | bytes 1638424
  4.9 0.0 copy-start.10
  4.9 0.0 copy-start.16
  4.9 4.0 %shard_map.95 = (f32[8,5,5,16,128]{4,3,2,1,0:T(8,128)S(1)}, f32[8,5,5,16,128]{4,3,2,1,0:T(8,128)S(1)}, f32[3,5,5,16,128]{4,3,2,1,0:T(8,128)}) custom-call(f32[8,5,5,16,128]{4,3,2,1,0:T(8,128)S(1)} %bitcast.22, f32[8,5,5,16,128]{4,3,2,1,0:T(8,128)S(1)} %bitcast.16, f32[8,5,5,16,128]{4,3,2,1,0:T(8,128)S(1)} %bitcast.19), custom_call_target="tpu_custom_call" | custom-call | flops 1000000 | bytes 8806400 | tf_op jit(solution)/shard_map/pallas_call | solution.py:23
  8.9 0.0 copy-start.17
  8.9 0.5 collective-permute-start.3
  9.4 0.0 copy-done.10
  9.4 0.6 slice_bitcast_fusion.2
  10.0 0.7 pad_maximum_fusion
  10.7 2.7 %collective-permute-start = (f32[6,5,16,128]{3,2,1,0:T(8,128)}, f32[6,5,16,128]{3,2,1,0:T(8,128)}, u32[]{:S(2)}, u32[]{:S(2)}) collective-permute-start(f32[6,5,16,128]{3,2,1,0:T(8,128)} %pad_maximum_fusion), channel_id=1, source_target_pairs={{0,1},{1,2},{2,3},{4,5},{5,6},{6,7},{8,9},{9,10},{10,11},{12,13},{... | collective-permute-start | bytes 737288 | tf_op jit(solution)/shard_map/ppermute | solution.py:309
  13.4 0.0 copy-done.16
  13.4 1.3 %shard_map.96 = f32[8,16,128]{2,1,0:T(8,128)} custom-call(s32[8]{0:T(128)S(1)} %copy-done.16, f32[8,5,16,128]{3,2,1,0:T(8,128)S(1)} %bitcast.27), custom_call_target="tpu_custom_call" | custom-call | flops 1000000 | bytes 393248 | tf_op jit(solution)/shard_map/pallas_call | solution.py:23
  14.7 7.3 %all-to-all-start = ((f32[8,16,128]{2,1,0:T(8,128)}), f32[8,16,128]{2,1,0:T(8,128)}, u32[]{:S(2)}, u32[]{:S(2)}) async-start(f32[8,16,128]{2,1,0:T(8,128)} %shard_map.96), calls=%async_computation | async-start | bytes 131072 | tf_op jit(solution)/shard_map/all_to_all | solution.py:301
  22.0 1.3 %collective-permute-start.1 = (f32[5,16,128]{2,1,0:T(8,128)}, f32[5,16,128]{2,1,0:T(8,128)S(1)}, u32[]{:S(2)}, u32[]{:S(2)}) collective-permute-start(f32[5,16,128]{2,1,0:T(8,128)} %get-tuple-element.26), channel_id=1, source_target_pairs={{1,0},{2,1},{3,2},{5,4},{6,5},{7,6},{9,8},{10,9},{11,10},{13,12},{... | collective-permute-start | bytes 122888 | tf_op jit(solution)/shard_map/ppermute | solution.py:304
  23.3 0.0 collective-permute-done.3.mats_other_ref.other_ref
  23.3 2.1 %shard_map.99 = f32[5,5,16,128]{3,2,1,0:T(8,128)} custom-call(f32[3,5,5,16,128]{4,3,2,1,0:T(8,128)} %get-tuple-element.18.mats_ref.mine_ref, f32[3,5,5,16,128]{4,3,2,1,0:T(8,128)} %collective-permute-done.3.mats_other_ref.other_ref), custom_call_target="tpu_custom_call" | custom-call | flops 1000000 | bytes 1433600 | tf_op jit(solution)/shard_map/pallas_call | solution.py:23
  25.4 1.3 %collective-permute-start.5 = (f32[5,5,16,128]{3,2,1,0:T(8,128)}, f32[5,5,16,128]{3,2,1,0:T(8,128)S(1)}, u32[]{:S(2)}, u32[]{:S(2)}) collective-permute-start(f32[5,5,16,128]{3,2,1,0:T(8,128)} %shard_map.99), channel_id=1, source_target_pairs={{2,0},{3,1},{6,4},{7,5},{10,8},{11,9},{14,12},{15,13},{18,16},{19,... | collective-permute-start | bytes 614408 | tf_op jit(solution)/shard_map/ppermute | solution.py:313
  26.7 0.0 collective-permute-done
  26.7 0.8 %slice_bitcast_fusion.1.below_ref = f32[5,16,128]{2,1,0:T(8,128)S(1)} fusion(f32[6,5,16,128]{3,2,1,0:T(8,128)} %collective-permute-done), kind=kLoop, calls=%fused_computation.2 | loop fusion | bytes 81920 | tf_op jit(solution)/shard_map/squeeze | solution.py:310
  27.4 0.0 collective-permute-done.1.above_ref
  27.4 0.0 copy-start.14
  27.4 0.6 copy-done.14
  28.1 0.9 %all-to-all-done.tiles_ref = f32[8,16,128]{2,1,0:T(8,128)} async-done(((f32[8,16,128]{2,1,0:T(8,128)}), f32[8,16,128]{2,1,0:T(8,128)}, u32[]{:S(2)}, u32[]{:S(2)}) %all-to-all-start) | async-done | bytes 65568 | tf_op jit(solution)/shard_map/all_to_all | solution.py:301
  29.0 0.0 copy-done.17
  29.0 0.0 copy-start.1
  29.0 1.4 %copy-done.1 = f32[1,8,5,5,16,128]{5,4,3,2,1,0:T(8,128)S(1)} copy-done((f32[1,8,5,5,16,128]{5,4,3,2,1,0:T(8,128)S(1)}, f32[1,8,5,5,16,128]{5,4,3,2,1,0:T(8,128)}, u32[]{:S(2)}) %copy-start.1) | copy-done | bytes 1638424
  30.4 0.0 copy-start.3
  30.4 1.4 %copy-done.3 = f32[1,8,5,5,16,128]{5,4,3,2,1,0:T(8,128)S(1)} copy-done((f32[1,8,5,5,16,128]{5,4,3,2,1,0:T(8,128)S(1)}, f32[1,8,5,5,16,128]{5,4,3,2,1,0:T(8,128)}, u32[]{:S(2)}) %copy-start.3) | copy-done | bytes 1638424
  31.9 0.0 copy-start.6
  31.9 1.4 %copy-done.6 = f32[1,8,5,5,16,128]{5,4,3,2,1,0:T(8,128)S(1)} copy-done((f32[1,8,5,5,16,128]{5,4,3,2,1,0:T(8,128)S(1)}, f32[1,8,5,5,16,128]{5,4,3,2,1,0:T(8,128)}, u32[]{:S(2)}) %copy-start.6) | copy-done | bytes 1638424
  33.3 0.0 copy-start.8
  33.3 1.4 %copy-done.8 = f32[1,8,5,5,16,128]{5,4,3,2,1,0:T(8,128)S(1)} copy-done((f32[1,8,5,5,16,128]{5,4,3,2,1,0:T(8,128)S(1)}, f32[1,8,5,5,16,128]{5,4,3,2,1,0:T(8,128)}, u32[]{:S(2)}) %copy-start.8) | copy-done | bytes 1638424
  34.7 0.0 copy-start.11
  34.7 1.0 %copy-done.11 = f32[1,8,5,16,128]{4,3,2,1,0:T(8,128)S(1)} copy-done((f32[1,8,5,16,128]{4,3,2,1,0:T(8,128)S(1)}, f32[1,8,5,16,128]{4,3,2,1,0:T(8,128)}, u32[]{:S(2)}) %copy-start.11) | copy-done | bytes 327704
  35.7 0.0 copy-start.12
  35.7 1.0 %copy-done.12 = f32[1,8,5,16,128]{4,3,2,1,0:T(8,128)S(1)} copy-done((f32[1,8,5,16,128]{4,3,2,1,0:T(8,128)S(1)}, f32[1,8,5,16,128]{4,3,2,1,0:T(8,128)}, u32[]{:S(2)}) %copy-start.12) | copy-done | bytes 327704
  36.7 0.8 %copy-done.15 = f32[5,16,128]{2,1,0:T(8,128)S(1)} copy-done((f32[5,16,128]{2,1,0:T(8,128)S(1)}, f32[5,16,128]{2,1,0:T(8,128)}, u32[]{:S(2)}) %copy-start.15) | copy-done | bytes 40984
  37.4 2.6 %shard_map.97 = (f32[8,5,16,128]{3,2,1,0:T(8,128)}, f32[8,5,16,128]{3,2,1,0:T(8,128)S(1)}, f32[2,5,16,128]{3,2,1,0:T(8,128)S(1)}) custom-call(s32[8]{0:T(128)S(1)} %copy-done.16, s32[8]{0:T(128)S(1)} %copy-done.17, f32[8,5,16,128]{3,2,1,0:T(8,128)S(1)} %bitcast.28, f32[8,5,16,128]{3,2,1,0:T(8,128)S(1)} %bitcast.30, f32[8,5,5,16,128]{4,3,2,1,0:T(8,128)S(1)} %bitcast.25, ...), custom_call_target="tpu_custom_call" | custom-call | flops 1000000 | bytes 11370560 | tf_op jit(solution)/shard_map/pallas_call | solution.py:23
  40.1 0.2 collective-permute-start.2
  40.3 1.1 %collective-permute-done.2.ends_other_ref = f32[2,5,16,128]{3,2,1,0:T(8,128)S(1)} collective-permute-done((f32[2,5,16,128]{3,2,1,0:T(8,128)S(1)}, f32[2,5,16,128]{3,2,1,0:T(8,128)S(1)}, u32[]{:S(2)}, u32[]{:S(2)}) %collective-permute-start.2) | collective-permute-done | bytes 81952 | tf_op jit(solution)/shard_map/ppermute | solution.py:298
  41.3 1.3 %shard_map.98.pair_ref = f32[5,16,128]{2,1,0:T(8,128)S(1)} custom-call(f32[2,5,16,128]{3,2,1,0:T(8,128)S(1)} %get-tuple-element.17.ends_ref, f32[2,5,16,128]{3,2,1,0:T(8,128)S(1)} %collective-permute-done.2.ends_other_ref, f32[3,5,5,16,128]{4,3,2,1,0:T(8,128)} %get-tuple-element.18.mats_ref.mine_ref, ...), custom_call_target="tpu_custom_call" | custom-call | flops 1000000 | bytes 1433600 | tf_op jit(solution)/shard_map/pallas_call | solution.py:23
  42.6 2.3 %collective-permute-start.4 = (f32[5,16,128]{2,1,0:T(8,128)S(1)}, f32[5,16,128]{2,1,0:T(8,128)S(1)}, u32[]{:S(2)}, u32[]{:S(2)}) collective-permute-start(f32[5,16,128]{2,1,0:T(8,128)S(1)} %shard_map.98.pair_ref), channel_id=1, source_target_pairs={{0,2},{1,3},{2,0},{3,1},{4,6},{5,7},{6,4},{7,5},{8,10},{9,11},{10,... | collective-permute-start | bytes 122888 | tf_op jit(solution)/shard_map/ppermute | solution.py:298
  44.9 0.9 %slice.26.f_below_ref = f32[5,5,16,128]{3,2,1,0:T(8,128)S(1)} slice(f32[6,5,16,128]{3,2,1,0:T(8,128)} %collective-permute-done), slice={[1:6], [0:5], [0:16], [0:128]} | slice | bytes 409600 | tf_op jit(solution)/shard_map/slice | solution.py:310
  45.9 1.1 %collective-permute-done.4.pair_other_ref = f32[5,16,128]{2,1,0:T(8,128)S(1)} collective-permute-done((f32[5,16,128]{2,1,0:T(8,128)S(1)}, f32[5,16,128]{2,1,0:T(8,128)S(1)}, u32[]{:S(2)}, u32[]{:S(2)}) %collective-permute-start.4) | collective-permute-done | bytes 40992 | tf_op jit(solution)/shard_map/ppermute | solution.py:298
  47.0 0.0 collective-permute-done.5.beta_ref
  47.0 0.0 copy-start.13
  47.0 1.9 %shard_map.100 = (f32[8,5,16,128]{3,2,1,0:T(8,128)S(1)}, f32[5,16,128]{2,1,0:T(8,128)S(1)}, f32[5,16,128]{2,1,0:T(8,128)S(1)}, f32[8,16,128]{2,1,0:T(8,128)S(1)}) custom-call(s32[8]{0:T(128)S(1)} %copy-done.16, f32[8,5,16,128]{3,2,1,0:T(8,128)S(1)} %bitcast.29, f32[8,5,16,128]{3,2,1,0:T(8,128)S(1)} %get-tuple-element.16.s_ref, ...), custom_call_target="tpu_custom_call" | custom-call | flops 1000000 | bytes 6373408 | tf_op jit(solution)/shard_map/pallas_call | solution.py:23
  48.9 12.8 %all_to_all.10.tiles_ref = f32[8,16,128]{2,1,0:T(8,128)S(1)} all-to-all(f32[8,16,128]{2,1,0:T(8,128)S(1)} %get-tuple-element.22), channel_id=1, replica_groups=mesh['zone'=8,'ja'=4] {'zone'}, dimensions={0} | all-to-all | bytes 131072 | tf_op jit(solution)/shard_map/all_to_all | solution.py:301
  61.8 0.0 copy-done.4
  61.8 0.0 copy-done.7
  61.8 0.0 copy-done.9
  61.8 0.0 copy-done.13
  61.8 2.3 %shard_map.101 = (f32[8,5,16,128]{3,2,1,0:T(8,128)}, f32[8,5,16,128]{3,2,1,0:T(8,128)S(1)}, f32[2,5,16,128]{3,2,1,0:T(8,128)S(1)}) custom-call(s32[8]{0:T(128)S(1)} %copy-done.16, s32[8]{0:T(128)S(1)} %copy-done.17, f32[8,5,16,128]{3,2,1,0:T(8,128)S(1)} %get-tuple-element.19.cur_ref, f32[8,5,16,128]{3,2,1,0:T(8,128)S(1)} %bitcast.31, ...), custom_call_target="tpu_custom_call" | custom-call | flops 1000000 | bytes 11370560 | tf_op jit(solution)/shard_map/pallas_call | solution.py:23
  64.1 0.0 collective-permute-start.6
  64.1 1.3 %collective-permute-done.6.ends_other_ref = f32[2,5,16,128]{3,2,1,0:T(8,128)S(1)} collective-permute-done((f32[2,5,16,128]{3,2,1,0:T(8,128)S(1)}, f32[2,5,16,128]{3,2,1,0:T(8,128)S(1)}, u32[]{:S(2)}, u32[]{:S(2)}) %collective-permute-start.6) | collective-permute-done | bytes 81952 | tf_op jit(solution)/shard_map/ppermute | solution.py:298
  65.3 1.3 %shard_map.102.pair_ref = f32[5,16,128]{2,1,0:T(8,128)S(1)} custom-call(f32[2,5,16,128]{3,2,1,0:T(8,128)S(1)} %get-tuple-element.24.ends_ref, f32[2,5,16,128]{3,2,1,0:T(8,128)S(1)} %collective-permute-done.6.ends_other_ref, f32[3,5,5,16,128]{4,3,2,1,0:T(8,128)} %get-tuple-element.18.mats_ref.mine_ref, ...), custom_call_target="tpu_custom_call" | custom-call | flops 1000000 | bytes 1433600 | tf_op jit(solution)/shard_map/pallas_call | solution.py:23
  66.6 2.0 %collective-permute-start.7 = (f32[5,16,128]{2,1,0:T(8,128)S(1)}, f32[5,16,128]{2,1,0:T(8,128)S(1)}, u32[]{:S(2)}, u32[]{:S(2)}) collective-permute-start(f32[5,16,128]{2,1,0:T(8,128)S(1)} %shard_map.102.pair_ref), channel_id=1, source_target_pairs={{0,2},{1,3},{2,0},{3,1},{4,6},{5,7},{6,4},{7,5},{8,10},{9,11},{10,... | collective-permute-start | bytes 122888 | tf_op jit(solution)/shard_map/ppermute | solution.py:298
  68.6 2.1 %collective-permute-done.7.pair_other_ref = f32[5,16,128]{2,1,0:T(8,128)S(1)} collective-permute-done((f32[5,16,128]{2,1,0:T(8,128)S(1)}, f32[5,16,128]{2,1,0:T(8,128)S(1)}, u32[]{:S(2)}, u32[]{:S(2)}) %collective-permute-start.7) | collective-permute-done | bytes 40992 | tf_op jit(solution)/shard_map/ppermute | solution.py:298
  70.7 2.3 %shard_map.103 = f32[8,5,16,128]{3,2,1,0:T(8,128)} custom-call(s32[8]{0:T(128)S(1)} %copy-done.16, f32[8,5,16,128]{3,2,1,0:T(8,128)S(1)} %get-tuple-element.19.cur_ref, f32[8,5,16,128]{3,2,1,0:T(8,128)S(1)} %get-tuple-element.23.s_ref, f32[8,5,5,16,128]{4,3,2,1,0:T(8,128)S(1)} %get-tuple-element.14.e_ref, f32[8,5,5,16,128]{4,3,2,1,0:T(8,128)S(1)} %get-tuple-element.15.f_ref, ...), custom_call_target="tpu_custom_call" | custom-call | flops 1000000 | bytes 6225952 | tf_op jit(solution)/shard_map/pallas_call | solution.py:23
  (5 shorter events, 0.0 us)
Async XLA Ops:
  0.6 1.4 %copy-start = (f32[1,8,5,5,16,128]{5,4,3,2,1,0:T(8,128)S(1)}, f32[1,8,5,5,16,128]{5,4,3,2,1,0:T(8,128)}, u32[]{:S(2)}) copy-start(f32[1,8,5,5,16,128]{5,4,3,2,1,0:T(8,128)} %param.11) | copy-start | bytes 4915204
  2.1 1.4 %copy-start.2 = (f32[1,8,5,5,16,128]{5,4,3,2,1,0:T(8,128)S(1)}, f32[1,8,5,5,16,128]{5,4,3,2,1,0:T(8,128)}, u32[]{:S(2)}) copy-start(f32[1,8,5,5,16,128]{5,4,3,2,1,0:T(8,128)} %param.12) | copy-start | bytes 4915204
  3.5 1.4 %copy-start.5 = (f32[1,8,5,5,16,128]{5,4,3,2,1,0:T(8,128)S(1)}, f32[1,8,5,5,16,128]{5,4,3,2,1,0:T(8,128)}, u32[]{:S(2)}) copy-start(f32[1,8,5,5,16,128]{5,4,3,2,1,0:T(8,128)} %param.13) | copy-start | bytes 4915204
  4.9 4.4 %copy-start.10 = (f32[1,8,5,16,128]{4,3,2,1,0:T(8,128)S(1)}, f32[1,8,5,16,128]{4,3,2,1,0:T(8,128)}, u32[]{:S(2)}) copy-start(f32[1,8,5,16,128]{4,3,2,1,0:T(8,128)} %param.8) | copy-start | bytes 983044
  4.9 8.4 %copy-start.16 = (s32[8]{0:T(128)S(1)}, s32[8]{0:T(128)}, u32[]{:S(2)}) copy-start(s32[8]{0:T(128)} %depth_ref.9) | copy-start | bytes 100
  8.9 20.1 %copy-start.17 = (s32[8]{0:T(128)S(1)}, s32[8]{0:T(128)}, u32[]{:S(2)}) copy-start(s32[8]{0:T(128)} %east_ref.3) | copy-start | bytes 100
  8.9 14.4 %collective-permute-start.3 = (f32[3,5,5,16,128]{4,3,2,1,0:T(8,128)}, f32[3,5,5,16,128]{4,3,2,1,0:T(8,128)}, u32[]{:S(2)}, u32[]{:S(2)}) collective-permute-start(f32[3,5,5,16,128]{4,3,2,1,0:T(8,128)} %get-tuple-element.18.mats_ref.mine_ref), channel_id=1, source_target_pairs={{0,1},{1,0},{2,3},{3,2},{4,5},{5,4},{6,7},{7,6},{8,9},{9,8},{10,11... | collective-permute-start | bytes 1843208 | tf_op jit(solution)/shard_map/ppermute | solution.py:298
  10.7 15.9 %collective-permute-start = (f32[6,5,16,128]{3,2,1,0:T(8,128)}, f32[6,5,16,128]{3,2,1,0:T(8,128)}, u32[]{:S(2)}, u32[]{:S(2)}) collective-permute-start(f32[6,5,16,128]{3,2,1,0:T(8,128)} %pad_maximum_fusion), channel_id=1, source_target_pairs={{0,1},{1,2},{2,3},{4,5},{5,6},{6,7},{8,9},{9,10},{10,11},{12,13},{... | collective-permute-start | bytes 737288 | tf_op jit(solution)/shard_map/ppermute | solution.py:309
  14.7 14.3 %all-to-all-start = ((f32[8,16,128]{2,1,0:T(8,128)}), f32[8,16,128]{2,1,0:T(8,128)}, u32[]{:S(2)}, u32[]{:S(2)}) async-start(f32[8,16,128]{2,1,0:T(8,128)} %shard_map.96), calls=%async_computation | async-start | bytes 131072 | tf_op jit(solution)/shard_map/all_to_all | solution.py:301
  22.0 5.5 %collective-permute-start.1 = (f32[5,16,128]{2,1,0:T(8,128)}, f32[5,16,128]{2,1,0:T(8,128)S(1)}, u32[]{:S(2)}, u32[]{:S(2)}) collective-permute-start(f32[5,16,128]{2,1,0:T(8,128)} %get-tuple-element.26), channel_id=1, source_target_pairs={{1,0},{2,1},{3,2},{5,4},{6,5},{7,6},{9,8},{10,9},{11,10},{13,12},{... | collective-permute-start | bytes 122888 | tf_op jit(solution)/shard_map/ppermute | solution.py:304
  25.4 21.6 %collective-permute-start.5 = (f32[5,5,16,128]{3,2,1,0:T(8,128)}, f32[5,5,16,128]{3,2,1,0:T(8,128)S(1)}, u32[]{:S(2)}, u32[]{:S(2)}) collective-permute-start(f32[5,5,16,128]{3,2,1,0:T(8,128)} %shard_map.99), channel_id=1, source_target_pairs={{2,0},{3,1},{6,4},{7,5},{10,8},{11,9},{14,12},{15,13},{18,16},{19,... | collective-permute-start | bytes 614408 | tf_op jit(solution)/shard_map/ppermute | solution.py:313
  27.4 0.6 copy-start.14
  29.0 1.4 %copy-start.1 = (f32[1,8,5,5,16,128]{5,4,3,2,1,0:T(8,128)S(1)}, f32[1,8,5,5,16,128]{5,4,3,2,1,0:T(8,128)}, u32[]{:S(2)}) copy-start(f32[1,8,5,5,16,128]{5,4,3,2,1,0:T(8,128)} %param.11) | copy-start | bytes 4915204
  30.4 1.4 %copy-start.3 = (f32[1,8,5,5,16,128]{5,4,3,2,1,0:T(8,128)S(1)}, f32[1,8,5,5,16,128]{5,4,3,2,1,0:T(8,128)}, u32[]{:S(2)}) copy-start(f32[1,8,5,5,16,128]{5,4,3,2,1,0:T(8,128)} %param.12) | copy-start | bytes 4915204
  31.9 1.4 %copy-start.6 = (f32[1,8,5,5,16,128]{5,4,3,2,1,0:T(8,128)S(1)}, f32[1,8,5,5,16,128]{5,4,3,2,1,0:T(8,128)}, u32[]{:S(2)}) copy-start(f32[1,8,5,5,16,128]{5,4,3,2,1,0:T(8,128)} %param.13) | copy-start | bytes 4915204
  33.3 1.4 %copy-start.8 = (f32[1,8,5,5,16,128]{5,4,3,2,1,0:T(8,128)S(1)}, f32[1,8,5,5,16,128]{5,4,3,2,1,0:T(8,128)}, u32[]{:S(2)}) copy-start(f32[1,8,5,5,16,128]{5,4,3,2,1,0:T(8,128)} %param.10) | copy-start | bytes 4915204
  34.7 1.0 %copy-start.11 = (f32[1,8,5,16,128]{4,3,2,1,0:T(8,128)S(1)}, f32[1,8,5,16,128]{4,3,2,1,0:T(8,128)}, u32[]{:S(2)}) copy-start(f32[1,8,5,16,128]{4,3,2,1,0:T(8,128)} %param.8) | copy-start | bytes 983044
  35.7 1.0 %copy-start.12 = (f32[1,8,5,16,128]{4,3,2,1,0:T(8,128)S(1)}, f32[1,8,5,16,128]{4,3,2,1,0:T(8,128)}, u32[]{:S(2)}) copy-start(f32[1,8,5,16,128]{4,3,2,1,0:T(8,128)} %param.9) | copy-start | bytes 983044
  36.7 0.8 %copy-start.15 = (f32[5,16,128]{2,1,0:T(8,128)S(1)}, f32[5,16,128]{2,1,0:T(8,128)}, u32[]{:S(2)}) copy-start(f32[5,16,128]{2,1,0:T(8,128)} %copy-done.14) | copy-start | bytes 122884
  40.1 1.3 %collective-permute-start.2 = (f32[2,5,16,128]{3,2,1,0:T(8,128)S(1)}, f32[2,5,16,128]{3,2,1,0:T(8,128)S(1)}, u32[]{:S(2)}, u32[]{:S(2)}) collective-permute-start(f32[2,5,16,128]{3,2,1,0:T(8,128)S(1)} %get-tuple-element.17.ends_ref), channel_id=1, source_target_pairs={{0,1},{1,0},{2,3},{3,2},{4,5},{5,4},{6,7},{7,6},{8,9},{9,8},{10,11... | collective-permute-start | bytes 245768 | tf_op jit(solution)/shard_map/ppermute | solution.py:298
  42.6 4.4 %collective-permute-start.4 = (f32[5,16,128]{2,1,0:T(8,128)S(1)}, f32[5,16,128]{2,1,0:T(8,128)S(1)}, u32[]{:S(2)}, u32[]{:S(2)}) collective-permute-start(f32[5,16,128]{2,1,0:T(8,128)S(1)} %shard_map.98.pair_ref), channel_id=1, source_target_pairs={{0,2},{1,3},{2,0},{3,1},{4,6},{5,7},{6,4},{7,5},{8,10},{9,11},{10,... | collective-permute-start | bytes 122888 | tf_op jit(solution)/shard_map/ppermute | solution.py:298
  47.0 14.7 %copy-start.4 = (f32[1,8,5,5,16,128]{5,4,3,2,1,0:T(8,128)S(1)}, f32[1,8,5,5,16,128]{5,4,3,2,1,0:T(8,128)}, u32[]{:S(2)}) copy-start(f32[1,8,5,5,16,128]{5,4,3,2,1,0:T(8,128)} %param.12) | copy-start | bytes 4915204
  47.0 14.7 %copy-start.7 = (f32[1,8,5,5,16,128]{5,4,3,2,1,0:T(8,128)S(1)}, f32[1,8,5,5,16,128]{5,4,3,2,1,0:T(8,128)}, u32[]{:S(2)}) copy-start(f32[1,8,5,5,16,128]{5,4,3,2,1,0:T(8,128)} %param.13) | copy-start | bytes 4915204
  47.0 14.7 %copy-start.9 = (f32[1,8,5,5,16,128]{5,4,3,2,1,0:T(8,128)S(1)}, f32[1,8,5,5,16,128]{5,4,3,2,1,0:T(8,128)}, u32[]{:S(2)}) copy-start(f32[1,8,5,5,16,128]{5,4,3,2,1,0:T(8,128)} %param.10) | copy-start | bytes 4915204
  47.0 14.7 %copy-start.13 = (f32[1,8,5,16,128]{4,3,2,1,0:T(8,128)S(1)}, f32[1,8,5,16,128]{4,3,2,1,0:T(8,128)}, u32[]{:S(2)}) copy-start(f32[1,8,5,16,128]{4,3,2,1,0:T(8,128)} %param.9) | copy-start | bytes 983044
  64.1 1.3 %collective-permute-start.6 = (f32[2,5,16,128]{3,2,1,0:T(8,128)S(1)}, f32[2,5,16,128]{3,2,1,0:T(8,128)S(1)}, u32[]{:S(2)}, u32[]{:S(2)}) collective-permute-start(f32[2,5,16,128]{3,2,1,0:T(8,128)S(1)} %get-tuple-element.24.ends_ref), channel_id=1, source_target_pairs={{0,1},{1,0},{2,3},{3,2},{4,5},{5,4},{6,7},{7,6},{8,9},{9,8},{10,11... | collective-permute-start | bytes 245768 | tf_op jit(solution)/shard_map/ppermute | solution.py:298
  66.6 4.1 %collective-permute-start.7 = (f32[5,16,128]{2,1,0:T(8,128)S(1)}, f32[5,16,128]{2,1,0:T(8,128)S(1)}, u32[]{:S(2)}, u32[]{:S(2)}) collective-permute-start(f32[5,16,128]{2,1,0:T(8,128)S(1)} %shard_map.102.pair_ref), channel_id=1, source_target_pairs={{0,2},{1,3},{2,0},{3,1},{4,6},{5,7},{6,4},{7,5},{8,10},{9,11},{10,... | collective-permute-start | bytes 122888 | tf_op jit(solution)/shard_map/ppermute | solution.py:298
where the time goes:
time: 73.9 us; the launch traced here: 73 us
  Pallas kernels  19.1 us (26%)
  starting transfers between devices  17.4 us (24%)
  local copies, waits for them, and re-layouts  15.7 us (21%)
  blocking collectives  12.8 us (17%)
  waiting for transfers between devices  6.51 us (9%)
  between operations  0.75 us (1%)
    pallas_call x9, Pallas kernels, run(): pl.pallas_call(kernel, out_shape=[jax.ShapeDtypeStruct(s, jnp.float32) fo...  19.1 us
    unnamed x36, local copies, waits for them, and re-layouts  13.4 us
    all_to_all x1, blocking collectives, faces(): return lax.all_to_all(x, 'zone', 0, 0, tiled=True)  12.8 us
    all_to_all x1, starting transfers between devices, faces(): return lax.all_to_all(x, 'zone', 0, 0, tiled=True)  7.28 us
    ppermute x5, waiting for transfers between devices, swap(): return lax.ppermute(x, 'ja', [(p, p ^ bit) for p in range(parts)])  5.58 us
    ppermute x5, starting transfers between devices, swap(): return lax.ppermute(x, 'ja', [(p, p ^ bit) for p in range(parts)])  4.93 us
    ppermute x1, starting transfers between devices, per_device(): edge = lax.ppermute(edge, 'ja', [(p, p + 1) for p in range(parts - 1)])  2.66 us
  transfers between devices with their start and end apart: 9, of which 5 were waited for; matrix products, arithmetic and copies ran while one was open for 4% of the time, Pallas kernels for 10%

commit v1 on v0

v1 whole, which is shorter than its diff:
```python
import functools

import jax
import jax.numpy as jnp
from jax import lax
from jax.experimental import pallas as pl
from jax.experimental.pallas import tpu as pltpu
from jax.sharding import PartitionSpec as P

ITERS = 2
OMEGA = 1.2
COUPLE = 0.25

VMEM = pl.BlockSpec(memory_space=pltpu.VMEM)
SMEM = pl.BlockSpec(memory_space=pltpu.SMEM)
HBM = pl.BlockSpec(memory_space=pltpu.HBM)


def call(kernel, shapes, scratch=(), flops=10**9, far=(), far_out=()):
    moved = sum(4 * functools.reduce(lambda a, b: a * b, s, 1) for s in shapes)

    def spec(i, a):
        return HBM if i in far else VMEM if a.dtype == jnp.float32 else SMEM

    def run(*arrays):
        total = moved + sum(a.size * 4 for a in arrays)
        return pl.pallas_call(
            kernel,
            out_shape=[jax.ShapeDtypeStruct(s, jnp.float32) for s in shapes],
            in_specs=[spec(i, a) for i, a in enumerate(arrays)],
            out_specs=[HBM if i in far_out else VMEM for i in range(len(shapes))],
            scratch_shapes=list(scratch),
            compiler_params=pltpu.CompilerParams(vmem_limit_bytes=12 * 2**20),
            cost_estimate=pl.CostEstimate(flops=flops, bytes_accessed=total, transcendentals=0),
        )(*arrays)

    return run


def buffer(*shape):
    return pltpu.VMEM(shape, jnp.float32)


def iota(dim):
    return lax.broadcasted_iota(jnp.int32, (16, 128), dim)


def matvec(matrix, vector):
    n = len(vector)
    out = []
    for r in range(n):
        acc = matrix[r][0] * vector[0]
        for c in range(1, n):
            acc = acc + matrix[r][c] * vector[c]
        out.append(acc)
    return out


def block(ref, *lead):
    return [[ref[(*lead, r, c)] for c in range(5)] for r in range(5)]


def cell(ref, *lead):
    return [ref[(*lead, v)] for v in range(5)]


def put(ref, values, *lead):
    for v, value in enumerate(values):
        ref[(*lead, v)] = value


def add(a, b):
    return [x + y for x, y in zip(a, b)]


def pack_faces(load, planes, tile_ref):
    lane = iota(1)
    tile = jnp.zeros((16, 128), jnp.float32)
    for j in range(planes):
        for v in range(5):
            q = 2 * (j * 5 + v)
            here = (lane == q) | (lane == (q - 1) % 128)
            x = load(j, v)
            tile = jnp.where(here, pltpu.roll(x, q, 1) if q else x, tile)
    for w in range(tile_ref.shape[0]):
        tile_ref[w] = tile


def live_rows(depth_ref):
    return iota(0) < depth_ref[lax.axis_index("zone")]


def pack_kernel(depth_ref, flow_hbm, tile_ref, cur_ref, first_ref, flow_ref, sem):
    copy = pltpu.make_async_copy(flow_hbm, flow_ref, sem)
    copy.start()
    live = live_rows(depth_ref)
    copy.wait()
    planes = flow_ref.shape[0]
    for j in range(planes):
        for v in range(5):
            cur_ref[j, v] = jnp.where(live, flow_ref[j, v], 0.0)
    for v in range(5):
        first_ref[v] = jnp.where(live, flow_ref[0, v], 0.0)
    pack_faces(lambda j, v: cur_ref[j, v], planes, tile_ref)


def neighbours(x):
    lane, row = iota(1), iota(0)
    total = jnp.where(lane == 0, 0.0, pltpu.roll(x, 1, 1))
    total = total + jnp.where(lane == 127, 0.0, pltpu.roll(x, 127, 1))
    total = total + jnp.where(row == 0, 0.0, pltpu.roll(x, 1, 0))
    return total + jnp.where(row == 15, 0.0, pltpu.roll(x, 15, 0))


def ghosts_of(east_ref, tiles_ref):
    zone = lax.axis_index("zone")
    east = east_ref[zone]
    west = jnp.int32(0)
    for w in range(tiles_ref.shape[0]):
        west = west + jnp.where(east_ref[w] == zone, w, 0)
    return jnp.where(
        iota(1) % 2 == 0, pltpu.roll(tiles_ref[west], 1, 1), pltpu.roll(tiles_ref[east], 127, 1)
    )


def ghost_at(ghosts, j, v, ends):
    q = 2 * (j * 5 + v)
    turned = pltpu.roll(ghosts, 128 - q, 1) if q else ghosts
    return jnp.where(ends, turned, 0.0)


def first_kernel(
    depth_ref, cur_ref, above_ref, force_hbm, diag_hbm, low_hbm, up_hbm, inv_hbm,
    e_ref, f_ref, inv_ref, s_ref, mats_ref,
    force_ref, diag_ref, low_ref, up_ref, y_ref, wide_ref, sems,
):
    planes = cur_ref.shape[0]
    pairs = [
        (inv_hbm, inv_ref), (low_hbm, low_ref), (up_hbm, up_ref),
        (diag_hbm, diag_ref), (force_hbm, force_ref),
    ]

    def copies(j):
        return [
            pltpu.make_async_copy(src.at[j], dst.at[j], sems.at[i, j])
            for i, (src, dst) in enumerate(pairs)
        ]

    for j in range(planes):
        for copy in copies(j):
            copy.start()
    live = live_rows(depth_ref)
    zero = jnp.zeros((16, 128), jnp.float32)
    for v in range(5):
        wide_ref[0, v] = zero
        wide_ref[planes + 1, v] = above_ref[v]
        for j in range(planes):
            wide_ref[j + 1, v] = cur_ref[j, v]

    halves = [pl.ds(0, 8), pl.ds(8, 8)]

    def col(ref, q, j, rows):
        return [ref[j, r, q, rows] for r in range(5)]

    def put_col(ref, values, q, j, rows):
        for r in range(5):
            ref[j, r, q, rows] = values[r]

    def mat(ref, j, rows):
        return [[ref[j, r, c, rows] for c in range(5)] for r in range(5)]

    def forward(j, carry):
        for copy in copies(j):
            copy.wait()
        for rows in halves:
            inv = mat(inv_ref, j, rows)
            for jac_ref, out_ref in ((low_ref, e_ref), (up_ref, f_ref)):
                for q in range(5):
                    product = matvec(inv, col(jac_ref, q, j, rows))
                    put_col(out_ref, [OMEGA * x for x in product], q, j, rows)
        here = cell(wide_ref, j + 1)
        own = matvec(block(diag_ref, j), here)
        lower = matvec(block(low_ref, j), cell(wide_ref, j))
        upper = matvec(block(up_ref, j), cell(wide_ref, j + 2))
        res = []
        for v in range(5):
            applied = own[v] - lower[v] - upper[v] - COUPLE * neighbours(here[v])
            res.append(jnp.where(live, force_ref[j, v] - applied, 0.0))
        put(s_ref, matvec(block(inv_ref, j), res), j)
        return carry

    def chain(j, carry):
        for rows in halves:
            e = mat(e_ref, j, rows)
            for q in range(5):
                put_col(y_ref, matvec(e, col(y_ref, q, j - 1, rows)), q, j, rows)
        return carry

    forward(0, 0)
    for rows in halves:
        for q in range(5):
            put_col(y_ref, col(e_ref, q, 0, rows), q, 0, rows)

    def both(j, carry):
        return chain(j, forward(j, carry))

    lax.fori_loop(1, planes, both, 0)
    last = planes - 1
    for rows in halves:
        for q in range(5):
            put_col(mats_ref, col(y_ref, q, last, rows), q, 0, rows)
            put_col(mats_ref, col(y_ref, q, last, rows), q, 1, rows)
            put_col(mats_ref, col(f_ref, q, last, rows), q, 2, rows)

    def backward(step, carry):
        j = planes - 2 - step
        for rows in halves:
            f = mat(f_ref, j, rows)
            for q in range(5):
                turned = matvec(f, col(mats_ref, q, 1, rows))
                put_col(mats_ref, add(col(y_ref, q, j, rows), turned), q, 1, rows)
                put_col(mats_ref, matvec(f, col(mats_ref, q, 2, rows)), q, 2, rows)
        return carry

    lax.fori_loop(0, planes - 1, backward, 0)


def by_place(mine_refs, other_refs, run):
    odd = lax.axis_index("ja") % 2

    @pl.when(odd == 0)
    def _():
        run(*mine_refs, *other_refs)

    @pl.when(odd == 1)
    def _():
        run(*other_refs, *mine_refs)


def beta_kernel(mine_ref, other_ref, beta_ref):
    def run(lo, hi):
        d_hi, n_lo = block(hi, 1), block(lo, 2)
        for q in range(5):
            m_col = [lo[0, r, q] for r in range(5)]
            d_col = [lo[1, r, q] for r in range(5)]
            out = add(d_col, matvec(n_lo, matvec(d_hi, m_col)))
            for r in range(5):
                beta_ref[r, q] = out[r]

    by_place([mine_ref], [other_ref], run)


def sweeps(s_ref, e_ref, f_ref, y_ref, ends_ref, last):
    planes = s_ref.shape[0]
    value = cell(s_ref, 0)
    put(y_ref, value, 0)
    for j in range(1, planes):
        value = add(cell(s_ref, j), matvec(block(e_ref, j), value))
        put(y_ref, value, j)
    put(ends_ref, [x + z * (1.0 / OMEGA) for x, z in zip(value, last)], 0)
    for j in range(planes - 2, -1, -1):
        value = add(cell(y_ref, j), matvec(block(f_ref, j), value))
    put(ends_ref, value, 1)


def ghost_kernel(
    depth_ref, east_ref, tiles_ref, cur_ref, s0_ref, inv_ref, e_ref, f_ref,
    s_ref, ends_ref, y_ref,
):
    planes = cur_ref.shape[0]
    ghosts = ghosts_of(east_ref, tiles_ref)
    ghosts = jnp.where(live_rows(depth_ref), COUPLE * ghosts, 0.0)
    lane = iota(1)
    ends = (lane == 0) | (lane == 127)
    for j in range(planes):
        extra = [ghost_at(ghosts, j, v, ends) for v in range(5)]
        put(s_ref, add(cell(s0_ref, j), matvec(block(inv_ref, j), extra)), j)
    sweeps(s_ref, e_ref, f_ref, y_ref, ends_ref, cell(cur_ref, planes - 1))


def local_kernel(
    depth_ref, east_ref, tiles_ref, cur_ref, above_ref, force_ref, diag_ref, low_ref, up_ref,
    inv_ref, e_ref, f_ref,
    res_ref, s_ref, ends_ref, y_ref,
):
    planes = cur_ref.shape[0]
    live = live_rows(depth_ref)
    ghosts = ghosts_of(east_ref, tiles_ref)
    lane = iota(1)
    ends = (lane == 0) | (lane == 127)
    for j in range(planes):
        here = cell(cur_ref, j)
        applied = matvec(block(diag_ref, j), here)
        if j > 0:
            lower = matvec(block(low_ref, j), cell(cur_ref, j - 1))
            applied = [x - z for x, z in zip(applied, lower)]
        above = cell(cur_ref, j + 1) if j < planes - 1 else cell(above_ref)
        upper = matvec(block(up_ref, j), above)
        res = []
        for v in range(5):
            sides = neighbours(here[v]) + ghost_at(ghosts, j, v, ends)
            all_of = applied[v] - upper[v] - COUPLE * sides
            res.append(jnp.where(live, force_ref[j, v] - all_of, 0.0))
        put(res_ref, res, j)
        put(s_ref, matvec(block(inv_ref, j), res), j)
    last = cell(cur_ref, planes - 1)
    sweeps(s_ref, e_ref, f_ref, y_ref, ends_ref, last)
    put(ends_ref, last, 2)


def mid_kernel(ends_ref, ends_other_ref, mats_ref, mats_other_ref, out_ref):
    def run(ends_lo, mats_lo, ends_hi, mats_hi):
        c_lo = cell(ends_lo, 0)

        @pl.when(lax.axis_index("ja") < 2)
        def _():
            put(out_ref, add(cell(ends_hi, 0), matvec(block(mats_hi, 0), c_lo)), 0)

        @pl.when(lax.axis_index("ja") >= 2)
        def _():
            turned = add(cell(ends_hi, 1), matvec(block(mats_hi, 1), c_lo))
            put(out_ref, add(cell(ends_lo, 1), matvec(block(mats_lo, 2), turned)), 0)

        if out_ref.shape[0] > 1:
            put(out_ref, cell(ends_hi, 2), 1)

    by_place([ends_ref, mats_ref], [ends_other_ref, mats_other_ref], run)


def inflows(
    ends_ref, ends_other_ref, mats_ref, mats_other_ref, pair_ref, pair_other_ref, beta_ref,
    inflow_ref,
):
    ja = lax.axis_index("ja")
    zeros = [jnp.zeros((16, 128), jnp.float32)] * 5

    def far(a, alpha):
        return add(cell(alpha, 0), matvec(block(beta_ref), cell(a, 0)))

    @pl.when(ja == 0)
    def _():
        put(inflow_ref, zeros, 0)
        b = add(cell(ends_other_ref, 1), matvec(block(mats_other_ref, 1), cell(ends_ref, 0)))
        b = add(b, matvec(block(mats_other_ref, 2), far(pair_ref, pair_other_ref)))
        put(inflow_ref, b, 1)

    @pl.when(ja == 1)
    def _():
        put(inflow_ref, cell(ends_other_ref, 0), 0)
        put(inflow_ref, far(pair_ref, pair_other_ref), 1)

    @pl.when(ja == 2)
    def _():
        a = cell(pair_other_ref, 0)
        put(inflow_ref, a, 0)
        a = add(cell(ends_ref, 0), matvec(block(mats_ref, 0), a))
        b = add(cell(ends_other_ref, 1), matvec(block(mats_other_ref, 1), a))
        put(inflow_ref, b, 1)

    @pl.when(ja == 3)
    def _():
        a = add(cell(ends_other_ref, 0), matvec(block(mats_other_ref, 0), cell(pair_other_ref, 0)))
        put(inflow_ref, a, 0)
        put(inflow_ref, zeros, 1)


def final_kernel(
    cur_ref, above_ref, s_ref, e_ref, f_ref,
    ends_ref, ends_other_ref, mats_ref, mats_other_ref, pair_ref, pair_other_ref, beta_ref,
    new_ref, above_new_ref, tile_ref, y_ref, inflow_ref,
):
    planes = cur_ref.shape[0]
    inflows(
        ends_ref, ends_other_ref, mats_ref, mats_other_ref, pair_ref, pair_other_ref, beta_ref,
        inflow_ref,
    )
    value = cell(inflow_ref, 0)
    for j in range(planes):
        value = add(cell(s_ref, j), matvec(block(e_ref, j), value))
        put(y_ref, value, j)
    value = cell(inflow_ref, 1)
    put(above_new_ref, add(cell(above_ref), value))
    for j in range(planes - 1, -1, -1):
        value = add(cell(y_ref, j), matvec(block(f_ref, j), value))
        put(new_ref, add(cell(cur_ref, j), value), j)
    pack_faces(lambda j, v: new_ref[j, v], planes, tile_ref)


def last_kernel(
    depth_ref, low_hbm, cur_ref, res_ref, s_ref, e_ref, f_ref,
    ends_ref, ends_other_ref, mats_ref, mats_other_ref, pair_ref, pair_other_ref, beta_ref,
    new_hbm, res_hbm, y_ref, inflow_ref, new_ref, low_ref, edge_ref, sems,
):
    planes = cur_ref.shape[0]
    low_copy = pltpu.make_async_copy(low_hbm.at[0], low_ref, sems.at[0, 0])
    low_copy.start()
    copies = []
    for j in range(1, planes):
        copies.append(pltpu.make_async_copy(res_ref.at[j], res_hbm.at[j], sems.at[0, j]))
        copies[-1].start()
    inflows(
        ends_ref, ends_other_ref, mats_ref, mats_other_ref, pair_ref, pair_other_ref, beta_ref,
        inflow_ref,
    )
    value = cell(inflow_ref, 0)
    for j in range(planes):
        value = add(cell(s_ref, j), matvec(block(e_ref, j), value))
        put(y_ref, value, j)
    ja = lax.axis_index("ja")
    live = live_rows(depth_ref)
    before = [
        jnp.where(ja == 0, 0.0, jnp.where(ja == 2, pair_other_ref[1, v], ends_other_ref[2, v]))
        for v in range(5)
    ]
    low_copy.wait()
    extra = matvec(block(low_ref), before)
    put(edge_ref, [res_ref[0, v] + jnp.where(live, extra[v], 0.0) for v in range(5)])
    copies.append(pltpu.make_async_copy(edge_ref, res_hbm.at[0], sems.at[1, planes]))
    copies[-1].start()
    value = cell(inflow_ref, 1)
    for j in range(planes - 1, -1, -1):
        value = add(cell(y_ref, j), matvec(block(f_ref, j), value))
        put(new_ref, add(cell(cur_ref, j), value), j)
        copies.append(pltpu.make_async_copy(new_ref.at[j], new_hbm.at[j], sems.at[1, j]))
        copies[-1].start()
    for copy in copies:
        copy.wait()


def per_device(
    flow_state, forcing, diag_block, lower_jac, upper_jac, block_inv, east_zone, zone_depth
):
    zones, parts = lax.axis_size("zone"), lax.axis_size("ja")
    assert parts == 4 and ITERS == 2
    current, force, diag, low, up, inv = (
        x[0] for x in (flow_state, forcing, diag_block, lower_jac, upper_jac, block_inv)
    )
    state = current.shape
    planes, plane, blocks, tiles = state[0], state[1:], diag.shape, (zones, *state[2:])
    matrix = blocks[1:]
    wide = buffer(planes + 2, *plane)

    def swap(x, bit):
        return lax.ppermute(x, "ja", [(p, p ^ bit) for p in range(parts)])

    def faces(x):
        return lax.all_to_all(x, "zone", 0, 0, tiled=True)

    tile, current, first = call(
        pack_kernel,
        [tiles, state, plane],
        [buffer(*state), pltpu.SemaphoreType.DMA],
        far=(1,),
    )(zone_depth, current)
    above = lax.ppermute(first, "ja", [(p + 1, p) for p in range(parts - 1)])
    got = faces(tile)
    e, f, inv, s0, mats = call(
        first_kernel,
        [blocks, blocks, blocks, state, (3, *matrix)],
        [buffer(*state)] + [buffer(*blocks)] * 4 + [wide, pltpu.SemaphoreType.DMA((5, planes))],
        flops=5 * 10**9,
        far=(3, 4, 5, 6, 7),
    )(zone_depth, current, above, force, diag, low, up, inv)
    mats_other = swap(mats, 1)
    s, ends = call(ghost_kernel, [state, (2, *plane)], [buffer(*state)])(
        zone_depth, east_zone, got, current, s0, inv, e, f
    )
    ends_other = swap(ends, 1)
    pair = call(mid_kernel, [(1, *plane)])(ends, ends_other, mats, mats_other)[0]
    beta = call(beta_kernel, [matrix])(mats, mats_other)[0]
    beta = lax.ppermute(beta, "ja", [(2, 0), (3, 1)])
    pair_other = swap(pair, 2)
    current, above, tile = call(
        final_kernel,
        [state, plane, tiles],
        [buffer(*state), buffer(2, *plane)],
    )(current, above, s, e, f, ends, ends_other, mats, mats_other, pair, pair_other, beta)

    got = faces(tile)
    residual, s, ends = call(local_kernel, [state, state, (3, *plane)], [buffer(*state)])(
        zone_depth, east_zone, got, current, above, force, diag, low, up, inv, e, f
    )
    ends_other = swap(ends, 1)
    pair = call(mid_kernel, [(2, *plane)])(ends, ends_other, mats, mats_other)[0]
    pair_other = swap(pair, 2)
    current, residual = call(
        last_kernel,
        [state, state],
        [
            buffer(*state), buffer(2, *plane), buffer(*state), buffer(*matrix), buffer(*plane),
            pltpu.SemaphoreType.DMA((2, planes + 1)),
        ],
        far=(1,),
        far_out=(0, 1),
    )(
        zone_depth, low, current, residual, s, e, f,
        ends, ends_other, mats, mats_other, pair, pair_other, beta,
    )
    return (current[None], residual[None])


def solution(mesh):
    state = P("zone", "ja", None, None, None)
    blocks = P("zone", "ja", None, None, None, None)
    return jax.shard_map(
        per_device,
        mesh=mesh,
        in_specs=(state, state, blocks, blocks, blocks, blocks, P(), P()),
        out_specs=(state, state),
        check_vma=False,
    )
```

time: 73.9 us -> 69.9 us (0.946)
  local copies, waits for them, and re-layouts: 15.7 us -> 4.49 us
  blocking collectives: 12.8 us -> 21.9 us
  starting transfers between devices: 17.4 us -> 9.25 us
  waiting for transfers between devices: 6.51 us -> 13.8 us
    all_to_all x1 -> x2, blocking collectives: 12.8 us -> 21.9 us  [faces(): return lax.all_to_all(x, 'zone', 0, 0, tiled=True)]
    unnamed x36 -> x18, local copies, waits for them, and re-layouts: 13.4 us -> 4.49 us
    all_to_all x1 -> x0, starting transfers between devices: 7.28 us -> none  [faces(): return lax.all_to_all(x, 'zone', 0, 0, tiled=True)]
    ppermute x5, waiting for transfers between devices: 5.58 us -> 11.9 us  [swap(): return lax.ppermute(x, 'ja', [(p, p ^ bit) for p in range(parts)])]
    ppermute x2 -> x1, starting transfers between devices: 3.94 us -> 1.42 us  [per_device(): above = lax.ppermute(first, 'ja', [(p + 1, p) for p in range(parts - 1)])]
    ppermute x2 -> x1, waiting for transfers between devices: 0.01 us -> 1.81 us  [per_device(): above = lax.ppermute(first, 'ja', [(p + 1, p) for p in range(parts - 1)])]
    ppermute x5, starting transfers between devices: 4.93 us -> 6.54 us  [swap(): return lax.ppermute(x, 'ja', [(p, p ^ bit) for p in range(parts)])]
    squeeze x3 -> x0, local copies, waits for them, and re-layouts: 1.42 us -> none  [the longest x1 0.78 us: per_device(): below, f_below = (edge[0], edge[1:])]
  transfers between devices with their start and end apart: 9 -> 7, of which waited for: 5 -> 4; matrix products, arithmetic and copies ran while one was open for 4% -> 0% of each run, Pallas kernels for 10% -> 2%
where the time goes in v1:
time: 69.9 us; the launch traced here: 69.5 us
  blocking collectives  21.9 us (31%)
  Pallas kernels  19.3 us (28%)
  waiting for transfers between devices  13.8 us (20%)
  starting transfers between devices  9.25 us (13%)
  local copies, waits for them, and re-layouts  4.49 us (6%)
  between operations  0.78 us (1%)
    all_to_all x2, blocking collectives, faces(): return lax.all_to_all(x, 'zone', 0, 0, tiled=True)  21.9 us
    pallas_call x9, Pallas kernels, run(): pl.pallas_call(kernel, out_shape=[jax.ShapeDtypeStruct(s, jnp.float32) fo...  19.3 us
    ppermute x5, waiting for transfers between devices, swap(): return lax.ppermute(x, 'ja', [(p, p ^ bit) for p in range(parts)])  11.9 us
    ppermute x5, starting transfers between devices, swap(): return lax.ppermute(x, 'ja', [(p, p ^ bit) for p in range(parts)])  6.54 us
    unnamed x18, local copies, waits for them, and re-layouts  4.49 us
    ppermute x1, waiting for transfers between devices, per_device(): above = lax.ppermute(first, 'ja', [(p + 1, p) for p in range(parts - 1)])  1.81 us
    ppermute x1, starting transfers between devices, per_device(): above = lax.ppermute(first, 'ja', [(p + 1, p) for p in range(parts - 1)])  1.42 us
  transfers between devices with their start and end apart: 7, of which 4 were waited for; matrix products, arithmetic and copies ran while one was open for 0% of the time, Pallas kernels for 2%

profile of v1, /device:TPU:0, one launch (start us, length us, event | category | flops | bytes accessed | tf_op | source)
XLA Modules:
  0.0 69.5 jit_solution(16989004576047655539)
XLA Ops:
  0.6 0.0 copy-start.5
  0.6 0.6 copy-done.5
  1.3 0.0 copy-start.8
  1.3 1.0 %copy-done.8 = f32[1,8,5,16,128]{4,3,2,1,0:T(8,128)S(1)} copy-done((f32[1,8,5,16,128]{4,3,2,1,0:T(8,128)S(1)}, f32[1,8,5,16,128]{4,3,2,1,0:T(8,128)}, u32[]{:S(2)}) %copy-start.8) | copy-done | bytes 327704
  2.3 0.0 copy-start
  2.3 0.0 copy-start.1
  2.3 0.0 copy-start.4
  2.3 0.8 %shard_map.95 = (f32[8,16,128]{2,1,0:T(8,128)S(1)}, f32[8,5,16,128]{3,2,1,0:T(8,128)S(1)}, f32[5,16,128]{2,1,0:T(8,128)S(1)}) custom-call(s32[8]{0:T(128)S(1)} %copy-done.5, f32[8,5,16,128]{3,2,1,0:T(8,128)S(1)} %bitcast.18), custom_call_target="tpu_custom_call" | custom-call | flops 1000000000 | bytes 761888 | tf_op jit(solution)/shard_map/pallas_call | solution.py:27
  3.1 1.4 %collective-permute-start = (f32[5,16,128]{2,1,0:T(8,128)S(1)}, f32[5,16,128]{2,1,0:T(8,128)S(1)}, u32[]{:S(2)}, u32[]{:S(2)}) collective-permute-start(f32[5,16,128]{2,1,0:T(8,128)S(1)} %get-tuple-element.21), channel_id=1, source_target_pairs={{1,0},{2,1},{3,2},{5,4},{6,5},{7,6},{9,8},{10,9},{11,10},{13,12},{... | collective-permute-start | bytes 122888 | tf_op jit(solution)/shard_map/ppermute | solution.py:455
  4.5 1.8 %collective-permute-done.above_ref = f32[5,16,128]{2,1,0:T(8,128)S(1)} collective-permute-done((f32[5,16,128]{2,1,0:T(8,128)S(1)}, f32[5,16,128]{2,1,0:T(8,128)S(1)}, u32[]{:S(2)}, u32[]{:S(2)}) %collective-permute-start) | collective-permute-done | bytes 40992 | tf_op jit(solution)/shard_map/ppermute | solution.py:455
  6.3 0.0 copy-done
  6.3 0.0 copy-done.1
  6.3 0.0 copy-done.4
  6.4 0.0 copy-start.2
  6.4 1.4 %copy-done.2 = f32[1,8,5,5,16,128]{5,4,3,2,1,0:T(8,128)S(1)} copy-done((f32[1,8,5,5,16,128]{5,4,3,2,1,0:T(8,128)S(1)}, f32[1,8,5,5,16,128]{5,4,3,2,1,0:T(8,128)}, u32[]{:S(2)}) %copy-start.2) | copy-done | bytes 1638424
  7.8 0.0 copy-start.7
  7.8 1.4 %copy-done.7 = f32[1,8,5,5,16,128]{5,4,3,2,1,0:T(8,128)S(1)} copy-done((f32[1,8,5,5,16,128]{5,4,3,2,1,0:T(8,128)S(1)}, f32[1,8,5,5,16,128]{5,4,3,2,1,0:T(8,128)}, u32[]{:S(2)}) %copy-start.7) | copy-done | bytes 1638424
  9.2 0.0 copy-start.6
  9.2 13.2 %shard_map.96 = (f32[8,5,5,16,128]{4,3,2,1,0:T(8,128)S(1)}, f32[8,5,5,16,128]{4,3,2,1,0:T(8,128)S(1)}, f32[8,5,5,16,128]{4,3,2,1,0:T(8,128)S(1)}, f32[8,5,16,128]{3,2,1,0:T(8,128)S(1)}, f32[3,5,5,16,128]{4,3,2,1,0:T(8,128)S(1)}) custom-call(s32[8]{0:T(128)S(1)} %copy-done.5, f32[8,5,16,128]{3,2,1,0:T(8,128)S(1)} %get-tuple-element.20.cur_ref, ...), custom_call_target="tpu_custom_call" | custom-call | flops 5000000000 | bytes 13107232 | tf_op jit(solution)/shard_map/pallas_call | solution.py:27
  22.5 3.6 %collective-permute-start.2 = (f32[3,5,5,16,128]{4,3,2,1,0:T(8,128)S(1)}, f32[3,5,5,16,128]{4,3,2,1,0:T(8,128)S(1)}, u32[]{:S(2)}, u32[]{:S(2)}) collective-permute-start(f32[3,5,5,16,128]{4,3,2,1,0:T(8,128)S(1)} %get-tuple-element.29.mats_ref.mine_ref), channel_id=1, source_target_pairs={{0,1},{1,0},{2,3},{3,2},{4,5},{5,4},{6,7},{7,6},{8,9},{9,8},{10,11... | collective-permute-start | bytes 1843208 | tf_op jit(solution)/shard_map/ppermute | solution.py:444
  26.0 12.5 %all_to_all.10.tiles_ref = f32[8,16,128]{2,1,0:T(8,128)S(1)} all-to-all(f32[8,16,128]{2,1,0:T(8,128)S(1)} %get-tuple-element.22), channel_id=1, replica_groups=mesh['zone'=8,'ja'=4] {'zone'}, dimensions={0} | all-to-all | bytes 131072 | tf_op jit(solution)/shard_map/all_to_all | solution.py:447
  38.6 0.0 copy-done.6
  38.6 1.0 %shard_map.97 = (f32[8,5,16,128]{3,2,1,0:T(8,128)S(1)}, f32[2,5,16,128]{3,2,1,0:T(8,128)S(1)}) custom-call(s32[8]{0:T(128)S(1)} %copy-done.5, s32[8]{0:T(128)S(1)} %copy-done.6, f32[8,16,128]{2,1,0:T(8,128)S(1)} %all_to_all.10.tiles_ref, f32[8,5,16,128]{3,2,1,0:T(8,128)S(1)} %get-tuple-element.20.cur_ref, f32[8,5,16,128]{3,2,1,0:T(8,128)S(1)} %get-tuple-element.23.s0_ref, ...), custom_call_target="tpu_custom_call" | custom-call | flops 1000000000 | bytes 6045760 | tf_op jit(solution)/shard_map/pallas_call | solution.py:27
  39.6 0.1 collective-permute-start.1
  39.7 0.0 collective-permute-done.2.mats_other_ref.other_ref
  39.7 0.2 shard_map.99
  39.9 1.3 %collective-permute-start.4 = (f32[5,5,16,128]{3,2,1,0:T(8,128)S(1)}, f32[5,5,16,128]{3,2,1,0:T(8,128)S(1)}, u32[]{:S(2)}, u32[]{:S(2)}) collective-permute-start(f32[5,5,16,128]{3,2,1,0:T(8,128)S(1)} %shard_map.99), channel_id=1, source_target_pairs={{2,0},{3,1},{6,4},{7,5},{10,8},{11,9},{14,12},{15,13},{18,16},{19,... | collective-permute-start | bytes 614408 | tf_op jit(solution)/shard_map/ppermute | solution.py:471
  41.2 0.0 collective-permute-done.1.ends_other_ref
  41.2 2.7 %collective-permute-start.3 = (f32[1,5,16,128]{3,2,1,0:T(8,128)S(1)}, f32[1,5,16,128]{3,2,1,0:T(8,128)S(1)}, u32[]{:S(2)}, u32[]{:S(2)}) collective-permute-start(f32[1,5,16,128]{3,2,1,0:T(8,128)S(1)} %shard_map.98.pair_ref), channel_id=1, source_target_pairs={{0,2},{1,3},{2,0},{3,1},{4,6},{5,7},{6,4},{7,5},{8,10},{9,11},{10,... | collective-permute-start | bytes 122888 | tf_op jit(solution)/shard_map/ppermute | solution.py:444
  44.0 6.1 %collective-permute-done.3.pair_other_ref = f32[1,5,16,128]{3,2,1,0:T(8,128)S(1)} collective-permute-done((f32[1,5,16,128]{3,2,1,0:T(8,128)S(1)}, f32[1,5,16,128]{3,2,1,0:T(8,128)S(1)}, u32[]{:S(2)}, u32[]{:S(2)}) %collective-permute-start.3) | collective-permute-done | bytes 40992 | tf_op jit(solution)/shard_map/ppermute | solution.py:444
  50.1 0.0 collective-permute-done.4.beta_ref
  50.1 0.0 copy-start.3
  50.1 0.4 shard_map.100
  50.5 9.4 %all_to_all.11.tiles_ref = f32[8,16,128]{2,1,0:T(8,128)S(1)} all-to-all(f32[8,16,128]{2,1,0:T(8,128)S(1)} %get-tuple-element.31), channel_id=1, replica_groups=mesh['zone'=8,'ja'=4] {'zone'}, dimensions={0} | all-to-all | bytes 131072 | tf_op jit(solution)/shard_map/all_to_all | solution.py:447
  60.0 0.0 copy-done.3
  60.0 1.6 %shard_map.101 = (f32[8,5,16,128]{3,2,1,0:T(8,128)S(1)}, f32[8,5,16,128]{3,2,1,0:T(8,128)S(1)}, f32[3,5,16,128]{3,2,1,0:T(8,128)S(1)}) custom-call(s32[8]{0:T(128)S(1)} %copy-done.5, s32[8]{0:T(128)S(1)} %copy-done.6, f32[8,16,128]{2,1,0:T(8,128)S(1)} %all_to_all.11.tiles_ref, f32[8,5,16,128]{3,2,1,0:T(8,128)S(1)} %get-tuple-element.30.cur_ref, ...), custom_call_target="tpu_custom_call" | custom-call | flops 1000000000 | bytes 11370560 | tf_op jit(solution)/shard_map/pallas_call | solution.py:27
  61.6 0.1 collective-permute-start.5
  61.7 1.3 %collective-permute-done.5.ends_other_ref = f32[3,5,16,128]{3,2,1,0:T(8,128)S(1)} collective-permute-done((f32[3,5,16,128]{3,2,1,0:T(8,128)S(1)}, f32[3,5,16,128]{3,2,1,0:T(8,128)S(1)}, u32[]{:S(2)}, u32[]{:S(2)}) %collective-permute-start.5) | collective-permute-done | bytes 122912 | tf_op jit(solution)/shard_map/ppermute | solution.py:444
  63.0 0.1 collective-permute-start.6
  63.1 4.5 %collective-permute-done.6.pair_other_ref = f32[2,5,16,128]{3,2,1,0:T(8,128)S(1)} collective-permute-done((f32[2,5,16,128]{3,2,1,0:T(8,128)S(1)}, f32[2,5,16,128]{3,2,1,0:T(8,128)S(1)}, u32[]{:S(2)}, u32[]{:S(2)}) %collective-permute-start.6) | collective-permute-done | bytes 81952 | tf_op jit(solution)/shard_map/ppermute | solution.py:444
  67.6 2.0 %shard_map.103 = (f32[8,5,16,128]{3,2,1,0:T(8,128)}, f32[8,5,16,128]{3,2,1,0:T(8,128)}) custom-call(s32[8]{0:T(128)S(1)} %copy-done.5, f32[8,5,5,16,128]{4,3,2,1,0:T(8,128)S(1)} %bitcast.10, f32[8,5,16,128]{3,2,1,0:T(8,128)S(1)} %get-tuple-element.30.cur_ref, f32[8,5,16,128]{3,2,1,0:T(8,128)S(1)} %get-tuple-element.33.res_ref, ...), custom_call_target="tpu_custom_call" | custom-call | flops 1000000000 | bytes 8396832 | tf_op jit(solution)/shard_map/pallas_call | solution.py:27
  (2 shorter events, 0.1 us)
Async XLA Ops:
  0.6 0.7 copy-start.5
  1.3 1.0 %copy-start.8 = (f32[1,8,5,16,128]{4,3,2,1,0:T(8,128)S(1)}, f32[1,8,5,16,128]{4,3,2,1,0:T(8,128)}, u32[]{:S(2)}) copy-start(f32[1,8,5,16,128]{4,3,2,1,0:T(8,128)} %param.8) | copy-start | bytes 983044
  2.3 4.1 %copy-start = (f32[1,8,5,5,16,128]{5,4,3,2,1,0:T(8,128)S(1)}, f32[1,8,5,5,16,128]{5,4,3,2,1,0:T(8,128)}, u32[]{:S(2)}) copy-start(f32[1,8,5,5,16,128]{5,4,3,2,1,0:T(8,128)} %param.11) | copy-start | bytes 4915204
  2.3 4.1 %copy-start.1 = (f32[1,8,5,5,16,128]{5,4,3,2,1,0:T(8,128)S(1)}, f32[1,8,5,5,16,128]{5,4,3,2,1,0:T(8,128)}, u32[]{:S(2)}) copy-start(f32[1,8,5,5,16,128]{5,4,3,2,1,0:T(8,128)} %param.10) | copy-start | bytes 4915204
  2.3 4.1 %copy-start.4 = (f32[1,8,5,16,128]{4,3,2,1,0:T(8,128)S(1)}, f32[1,8,5,16,128]{4,3,2,1,0:T(8,128)}, u32[]{:S(2)}) copy-start(f32[1,8,5,16,128]{4,3,2,1,0:T(8,128)} %param.9) | copy-start | bytes 983044
  3.1 3.2 %collective-permute-start = (f32[5,16,128]{2,1,0:T(8,128)S(1)}, f32[5,16,128]{2,1,0:T(8,128)S(1)}, u32[]{:S(2)}, u32[]{:S(2)}) collective-permute-start(f32[5,16,128]{2,1,0:T(8,128)S(1)} %get-tuple-element.21), channel_id=1, source_target_pairs={{1,0},{2,1},{3,2},{5,4},{6,5},{7,6},{9,8},{10,9},{11,10},{13,12},{... | collective-permute-start | bytes 122888 | tf_op jit(solution)/shard_map/ppermute | solution.py:455
  6.4 1.4 %copy-start.2 = (f32[1,8,5,5,16,128]{5,4,3,2,1,0:T(8,128)S(1)}, f32[1,8,5,5,16,128]{5,4,3,2,1,0:T(8,128)}, u32[]{:S(2)}) copy-start(f32[1,8,5,5,16,128]{5,4,3,2,1,0:T(8,128)} %param.12) | copy-start | bytes 4915204
  7.8 1.4 %copy-start.7 = (f32[1,8,5,5,16,128]{5,4,3,2,1,0:T(8,128)S(1)}, f32[1,8,5,5,16,128]{5,4,3,2,1,0:T(8,128)}, u32[]{:S(2)}) copy-start(f32[1,8,5,5,16,128]{5,4,3,2,1,0:T(8,128)} %param.13) | copy-start | bytes 4915204
  9.2 29.4 %copy-start.6 = (s32[8]{0:T(128)S(1)}, s32[8]{0:T(128)}, u32[]{:S(2)}) copy-start(s32[8]{0:T(128)} %east_ref.3) | copy-start | bytes 100
  22.5 17.2 %collective-permute-start.2 = (f32[3,5,5,16,128]{4,3,2,1,0:T(8,128)S(1)}, f32[3,5,5,16,128]{4,3,2,1,0:T(8,128)S(1)}, u32[]{:S(2)}, u32[]{:S(2)}) collective-permute-start(f32[3,5,5,16,128]{4,3,2,1,0:T(8,128)S(1)} %get-tuple-element.29.mats_ref.mine_ref), channel_id=1, source_target_pairs={{0,1},{1,0},{2,3},{3,2},{4,5},{5,4},{6,7},{7,6},{8,9},{9,8},{10,11... | collective-permute-start | bytes 1843208 | tf_op jit(solution)/shard_map/ppermute | solution.py:444
  39.6 1.6 %collective-permute-start.1 = (f32[2,5,16,128]{3,2,1,0:T(8,128)S(1)}, f32[2,5,16,128]{3,2,1,0:T(8,128)S(1)}, u32[]{:S(2)}, u32[]{:S(2)}) collective-permute-start(f32[2,5,16,128]{3,2,1,0:T(8,128)S(1)} %get-tuple-element.28.ends_ref), channel_id=1, source_target_pairs={{0,1},{1,0},{2,3},{3,2},{4,5},{5,4},{6,7},{7,6},{8,9},{9,8},{10,11... | collective-permute-start | bytes 245768 | tf_op jit(solution)/shard_map/ppermute | solution.py:444
  39.9 10.2 %collective-permute-start.4 = (f32[5,5,16,128]{3,2,1,0:T(8,128)S(1)}, f32[5,5,16,128]{3,2,1,0:T(8,128)S(1)}, u32[]{:S(2)}, u32[]{:S(2)}) collective-permute-start(f32[5,5,16,128]{3,2,1,0:T(8,128)S(1)} %shard_map.99), channel_id=1, source_target_pairs={{2,0},{3,1},{6,4},{7,5},{10,8},{11,9},{14,12},{15,13},{18,16},{19,... | collective-permute-start | bytes 614408 | tf_op jit(solution)/shard_map/ppermute | solution.py:471
  41.2 8.9 %collective-permute-start.3 = (f32[1,5,16,128]{3,2,1,0:T(8,128)S(1)}, f32[1,5,16,128]{3,2,1,0:T(8,128)S(1)}, u32[]{:S(2)}, u32[]{:S(2)}) collective-permute-start(f32[1,5,16,128]{3,2,1,0:T(8,128)S(1)} %shard_map.98.pair_ref), channel_id=1, source_target_pairs={{0,2},{1,3},{2,0},{3,1},{4,6},{5,7},{6,4},{7,5},{8,10},{9,11},{10,... | collective-permute-start | bytes 122888 | tf_op jit(solution)/shard_map/ppermute | solution.py:444
  50.1 9.9 %copy-start.3 = (f32[1,8,5,5,16,128]{5,4,3,2,1,0:T(8,128)S(1)}, f32[1,8,5,5,16,128]{5,4,3,2,1,0:T(8,128)}, u32[]{:S(2)}) copy-start(f32[1,8,5,5,16,128]{5,4,3,2,1,0:T(8,128)} %param.12) | copy-start | bytes 4915204
  61.6 1.4 %collective-permute-start.5 = (f32[3,5,16,128]{3,2,1,0:T(8,128)S(1)}, f32[3,5,16,128]{3,2,1,0:T(8,128)S(1)}, u32[]{:S(2)}, u32[]{:S(2)}) collective-permute-start(f32[3,5,16,128]{3,2,1,0:T(8,128)S(1)} %get-tuple-element.35.ends_ref), channel_id=1, source_target_pairs={{0,1},{1,0},{2,3},{3,2},{4,5},{5,4},{6,7},{7,6},{8,9},{9,8},{10,11... | collective-permute-start | bytes 368648 | tf_op jit(solution)/shard_map/ppermute | solution.py:444
  63.0 4.6 %collective-permute-start.6 = (f32[2,5,16,128]{3,2,1,0:T(8,128)S(1)}, f32[2,5,16,128]{3,2,1,0:T(8,128)S(1)}, u32[]{:S(2)}, u32[]{:S(2)}) collective-permute-start(f32[2,5,16,128]{3,2,1,0:T(8,128)S(1)} %shard_map.102.pair_ref), channel_id=1, source_target_pairs={{0,2},{1,3},{2,0},{3,1},{4,6},{5,7},{6,4},{7,5},{8,10},{9,11},{10,... | collective-permute-start | bytes 245768 | tf_op jit(solution)/shard_map/ppermute | solution.py:444

commit v2 on v1

v2 whole, which is shorter than its diff:
```python
import functools

import jax
import jax.numpy as jnp
from jax import lax
from jax.experimental import pallas as pl
from jax.experimental.pallas import tpu as pltpu
from jax.sharding import PartitionSpec as P

ITERS = 2
OMEGA = 1.2
COUPLE = 0.25

VMEM = pl.BlockSpec(memory_space=pltpu.VMEM)
SMEM = pl.BlockSpec(memory_space=pltpu.SMEM)
ANY = pl.BlockSpec(memory_space=pl.ANY)
HBM = pl.BlockSpec(memory_space=pltpu.HBM)


def call(kernel, shapes, scratch=(), flops=10**9, out_specs=None, alias=None):
    moved = sum(4 * functools.reduce(lambda a, b: a * b, s, 1) for s in shapes)
    alias = alias or {}

    def spec(i, a):
        return ANY if i in alias else VMEM if a.dtype == jnp.float32 else SMEM

    def run(*arrays):
        total = moved + sum(a.size * 4 for a in arrays)
        return pl.pallas_call(
            kernel,
            out_shape=[jax.ShapeDtypeStruct(s, jnp.float32) for s in shapes],
            in_specs=[spec(i, a) for i, a in enumerate(arrays)],
            out_specs=out_specs or [VMEM] * len(shapes),
            scratch_shapes=list(scratch),
            input_output_aliases=alias,
            compiler_params=pltpu.CompilerParams(vmem_limit_bytes=12 * 2**20),
            cost_estimate=pl.CostEstimate(flops=flops, bytes_accessed=total, transcendentals=0),
        )(*arrays)

    return run


def buffer(*shape):
    return pltpu.VMEM(shape, jnp.float32)


def iota(dim):
    return lax.broadcasted_iota(jnp.int32, (16, 128), dim)


def matvec(matrix, vector):
    n = len(vector)
    out = []
    for r in range(n):
        acc = matrix[r][0] * vector[0]
        for c in range(1, n):
            acc = acc + matrix[r][c] * vector[c]
        out.append(acc)
    return out


def block(ref, *lead):
    return [[ref[(*lead, r, c)] for c in range(5)] for r in range(5)]


def cell(ref, *lead):
    return [ref[(*lead, v)] for v in range(5)]


def put(ref, values, *lead):
    for v, value in enumerate(values):
        ref[(*lead, v)] = value


def add(a, b):
    return [x + y for x, y in zip(a, b)]


def pack_faces(load, planes, tile_ref):
    lane = iota(1)
    tile = jnp.zeros((16, 128), jnp.float32)
    for j in range(planes):
        for v in range(5):
            q = 2 * (j * 5 + v)
            here = (lane == q) | (lane == (q - 1) % 128)
            x = load(j, v)
            tile = jnp.where(here, pltpu.roll(x, q, 1) if q else x, tile)
    for w in range(tile_ref.shape[0]):
        tile_ref[w] = tile


def live_rows(depth_ref):
    return iota(0) < depth_ref[lax.axis_index("zone")]


def masked(live, values):
    return [jnp.where(live, x, 0.0) for x in values]


def pack_kernel(flow_ref, tile_ref, first_ref):
    put(first_ref, cell(flow_ref, 0))
    pack_faces(lambda j, v: flow_ref[j, v], flow_ref.shape[0], tile_ref)


def neighbours(x):
    lane, row = iota(1), iota(0)
    total = jnp.where(lane == 0, 0.0, pltpu.roll(x, 1, 1))
    total = total + jnp.where(lane == 127, 0.0, pltpu.roll(x, 127, 1))
    total = total + jnp.where(row == 0, 0.0, pltpu.roll(x, 1, 0))
    return total + jnp.where(row == 15, 0.0, pltpu.roll(x, 15, 0))


def ghosts_of(depth_ref, east_ref, tiles_ref):
    zone = lax.axis_index("zone")
    east = east_ref[zone]
    west = jnp.int32(0)
    for w in range(tiles_ref.shape[0]):
        west = west + jnp.where(east_ref[w] == zone, w, 0)
    row = iota(0)
    low = jnp.where(row < depth_ref[west], tiles_ref[west], 0.0)
    high = jnp.where(row < depth_ref[east], tiles_ref[east], 0.0)
    return jnp.where(iota(1) % 2 == 0, pltpu.roll(low, 1, 1), pltpu.roll(high, 127, 1))


def ghost_at(ghosts, j, v):
    lane = iota(1)
    q = 2 * (j * 5 + v)
    turned = pltpu.roll(ghosts, 128 - q, 1) if q else ghosts
    return jnp.where((lane == 0) | (lane == 127), turned, 0.0)


def matrix_kernel(inv_ref, low_ref, up_ref, e_ref, f_ref, mats_ref, y_ref):
    planes = inv_ref.shape[0]
    last = planes - 1
    halves = [pl.ds(0, 8), pl.ds(8, 8)]

    def col(ref, q, j, rows):
        return [ref[j, r, q, rows] for r in range(5)]

    def put_col(ref, values, q, j, rows):
        for r in range(5):
            ref[j, r, q, rows] = values[r]

    def mat(ref, j, rows):
        return [[ref[j, r, c, rows] for c in range(5)] for r in range(5)]

    def products(j, rows):
        inv = mat(inv_ref, j, rows)
        for jac_ref, out_ref in ((low_ref, e_ref), (up_ref, f_ref)):
            for q in range(5):
                product = matvec(inv, col(jac_ref, q, j, rows))
                put_col(out_ref, [OMEGA * x for x in product], q, j, rows)

    def forward(j, carry):
        for rows in halves:
            products(j, rows)
            e = mat(e_ref, j, rows)
            for q in range(5):
                put_col(y_ref, matvec(e, col(y_ref, q, j - 1, rows)), q, j, rows)
        return carry

    for rows in halves:
        products(0, rows)
        for q in range(5):
            put_col(y_ref, col(e_ref, q, 0, rows), q, 0, rows)
    lax.fori_loop(1, planes, forward, 0)
    for rows in halves:
        for q in range(5):
            put_col(mats_ref, col(y_ref, q, last, rows), q, 0, rows)
            put_col(mats_ref, col(y_ref, q, last, rows), q, 1, rows)
            put_col(mats_ref, col(f_ref, q, last, rows), q, 2, rows)

    def backward(step, carry):
        j = planes - 2 - step
        for rows in halves:
            f = mat(f_ref, j, rows)
            for q in range(5):
                turned = matvec(f, col(mats_ref, q, 1, rows))
                put_col(mats_ref, add(col(y_ref, q, j, rows), turned), q, 1, rows)
                put_col(mats_ref, matvec(f, col(mats_ref, q, 2, rows)), q, 2, rows)
        return carry

    lax.fori_loop(0, planes - 1, backward, 0)


def by_place(mine_refs, other_refs, run):
    odd = lax.axis_index("ja") % 2

    @pl.when(odd == 0)
    def _():
        run(*mine_refs, *other_refs)

    @pl.when(odd == 1)
    def _():
        run(*other_refs, *mine_refs)


def beta_kernel(mine_ref, other_ref, beta_ref):
    def run(lo, hi):
        d_hi, n_lo = block(hi, 1), block(lo, 2)
        for q in range(5):
            m_col = [lo[0, r, q] for r in range(5)]
            d_col = [lo[1, r, q] for r in range(5)]
            out = add(d_col, matvec(n_lo, matvec(d_hi, m_col)))
            for r in range(5):
                beta_ref[r, q] = out[r]

    by_place([mine_ref], [other_ref], run)


def sweeps(s_ref, e_ref, f_ref, y_ref, ends_ref, last):
    planes = s_ref.shape[0]
    value = cell(s_ref, 0)
    put(y_ref, value, 0)
    for j in range(1, planes):
        value = add(cell(s_ref, j), matvec(block(e_ref, j), value))
        put(y_ref, value, j)
    put(ends_ref, [x + z * (1.0 / OMEGA) for x, z in zip(value, last)], 0)
    for j in range(planes - 2, -1, -1):
        value = add(cell(y_ref, j), matvec(block(f_ref, j), value))
    put(ends_ref, value, 1)


def local_kernel(
    depth_ref, east_ref, tiles_ref, cur_ref, above_ref, force_ref, diag_ref, inv_ref,
    e_ref, f_ref, mats_ref,
    s_ref, ends_ref, mats_out_ref, y_ref,
):
    del mats_ref, mats_out_ref
    planes = cur_ref.shape[0]
    live = live_rows(depth_ref)
    ghosts = ghosts_of(depth_ref, east_ref, tiles_ref)
    before, here = None, masked(live, cell(cur_ref, 0))
    for j in range(planes):
        after = masked(live, cell(cur_ref, j + 1) if j < planes - 1 else cell(above_ref))
        own = matvec(block(diag_ref, j), here)
        res = []
        for v in range(5):
            sides = neighbours(here[v]) + ghost_at(ghosts, j, v)
            res.append(force_ref[j, v] - own[v] + COUPLE * sides)
        linked = matvec(block(f_ref, j), after)
        if before is not None:
            linked = add(linked, matvec(block(e_ref, j), before))
        linked = [x * (1.0 / OMEGA) for x in linked]
        put(s_ref, add(matvec(block(inv_ref, j), masked(live, res)), linked), j)
        before, here = here, after
    sweeps(s_ref, e_ref, f_ref, y_ref, ends_ref, before)


def residual_kernel(
    depth_ref, cur_ref, above_ref, force_ref, diag_ref, low_ref, up_ref, inv_ref,
    res_ref, s_ref, low0_ref,
):
    planes = cur_ref.shape[0]
    live = live_rows(depth_ref)
    for r in range(5):
        put(low0_ref, cell(low_ref, 0, r), r)
    for j in range(planes):
        here = cell(cur_ref, j)
        applied = matvec(block(diag_ref, j), here)
        if j > 0:
            lower = matvec(block(low_ref, j), cell(cur_ref, j - 1))
            applied = [x - z for x, z in zip(applied, lower)]
        above = cell(cur_ref, j + 1) if j < planes - 1 else cell(above_ref)
        upper = matvec(block(up_ref, j), above)
        res = []
        for v in range(5):
            all_of = applied[v] - upper[v] - COUPLE * neighbours(here[v])
            res.append(jnp.where(live, force_ref[j, v] - all_of, 0.0))
        put(res_ref, res, j)
        put(s_ref, matvec(block(inv_ref, j), res), j)


def ghost_kernel(
    depth_ref, east_ref, tiles_ref, cur_ref, res0_ref, s0_ref, inv_ref, e_ref, f_ref,
    res_ref, s_ref, ends_ref, y_ref,
):
    planes = cur_ref.shape[0]
    live = live_rows(depth_ref)
    ghosts = jnp.where(live, COUPLE * ghosts_of(depth_ref, east_ref, tiles_ref), 0.0)
    for j in range(planes):
        extra = [ghost_at(ghosts, j, v) for v in range(5)]
        put(res_ref, add(cell(res0_ref, j), extra), j)
        put(s_ref, add(cell(s0_ref, j), matvec(block(inv_ref, j), extra)), j)
    last = cell(cur_ref, planes - 1)
    sweeps(s_ref, e_ref, f_ref, y_ref, ends_ref, last)
    put(ends_ref, last, 2)


def write_kernel(res_ref, edge_ref, res_hbm, edge_out_ref, sem):
    copy = pltpu.make_async_copy(res_ref, res_hbm, sem)
    copy.start()
    put(edge_out_ref, cell(edge_ref))
    copy.wait()


def mid_kernel(ends_ref, ends_other_ref, mats_ref, mats_other_ref, out_ref, *more):
    def run(ends_lo, mats_lo, ends_hi, mats_hi):
        c_lo = cell(ends_lo, 0)

        @pl.when(lax.axis_index("ja") < 2)
        def _():
            put(out_ref, add(cell(ends_hi, 0), matvec(block(mats_hi, 0), c_lo)))

        @pl.when(lax.axis_index("ja") >= 2)
        def _():
            turned = add(cell(ends_hi, 1), matvec(block(mats_hi, 1), c_lo))
            put(out_ref, add(cell(ends_lo, 1), matvec(block(mats_lo, 2), turned)))

        if more:
            put(more[0], cell(ends_hi, 2))

    by_place([ends_ref, mats_ref], [ends_other_ref, mats_other_ref], run)


def inflows(
    ends_ref, ends_other_ref, mats_ref, mats_other_ref, pair_ref, pair_other_ref, beta_ref,
    inflow_ref,
):
    ja = lax.axis_index("ja")
    zeros = [jnp.zeros((16, 128), jnp.float32)] * 5

    def far(a, alpha):
        return add(cell(alpha), matvec(block(beta_ref), cell(a)))

    @pl.when(ja == 0)
    def _():
        put(inflow_ref, zeros, 0)
        b = add(cell(ends_other_ref, 1), matvec(block(mats_other_ref, 1), cell(ends_ref, 0)))
        b = add(b, matvec(block(mats_other_ref, 2), far(pair_ref, pair_other_ref)))
        put(inflow_ref, b, 1)

    @pl.when(ja == 1)
    def _():
        put(inflow_ref, cell(ends_other_ref, 0), 0)
        put(inflow_ref, far(pair_ref, pair_other_ref), 1)

    @pl.when(ja == 2)
    def _():
        a = cell(pair_other_ref)
        put(inflow_ref, a, 0)
        a = add(cell(ends_ref, 0), matvec(block(mats_ref, 0), a))
        b = add(cell(ends_other_ref, 1), matvec(block(mats_other_ref, 1), a))
        put(inflow_ref, b, 1)

    @pl.when(ja == 3)
    def _():
        a = add(cell(ends_other_ref, 0), matvec(block(mats_other_ref, 0), cell(pair_other_ref)))
        put(inflow_ref, a, 0)
        put(inflow_ref, zeros, 1)


def final_kernel(
    depth_ref, cur_ref, above_ref, s_ref, e_ref, f_ref,
    ends_ref, ends_other_ref, mats_ref, mats_other_ref, pair_ref, pair_other_ref, beta_ref,
    new_ref, above_new_ref, tile_ref, y_ref, inflow_ref,
):
    planes = cur_ref.shape[0]
    inflows(
        ends_ref, ends_other_ref, mats_ref, mats_other_ref, pair_ref, pair_other_ref, beta_ref,
        inflow_ref,
    )
    value = cell(inflow_ref, 0)
    for j in range(planes):
        value = add(cell(s_ref, j), matvec(block(e_ref, j), value))
        put(y_ref, value, j)
    value = cell(inflow_ref, 1)
    live = live_rows(depth_ref)
    put(above_new_ref, add(masked(live, cell(above_ref)), value))
    for j in range(planes - 1, -1, -1):
        value = add(cell(y_ref, j), matvec(block(f_ref, j), value))
        put(new_ref, add(masked(live, cell(cur_ref, j)), value), j)
    pack_faces(lambda j, v: new_ref[j, v], planes, tile_ref)


def last_kernel(
    depth_ref, low0_ref, edge_ref, cur_ref, res_ref, s_ref, e_ref, f_ref,
    ends_ref, ends_other_ref, mats_ref, mats_other_ref, pair_ref, pair_other_ref, beta_ref,
    res_in_hbm,
    new_hbm, res_hbm, y_ref, inflow_ref, new_ref, res0_ref, sems,
):
    del res_in_hbm
    planes = cur_ref.shape[0]
    ja = lax.axis_index("ja")
    live = live_rows(depth_ref)
    before = [
        jnp.where(ja == 0, 0.0, jnp.where(ja == 2, edge_ref[v], ends_other_ref[2, v]))
        for v in range(5)
    ]
    put(res0_ref, add(cell(res_ref, 0), masked(live, matvec(block(low0_ref), before))))
    copies = [pltpu.make_async_copy(res0_ref, res_hbm.at[0], sems.at[planes])]
    copies[0].start()
    inflows(
        ends_ref, ends_other_ref, mats_ref, mats_other_ref, pair_ref, pair_other_ref, beta_ref,
        inflow_ref,
    )
    value = cell(inflow_ref, 0)
    for j in range(planes):
        value = add(cell(s_ref, j), matvec(block(e_ref, j), value))
        put(y_ref, value, j)
    value = cell(inflow_ref, 1)
    for j in range(planes - 1, -1, -1):
        value = add(cell(y_ref, j), matvec(block(f_ref, j), value))
        put(new_ref, add(cell(cur_ref, j), value), j)
        copies.append(pltpu.make_async_copy(new_ref.at[j], new_hbm.at[j], sems.at[j]))
        copies[-1].start()
    for copy in copies:
        copy.wait()


def per_device(
    flow_state, forcing, diag_block, lower_jac, upper_jac, block_inv, east_zone, zone_depth
):
    zones, parts = lax.axis_size("zone"), lax.axis_size("ja")
    assert parts == 4 and ITERS == 2
    current, force, diag, low, up, inv = (
        x[0] for x in (flow_state, forcing, diag_block, lower_jac, upper_jac, block_inv)
    )
    state = current.shape
    planes, plane, blocks, tiles = state[0], state[1:], diag.shape, (zones, *state[2:])
    matrix = blocks[1:]
    work = [buffer(*state)]

    def swap(x, bit):
        return lax.ppermute(x, "ja", [(p, p ^ bit) for p in range(parts)])

    def faces(x):
        return lax.all_to_all(x, "zone", 0, 0, tiled=True)

    tile, first = call(pack_kernel, [tiles, plane], flops=2 * 10**10)(current)
    got = faces(tile)
    above = lax.ppermute(first, "ja", [(p + 1, p) for p in range(parts - 1)])
    e, f, mats = call(
        matrix_kernel, [blocks, blocks, (3, *matrix)], [buffer(*blocks)], flops=5 * 10**9
    )(inv, low, up)
    s, ends, mats = call(
        local_kernel,
        [state, (2, *plane), (3, *matrix)],
        work,
        out_specs=[VMEM, VMEM, ANY],
        alias={10: 2},
    )(zone_depth, east_zone, got, current, above, force, diag, inv, e, f, mats)
    ends_other = swap(ends, 1)
    mats_other = swap(mats, 1)
    beta = call(beta_kernel, [matrix])(mats, mats_other)[0]
    beta = lax.ppermute(beta, "ja", [(2, 0), (3, 1)])
    pair = call(mid_kernel, [plane])(ends, ends_other, mats, mats_other)[0]
    pair_other = swap(pair, 2)
    flows = [buffer(2, *plane)]
    current, above, tile = call(final_kernel, [state, plane, tiles], work + flows)(
        zone_depth, current, above, s, e, f,
        ends, ends_other, mats, mats_other, pair, pair_other, beta,
    )

    got = faces(tile)
    residual, s, low0 = call(residual_kernel, [state, state, matrix], flops=2 * 10**9)(
        zone_depth, current, above, force, diag, low, up, inv
    )
    residual, s, ends = call(ghost_kernel, [state, state, (3, *plane)], work)(
        zone_depth, east_zone, got, current, residual, s, inv, e, f
    )
    ends_other = swap(ends, 1)
    pair, edge = call(mid_kernel, [plane, plane])(ends, ends_other, mats, mats_other)
    pair_other = swap(pair, 2)
    written, edge = call(
        write_kernel, [state, plane], [pltpu.SemaphoreType.DMA], out_specs=[HBM, VMEM]
    )(residual, edge)
    edge = lax.ppermute(edge, "ja", [(1, 2)])
    current, residual = call(
        last_kernel,
        [state, state],
        work + flows + work + [buffer(*plane), pltpu.SemaphoreType.DMA((planes + 1,))],
        out_specs=[HBM, HBM],
        alias={15: 1},
    )(
        zone_depth, low0, edge, current, residual, s, e, f,
        ends, ends_other, mats, mats_other, pair, pair_other, beta, written,
    )
    return (current[None], residual[None])


def solution(mesh):
    state = P("zone", "ja", None, None, None)
    blocks = P("zone", "ja", None, None, None, None)
    return jax.shard_map(
        per_device,
        mesh=mesh,
        in_specs=(state, state, blocks, blocks, blocks, blocks, P(), P()),
        out_specs=(state, state),
        check_vma=False,
    )
```

time: 69.9 us -> 75.2 us (1.076)
  the two profiles are of different devices: /device:TPU:0 before, /device:TPU:6 now
where the time goes in v2:
time: 75.2 us; the launch traced here: 74.2 us
  local copies, waits for them, and re-layouts  28.9 us (38%)
  starting transfers between devices  21.3 us (28%)
  waiting for transfers between devices  12.5 us (17%)
  Pallas kernels  10.7 us (14%)
  between operations  0.85 us (1%)
    unnamed x70, local copies, waits for them, and re-layouts  28.9 us
    all_to_all x2, starting transfers between devices, faces(): return lax.all_to_all(x, 'zone', 0, 0, tiled=True)  12.3 us
    pallas_call x11, Pallas kernels, run(): pl.pallas_call(kernel, out_shape=[jax.ShapeDtypeStruct(s, jnp.float32) fo...  10.7 us
    ppermute x5, waiting for transfers between devices, swap(): return lax.ppermute(x, 'ja', [(p, p ^ bit) for p in range(parts)])  8.45 us
    ppermute x1, waiting for transfers between devices, per_device(): edge = lax.ppermute(edge, 'ja', [(1, 2)])  4.01 us
    ppermute x5, starting transfers between devices, swap(): return lax.ppermute(x, 'ja', [(p, p ^ bit) for p in range(parts)])  3.34 us
    ppermute x1, starting transfers between devices, per_device(): beta = lax.ppermute(beta, 'ja', [(2, 0), (3, 1)])  2.47 us
    ppermute x1, starting transfers between devices, per_device(): above = lax.ppermute(first, 'ja', [(p + 1, p) for p in range(parts - 1)])  1.91 us
  transfers between devices with their start and end apart: 10, of which 4 were waited for; matrix products, arithmetic and copies ran while one was open for 0% of the time, Pallas kernels for 7%

profile of v2, /device:TPU:6, one launch (start us, length us, event | category | flops | bytes accessed | tf_op | source)
XLA Modules:
  0.0 74.2 jit_solution(8125589587649367590)
XLA Ops:
  0.6 0.0 copy-start.12
  0.6 1.0 %copy-done.12 = f32[1,8,5,16,128]{4,3,2,1,0:T(8,128)S(1)} copy-done((f32[1,8,5,16,128]{4,3,2,1,0:T(8,128)S(1)}, f32[1,8,5,16,128]{4,3,2,1,0:T(8,128)}, u32[]{:S(2)}) %copy-start.12) | copy-done | bytes 327704
  1.6 0.8 %shard_map.95 = (f32[8,16,128]{2,1,0:T(8,128)}, f32[5,16,128]{2,1,0:T(8,128)S(1)}) custom-call(f32[8,5,16,128]{3,2,1,0:T(8,128)S(1)} %bitcast.14), custom_call_target="tpu_custom_call" | custom-call | flops 20000000000 | bytes 434176 | tf_op jit(solution)/shard_map/pallas_call | solution.py:29
  2.4 6.3 %all-to-all-start = ((f32[8,16,128]{2,1,0:T(8,128)}), f32[8,16,128]{2,1,0:T(8,128)S(1)}, u32[]{:S(2)}, u32[]{:S(2)}) async-start(f32[8,16,128]{2,1,0:T(8,128)} %get-tuple-element.26), calls=%async_computation | async-start | bytes 131072 | tf_op jit(solution)/shard_map/all_to_all | solution.py:428
  8.7 1.9 %collective-permute-start = (f32[5,16,128]{2,1,0:T(8,128)S(1)}, f32[5,16,128]{2,1,0:T(8,128)S(1)}, u32[]{:S(2)}, u32[]{:S(2)}) collective-permute-start(f32[5,16,128]{2,1,0:T(8,128)S(1)} %get-tuple-element.25), channel_id=1, source_target_pairs={{1,0},{2,1},{3,2},{5,4},{6,5},{7,6},{9,8},{10,9},{11,10},{13,12},{... | collective-permute-start | bytes 122888 | tf_op jit(solution)/shard_map/ppermute | solution.py:432
  10.6 0.0 copy-start
  10.7 1.4 %copy-done = f32[1,8,5,5,16,128]{5,4,3,2,1,0:T(8,128)S(1)} copy-done((f32[1,8,5,5,16,128]{5,4,3,2,1,0:T(8,128)S(1)}, f32[1,8,5,5,16,128]{5,4,3,2,1,0:T(8,128)}, u32[]{:S(2)}) %copy-start) | copy-done | bytes 1638424
  12.1 1.4 %copy-done.29 = f32[1,8,5,5,16,128]{5,4,3,2,1,0:T(8,128)S(1)} copy-done((f32[1,8,5,5,16,128]{5,4,3,2,1,0:T(8,128)S(1)}, f32[1,8,5,5,16,128]{5,4,3,2,1,0:T(8,128)}, u32[]{:S(2)}) %copy-start.29) | copy-done | bytes 1638424
  13.5 1.4 %copy-done.31 = f32[1,8,5,5,16,128]{5,4,3,2,1,0:T(8,128)S(1)} copy-done((f32[1,8,5,5,16,128]{5,4,3,2,1,0:T(8,128)S(1)}, f32[1,8,5,5,16,128]{5,4,3,2,1,0:T(8,128)}, u32[]{:S(2)}) %copy-start.31) | copy-done | bytes 1638424
  14.9 2.8 %shard_map.96 = (f32[8,5,5,16,128]{4,3,2,1,0:T(8,128)S(1)}, f32[8,5,5,16,128]{4,3,2,1,0:T(8,128)S(1)}, f32[3,5,5,16,128]{4,3,2,1,0:T(8,128)S(1)}) custom-call(f32[8,5,5,16,128]{4,3,2,1,0:T(8,128)S(1)} %bitcast.8, f32[8,5,5,16,128]{4,3,2,1,0:T(8,128)S(1)} %bitcast.19, f32[8,5,5,16,128]{4,3,2,1,0:T(8,128)S(1)} %bitcast.21), custom_call_target="tpu_custom_call" | custom-call | flops 5000000000 | bytes 8806400 | tf_op jit(solution)/shard_map/pallas_call | solution.py:29
  17.7 0.8 %copy-done.4 = f32[3,5,5,16,128]{4,3,2,1,0:T(8,128)} copy-done((f32[3,5,5,16,128]{4,3,2,1,0:T(8,128)}, f32[3,5,5,16,128]{4,3,2,1,0:T(8,128)S(1)}, u32[]{:S(2)}) %copy-start.4) | copy-done | bytes 614424
  18.5 0.0 collective-permute-done.above_ref
  18.6 0.0 all-to-all-done.tiles_ref
  18.6 0.0 copy-start.1
  18.6 1.4 %copy-done.1 = f32[1,8,5,5,16,128]{5,4,3,2,1,0:T(8,128)S(1)} copy-done((f32[1,8,5,5,16,128]{5,4,3,2,1,0:T(8,128)S(1)}, f32[1,8,5,5,16,128]{5,4,3,2,1,0:T(8,128)}, u32[]{:S(2)}) %copy-start.1) | copy-done | bytes 1638424
  20.0 1.1 %copy-done.5 = f32[3,5,5,16,128]{4,3,2,1,0:T(8,128)S(1)} copy-done((f32[3,5,5,16,128]{4,3,2,1,0:T(8,128)S(1)}, f32[3,5,5,16,128]{4,3,2,1,0:T(8,128)}, u32[]{:S(2)}) %copy-start.5) | copy-done | bytes 614424
  21.1 1.4 %copy-done.10 = f32[1,8,5,5,16,128]{5,4,3,2,1,0:T(8,128)S(1)} copy-done((f32[1,8,5,5,16,128]{5,4,3,2,1,0:T(8,128)S(1)}, f32[1,8,5,5,16,128]{5,4,3,2,1,0:T(8,128)}, u32[]{:S(2)}) %copy-start.10) | copy-done | bytes 1638424
  22.5 1.0 %copy-done.13 = f32[1,8,5,16,128]{4,3,2,1,0:T(8,128)S(1)} copy-done((f32[1,8,5,16,128]{4,3,2,1,0:T(8,128)S(1)}, f32[1,8,5,16,128]{4,3,2,1,0:T(8,128)}, u32[]{:S(2)}) %copy-start.13) | copy-done | bytes 327704
  23.5 1.0 %copy-done.18 = f32[1,8,5,16,128]{4,3,2,1,0:T(8,128)S(1)} copy-done((f32[1,8,5,16,128]{4,3,2,1,0:T(8,128)S(1)}, f32[1,8,5,16,128]{4,3,2,1,0:T(8,128)}, u32[]{:S(2)}) %copy-start.18) | copy-done | bytes 327704
  24.5 1.4 %shard_map.97 = (f32[8,5,16,128]{3,2,1,0:T(8,128)S(1)}, f32[2,5,16,128]{3,2,1,0:T(8,128)S(1)}, f32[3,5,5,16,128]{4,3,2,1,0:T(8,128)S(1)}) custom-call(s32[8]{0:T(128)S(1)} %copy-done.27, s32[8]{0:T(128)S(1)} %copy-done.28, f32[8,16,128]{2,1,0:T(8,128)S(1)} %all-to-all-done.tiles_ref, ...), custom_call_target="tpu_custom_call", output_to_operand_aliasing={{2}: (10, {})} | custom-call | flops 1000000000 | bytes 8953920 | tf_op jit(solution)/shard_map/pallas_call | solution.py:29
  25.9 0.6 collective-permute-start.2
  26.5 0.1 collective-permute-start.1
  26.5 1.6 %collective-permute-done.2.mats_other_ref.other_ref = f32[3,5,5,16,128]{4,3,2,1,0:T(8,128)S(1)} collective-permute-done((f32[3,5,5,16,128]{4,3,2,1,0:T(8,128)S(1)}, f32[3,5,5,16,128]{4,3,2,1,0:T(8,128)S(1)}, u32[]{:S(2)}, u32[]{:S(2)}) %collective-permute-start.2) | collective-permute-done | bytes 614432 | tf_op jit(solution)/shard_map/ppermute | solution.py:425
  28.1 0.2 shard_map.99
  28.3 2.5 %collective-permute-start.4 = (f32[5,5,16,128]{3,2,1,0:T(8,128)S(1)}, f32[5,5,16,128]{3,2,1,0:T(8,128)S(1)}, u32[]{:S(2)}, u32[]{:S(2)}) collective-permute-start(f32[5,5,16,128]{3,2,1,0:T(8,128)S(1)} %shard_map.99), channel_id=1, source_target_pairs={{2,0},{3,1},{6,4},{7,5},{10,8},{11,9},{14,12},{15,13},{18,16},{19,... | collective-permute-start | bytes 614408 | tf_op jit(solution)/shard_map/ppermute | solution.py:446
  30.8 0.0 collective-permute-done.1.ends_other_ref
  30.8 0.1 shard_map.98.pair_ref
  30.8 0.1 collective-permute-start.3
  30.9 5.5 %collective-permute-done.3.pair_other_ref = f32[5,16,128]{2,1,0:T(8,128)S(1)} collective-permute-done((f32[5,16,128]{2,1,0:T(8,128)S(1)}, f32[5,16,128]{2,1,0:T(8,128)S(1)}, u32[]{:S(2)}, u32[]{:S(2)}) %collective-permute-start.3) | collective-permute-done | bytes 40992 | tf_op jit(solution)/shard_map/ppermute | solution.py:425
  36.5 0.0 collective-permute-done.4.beta_ref
  36.5 0.0 copy-done.6
  36.5 0.9 %shard_map.100 = (f32[8,5,16,128]{3,2,1,0:T(8,128)S(1)}, f32[5,16,128]{2,1,0:T(8,128)S(1)}, f32[8,16,128]{2,1,0:T(8,128)S(1)}) custom-call(s32[8]{0:T(128)S(1)} %copy-done.27, f32[8,5,16,128]{3,2,1,0:T(8,128)S(1)} %bitcast.16, f32[5,16,128]{2,1,0:T(8,128)S(1)} %collective-permute-done.above_ref, f32[8,5,16,128]{3,2,1,0:T(8,128)S(1)} %get-tuple-element.30.s_ref, ...), custom_call_target="tpu_custom_call" | custom-call | flops 1000000000 | bytes 6086688 | tf_op jit(solution)/shard_map/pallas_call | solution.py:29
  37.4 0.0 copy-start.14
  37.4 0.7 copy-done.14
  38.1 0.6 copy-done.26
  38.8 0.6 copy-done.33
  39.4 6.0 %all-to-all-start.1 = ((f32[8,16,128]{2,1,0:T(8,128)}), f32[8,16,128]{2,1,0:T(8,128)S(1)}, u32[]{:S(2)}, u32[]{:S(2)}) async-start(f32[8,16,128]{2,1,0:T(8,128)} %copy-done.26), calls=%async_computation.1 | async-start | bytes 131072 | tf_op jit(solution)/shard_map/all_to_all | solution.py:428
  45.4 1.4 %copy-done.2 = f32[1,8,5,5,16,128]{5,4,3,2,1,0:T(8,128)S(1)} copy-done((f32[1,8,5,5,16,128]{5,4,3,2,1,0:T(8,128)S(1)}, f32[1,8,5,5,16,128]{5,4,3,2,1,0:T(8,128)}, u32[]{:S(2)}) %copy-start.2) | copy-done | bytes 1638424
  46.8 1.4 %copy-done.11 = f32[1,8,5,5,16,128]{5,4,3,2,1,0:T(8,128)S(1)} copy-done((f32[1,8,5,5,16,128]{5,4,3,2,1,0:T(8,128)S(1)}, f32[1,8,5,5,16,128]{5,4,3,2,1,0:T(8,128)}, u32[]{:S(2)}) %copy-start.11) | copy-done | bytes 1638424
  48.2 1.0 %copy-done.15 = f32[8,5,16,128]{3,2,1,0:T(8,128)S(1)} copy-done((f32[8,5,16,128]{3,2,1,0:T(8,128)S(1)}, f32[8,5,16,128]{3,2,1,0:T(8,128)}, u32[]{:S(2)}) %copy-start.15) | copy-done | bytes 327704
  49.2 1.0 %copy-done.19 = f32[1,8,5,16,128]{4,3,2,1,0:T(8,128)S(1)} copy-done((f32[1,8,5,16,128]{4,3,2,1,0:T(8,128)S(1)}, f32[1,8,5,16,128]{4,3,2,1,0:T(8,128)}, u32[]{:S(2)}) %copy-start.19) | copy-done | bytes 327704
  50.2 1.4 %copy-done.30 = f32[1,8,5,5,16,128]{5,4,3,2,1,0:T(8,128)S(1)} copy-done((f32[1,8,5,5,16,128]{5,4,3,2,1,0:T(8,128)S(1)}, f32[1,8,5,5,16,128]{5,4,3,2,1,0:T(8,128)}, u32[]{:S(2)}) %copy-start.30) | copy-done | bytes 1638424
  51.6 1.4 %copy-done.32 = f32[1,8,5,5,16,128]{5,4,3,2,1,0:T(8,128)S(1)} copy-done((f32[1,8,5,5,16,128]{5,4,3,2,1,0:T(8,128)S(1)}, f32[1,8,5,5,16,128]{5,4,3,2,1,0:T(8,128)}, u32[]{:S(2)}) %copy-start.32) | copy-done | bytes 1638424
  53.1 0.8 %copy-done.34 = f32[5,16,128]{2,1,0:T(8,128)S(1)} copy-done((f32[5,16,128]{2,1,0:T(8,128)S(1)}, f32[5,16,128]{2,1,0:T(8,128)}, u32[]{:S(2)}) %copy-start.34) | copy-done | bytes 40984
  53.8 1.2 %shard_map.101 = (f32[8,5,16,128]{3,2,1,0:T(8,128)S(1)}, f32[8,5,16,128]{3,2,1,0:T(8,128)S(1)}, f32[5,5,16,128]{3,2,1,0:T(8,128)S(1)}) custom-call(s32[8]{0:T(128)S(1)} %copy-done.27, f32[8,5,16,128]{3,2,1,0:T(8,128)S(1)} %copy-done.15, f32[5,16,128]{2,1,0:T(8,128)S(1)} %copy-done.34, f32[8,5,16,128]{3,2,1,0:T(8,128)S(1)} %bitcast.18, ...), custom_call_target="tpu_custom_call" | custom-call | flops 2000000000 | bytes 8110112 | tf_op jit(solution)/shard_map/pallas_call | solution.py:29
  55.0 0.0 copy-start.20
  55.0 0.7 copy-done.20
  55.8 0.7 copy-done.22
  56.5 0.7 copy-done.24
  57.2 0.0 all-to-all-done.1.tiles_ref
  57.2 1.4 %copy-done.3 = f32[1,8,5,5,16,128]{5,4,3,2,1,0:T(8,128)S(1)} copy-done((f32[1,8,5,5,16,128]{5,4,3,2,1,0:T(8,128)S(1)}, f32[1,8,5,5,16,128]{5,4,3,2,1,0:T(8,128)}, u32[]{:S(2)}) %copy-start.3) | copy-done | bytes 1638424
  58.6 1.0 %copy-done.16 = f32[8,5,16,128]{3,2,1,0:T(8,128)S(1)} copy-done((f32[8,5,16,128]{3,2,1,0:T(8,128)S(1)}, f32[8,5,16,128]{3,2,1,0:T(8,128)}, u32[]{:S(2)}) %copy-start.16) | copy-done | bytes 327704
  59.6 1.0 %copy-done.21 = f32[8,5,16,128]{3,2,1,0:T(8,128)S(1)} copy-done((f32[8,5,16,128]{3,2,1,0:T(8,128)S(1)}, f32[8,5,16,128]{3,2,1,0:T(8,128)}, u32[]{:S(2)}) %copy-start.21) | copy-done | bytes 327704
  60.5 1.0 %copy-done.23 = f32[8,5,16,128]{3,2,1,0:T(8,128)S(1)} copy-done((f32[8,5,16,128]{3,2,1,0:T(8,128)S(1)}, f32[8,5,16,128]{3,2,1,0:T(8,128)}, u32[]{:S(2)}) %copy-start.23) | copy-done | bytes 327704
  61.5 1.0 %shard_map.102 = (f32[8,5,16,128]{3,2,1,0:T(8,128)S(1)}, f32[8,5,16,128]{3,2,1,0:T(8,128)S(1)}, f32[3,5,16,128]{3,2,1,0:T(8,128)S(1)}) custom-call(s32[8]{0:T(128)S(1)} %copy-done.27, s32[8]{0:T(128)S(1)} %copy-done.28, f32[8,16,128]{2,1,0:T(8,128)S(1)} %all-to-all-done.1.tiles_ref, f32[8,5,16,128]{3,2,1,0:T(8,128)S(1)} %copy-done.16, ...), custom_call_target="tpu_custom_call" | custom-call | flops 1000000000 | bytes 6742080 | tf_op jit(solution)/shard_map/pallas_call | solution.py:29
  62.5 0.1 collective-permute-start.5
  62.6 1.3 %collective-permute-done.5.ends_other_ref = f32[3,5,16,128]{3,2,1,0:T(8,128)S(1)} collective-permute-done((f32[3,5,16,128]{3,2,1,0:T(8,128)S(1)}, f32[3,5,16,128]{3,2,1,0:T(8,128)S(1)}, u32[]{:S(2)}, u32[]{:S(2)}) %collective-permute-start.5) | collective-permute-done | bytes 122912 | tf_op jit(solution)/shard_map/ppermute | solution.py:425
  63.9 0.0 copy-done.7
  64.0 2.6 %collective-permute-start.7 = (f32[5,16,128]{2,1,0:T(8,128)S(1)}, f32[5,16,128]{2,1,0:T(8,128)S(1)}, u32[]{:S(2)}, u32[]{:S(2)}) collective-permute-start(f32[5,16,128]{2,1,0:T(8,128)S(1)} %get-tuple-element.44.pair_ref), channel_id=1, source_target_pairs={{0,2},{1,3},{2,0},{3,1},{4,6},{5,7},{6,4},{7,5},{8,10},{9,11},{10,... | collective-permute-start | bytes 122888 | tf_op jit(solution)/shard_map/ppermute | solution.py:425
  66.6 0.7 shard_map.104
  67.3 1.3 %collective-permute-start.6 = (f32[5,16,128]{2,1,0:T(8,128)S(1)}, f32[5,16,128]{2,1,0:T(8,128)S(1)}, u32[]{:S(2)}, u32[]{:S(2)}) collective-permute-start(f32[5,16,128]{2,1,0:T(8,128)S(1)} %get-tuple-element.42), channel_id=1, source_target_pairs={{1,2},{5,6},{9,10},{13,14},{17,18},{21,22},{25,26},{29,30}} | collective-permute-start | bytes 122888 | tf_op jit(solution)/shard_map/ppermute | solution.py:468
  68.6 0.0 collective-permute-done.7.pair_other_ref
  68.6 4.0 %collective-permute-done.6.edge_ref = f32[5,16,128]{2,1,0:T(8,128)S(1)} collective-permute-done((f32[5,16,128]{2,1,0:T(8,128)S(1)}, f32[5,16,128]{2,1,0:T(8,128)S(1)}, u32[]{:S(2)}, u32[]{:S(2)}) %collective-permute-start.6) | collective-permute-done | bytes 40992 | tf_op jit(solution)/shard_map/ppermute | solution.py:468
  72.6 1.6 %shard_map.105 = (f32[8,5,16,128]{3,2,1,0:T(8,128)}, f32[8,5,16,128]{3,2,1,0:T(8,128)}) custom-call(s32[8]{0:T(128)S(1)} %copy-done.27, f32[5,5,16,128]{3,2,1,0:T(8,128)S(1)} %copy-done.25, f32[5,16,128]{2,1,0:T(8,128)S(1)} %collective-permute-done.6.edge_ref, f32[8,5,16,128]{3,2,1,0:T(8,128)S(1)} %copy-done.17, ...), custom_call_target="tpu_custom_call", output_to_operand_aliasing={{1}: (15, {})} | custom-call | flops 1000000000 | bytes 7249952 | tf_op jit(solution)/shard_map/pallas_call | solution.py:29
  (37 shorter events, 0.1 us)
Async XLA Ops:
  0.6 1.0 %copy-start.12 = (f32[1,8,5,16,128]{4,3,2,1,0:T(8,128)S(1)}, f32[1,8,5,16,128]{4,3,2,1,0:T(8,128)}, u32[]{:S(2)}) copy-start(f32[1,8,5,16,128]{4,3,2,1,0:T(8,128)} %param.8) | copy-start | bytes 983044
  2.4 16.2 %all-to-all-start = ((f32[8,16,128]{2,1,0:T(8,128)}), f32[8,16,128]{2,1,0:T(8,128)S(1)}, u32[]{:S(2)}, u32[]{:S(2)}) async-start(f32[8,16,128]{2,1,0:T(8,128)} %get-tuple-element.26), calls=%async_computation | async-start | bytes 131072 | tf_op jit(solution)/shard_map/all_to_all | solution.py:428
  8.7 9.8 %collective-permute-start = (f32[5,16,128]{2,1,0:T(8,128)S(1)}, f32[5,16,128]{2,1,0:T(8,128)S(1)}, u32[]{:S(2)}, u32[]{:S(2)}) collective-permute-start(f32[5,16,128]{2,1,0:T(8,128)S(1)} %get-tuple-element.25), channel_id=1, source_target_pairs={{1,0},{2,1},{3,2},{5,4},{6,5},{7,6},{9,8},{10,9},{11,10},{13,12},{... | collective-permute-start | bytes 122888 | tf_op jit(solution)/shard_map/ppermute | solution.py:432
  10.6 1.4 %copy-start = (f32[1,8,5,5,16,128]{5,4,3,2,1,0:T(8,128)S(1)}, f32[1,8,5,5,16,128]{5,4,3,2,1,0:T(8,128)}, u32[]{:S(2)}) copy-start(f32[1,8,5,5,16,128]{5,4,3,2,1,0:T(8,128)} %param.13) | copy-start | bytes 4915204
  12.1 1.4 %copy-start.29 = (f32[1,8,5,5,16,128]{5,4,3,2,1,0:T(8,128)S(1)}, f32[1,8,5,5,16,128]{5,4,3,2,1,0:T(8,128)}, u32[]{:S(2)}) copy-start(f32[1,8,5,5,16,128]{5,4,3,2,1,0:T(8,128)} %param.11) | copy-start | bytes 4915204
  13.5 1.4 %copy-start.31 = (f32[1,8,5,5,16,128]{5,4,3,2,1,0:T(8,128)S(1)}, f32[1,8,5,5,16,128]{5,4,3,2,1,0:T(8,128)}, u32[]{:S(2)}) copy-start(f32[1,8,5,5,16,128]{5,4,3,2,1,0:T(8,128)} %param.12) | copy-start | bytes 4915204
  14.9 3.6 %copy-start.27 = (s32[8]{0:T(128)S(1)}, s32[8]{0:T(128)}, u32[]{:S(2)}) copy-start(s32[8]{0:T(128)} %depth_ref.9) | copy-start | bytes 100
  14.9 3.6 %copy-start.28 = (s32[8]{0:T(128)S(1)}, s32[8]{0:T(128)}, u32[]{:S(2)}) copy-start(s32[8]{0:T(128)} %east_ref.3) | copy-start | bytes 100
  17.7 0.8 %copy-start.4 = (f32[3,5,5,16,128]{4,3,2,1,0:T(8,128)}, f32[3,5,5,16,128]{4,3,2,1,0:T(8,128)S(1)}, u32[]{:S(2)}) copy-start(f32[3,5,5,16,128]{4,3,2,1,0:T(8,128)S(1)} %get-tuple-element.29.mats_ref) | copy-start | bytes 1843204
  18.6 1.4 %copy-start.1 = (f32[1,8,5,5,16,128]{5,4,3,2,1,0:T(8,128)S(1)}, f32[1,8,5,5,16,128]{5,4,3,2,1,0:T(8,128)}, u32[]{:S(2)}) copy-start(f32[1,8,5,5,16,128]{5,4,3,2,1,0:T(8,128)} %param.13) | copy-start | bytes 4915204
  20.0 1.1 %copy-start.5 = (f32[3,5,5,16,128]{4,3,2,1,0:T(8,128)S(1)}, f32[3,5,5,16,128]{4,3,2,1,0:T(8,128)}, u32[]{:S(2)}) copy-start(f32[3,5,5,16,128]{4,3,2,1,0:T(8,128)} %copy-done.4) | copy-start | bytes 1843204
  21.1 1.4 %copy-start.10 = (f32[1,8,5,5,16,128]{5,4,3,2,1,0:T(8,128)S(1)}, f32[1,8,5,5,16,128]{5,4,3,2,1,0:T(8,128)}, u32[]{:S(2)}) copy-start(f32[1,8,5,5,16,128]{5,4,3,2,1,0:T(8,128)} %param.10) | copy-start | bytes 4915204
  22.5 1.0 %copy-start.13 = (f32[1,8,5,16,128]{4,3,2,1,0:T(8,128)S(1)}, f32[1,8,5,16,128]{4,3,2,1,0:T(8,128)}, u32[]{:S(2)}) copy-start(f32[1,8,5,16,128]{4,3,2,1,0:T(8,128)} %param.8) | copy-start | bytes 983044
  23.5 1.0 %copy-start.18 = (f32[1,8,5,16,128]{4,3,2,1,0:T(8,128)S(1)}, f32[1,8,5,16,128]{4,3,2,1,0:T(8,128)}, u32[]{:S(2)}) copy-start(f32[1,8,5,16,128]{4,3,2,1,0:T(8,128)} %param.9) | copy-start | bytes 983044
  25.9 10.6 %copy-start.6 = (f32[3,5,5,16,128]{4,3,2,1,0:T(8,128)}, f32[3,5,5,16,128]{4,3,2,1,0:T(8,128)S(1)}, u32[]{:S(2)}) copy-start(f32[3,5,5,16,128]{4,3,2,1,0:T(8,128)S(1)} %get-tuple-element.32.mats_ref.mine_ref) | copy-start | bytes 1843204
  25.9 2.2 %collective-permute-start.2 = (f32[3,5,5,16,128]{4,3,2,1,0:T(8,128)S(1)}, f32[3,5,5,16,128]{4,3,2,1,0:T(8,128)S(1)}, u32[]{:S(2)}, u32[]{:S(2)}) collective-permute-start(f32[3,5,5,16,128]{4,3,2,1,0:T(8,128)S(1)} %get-tuple-element.32.mats_ref.mine_ref), channel_id=1, source_target_pairs={{0,1},{1,0},{2,3},{3,2},{4,5},{5,4},{6,7},{7,6},{8,9},{9,8},{10,11... | collective-permute-start | bytes 1843208 | tf_op jit(solution)/shard_map/ppermute | solution.py:425
  26.5 4.3 %collective-permute-start.1 = (f32[2,5,16,128]{3,2,1,0:T(8,128)S(1)}, f32[2,5,16,128]{3,2,1,0:T(8,128)S(1)}, u32[]{:S(2)}, u32[]{:S(2)}) collective-permute-start(f32[2,5,16,128]{3,2,1,0:T(8,128)S(1)} %get-tuple-element.31.ends_ref), channel_id=1, source_target_pairs={{0,1},{1,0},{2,3},{3,2},{4,5},{5,4},{6,7},{7,6},{8,9},{9,8},{10,11... | collective-permute-start | bytes 245768 | tf_op jit(solution)/shard_map/ppermute | solution.py:425
  28.1 8.3 %copy-start.8 = (f32[3,5,5,16,128]{4,3,2,1,0:T(8,128)}, f32[3,5,5,16,128]{4,3,2,1,0:T(8,128)S(1)}, u32[]{:S(2)}) copy-start(f32[3,5,5,16,128]{4,3,2,1,0:T(8,128)S(1)} %collective-permute-done.2.mats_other_ref.other_ref) | copy-start | bytes 1843204
  28.3 8.2 %collective-permute-start.4 = (f32[5,5,16,128]{3,2,1,0:T(8,128)S(1)}, f32[5,5,16,128]{3,2,1,0:T(8,128)S(1)}, u32[]{:S(2)}, u32[]{:S(2)}) collective-permute-start(f32[5,5,16,128]{3,2,1,0:T(8,128)S(1)} %shard_map.99), channel_id=1, source_target_pairs={{2,0},{3,1},{6,4},{7,5},{10,8},{11,9},{14,12},{15,13},{18,16},{19,... | collective-permute-start | bytes 614408 | tf_op jit(solution)/shard_map/ppermute | solution.py:446
  30.8 5.6 %collective-permute-start.3 = (f32[5,16,128]{2,1,0:T(8,128)S(1)}, f32[5,16,128]{2,1,0:T(8,128)S(1)}, u32[]{:S(2)}, u32[]{:S(2)}) collective-permute-start(f32[5,16,128]{2,1,0:T(8,128)S(1)} %shard_map.98.pair_ref), channel_id=1, source_target_pairs={{0,2},{1,3},{2,0},{3,1},{4,6},{5,7},{6,4},{7,5},{8,10},{9,11},{10,... | collective-permute-start | bytes 122888 | tf_op jit(solution)/shard_map/ppermute | solution.py:425
  37.4 0.7 copy-start.14
  38.1 0.6 copy-start.26
  38.8 0.6 copy-start.33
  39.4 17.8 %all-to-all-start.1 = ((f32[8,16,128]{2,1,0:T(8,128)}), f32[8,16,128]{2,1,0:T(8,128)S(1)}, u32[]{:S(2)}, u32[]{:S(2)}) async-start(f32[8,16,128]{2,1,0:T(8,128)} %copy-done.26), calls=%async_computation.1 | async-start | bytes 131072 | tf_op jit(solution)/shard_map/all_to_all | solution.py:428
  45.4 1.4 %copy-start.2 = (f32[1,8,5,5,16,128]{5,4,3,2,1,0:T(8,128)S(1)}, f32[1,8,5,5,16,128]{5,4,3,2,1,0:T(8,128)}, u32[]{:S(2)}) copy-start(f32[1,8,5,5,16,128]{5,4,3,2,1,0:T(8,128)} %param.13) | copy-start | bytes 4915204
  46.8 1.4 %copy-start.11 = (f32[1,8,5,5,16,128]{5,4,3,2,1,0:T(8,128)S(1)}, f32[1,8,5,5,16,128]{5,4,3,2,1,0:T(8,128)}, u32[]{:S(2)}) copy-start(f32[1,8,5,5,16,128]{5,4,3,2,1,0:T(8,128)} %param.10) | copy-start | bytes 4915204
  48.2 1.0 %copy-start.15 = (f32[8,5,16,128]{3,2,1,0:T(8,128)S(1)}, f32[8,5,16,128]{3,2,1,0:T(8,128)}, u32[]{:S(2)}) copy-start(f32[8,5,16,128]{3,2,1,0:T(8,128)} %copy-done.14) | copy-start | bytes 983044
  49.2 1.0 %copy-start.19 = (f32[1,8,5,16,128]{4,3,2,1,0:T(8,128)S(1)}, f32[1,8,5,16,128]{4,3,2,1,0:T(8,128)}, u32[]{:S(2)}) copy-start(f32[1,8,5,16,128]{4,3,2,1,0:T(8,128)} %param.9) | copy-start | bytes 983044
  50.2 1.4 %copy-start.30 = (f32[1,8,5,5,16,128]{5,4,3,2,1,0:T(8,128)S(1)}, f32[1,8,5,5,16,128]{5,4,3,2,1,0:T(8,128)}, u32[]{:S(2)}) copy-start(f32[1,8,5,5,16,128]{5,4,3,2,1,0:T(8,128)} %param.11) | copy-start | bytes 4915204
  51.6 1.4 %copy-start.32 = (f32[1,8,5,5,16,128]{5,4,3,2,1,0:T(8,128)S(1)}, f32[1,8,5,5,16,128]{5,4,3,2,1,0:T(8,128)}, u32[]{:S(2)}) copy-start(f32[1,8,5,5,16,128]{5,4,3,2,1,0:T(8,128)} %param.12) | copy-start | bytes 4915204
  53.1 0.8 %copy-start.34 = (f32[5,16,128]{2,1,0:T(8,128)S(1)}, f32[5,16,128]{2,1,0:T(8,128)}, u32[]{:S(2)}) copy-start(f32[5,16,128]{2,1,0:T(8,128)} %copy-done.33) | copy-start | bytes 122884
  55.0 0.7 copy-start.20
  55.8 0.7 copy-start.22
  56.5 0.7 copy-start.24
  57.2 1.4 %copy-start.3 = (f32[1,8,5,5,16,128]{5,4,3,2,1,0:T(8,128)S(1)}, f32[1,8,5,5,16,128]{5,4,3,2,1,0:T(8,128)}, u32[]{:S(2)}) copy-start(f32[1,8,5,5,16,128]{5,4,3,2,1,0:T(8,128)} %param.13) | copy-start | bytes 4915204
  58.6 1.0 %copy-start.16 = (f32[8,5,16,128]{3,2,1,0:T(8,128)S(1)}, f32[8,5,16,128]{3,2,1,0:T(8,128)}, u32[]{:S(2)}) copy-start(f32[8,5,16,128]{3,2,1,0:T(8,128)} %copy-done.14) | copy-start | bytes 983044
  59.6 1.0 %copy-start.21 = (f32[8,5,16,128]{3,2,1,0:T(8,128)S(1)}, f32[8,5,16,128]{3,2,1,0:T(8,128)}, u32[]{:S(2)}) copy-start(f32[8,5,16,128]{3,2,1,0:T(8,128)} %copy-done.20) | copy-start | bytes 983044
  60.5 1.0 %copy-start.23 = (f32[8,5,16,128]{3,2,1,0:T(8,128)S(1)}, f32[8,5,16,128]{3,2,1,0:T(8,128)}, u32[]{:S(2)}) copy-start(f32[8,5,16,128]{3,2,1,0:T(8,128)} %copy-done.22) | copy-start | bytes 983044
  61.5 2.4 %copy-start.7 = (f32[3,5,5,16,128]{4,3,2,1,0:T(8,128)S(1)}, f32[3,5,5,16,128]{4,3,2,1,0:T(8,128)}, u32[]{:S(2)}) copy-start(f32[3,5,5,16,128]{4,3,2,1,0:T(8,128)} %copy-done.6) | copy-start | bytes 1843204
  61.5 2.4 %copy-start.9 = (f32[3,5,5,16,128]{4,3,2,1,0:T(8,128)S(1)}, f32[3,5,5,16,128]{4,3,2,1,0:T(8,128)}, u32[]{:S(2)}) copy-start(f32[3,5,5,16,128]{4,3,2,1,0:T(8,128)} %copy-done.8) | copy-start | bytes 1843204
  62.5 1.4 %collective-permute-start.5 = (f32[3,5,16,128]{3,2,1,0:T(8,128)S(1)}, f32[3,5,16,128]{3,2,1,0:T(8,128)S(1)}, u32[]{:S(2)}, u32[]{:S(2)}) collective-permute-start(f32[3,5,16,128]{3,2,1,0:T(8,128)S(1)} %get-tuple-element.40.ends_ref), channel_id=1, source_target_pairs={{0,1},{1,0},{2,3},{3,2},{4,5},{5,4},{6,7},{7,6},{8,9},{9,8},{10,11... | collective-permute-start | bytes 368648 | tf_op jit(solution)/shard_map/ppermute | solution.py:425
  64.0 4.6 %collective-permute-start.7 = (f32[5,16,128]{2,1,0:T(8,128)S(1)}, f32[5,16,128]{2,1,0:T(8,128)S(1)}, u32[]{:S(2)}, u32[]{:S(2)}) collective-permute-start(f32[5,16,128]{2,1,0:T(8,128)S(1)} %get-tuple-element.44.pair_ref), channel_id=1, source_target_pairs={{0,2},{1,3},{2,0},{3,1},{4,6},{5,7},{6,4},{7,5},{8,10},{9,11},{10,... | collective-permute-start | bytes 122888 | tf_op jit(solution)/shard_map/ppermute | solution.py:425
  66.6 6.1 %copy-start.17 = (f32[8,5,16,128]{3,2,1,0:T(8,128)S(1)}, f32[8,5,16,128]{3,2,1,0:T(8,128)}, u32[]{:S(2)}) copy-start(f32[8,5,16,128]{3,2,1,0:T(8,128)} %copy-done.14) | copy-start | bytes 983044
  66.6 6.1 %copy-start.25 = (f32[5,5,16,128]{3,2,1,0:T(8,128)S(1)}, f32[5,5,16,128]{3,2,1,0:T(8,128)}, u32[]{:S(2)}) copy-start(f32[5,5,16,128]{3,2,1,0:T(8,128)} %copy-done.24) | copy-start | bytes 614404
  67.3 5.3 %collective-permute-start.6 = (f32[5,16,128]{2,1,0:T(8,128)S(1)}, f32[5,16,128]{2,1,0:T(8,128)S(1)}, u32[]{:S(2)}, u32[]{:S(2)}) collective-permute-start(f32[5,16,128]{2,1,0:T(8,128)S(1)} %get-tuple-element.42), channel_id=1, source_target_pairs={{1,2},{5,6},{9,10},{13,14},{17,18},{21,22},{25,26},{29,30}} | collective-permute-start | bytes 122888 | tf_op jit(solution)/shard_map/ppermute | solution.py:468

commit v3 on v2

--- a/solution.py
+++ b/solution.py
@@ -129,7 +129,8 @@
     return jnp.where((lane == 0) | (lane == 127), turned, 0.0)
 
 
-def matrix_kernel(inv_ref, low_ref, up_ref, e_ref, f_ref, mats_ref, y_ref):
+def matrix_kernel(tiles_ref, inv_ref, low_ref, up_ref, e_ref, f_ref, mats_ref, y_ref):
+    del tiles_ref
     planes = inv_ref.shape[0]
     last = planes - 1
     halves = [pl.ds(0, 8), pl.ds(8, 8)]
@@ -195,17 +196,31 @@
         run(*other_refs, *mine_refs)
 
 
-def beta_kernel(mine_ref, other_ref, beta_ref):
+def beta_kernel(mine_ref, other_ref, half_ref):
     def run(lo, hi):
-        d_hi, n_lo = block(hi, 1), block(lo, 2)
+        def part(ref, *at):
+            return ref[at][rows]
+
+        d_hi = [[part(hi, 1, r, c) for c in range(5)] for r in range(5)]
+        n_lo = [[part(lo, 2, r, c) for c in range(5)] for r in range(5)]
         for q in range(5):
-            m_col = [lo[0, r, q] for r in range(5)]
-            d_col = [lo[1, r, q] for r in range(5)]
+            m_col = [part(lo, 0, r, q) for r in range(5)]
+            d_col = [part(lo, 1, r, q) for r in range(5)]
             out = add(d_col, matvec(n_lo, matvec(d_hi, m_col)))
             for r in range(5):
-                beta_ref[r, q] = out[r]
-
-    by_place([mine_ref], [other_ref], run)
+                half_ref[r, q] = out[r]
+
+    odd = lax.axis_index("ja") % 2
+    for side in range(2):
+        rows = slice(8 * side, 8 * side + 8)
+        pair = (mine_ref, other_ref) if side == 0 else (other_ref, mine_ref)
+        pl.when(odd == side)(functools.partial(run, *pair))
+
+
+def relay_kernel(half_ref, pair_ref, out_ref):
+    del pair_ref
+    for r in range(5):
+        put(out_ref, cell(half_ref, r), r)
 
 
 def sweeps(s_ref, e_ref, f_ref, y_ref, ends_ref, last):
@@ -223,10 +238,9 @@
 
 def local_kernel(
     depth_ref, east_ref, tiles_ref, cur_ref, above_ref, force_ref, diag_ref, inv_ref,
-    e_ref, f_ref, mats_ref,
-    s_ref, ends_ref, mats_out_ref, y_ref,
-):
-    del mats_ref, mats_out_ref
+    e_ref, f_ref,
+    s_ref, ends_ref, y_ref,
+):
     planes = cur_ref.shape[0]
     live = live_rows(depth_ref)
     ghosts = ghosts_of(depth_ref, east_ref, tiles_ref)
@@ -247,12 +261,14 @@
     sweeps(s_ref, e_ref, f_ref, y_ref, ends_ref, before)
 
 
-def residual_kernel(
-    depth_ref, cur_ref, above_ref, force_ref, diag_ref, low_ref, up_ref, inv_ref,
-    res_ref, s_ref, low0_ref,
+def second_kernel(
+    depth_ref, east_ref, tiles_ref, cur_ref, above_ref, force_ref, diag_ref, low_ref, up_ref,
+    inv_ref, e_ref, f_ref,
+    res_ref, s_ref, ends_ref, low0_ref, y_ref,
 ):
     planes = cur_ref.shape[0]
     live = live_rows(depth_ref)
+    ghosts = ghosts_of(depth_ref, east_ref, tiles_ref)
     for r in range(5):
         put(low0_ref, cell(low_ref, 0, r), r)
     for j in range(planes):
@@ -265,79 +281,70 @@
         upper = matvec(block(up_ref, j), above)
         res = []
         for v in range(5):
-            all_of = applied[v] - upper[v] - COUPLE * neighbours(here[v])
+            sides = neighbours(here[v]) + ghost_at(ghosts, j, v)
+            all_of = applied[v] - upper[v] - COUPLE * sides
             res.append(jnp.where(live, force_ref[j, v] - all_of, 0.0))
         put(res_ref, res, j)
         put(s_ref, matvec(block(inv_ref, j), res), j)
-
-
-def ghost_kernel(
-    depth_ref, east_ref, tiles_ref, cur_ref, res0_ref, s0_ref, inv_ref, e_ref, f_ref,
-    res_ref, s_ref, ends_ref, y_ref,
-):
-    planes = cur_ref.shape[0]
-    live = live_rows(depth_ref)
-    ghosts = jnp.where(live, COUPLE * ghosts_of(depth_ref, east_ref, tiles_ref), 0.0)
-    for j in range(planes):
-        extra = [ghost_at(ghosts, j, v) for v in range(5)]
-        put(res_ref, add(cell(res0_ref, j), extra), j)
-        put(s_ref, add(cell(s0_ref, j), matvec(block(inv_ref, j), extra)), j)
     last = cell(cur_ref, planes - 1)
     sweeps(s_ref, e_ref, f_ref, y_ref, ends_ref, last)
     put(ends_ref, last, 2)
 
 
-def write_kernel(res_ref, edge_ref, res_hbm, edge_out_ref, sem):
+def write_kernel(res_ref, res_hbm, sem):
     copy = pltpu.make_async_copy(res_ref, res_hbm, sem)
     copy.start()
-    put(edge_out_ref, cell(edge_ref))
     copy.wait()
 
 
-def mid_kernel(ends_ref, ends_other_ref, mats_ref, mats_other_ref, out_ref, *more):
+def mid_kernel(ends_ref, ends_other_ref, mats_ref, mats_other_ref, out_ref):
     def run(ends_lo, mats_lo, ends_hi, mats_hi):
         c_lo = cell(ends_lo, 0)
 
         @pl.when(lax.axis_index("ja") < 2)
         def _():
-            put(out_ref, add(cell(ends_hi, 0), matvec(block(mats_hi, 0), c_lo)))
+            put(out_ref, add(cell(ends_hi, 0), matvec(block(mats_hi, 0), c_lo)), 0)
 
         @pl.when(lax.axis_index("ja") >= 2)
         def _():
             turned = add(cell(ends_hi, 1), matvec(block(mats_hi, 1), c_lo))
-            put(out_ref, add(cell(ends_lo, 1), matvec(block(mats_lo, 2), turned)))
-
-        if more:
-            put(more[0], cell(ends_hi, 2))
+            put(out_ref, add(cell(ends_lo, 1), matvec(block(mats_lo, 2), turned)), 0)
+
+        if out_ref.shape[0] > 1:
+            put(out_ref, cell(ends_hi, 2), 1)
 
     by_place([ends_ref, mats_ref], [ends_other_ref, mats_other_ref], run)
 
 
 def inflows(
-    ends_ref, ends_other_ref, mats_ref, mats_other_ref, pair_ref, pair_other_ref, beta_ref,
-    inflow_ref,
+    ends_ref, ends_other_ref, mats_ref, mats_other_ref, pair_ref, pair_other_ref,
+    half_ref, half_other_ref, inflow_ref,
 ):
     ja = lax.axis_index("ja")
     zeros = [jnp.zeros((16, 128), jnp.float32)] * 5
 
-    def far(a, alpha):
-        return add(cell(alpha), matvec(block(beta_ref), cell(a)))
+    def far(top_ref, bottom_ref):
+        beta = [
+            [jnp.concatenate([top_ref[r, c], bottom_ref[r, c]], axis=0) for c in range(5)]
+            for r in range(5)
+        ]
+        return add(cell(pair_other_ref, 0), matvec(beta, cell(pair_ref, 0)))
 
     @pl.when(ja == 0)
     def _():
         put(inflow_ref, zeros, 0)
         b = add(cell(ends_other_ref, 1), matvec(block(mats_other_ref, 1), cell(ends_ref, 0)))
-        b = add(b, matvec(block(mats_other_ref, 2), far(pair_ref, pair_other_ref)))
+        b = add(b, matvec(block(mats_other_ref, 2), far(half_ref, half_other_ref)))
         put(inflow_ref, b, 1)
 
     @pl.when(ja == 1)
     def _():
         put(inflow_ref, cell(ends_other_ref, 0), 0)
-        put(inflow_ref, far(pair_ref, pair_other_ref), 1)
+        put(inflow_ref, far(half_other_ref, half_ref), 1)
 
     @pl.when(ja == 2)
     def _():
-        a = cell(pair_other_ref)
+        a = cell(pair_other_ref, 0)
         put(inflow_ref, a, 0)
         a = add(cell(ends_ref, 0), matvec(block(mats_ref, 0), a))
         b = add(cell(ends_other_ref, 1), matvec(block(mats_other_ref, 1), a))
@@ -345,20 +352,21 @@
 
     @pl.when(ja == 3)
     def _():
-        a = add(cell(ends_other_ref, 0), matvec(block(mats_other_ref, 0), cell(pair_other_ref)))
+        a = add(cell(ends_other_ref, 0), matvec(block(mats_other_ref, 0), cell(pair_other_ref, 0)))
         put(inflow_ref, a, 0)
         put(inflow_ref, zeros, 1)
 
 
 def final_kernel(
     depth_ref, cur_ref, above_ref, s_ref, e_ref, f_ref,
-    ends_ref, ends_other_ref, mats_ref, mats_other_ref, pair_ref, pair_other_ref, beta_ref,
+    ends_ref, ends_other_ref, mats_ref, mats_other_ref, pair_ref, pair_other_ref,
+    half_ref, half_other_ref,
     new_ref, above_new_ref, tile_ref, y_ref, inflow_ref,
 ):
     planes = cur_ref.shape[0]
     inflows(
-        ends_ref, ends_other_ref, mats_ref, mats_other_ref, pair_ref, pair_other_ref, beta_ref,
-        inflow_ref,
+        ends_ref, ends_other_ref, mats_ref, mats_other_ref, pair_ref, pair_other_ref,
+        half_ref, half_other_ref, inflow_ref,
     )
     value = cell(inflow_ref, 0)
     for j in range(planes):
@@ -374,8 +382,9 @@
 
 
 def last_kernel(
-    depth_ref, low0_ref, edge_ref, cur_ref, res_ref, s_ref, e_ref, f_ref,
-    ends_ref, ends_other_ref, mats_ref, mats_other_ref, pair_ref, pair_other_ref, beta_ref,
+    depth_ref, low0_ref, cur_ref, res_ref, s_ref, e_ref, f_ref,
+    ends_ref, ends_other_ref, mats_ref, mats_other_ref, pair_ref, pair_other_ref,
+    half_ref, half_other_ref,
     res_in_hbm,
     new_hbm, res_hbm, y_ref, inflow_ref, new_ref, res0_ref, sems,
 ):
@@ -384,15 +393,15 @@
     ja = lax.axis_index("ja")
     live = live_rows(depth_ref)
     before = [
-        jnp.where(ja == 0, 0.0, jnp.where(ja == 2, edge_ref[v], ends_other_ref[2, v]))
+        jnp.where(ja == 0, 0.0, jnp.where(ja == 2, pair_other_ref[1, v], ends_other_ref[2, v]))
         for v in range(5)
     ]
     put(res0_ref, add(cell(res_ref, 0), masked(live, matvec(block(low0_ref), before))))
     copies = [pltpu.make_async_copy(res0_ref, res_hbm.at[0], sems.at[planes])]
     copies[0].start()
     inflows(
-        ends_ref, ends_other_ref, mats_ref, mats_other_ref, pair_ref, pair_other_ref, beta_ref,
-        inflow_ref,
+        ends_ref, ends_other_ref, mats_ref, mats_other_ref, pair_ref, pair_other_ref,
+        half_ref, half_other_ref, inflow_ref,
     )
     value = cell(inflow_ref, 0)
     for j in range(planes):
@@ -428,44 +437,38 @@
         return lax.all_to_all(x, "zone", 0, 0, tiled=True)
 
     tile, first = call(pack_kernel, [tiles, plane], flops=2 * 10**10)(current)
+    above = lax.ppermute(first, "ja", [(p + 1, p) for p in range(parts - 1)])
     got = faces(tile)
-    above = lax.ppermute(first, "ja", [(p + 1, p) for p in range(parts - 1)])
     e, f, mats = call(
         matrix_kernel, [blocks, blocks, (3, *matrix)], [buffer(*blocks)], flops=5 * 10**9
-    )(inv, low, up)
-    s, ends, mats = call(
-        local_kernel,
-        [state, (2, *plane), (3, *matrix)],
-        work,
-        out_specs=[VMEM, VMEM, ANY],
-        alias={10: 2},
-    )(zone_depth, east_zone, got, current, above, force, diag, inv, e, f, mats)
+    )(got, inv, low, up)
+    mats_other = swap(mats, 1)
+    s, ends = call(local_kernel, [state, (2, *plane)], work)(
+        zone_depth, east_zone, got, current, above, force, diag, inv, e, f
+    )
     ends_other = swap(ends, 1)
-    mats_other = swap(mats, 1)
-    beta = call(beta_kernel, [matrix])(mats, mats_other)[0]
-    beta = lax.ppermute(beta, "ja", [(2, 0), (3, 1)])
-    pair = call(mid_kernel, [plane])(ends, ends_other, mats, mats_other)[0]
+    half = call(beta_kernel, [(*matrix[:2], 8, matrix[3])])(mats, mats_other)[0]
+    half = lax.ppermute(half, "ja", [(2, 0), (3, 1)])
+    pair = call(mid_kernel, [(1, *plane)])(ends, ends_other, mats, mats_other)[0]
     pair_other = swap(pair, 2)
+    half_sent = call(relay_kernel, [half.shape])(half, pair)[0]
+    half_other = lax.ppermute(half_sent, "ja", [(0, 1), (1, 0)])
     flows = [buffer(2, *plane)]
     current, above, tile = call(final_kernel, [state, plane, tiles], work + flows)(
         zone_depth, current, above, s, e, f,
-        ends, ends_other, mats, mats_other, pair, pair_other, beta,
+        ends, ends_other, mats, mats_other, pair, pair_other, half, half_other,
     )
 
     got = faces(tile)
-    residual, s, low0 = call(residual_kernel, [state, state, matrix], flops=2 * 10**9)(
-        zone_depth, current, above, force, diag, low, up, inv
-    )
-    residual, s, ends = call(ghost_kernel, [state, state, (3, *plane)], work)(
-        zone_depth, east_zone, got, current, residual, s, inv, e, f
+    residual, s, ends, low0 = call(
+        second_kernel, [state, state, (3, *plane), matrix], work
+    )(
+        zone_depth, east_zone, got, current, above, force, diag, low, up, inv, e, f
     )
     ends_other = swap(ends, 1)
-    pair, edge = call(mid_kernel, [plane, plane])(ends, ends_other, mats, mats_other)
+    pair = call(mid_kernel, [(2, *plane)])(ends, ends_other, mats, mats_other)[0]
     pair_other = swap(pair, 2)
-    written, edge = call(
-        write_kernel, [state, plane], [pltpu.SemaphoreType.DMA], out_specs=[HBM, VMEM]
-    )(residual, edge)
-    edge = lax.ppermute(edge, "ja", [(1, 2)])
+    written = call(write_kernel, [state], [pltpu.SemaphoreType.DMA], out_specs=[HBM])(residual)[0]
     current, residual = call(
         last_kernel,
         [state, state],
@@ -473,8 +476,8 @@
         out_specs=[HBM, HBM],
         alias={15: 1},
     )(
-        zone_depth, low0, edge, current, residual, s, e, f,
-        ends, ends_other, mats, mats_other, pair, pair_other, beta, written,
+        zone_depth, low0, current, residual, s, e, f,
+        ends, ends_other, mats, mats_other, pair, pair_other, half, half_other, written,
     )
     return (current[None], residual[None])
 

time: 75.2 us -> 58.8 us (0.78)
  the two profiles are of different devices: /device:TPU:6 before, /device:TPU:0 now
where the time goes in v3:
time: 58.8 us; the launch traced here: 58.5 us
  blocking collectives  23.5 us (40%)
  waiting for transfers between devices  16 us (27%)
  Pallas kernels  9.35 us (16%)
  starting transfers between devices  7.79 us (13%)
  local copies, waits for them, and re-layouts  1.01 us (2%)
  between operations  0.83 us (1%)
    all_to_all x2, blocking collectives, faces(): return lax.all_to_all(x, 'zone', 0, 0, tiled=True)  23.5 us
    pallas_call x11, Pallas kernels, run(): pl.pallas_call(kernel, out_shape=[jax.ShapeDtypeStruct(s, jnp.float32) fo...  9.35 us
    ppermute x5, waiting for transfers between devices, swap(): return lax.ppermute(x, 'ja', [(p, p ^ bit) for p in range(parts)])  8.82 us
    ppermute x1, waiting for transfers between devices, per_device(): half = lax.ppermute(half, 'ja', [(2, 0), (3, 1)])  5.36 us
    ppermute x5, starting transfers between devices, swap(): return lax.ppermute(x, 'ja', [(p, p ^ bit) for p in range(parts)])  3.29 us
    ppermute x1, starting transfers between devices, per_device(): half_other = lax.ppermute(half_sent, 'ja', [(0, 1), (1, 0)])  1.92 us
    ppermute x1, waiting for transfers between devices, per_device(): above = lax.ppermute(first, 'ja', [(p + 1, p) for p in range(parts - 1)])  1.81 us
    ppermute x1, starting transfers between devices, per_device(): above = lax.ppermute(first, 'ja', [(p + 1, p) for p in range(parts - 1)])  1.29 us
  transfers between devices with their start and end apart: 8, of which 5 were waited for; matrix products, arithmetic and copies ran while one was open for 0% of the time, Pallas kernels for 4%

profile of v3, /device:TPU:0, one launch (start us, length us, event | category | flops | bytes accessed | tf_op | source)
XLA Modules:
  0.0 58.5 jit_solution(12804906387162140543)
XLA Ops:
  0.6 0.0 copy-start.4
  0.6 1.0 %copy-done.4 = f32[1,8,5,16,128]{4,3,2,1,0:T(8,128)S(1)} copy-done((f32[1,8,5,16,128]{4,3,2,1,0:T(8,128)S(1)}, f32[1,8,5,16,128]{4,3,2,1,0:T(8,128)}, u32[]{:S(2)}) %copy-start.4) | copy-done | bytes 327704
  1.6 0.0 copy-start.1
  1.6 0.0 copy-start.2
  1.6 0.0 copy-start.3
  1.6 0.1 shard_map.95
  1.8 14.2 %all_to_all.10.tiles_ref = f32[8,16,128]{2,1,0:T(8,128)S(1)} all-to-all(f32[8,16,128]{2,1,0:T(8,128)S(1)} %get-tuple-element.19), channel_id=1, replica_groups=mesh['zone'=8,'ja'=4] {'zone'}, dimensions={0} | all-to-all | bytes 131072 | tf_op jit(solution)/shard_map/all_to_all | solution.py:437
  16.0 0.0 copy-done.1
  16.0 0.0 copy-done.2
  16.0 0.0 copy-done.3
  16.0 0.0 copy-start
  16.0 0.0 copy-start.5
  16.0 0.0 copy-start.6
  16.1 0.0 copy-start.7
  16.1 0.0 copy-start.8
  16.1 2.7 %shard_map.96 = (f32[8,5,5,16,128]{4,3,2,1,0:T(8,128)S(1)}, f32[8,5,5,16,128]{4,3,2,1,0:T(8,128)S(1)}, f32[3,5,5,16,128]{4,3,2,1,0:T(8,128)S(1)}) custom-call(f32[8,16,128]{2,1,0:T(8,128)S(1)} %all_to_all.10.tiles_ref, f32[8,5,5,16,128]{4,3,2,1,0:T(8,128)S(1)} %bitcast.10, f32[8,5,5,16,128]{4,3,2,1,0:T(8,128)S(1)} %bitcast.13, f32[8,5,5,16,128]{4,3,2,1,0:T(8,128)S(1)} %bitcast.15), custom_call_target="tpu_custom_call" | custom-call | flops 5000000000 | bytes 8871936 | tf_op jit(solution)/shard_map/pallas_call | solution.py:29
  18.8 0.1 collective-permute-start.2
  18.9 1.3 %collective-permute-start = (f32[5,16,128]{2,1,0:T(8,128)S(1)}, f32[5,16,128]{2,1,0:T(8,128)S(1)}, u32[]{:S(2)}, u32[]{:S(2)}) collective-permute-start(f32[5,16,128]{2,1,0:T(8,128)S(1)} %get-tuple-element.18), channel_id=1, source_target_pairs={{1,0},{2,1},{3,2},{5,4},{6,5},{7,6},{9,8},{10,9},{11,10},{13,12},{... | collective-permute-start | bytes 122888 | tf_op jit(solution)/shard_map/ppermute | solution.py:440
  20.2 1.8 %collective-permute-done.above_ref = f32[5,16,128]{2,1,0:T(8,128)S(1)} collective-permute-done((f32[5,16,128]{2,1,0:T(8,128)S(1)}, f32[5,16,128]{2,1,0:T(8,128)S(1)}, u32[]{:S(2)}, u32[]{:S(2)}) %collective-permute-start) | collective-permute-done | bytes 40992 | tf_op jit(solution)/shard_map/ppermute | solution.py:440
  22.0 0.0 copy-done
  22.0 0.0 copy-done.5
  22.0 0.0 copy-done.6
  22.0 0.0 copy-done.7
  22.0 0.0 copy-done.8
  22.1 1.5 %shard_map.97 = (f32[8,5,16,128]{3,2,1,0:T(8,128)S(1)}, f32[2,5,16,128]{3,2,1,0:T(8,128)S(1)}) custom-call(s32[8]{0:T(128)S(1)} %copy-done.7, s32[8]{0:T(128)S(1)} %copy-done.8, f32[8,16,128]{2,1,0:T(8,128)S(1)} %all_to_all.10.tiles_ref, f32[8,5,16,128]{3,2,1,0:T(8,128)S(1)} %bitcast.18, f32[5,16,128]{2,1,0:T(8,128)S(1)} %collective-permute-done.above_ref, ...), custom_call_target="tpu_custom_call" | custom-call | flops 1000000000 | bytes 7725120 | tf_op jit(solution)/shard_map/pallas_call | solution.py:29
  23.5 2.8 %collective-permute-start.1 = (f32[2,5,16,128]{3,2,1,0:T(8,128)S(1)}, f32[2,5,16,128]{3,2,1,0:T(8,128)S(1)}, u32[]{:S(2)}, u32[]{:S(2)}) collective-permute-start(f32[2,5,16,128]{3,2,1,0:T(8,128)S(1)} %get-tuple-element.23.ends_ref), channel_id=1, source_target_pairs={{0,1},{1,0},{2,3},{3,2},{4,5},{5,4},{6,7},{7,6},{8,9},{9,8},{10,11... | collective-permute-start | bytes 245768 | tf_op jit(solution)/shard_map/ppermute | solution.py:434
  26.3 0.0 collective-permute-done.2.mats_other_ref.other_ref
  26.3 0.1 shard_map.99
  26.4 1.3 %collective-permute-start.4 = (f32[5,5,8,128]{3,2,1,0:T(8,128)S(1)}, f32[5,5,8,128]{3,2,1,0:T(8,128)S(1)}, u32[]{:S(2)}, u32[]{:S(2)}) collective-permute-start(f32[5,5,8,128]{3,2,1,0:T(8,128)S(1)} %shard_map.99), channel_id=1, source_target_pairs={{2,0},{3,1},{6,4},{7,5},{10,8},{11,9},{14,12},{15,13},{18,16},{19,... | collective-permute-start | bytes 307208 | tf_op jit(solution)/shard_map/ppermute | solution.py:451
  27.7 0.0 collective-permute-done.1.ends_other_ref
  27.7 5.4 %collective-permute-done.4.half_ref = f32[5,5,8,128]{3,2,1,0:T(8,128)S(1)} collective-permute-done((f32[5,5,8,128]{3,2,1,0:T(8,128)S(1)}, f32[5,5,8,128]{3,2,1,0:T(8,128)S(1)}, u32[]{:S(2)}, u32[]{:S(2)}) %collective-permute-start.4) | collective-permute-done | bytes 102432 | tf_op jit(solution)/shard_map/ppermute | solution.py:451
  33.1 1.9 %collective-permute-start.5 = (f32[5,5,8,128]{3,2,1,0:T(8,128)S(1)}, f32[5,5,8,128]{3,2,1,0:T(8,128)S(1)}, u32[]{:S(2)}, u32[]{:S(2)}) collective-permute-start(f32[5,5,8,128]{3,2,1,0:T(8,128)S(1)} %shard_map.100), channel_id=1, source_target_pairs={{0,1},{1,0},{4,5},{5,4},{8,9},{9,8},{12,13},{13,12},{16,17},{17,16... | collective-permute-start | bytes 307208 | tf_op jit(solution)/shard_map/ppermute | solution.py:455
  35.0 0.1 collective-permute-start.3
  35.1 4.0 %collective-permute-done.3.pair_other_ref = f32[1,5,16,128]{3,2,1,0:T(8,128)S(1)} collective-permute-done((f32[1,5,16,128]{3,2,1,0:T(8,128)S(1)}, f32[1,5,16,128]{3,2,1,0:T(8,128)S(1)}, u32[]{:S(2)}, u32[]{:S(2)}) %collective-permute-start.3) | collective-permute-done | bytes 40992 | tf_op jit(solution)/shard_map/ppermute | solution.py:434
  39.1 0.0 collective-permute-done.5.half_other_ref
  39.1 1.0 %shard_map.101 = (f32[8,5,16,128]{3,2,1,0:T(8,128)S(1)}, f32[5,16,128]{2,1,0:T(8,128)S(1)}, f32[8,16,128]{2,1,0:T(8,128)S(1)}) custom-call(s32[8]{0:T(128)S(1)} %copy-done.7, f32[8,5,16,128]{3,2,1,0:T(8,128)S(1)} %bitcast.19, f32[5,16,128]{2,1,0:T(8,128)S(1)} %collective-permute-done.above_ref, f32[8,5,16,128]{3,2,1,0:T(8,128)S(1)} %get-tuple-element.22.s_ref, ...), custom_call_target="tpu_custom_call" | custom-call | flops 1000000000 | bytes 6086688 | tf_op jit(solution)/shard_map/pallas_call | solution.py:29
  40.1 9.3 %all_to_all.11.tiles_ref = f32[8,16,128]{2,1,0:T(8,128)S(1)} all-to-all(f32[8,16,128]{2,1,0:T(8,128)S(1)} %get-tuple-element.25), channel_id=1, replica_groups=mesh['zone'=8,'ja'=4] {'zone'}, dimensions={0} | all-to-all | bytes 131072 | tf_op jit(solution)/shard_map/all_to_all | solution.py:437
  49.4 1.5 %shard_map.102 = (f32[8,5,16,128]{3,2,1,0:T(8,128)S(1)}, f32[8,5,16,128]{3,2,1,0:T(8,128)S(1)}, f32[3,5,16,128]{3,2,1,0:T(8,128)S(1)}, f32[5,5,16,128]{3,2,1,0:T(8,128)S(1)}) custom-call(s32[8]{0:T(128)S(1)} %copy-done.7, s32[8]{0:T(128)S(1)} %copy-done.8, f32[8,16,128]{2,1,0:T(8,128)S(1)} %all_to_all.11.tiles_ref, ...), custom_call_target="tpu_custom_call" | custom-call | flops 1000000000 | bytes 11575360 | tf_op jit(solution)/shard_map/pallas_call | solution.py:29
  50.9 0.1 collective-permute-start.6
  51.0 1.3 %collective-permute-done.6.ends_other_ref = f32[3,5,16,128]{3,2,1,0:T(8,128)S(1)} collective-permute-done((f32[3,5,16,128]{3,2,1,0:T(8,128)S(1)}, f32[3,5,16,128]{3,2,1,0:T(8,128)S(1)}, u32[]{:S(2)}, u32[]{:S(2)}) %collective-permute-start.6) | collective-permute-done | bytes 122912 | tf_op jit(solution)/shard_map/ppermute | solution.py:434
  52.3 0.3 collective-permute-start.7
  52.7 0.7 %shard_map.104.res_in_hbm = f32[8,5,16,128]{3,2,1,0:T(8,128)} custom-call(f32[8,5,16,128]{3,2,1,0:T(8,128)S(1)} %get-tuple-element.29.res_ref), custom_call_target="tpu_custom_call" | custom-call | flops 1000000000 | bytes 655360 | tf_op jit(solution)/shard_map/pallas_call | solution.py:29
  53.4 3.5 %collective-permute-done.7.pair_other_ref = f32[2,5,16,128]{3,2,1,0:T(8,128)S(1)} collective-permute-done((f32[2,5,16,128]{3,2,1,0:T(8,128)S(1)}, f32[2,5,16,128]{3,2,1,0:T(8,128)S(1)}, u32[]{:S(2)}, u32[]{:S(2)}) %collective-permute-start.7) | collective-permute-done | bytes 81952 | tf_op jit(solution)/shard_map/ppermute | solution.py:434
  56.9 1.6 %shard_map.105 = (f32[8,5,16,128]{3,2,1,0:T(8,128)}, f32[8,5,16,128]{3,2,1,0:T(8,128)}) custom-call(s32[8]{0:T(128)S(1)} %copy-done.7, f32[5,5,16,128]{3,2,1,0:T(8,128)S(1)} %get-tuple-element.28.low0_ref, f32[8,5,16,128]{3,2,1,0:T(8,128)S(1)} %get-tuple-element.26.cur_ref, ...), custom_call_target="tpu_custom_call", output_to_operand_aliasing={{1}: (15, {})} | custom-call | flops 1000000000 | bytes 7290912 | tf_op jit(solution)/shard_map/pallas_call | solution.py:29
  (3 shorter events, 0.1 us)
Async XLA Ops:
  0.6 1.0 %copy-start.4 = (f32[1,8,5,16,128]{4,3,2,1,0:T(8,128)S(1)}, f32[1,8,5,16,128]{4,3,2,1,0:T(8,128)}, u32[]{:S(2)}) copy-start(f32[1,8,5,16,128]{4,3,2,1,0:T(8,128)} %param.8) | copy-start | bytes 983044
  1.6 14.4 %copy-start.1 = (f32[1,8,5,5,16,128]{5,4,3,2,1,0:T(8,128)S(1)}, f32[1,8,5,5,16,128]{5,4,3,2,1,0:T(8,128)}, u32[]{:S(2)}) copy-start(f32[1,8,5,5,16,128]{5,4,3,2,1,0:T(8,128)} %param.13) | copy-start | bytes 4915204
  1.6 14.4 %copy-start.2 = (f32[1,8,5,5,16,128]{5,4,3,2,1,0:T(8,128)S(1)}, f32[1,8,5,5,16,128]{5,4,3,2,1,0:T(8,128)}, u32[]{:S(2)}) copy-start(f32[1,8,5,5,16,128]{5,4,3,2,1,0:T(8,128)} %param.11) | copy-start | bytes 4915204
  1.6 14.4 %copy-start.3 = (f32[1,8,5,5,16,128]{5,4,3,2,1,0:T(8,128)S(1)}, f32[1,8,5,5,16,128]{5,4,3,2,1,0:T(8,128)}, u32[]{:S(2)}) copy-start(f32[1,8,5,5,16,128]{5,4,3,2,1,0:T(8,128)} %param.12) | copy-start | bytes 4915204
  16.0 6.0 %copy-start = (f32[1,8,5,5,16,128]{5,4,3,2,1,0:T(8,128)S(1)}, f32[1,8,5,5,16,128]{5,4,3,2,1,0:T(8,128)}, u32[]{:S(2)}) copy-start(f32[1,8,5,5,16,128]{5,4,3,2,1,0:T(8,128)} %param.10) | copy-start | bytes 4915204
  16.0 6.0 %copy-start.5 = (f32[1,8,5,16,128]{4,3,2,1,0:T(8,128)S(1)}, f32[1,8,5,16,128]{4,3,2,1,0:T(8,128)}, u32[]{:S(2)}) copy-start(f32[1,8,5,16,128]{4,3,2,1,0:T(8,128)} %param.8) | copy-start | bytes 983044
  16.0 6.0 %copy-start.6 = (f32[1,8,5,16,128]{4,3,2,1,0:T(8,128)S(1)}, f32[1,8,5,16,128]{4,3,2,1,0:T(8,128)}, u32[]{:S(2)}) copy-start(f32[1,8,5,16,128]{4,3,2,1,0:T(8,128)} %param.9) | copy-start | bytes 983044
  16.1 6.0 %copy-start.7 = (s32[8]{0:T(128)S(1)}, s32[8]{0:T(128)}, u32[]{:S(2)}) copy-start(s32[8]{0:T(128)} %depth_ref.7) | copy-start | bytes 100
  16.1 6.0 %copy-start.8 = (s32[8]{0:T(128)S(1)}, s32[8]{0:T(128)}, u32[]{:S(2)}) copy-start(s32[8]{0:T(128)} %east_ref.3) | copy-start | bytes 100
  18.8 7.4 %collective-permute-start.2 = (f32[3,5,5,16,128]{4,3,2,1,0:T(8,128)S(1)}, f32[3,5,5,16,128]{4,3,2,1,0:T(8,128)S(1)}, u32[]{:S(2)}, u32[]{:S(2)}) collective-permute-start(f32[3,5,5,16,128]{4,3,2,1,0:T(8,128)S(1)} %get-tuple-element.24.mats_ref.mine_ref), channel_id=1, source_target_pairs={{0,1},{1,0},{2,3},{3,2},{4,5},{5,4},{6,7},{7,6},{8,9},{9,8},{10,11... | collective-permute-start | bytes 1843208 | tf_op jit(solution)/shard_map/ppermute | solution.py:434
  18.9 3.1 %collective-permute-start = (f32[5,16,128]{2,1,0:T(8,128)S(1)}, f32[5,16,128]{2,1,0:T(8,128)S(1)}, u32[]{:S(2)}, u32[]{:S(2)}) collective-permute-start(f32[5,16,128]{2,1,0:T(8,128)S(1)} %get-tuple-element.18), channel_id=1, source_target_pairs={{1,0},{2,1},{3,2},{5,4},{6,5},{7,6},{9,8},{10,9},{11,10},{13,12},{... | collective-permute-start | bytes 122888 | tf_op jit(solution)/shard_map/ppermute | solution.py:440
  23.5 4.1 %collective-permute-start.1 = (f32[2,5,16,128]{3,2,1,0:T(8,128)S(1)}, f32[2,5,16,128]{3,2,1,0:T(8,128)S(1)}, u32[]{:S(2)}, u32[]{:S(2)}) collective-permute-start(f32[2,5,16,128]{3,2,1,0:T(8,128)S(1)} %get-tuple-element.23.ends_ref), channel_id=1, source_target_pairs={{0,1},{1,0},{2,3},{3,2},{4,5},{5,4},{6,7},{7,6},{8,9},{9,8},{10,11... | collective-permute-start | bytes 245768 | tf_op jit(solution)/shard_map/ppermute | solution.py:434
  26.4 6.7 %collective-permute-start.4 = (f32[5,5,8,128]{3,2,1,0:T(8,128)S(1)}, f32[5,5,8,128]{3,2,1,0:T(8,128)S(1)}, u32[]{:S(2)}, u32[]{:S(2)}) collective-permute-start(f32[5,5,8,128]{3,2,1,0:T(8,128)S(1)} %shard_map.99), channel_id=1, source_target_pairs={{2,0},{3,1},{6,4},{7,5},{10,8},{11,9},{14,12},{15,13},{18,16},{19,... | collective-permute-start | bytes 307208 | tf_op jit(solution)/shard_map/ppermute | solution.py:451
  33.1 6.0 %collective-permute-start.5 = (f32[5,5,8,128]{3,2,1,0:T(8,128)S(1)}, f32[5,5,8,128]{3,2,1,0:T(8,128)S(1)}, u32[]{:S(2)}, u32[]{:S(2)}) collective-permute-start(f32[5,5,8,128]{3,2,1,0:T(8,128)S(1)} %shard_map.100), channel_id=1, source_target_pairs={{0,1},{1,0},{4,5},{5,4},{8,9},{9,8},{12,13},{13,12},{16,17},{17,16... | collective-permute-start | bytes 307208 | tf_op jit(solution)/shard_map/ppermute | solution.py:455
  35.0 4.1 %collective-permute-start.3 = (f32[1,5,16,128]{3,2,1,0:T(8,128)S(1)}, f32[1,5,16,128]{3,2,1,0:T(8,128)S(1)}, u32[]{:S(2)}, u32[]{:S(2)}) collective-permute-start(f32[1,5,16,128]{3,2,1,0:T(8,128)S(1)} %shard_map.98.pair_ref), channel_id=1, source_target_pairs={{0,2},{1,3},{2,0},{3,1},{4,6},{5,7},{6,4},{7,5},{8,10},{9,11},{10,... | collective-permute-start | bytes 122888 | tf_op jit(solution)/shard_map/ppermute | solution.py:434
  50.9 1.4 %collective-permute-start.6 = (f32[3,5,16,128]{3,2,1,0:T(8,128)S(1)}, f32[3,5,16,128]{3,2,1,0:T(8,128)S(1)}, u32[]{:S(2)}, u32[]{:S(2)}) collective-permute-start(f32[3,5,16,128]{3,2,1,0:T(8,128)S(1)} %get-tuple-element.31.ends_ref), channel_id=1, source_target_pairs={{0,1},{1,0},{2,3},{3,2},{4,5},{5,4},{6,7},{7,6},{8,9},{9,8},{10,11... | collective-permute-start | bytes 368648 | tf_op jit(solution)/shard_map/ppermute | solution.py:434
  52.3 4.6 %collective-permute-start.7 = (f32[2,5,16,128]{3,2,1,0:T(8,128)S(1)}, f32[2,5,16,128]{3,2,1,0:T(8,128)S(1)}, u32[]{:S(2)}, u32[]{:S(2)}) collective-permute-start(f32[2,5,16,128]{3,2,1,0:T(8,128)S(1)} %shard_map.103.pair_ref), channel_id=1, source_target_pairs={{0,2},{1,3},{2,0},{3,1},{4,6},{5,7},{6,4},{7,5},{8,10},{9,11},{10,... | collective-permute-start | bytes 245768 | tf_op jit(solution)/shard_map/ppermute | solution.py:434

commit v4 on v3

--- a/solution.py
+++ b/solution.py
@@ -1,5 +1,3 @@
-import functools
-
 import jax
 import jax.numpy as jnp
 from jax import lax
@@ -12,29 +10,29 @@
 COUPLE = 0.25
 
 VMEM = pl.BlockSpec(memory_space=pltpu.VMEM)
-SMEM = pl.BlockSpec(memory_space=pltpu.SMEM)
 ANY = pl.BlockSpec(memory_space=pl.ANY)
 HBM = pl.BlockSpec(memory_space=pltpu.HBM)
 
 
-def call(kernel, shapes, scratch=(), flops=10**9, out_specs=None, alias=None):
-    moved = sum(4 * functools.reduce(lambda a, b: a * b, s, 1) for s in shapes)
+def call(kernel, shapes, scratch=(), flops=10**9, far=(), out_specs=None, alias=None):
     alias = alias or {}
 
-    def spec(i, a):
-        return ANY if i in alias else VMEM if a.dtype == jnp.float32 else SMEM
-
     def run(*arrays):
-        total = moved + sum(a.size * 4 for a in arrays)
+        arrays = [
+            pltpu.with_memory_space_constraint(a, pltpu.HBM) if i in far else a
+            for i, a in enumerate(arrays)
+        ]
         return pl.pallas_call(
             kernel,
             out_shape=[jax.ShapeDtypeStruct(s, jnp.float32) for s in shapes],
-            in_specs=[spec(i, a) for i, a in enumerate(arrays)],
+            in_specs=[
+                HBM if i in far else ANY if i in alias else VMEM for i in range(len(arrays))
+            ],
             out_specs=out_specs or [VMEM] * len(shapes),
             scratch_shapes=list(scratch),
             input_output_aliases=alias,
             compiler_params=pltpu.CompilerParams(vmem_limit_bytes=12 * 2**20),
-            cost_estimate=pl.CostEstimate(flops=flops, bytes_accessed=total, transcendentals=0),
+            cost_estimate=pl.CostEstimate(flops=flops, bytes_accessed=flops // 10**3, transcendentals=0),
         )(*arrays)
 
     return run
@@ -89,15 +87,18 @@
         tile_ref[w] = tile
 
 
-def live_rows(depth_ref):
-    return iota(0) < depth_ref[lax.axis_index("zone")]
-
-
-def masked(live, values):
+def masked(live_ref, values):
+    live = live_ref[...] > 0.0
     return [jnp.where(live, x, 0.0) for x in values]
 
 
-def pack_kernel(flow_ref, tile_ref, first_ref):
+def has_above(values):
+    inner = lax.axis_index("ja") < lax.axis_size("ja") - 1
+    return [jnp.where(inner, x, 0.0) for x in values]
+
+
+def pack_kernel(mats_ref, flow_ref, tile_ref, first_ref):
+    del mats_ref
     put(first_ref, cell(flow_ref, 0))
     pack_faces(lambda j, v: flow_ref[j, v], flow_ref.shape[0], tile_ref)
 
@@ -110,15 +111,11 @@
     return total + jnp.where(row == 15, 0.0, pltpu.roll(x, 15, 0))
 
 
-def ghosts_of(depth_ref, east_ref, tiles_ref):
-    zone = lax.axis_index("zone")
-    east = east_ref[zone]
-    west = jnp.int32(0)
+def ghosts_of(pick_ref, tiles_ref):
+    low = high = jnp.zeros((16, 128), jnp.float32)
     for w in range(tiles_ref.shape[0]):
-        west = west + jnp.where(east_ref[w] == zone, w, 0)
-    row = iota(0)
-    low = jnp.where(row < depth_ref[west], tiles_ref[west], 0.0)
-    high = jnp.where(row < depth_ref[east], tiles_ref[east], 0.0)
+        low = jnp.where(pick_ref[0, w] > 0.0, tiles_ref[w], low)
+        high = jnp.where(pick_ref[1, w] > 0.0, tiles_ref[w], high)
     return jnp.where(iota(1) % 2 == 0, pltpu.roll(low, 1, 1), pltpu.roll(high, 127, 1))
 
 
@@ -129,9 +126,30 @@
     return jnp.where((lane == 0) | (lane == 127), turned, 0.0)
 
 
-def matrix_kernel(tiles_ref, inv_ref, low_ref, up_ref, e_ref, f_ref, mats_ref, y_ref):
-    del tiles_ref
+def matrix_kernel(
+    depth_hbm, east_hbm, inv_hbm, low_hbm, up_hbm,
+    e_ref, f_ref, mats_ref, live_ref, pick_ref,
+    inv_ref, low_ref, up_ref, y_ref, depth_ref, east_ref, sems, small_sems,
+):
     planes = inv_ref.shape[0]
+
+    def copies(j):
+        return [
+            pltpu.make_async_copy(src.at[j], dst.at[j], sems.at[i, j])
+            for i, (src, dst) in enumerate(
+                [(inv_hbm, inv_ref), (low_hbm, low_ref), (up_hbm, up_ref)]
+            )
+        ]
+
+    for j in range(planes):
+        for copy in copies(j):
+            copy.start()
+    scalars = [
+        pltpu.make_async_copy(depth_hbm, depth_ref, small_sems.at[0]),
+        pltpu.make_async_copy(east_hbm, east_ref, small_sems.at[1]),
+    ]
+    for copy in scalars:
+        copy.start()
     last = planes - 1
     halves = [pl.ds(0, 8), pl.ds(8, 8)]
 
@@ -153,6 +171,8 @@
                 put_col(out_ref, [OMEGA * x for x in product], q, j, rows)
 
     def forward(j, carry):
+        for copy in copies(j):
+            copy.wait()
         for rows in halves:
             products(j, rows)
             e = mat(e_ref, j, rows)
@@ -160,6 +180,8 @@
                 put_col(y_ref, matvec(e, col(y_ref, q, j - 1, rows)), q, j, rows)
         return carry
 
+    for copy in copies(0):
+        copy.wait()
     for rows in halves:
         products(0, rows)
         for q in range(5):
@@ -182,6 +204,15 @@
         return carry
 
     lax.fori_loop(0, planes - 1, backward, 0)
+    for copy in scalars:
+        copy.wait()
+    zone = lax.axis_index("zone")
+    row = iota(0)
+    live_ref[...] = jnp.where(row < depth_ref[zone], 1.0, 0.0)
+    for w in range(pick_ref.shape[1]):
+        rows = row < depth_ref[w]
+        pick_ref[0, w] = jnp.where(rows & (east_ref[w] == zone), 1.0, 0.0)
+        pick_ref[1, w] = jnp.where(rows & (east_ref[zone] == w), 1.0, 0.0)
 
 
 def by_place(mine_refs, other_refs, run):
@@ -196,31 +227,17 @@
         run(*other_refs, *mine_refs)
 
 
-def beta_kernel(mine_ref, other_ref, half_ref):
+def beta_kernel(mine_ref, other_ref, beta_ref):
     def run(lo, hi):
-        def part(ref, *at):
-            return ref[at][rows]
-
-        d_hi = [[part(hi, 1, r, c) for c in range(5)] for r in range(5)]
-        n_lo = [[part(lo, 2, r, c) for c in range(5)] for r in range(5)]
+        d_hi, n_lo = block(hi, 1), block(lo, 2)
         for q in range(5):
-            m_col = [part(lo, 0, r, q) for r in range(5)]
-            d_col = [part(lo, 1, r, q) for r in range(5)]
+            m_col = [lo[0, r, q] for r in range(5)]
+            d_col = [lo[1, r, q] for r in range(5)]
             out = add(d_col, matvec(n_lo, matvec(d_hi, m_col)))
             for r in range(5):
-                half_ref[r, q] = out[r]
-
-    odd = lax.axis_index("ja") % 2
-    for side in range(2):
-        rows = slice(8 * side, 8 * side + 8)
-        pair = (mine_ref, other_ref) if side == 0 else (other_ref, mine_ref)
-        pl.when(odd == side)(functools.partial(run, *pair))
-
-
-def relay_kernel(half_ref, pair_ref, out_ref):
-    del pair_ref
-    for r in range(5):
-        put(out_ref, cell(half_ref, r), r)
+                beta_ref[r, q] = out[r]
+
+    by_place([mine_ref], [other_ref], run)
 
 
 def sweeps(s_ref, e_ref, f_ref, y_ref, ends_ref, last):
@@ -237,16 +254,17 @@
 
 
 def local_kernel(
-    depth_ref, east_ref, tiles_ref, cur_ref, above_ref, force_ref, diag_ref, inv_ref,
+    beta_ref, live_ref, pick_ref, tiles_ref, cur_ref, above_ref, force_ref, diag_ref, inv_ref,
     e_ref, f_ref,
     s_ref, ends_ref, y_ref,
 ):
+    del beta_ref
     planes = cur_ref.shape[0]
-    live = live_rows(depth_ref)
-    ghosts = ghosts_of(depth_ref, east_ref, tiles_ref)
-    before, here = None, masked(live, cell(cur_ref, 0))
+    ghosts = ghosts_of(pick_ref, tiles_ref)
+    before, here = None, masked(live_ref, cell(cur_ref, 0))
     for j in range(planes):
-        after = masked(live, cell(cur_ref, j + 1) if j < planes - 1 else cell(above_ref))
+        after = cell(cur_ref, j + 1) if j < planes - 1 else has_above(cell(above_ref))
+        after = masked(live_ref, after)
         own = matvec(block(diag_ref, j), here)
         res = []
         for v in range(5):
@@ -256,19 +274,18 @@
         if before is not None:
             linked = add(linked, matvec(block(e_ref, j), before))
         linked = [x * (1.0 / OMEGA) for x in linked]
-        put(s_ref, add(matvec(block(inv_ref, j), masked(live, res)), linked), j)
+        put(s_ref, add(matvec(block(inv_ref, j), masked(live_ref, res)), linked), j)
         before, here = here, after
-    sweeps(s_ref, e_ref, f_ref, y_ref, ends_ref, before)
+    sweeps(s_ref, e_ref, f_ref, y_ref, ends_ref, masked(live_ref, cell(cur_ref, planes - 1)))
 
 
 def second_kernel(
-    depth_ref, east_ref, tiles_ref, cur_ref, above_ref, force_ref, diag_ref, low_ref, up_ref,
+    live_ref, pick_ref, tiles_ref, cur_ref, above_ref, force_ref, diag_ref, low_ref, up_ref,
     inv_ref, e_ref, f_ref,
     res_ref, s_ref, ends_ref, low0_ref, y_ref,
 ):
     planes = cur_ref.shape[0]
-    live = live_rows(depth_ref)
-    ghosts = ghosts_of(depth_ref, east_ref, tiles_ref)
+    ghosts = ghosts_of(pick_ref, tiles_ref)
     for r in range(5):
         put(low0_ref, cell(low_ref, 0, r), r)
     for j in range(planes):
@@ -283,7 +300,8 @@
         for v in range(5):
             sides = neighbours(here[v]) + ghost_at(ghosts, j, v)
             all_of = applied[v] - upper[v] - COUPLE * sides
-            res.append(jnp.where(live, force_ref[j, v] - all_of, 0.0))
+            res.append(force_ref[j, v] - all_of)
+        res = masked(live_ref, res)
         put(res_ref, res, j)
         put(s_ref, matvec(block(inv_ref, j), res), j)
     last = cell(cur_ref, planes - 1)
@@ -318,29 +336,25 @@
 
 def inflows(
     ends_ref, ends_other_ref, mats_ref, mats_other_ref, pair_ref, pair_other_ref,
-    half_ref, half_other_ref, inflow_ref,
+    beta_ref, inflow_ref,
 ):
     ja = lax.axis_index("ja")
     zeros = [jnp.zeros((16, 128), jnp.float32)] * 5
 
-    def far(top_ref, bottom_ref):
-        beta = [
-            [jnp.concatenate([top_ref[r, c], bottom_ref[r, c]], axis=0) for c in range(5)]
-            for r in range(5)
-        ]
-        return add(cell(pair_other_ref, 0), matvec(beta, cell(pair_ref, 0)))
+    def far():
+        return add(cell(pair_other_ref, 0), matvec(block(beta_ref), cell(pair_ref, 0)))
 
     @pl.when(ja == 0)
     def _():
         put(inflow_ref, zeros, 0)
         b = add(cell(ends_other_ref, 1), matvec(block(mats_other_ref, 1), cell(ends_ref, 0)))
-        b = add(b, matvec(block(mats_other_ref, 2), far(half_ref, half_other_ref)))
+        b = add(b, matvec(block(mats_other_ref, 2), far()))
         put(inflow_ref, b, 1)
 
     @pl.when(ja == 1)
     def _():
         put(inflow_ref, cell(ends_other_ref, 0), 0)
-        put(inflow_ref, far(half_other_ref, half_ref), 1)
+        put(inflow_ref, far(), 1)
 
     @pl.when(ja == 2)
     def _():
@@ -358,50 +372,48 @@
 
 
 def final_kernel(
-    depth_ref, cur_ref, above_ref, s_ref, e_ref, f_ref,
+    live_ref, cur_ref, above_ref, s_ref, e_ref, f_ref,
     ends_ref, ends_other_ref, mats_ref, mats_other_ref, pair_ref, pair_other_ref,
-    half_ref, half_other_ref,
+    beta_ref,
     new_ref, above_new_ref, tile_ref, y_ref, inflow_ref,
 ):
     planes = cur_ref.shape[0]
     inflows(
         ends_ref, ends_other_ref, mats_ref, mats_other_ref, pair_ref, pair_other_ref,
-        half_ref, half_other_ref, inflow_ref,
+        beta_ref, inflow_ref,
     )
     value = cell(inflow_ref, 0)
     for j in range(planes):
         value = add(cell(s_ref, j), matvec(block(e_ref, j), value))
         put(y_ref, value, j)
     value = cell(inflow_ref, 1)
-    live = live_rows(depth_ref)
-    put(above_new_ref, add(masked(live, cell(above_ref)), value))
+    put(above_new_ref, add(masked(live_ref, has_above(cell(above_ref))), value))
     for j in range(planes - 1, -1, -1):
         value = add(cell(y_ref, j), matvec(block(f_ref, j), value))
-        put(new_ref, add(masked(live, cell(cur_ref, j)), value), j)
+        put(new_ref, add(masked(live_ref, cell(cur_ref, j)), value), j)
     pack_faces(lambda j, v: new_ref[j, v], planes, tile_ref)
 
 
 def last_kernel(
-    depth_ref, low0_ref, cur_ref, res_ref, s_ref, e_ref, f_ref,
+    live_ref, low0_ref, cur_ref, res_ref, s_ref, e_ref, f_ref,
     ends_ref, ends_other_ref, mats_ref, mats_other_ref, pair_ref, pair_other_ref,
-    half_ref, half_other_ref,
+    beta_ref,
     res_in_hbm,
     new_hbm, res_hbm, y_ref, inflow_ref, new_ref, res0_ref, sems,
 ):
     del res_in_hbm
     planes = cur_ref.shape[0]
     ja = lax.axis_index("ja")
-    live = live_rows(depth_ref)
     before = [
         jnp.where(ja == 0, 0.0, jnp.where(ja == 2, pair_other_ref[1, v], ends_other_ref[2, v]))
         for v in range(5)
     ]
-    put(res0_ref, add(cell(res_ref, 0), masked(live, matvec(block(low0_ref), before))))
+    put(res0_ref, add(cell(res_ref, 0), masked(live_ref, matvec(block(low0_ref), before))))
     copies = [pltpu.make_async_copy(res0_ref, res_hbm.at[0], sems.at[planes])]
     copies[0].start()
     inflows(
         ends_ref, ends_other_ref, mats_ref, mats_other_ref, pair_ref, pair_other_ref,
-        half_ref, half_other_ref, inflow_ref,
+        beta_ref, inflow_ref,
     )
     value = cell(inflow_ref, 0)
     for j in range(planes):
@@ -436,34 +448,38 @@
     def faces(x):
         return lax.all_to_all(x, "zone", 0, 0, tiled=True)
 
-    tile, first = call(pack_kernel, [tiles, plane], flops=2 * 10**10)(current)
-    above = lax.ppermute(first, "ja", [(p + 1, p) for p in range(parts - 1)])
+    e, f, mats, live, pick = call(
+        matrix_kernel,
+        [blocks, blocks, (3, *matrix), state[2:], (2, *tiles)],
+        [buffer(*blocks)] * 4
+        + [pltpu.SMEM((zones,), jnp.int32)] * 2
+        + [pltpu.SemaphoreType.DMA((3, planes)), pltpu.SemaphoreType.DMA((2,))],
+        flops=5 * 10**9,
+        far=(0, 1, 2, 3, 4),
+    )(zone_depth, east_zone, inv, low, up)
+    tile, first = call(pack_kernel, [tiles, plane], flops=2 * 10**10)(mats, current)
+    above = lax.ppermute(first, "ja", [((p + 1) % parts, p) for p in range(parts)])
+    mats_other = swap(mats, 1)
     got = faces(tile)
-    e, f, mats = call(
-        matrix_kernel, [blocks, blocks, (3, *matrix)], [buffer(*blocks)], flops=5 * 10**9
-    )(got, inv, low, up)
-    mats_other = swap(mats, 1)
+    beta = call(beta_kernel, [matrix], flops=10**5)(mats, mats_other)[0]
     s, ends = call(local_kernel, [state, (2, *plane)], work)(
-        zone_depth, east_zone, got, current, above, force, diag, inv, e, f
-    )
+        beta, live, pick, got, current, above, force, diag, inv, e, f
+    )
+    beta = swap(beta, 2)
     ends_other = swap(ends, 1)
-    half = call(beta_kernel, [(*matrix[:2], 8, matrix[3])])(mats, mats_other)[0]
-    half = lax.ppermute(half, "ja", [(2, 0), (3, 1)])
     pair = call(mid_kernel, [(1, *plane)])(ends, ends_other, mats, mats_other)[0]
     pair_other = swap(pair, 2)
-    half_sent = call(relay_kernel, [half.shape])(half, pair)[0]
-    half_other = lax.ppermute(half_sent, "ja", [(0, 1), (1, 0)])
     flows = [buffer(2, *plane)]
     current, above, tile = call(final_kernel, [state, plane, tiles], work + flows)(
-        zone_depth, current, above, s, e, f,
-        ends, ends_other, mats, mats_other, pair, pair_other, half, half_other,
+        live, current, above, s, e, f,
+        ends, ends_other, mats, mats_other, pair, pair_other, beta,
     )
 
     got = faces(tile)
     residual, s, ends, low0 = call(
         second_kernel, [state, state, (3, *plane), matrix], work
     )(
-        zone_depth, east_zone, got, current, above, force, diag, low, up, inv, e, f
+        live, pick, got, current, above, force, diag, low, up, inv, e, f
     )
     ends_other = swap(ends, 1)
     pair = call(mid_kernel, [(2, *plane)])(ends, ends_other, mats, mats_other)[0]
@@ -474,10 +490,10 @@
         [state, state],
         work + flows + work + [buffer(*plane), pltpu.SemaphoreType.DMA((planes + 1,))],
         out_specs=[HBM, HBM],
-        alias={15: 1},
+        alias={14: 1},
     )(
-        zone_depth, low0, current, residual, s, e, f,
-        ends, ends_other, mats, mats_other, pair, pair_other, half, half_other, written,
+        live, low0, current, residual, s, e, f,
+        ends, ends_other, mats, mats_other, pair, pair_other, beta, written,
     )
     return (current[None], residual[None])
 

time: 58.8 us -> 61.2 us (1.041)
  blocking collectives: 23.5 us -> 9.69 us
  Pallas kernels: 9.35 us -> 17.9 us
  local copies, waits for them, and re-layouts: 1.01 us -> 7.81 us
  starting transfers between devices: 7.79 us -> 13.1 us
  waiting for transfers between devices: 16 us -> 11.3 us
    all_to_all x2 -> x1, blocking collectives: 23.5 us -> 9.69 us  [faces(): return lax.all_to_all(x, 'zone', 0, 0, tiled=True)]
    pallas_call x11 -> x10, Pallas kernels: 9.35 us -> 17.9 us  [run(): pl.pallas_call(kernel, out_shape=[jax.ShapeDtypeStruct(s, jnp.float32) fo...]
    all_to_all x0 -> x1, starting transfers between devices: none -> 6.83 us  [faces(): return lax.all_to_all(x, 'zone', 0, 0, tiled=True)]
    unnamed x18 -> x34, local copies, waits for them, and re-layouts: 1.01 us -> 7.81 us
    ppermute x3 -> x1, waiting for transfers between devices: 7.17 us -> 0.58 us  [per_device(): lax.ppermute(first, 'ja', [((p + 1) % parts, p) for p in range(parts)])]
    ppermute x3 -> x1, starting transfers between devices: 4.5 us -> 1.32 us  [per_device(): lax.ppermute(first, 'ja', [((p + 1) % parts, p) for p in range(parts)])]
    all_to_all x0 -> x1, waiting for transfers between devices: none -> 2.97 us  [faces(): return lax.all_to_all(x, 'zone', 0, 0, tiled=True)]
    ppermute x5 -> x6, starting transfers between devices: 3.29 us -> 4.96 us  [swap(): return lax.ppermute(x, 'ja', [(p, p ^ bit) for p in range(parts)])]
  transfers between devices with their start and end apart: 8 -> 8, of which waited for: 5 -> 5; matrix products, arithmetic and copies ran while one was open for 0% -> 0% of each run, Pallas kernels for 4% -> 9%
where the time goes in v4:
time: 61.2 us; the launch traced here: 60.6 us
  Pallas kernels  17.9 us (29%)
  starting transfers between devices  13.1 us (21%)
  waiting for transfers between devices  11.3 us (18%)
  blocking collectives  9.69 us (16%)
  local copies, waits for them, and re-layouts  7.81 us (13%)
  between operations  0.82 us (1%)
    pallas_call x10, Pallas kernels, run(): pl.pallas_call(kernel, out_shape=[jax.ShapeDtypeStruct(s, jnp.float32) fo...  17.9 us
    all_to_all x1, blocking collectives, faces(): return lax.all_to_all(x, 'zone', 0, 0, tiled=True)  9.69 us
    unnamed x34, local copies, waits for them, and re-layouts  7.81 us
    ppermute x6, waiting for transfers between devices, swap(): return lax.ppermute(x, 'ja', [(p, p ^ bit) for p in range(parts)])  7.74 us
    all_to_all x1, starting transfers between devices, faces(): return lax.all_to_all(x, 'zone', 0, 0, tiled=True)  6.83 us
    ppermute x6, starting transfers between devices, swap(): return lax.ppermute(x, 'ja', [(p, p ^ bit) for p in range(parts)])  4.96 us
    all_to_all x1, waiting for transfers between devices, faces(): return lax.all_to_all(x, 'zone', 0, 0, tiled=True)  2.97 us
    ppermute x1, starting transfers between devices, per_device(): lax.ppermute(first, 'ja', [((p + 1) % parts, p) for p in range(parts)])  1.32 us
  transfers between devices with their start and end apart: 8, of which 5 were waited for; matrix products, arithmetic and copies ran while one was open for 0% of the time, Pallas kernels for 9%

profile of v4, /device:TPU:0, one launch (start us, length us, event | category | flops | bytes accessed | tf_op | source)
XLA Modules:
  0.0 60.6 jit_solution(17655916264898905659)
XLA Ops:
  0.6 0.0 copy-start.6
  0.6 5.1 %shard_map.95 = (f32[8,5,5,16,128]{4,3,2,1,0:T(8,128)S(1)}, f32[8,5,5,16,128]{4,3,2,1,0:T(8,128)S(1)}, f32[3,5,5,16,128]{4,3,2,1,0:T(8,128)}, f32[16,128]{1,0:T(8,128)S(1)}, f32[2,8,16,128]{3,2,1,0:T(8,128)S(1)}) custom-call(s32[8]{0:T(128)} %depth_hbm.1, s32[8]{0:T(128)} %east_hbm.1, f32[8,5,5,16,128]{4,3,2,1,0:T(8,128)} %bitcast.8, ...), custom_call_target="tpu_custom_call" | custom-call | flops 5000000000 | bytes 5000000 | tf_op jit(solution)/shard_map/pallas_call | solution.py:25
  5.8 0.0 copy-start.11
  5.8 0.6 %copy-done.11 = f32[2,8,16,128]{3,2,1,0:T(8,128)} copy-done((f32[2,8,16,128]{3,2,1,0:T(8,128)}, f32[2,8,16,128]{3,2,1,0:T(8,128)S(1)}, u32[]{:S(2)}) %copy-start.11) | copy-done | bytes 131096
  6.4 0.5 collective-permute-start.1
  6.9 0.0 copy-done.6
  6.9 1.9 %shard_map.96 = (f32[8,16,128]{2,1,0:T(8,128)}, f32[5,16,128]{2,1,0:T(8,128)}) custom-call(f32[3,5,5,16,128]{4,3,2,1,0:T(8,128)} %get-tuple-element.22.mats_ref.mine_ref, f32[8,5,16,128]{3,2,1,0:T(8,128)S(1)} %bitcast.17), custom_call_target="tpu_custom_call" | custom-call | flops 20000000000 | bytes 20000000 | tf_op jit(solution)/shard_map/pallas_call | solution.py:25
  8.7 6.8 %all-to-all-start = ((f32[8,16,128]{2,1,0:T(8,128)}), f32[8,16,128]{2,1,0:T(8,128)S(1)}, u32[]{:S(2)}, u32[]{:S(2)}) async-start(f32[8,16,128]{2,1,0:T(8,128)} %get-tuple-element.24), calls=%async_computation | async-start | bytes 131072 | tf_op jit(solution)/shard_map/all_to_all | solution.py:449
  15.6 1.3 %collective-permute-start = (f32[5,16,128]{2,1,0:T(8,128)}, f32[5,16,128]{2,1,0:T(8,128)S(1)}, u32[]{:S(2)}, u32[]{:S(2)}) collective-permute-start(f32[5,16,128]{2,1,0:T(8,128)} %get-tuple-element.23), channel_id=1, source_target_pairs={{1,0},{2,1},{3,2},{0,3},{5,4},{6,5},{7,6},{4,7},{9,8},{10,9},{11,1... | collective-permute-start | bytes 122888 | tf_op jit(solution)/shard_map/ppermute | solution.py:461
  16.9 0.0 collective-permute-done.1.other_ref.mats_other_ref
  16.9 1.4 %shard_map.97.beta_ref = f32[5,5,16,128]{3,2,1,0:T(8,128)S(1)} custom-call(f32[3,5,5,16,128]{4,3,2,1,0:T(8,128)} %get-tuple-element.22.mats_ref.mine_ref, f32[3,5,5,16,128]{4,3,2,1,0:T(8,128)} %collective-permute-done.1.other_ref.mats_other_ref), custom_call_target="tpu_custom_call" | custom-call | flops 100000 | bytes 100 | tf_op jit(solution)/shard_map/pallas_call | solution.py:25
  18.3 0.6 collective-permute-done.above_ref
  18.9 0.0 copy-start.14
  18.9 0.6 %copy-done.14 = f32[5,16,128]{2,1,0:T(8,128)} copy-done((f32[5,16,128]{2,1,0:T(8,128)}, f32[5,16,128]{2,1,0:T(8,128)S(1)}, u32[]{:S(2)}) %copy-start.14) | copy-done | bytes 40984
  19.5 3.0 %all-to-all-done.tiles_ref = f32[8,16,128]{2,1,0:T(8,128)S(1)} async-done(((f32[8,16,128]{2,1,0:T(8,128)}), f32[8,16,128]{2,1,0:T(8,128)S(1)}, u32[]{:S(2)}, u32[]{:S(2)}) %all-to-all-start) | async-done | bytes 65568 | tf_op jit(solution)/shard_map/all_to_all | solution.py:449
  22.5 0.0 copy-start
  22.5 1.4 %copy-done = f32[1,8,5,5,16,128]{5,4,3,2,1,0:T(8,128)S(1)} copy-done((f32[1,8,5,5,16,128]{5,4,3,2,1,0:T(8,128)S(1)}, f32[1,8,5,5,16,128]{5,4,3,2,1,0:T(8,128)}, u32[]{:S(2)}) %copy-start) | copy-done | bytes 1638424
  23.9 0.0 copy-start.2
  23.9 1.4 %copy-done.2 = f32[1,8,5,5,16,128]{5,4,3,2,1,0:T(8,128)S(1)} copy-done((f32[1,8,5,5,16,128]{5,4,3,2,1,0:T(8,128)S(1)}, f32[1,8,5,5,16,128]{5,4,3,2,1,0:T(8,128)}, u32[]{:S(2)}) %copy-start.2) | copy-done | bytes 1638424
  25.3 0.0 copy-start.7
  25.3 1.0 %copy-done.7 = f32[1,8,5,16,128]{4,3,2,1,0:T(8,128)S(1)} copy-done((f32[1,8,5,16,128]{4,3,2,1,0:T(8,128)S(1)}, f32[1,8,5,16,128]{4,3,2,1,0:T(8,128)}, u32[]{:S(2)}) %copy-start.7) | copy-done | bytes 327704
  26.3 0.0 copy-start.9
  26.3 1.0 %copy-done.9 = f32[1,8,5,16,128]{4,3,2,1,0:T(8,128)S(1)} copy-done((f32[1,8,5,16,128]{4,3,2,1,0:T(8,128)S(1)}, f32[1,8,5,16,128]{4,3,2,1,0:T(8,128)}, u32[]{:S(2)}) %copy-start.9) | copy-done | bytes 327704
  27.3 0.0 copy-start.12
  27.3 0.9 %copy-done.12 = f32[2,8,16,128]{3,2,1,0:T(8,128)S(1)} copy-done((f32[2,8,16,128]{3,2,1,0:T(8,128)S(1)}, f32[2,8,16,128]{3,2,1,0:T(8,128)}, u32[]{:S(2)}) %copy-start.12) | copy-done | bytes 131096
  28.2 0.0 copy-start.15
  28.2 0.8 %copy-done.15 = f32[5,16,128]{2,1,0:T(8,128)S(1)} copy-done((f32[5,16,128]{2,1,0:T(8,128)S(1)}, f32[5,16,128]{2,1,0:T(8,128)}, u32[]{:S(2)}) %copy-start.15) | copy-done | bytes 40984
  29.0 0.9 %shard_map.98 = (f32[8,5,16,128]{3,2,1,0:T(8,128)S(1)}, f32[2,5,16,128]{3,2,1,0:T(8,128)S(1)}) custom-call(f32[5,5,16,128]{3,2,1,0:T(8,128)S(1)} %shard_map.97.beta_ref, f32[16,128]{1,0:T(8,128)S(1)} %get-tuple-element.20.live_ref, f32[2,8,16,128]{3,2,1,0:T(8,128)S(1)} %copy-done.12, f32[8,16,128]{2,1,0:T(8,128)S(1)} %all-to-all-done.tiles_ref, ...), custom_call_target="tpu_custom_call" | custom-call | flops 1000000000 | bytes 1000000 | tf_op jit(solution)/shard_map/pallas_call | solution.py:25
  29.9 0.0 copy-start.8
  29.9 0.0 copy-start.16
  29.9 0.1 collective-permute-start.2
  30.0 1.6 %collective-permute-start.4 = (f32[5,5,16,128]{3,2,1,0:T(8,128)S(1)}, f32[5,5,16,128]{3,2,1,0:T(8,128)S(1)}, u32[]{:S(2)}, u32[]{:S(2)}) collective-permute-start(f32[5,5,16,128]{3,2,1,0:T(8,128)S(1)} %shard_map.97.beta_ref), channel_id=1, source_target_pairs={{0,2},{1,3},{2,0},{3,1},{4,6},{5,7},{6,4},{7,5},{8,10},{9,11},{10,... | collective-permute-start | bytes 614408 | tf_op jit(solution)/shard_map/ppermute | solution.py:446
  31.5 0.0 collective-permute-done.2.ends_other_ref
  31.5 0.0 copy-start.5
  31.5 1.4 %shard_map.99.pair_ref = f32[1,5,16,128]{3,2,1,0:T(8,128)S(1)} custom-call(f32[2,5,16,128]{3,2,1,0:T(8,128)S(1)} %get-tuple-element.28.ends_ref, f32[2,5,16,128]{3,2,1,0:T(8,128)S(1)} %collective-permute-done.2.ends_other_ref, f32[3,5,5,16,128]{4,3,2,1,0:T(8,128)} %get-tuple-element.22.mats_ref.mine_ref, ...), custom_call_target="tpu_custom_call" | custom-call | flops 1000000000 | bytes 1000000 | tf_op jit(solution)/shard_map/pallas_call | solution.py:25
  33.0 1.3 %collective-permute-start.3 = (f32[1,5,16,128]{3,2,1,0:T(8,128)S(1)}, f32[1,5,16,128]{3,2,1,0:T(8,128)S(1)}, u32[]{:S(2)}, u32[]{:S(2)}) collective-permute-start(f32[1,5,16,128]{3,2,1,0:T(8,128)S(1)} %shard_map.99.pair_ref), channel_id=1, source_target_pairs={{0,2},{1,3},{2,0},{3,1},{4,6},{5,7},{6,4},{7,5},{8,10},{9,11},{10,... | collective-permute-start | bytes 122888 | tf_op jit(solution)/shard_map/ppermute | solution.py:446
  34.2 4.1 %collective-permute-done.3.pair_other_ref = f32[1,5,16,128]{3,2,1,0:T(8,128)S(1)} collective-permute-done((f32[1,5,16,128]{3,2,1,0:T(8,128)S(1)}, f32[1,5,16,128]{3,2,1,0:T(8,128)S(1)}, u32[]{:S(2)}, u32[]{:S(2)}) %collective-permute-start.3) | collective-permute-done | bytes 40992 | tf_op jit(solution)/shard_map/ppermute | solution.py:446
  38.4 0.0 collective-permute-done.4.beta_ref
  38.4 0.0 copy-done.8
  38.4 0.0 copy-done.16
  38.4 0.0 copy-start.1
  38.4 0.0 copy-start.3
  38.4 0.0 copy-start.4
  38.4 0.0 copy-start.10
  38.4 0.0 copy-start.13
  38.4 1.9 %shard_map.100 = (f32[8,5,16,128]{3,2,1,0:T(8,128)S(1)}, f32[5,16,128]{2,1,0:T(8,128)S(1)}, f32[8,16,128]{2,1,0:T(8,128)S(1)}) custom-call(f32[16,128]{1,0:T(8,128)S(1)} %get-tuple-element.20.live_ref, f32[8,5,16,128]{3,2,1,0:T(8,128)S(1)} %bitcast.19, f32[5,16,128]{2,1,0:T(8,128)S(1)} %copy-done.16, f32[8,5,16,128]{3,2,1,0:T(8,128)S(1)} %get-tuple-element.27.s_ref, ...), custom_call_target="tpu_custom_call" | custom-call | flops 1000000000 | bytes 1000000 | tf_op jit(solution)/shard_map/pallas_call | solution.py:25
  40.3 9.7 %all_to_all.10.tiles_ref = f32[8,16,128]{2,1,0:T(8,128)S(1)} all-to-all(f32[8,16,128]{2,1,0:T(8,128)S(1)} %get-tuple-element.29), channel_id=1, replica_groups=mesh['zone'=8,'ja'=4] {'zone'}, dimensions={0} | all-to-all | bytes 131072 | tf_op jit(solution)/shard_map/all_to_all | solution.py:449
  50.0 0.0 copy-done.5
  50.0 0.0 copy-done.1
  50.0 0.0 copy-done.3
  50.0 0.0 copy-done.4
  50.0 0.0 copy-done.10
  50.0 0.0 copy-done.13
  50.0 1.0 %shard_map.101 = (f32[8,5,16,128]{3,2,1,0:T(8,128)S(1)}, f32[8,5,16,128]{3,2,1,0:T(8,128)S(1)}, f32[3,5,16,128]{3,2,1,0:T(8,128)S(1)}, f32[5,5,16,128]{3,2,1,0:T(8,128)S(1)}) custom-call(f32[16,128]{1,0:T(8,128)S(1)} %get-tuple-element.20.live_ref, f32[2,8,16,128]{3,2,1,0:T(8,128)S(1)} %copy-done.13, f32[8,16,128]{2,1,0:T(8,128)S(1)} %all_to_all.10.tiles_ref, ...), custom_call_target="tpu_custom_call" | custom-call | flops 1000000000 | bytes 1000000 | tf_op jit(solution)/shard_map/pallas_call | solution.py:25
  51.1 0.1 collective-permute-start.5
  51.1 1.3 %collective-permute-done.5.ends_other_ref = f32[3,5,16,128]{3,2,1,0:T(8,128)S(1)} collective-permute-done((f32[3,5,16,128]{3,2,1,0:T(8,128)S(1)}, f32[3,5,16,128]{3,2,1,0:T(8,128)S(1)}, u32[]{:S(2)}, u32[]{:S(2)}) %collective-permute-start.5) | collective-permute-done | bytes 122912 | tf_op jit(solution)/shard_map/ppermute | solution.py:446
  52.5 1.3 %shard_map.102.pair_ref = f32[2,5,16,128]{3,2,1,0:T(8,128)S(1)} custom-call(f32[3,5,16,128]{3,2,1,0:T(8,128)S(1)} %get-tuple-element.35.ends_ref, f32[3,5,16,128]{3,2,1,0:T(8,128)S(1)} %collective-permute-done.5.ends_other_ref, f32[3,5,5,16,128]{4,3,2,1,0:T(8,128)} %get-tuple-element.22.mats_ref.mine_ref, ...), custom_call_target="tpu_custom_call" | custom-call | flops 1000000000 | bytes 1000000 | tf_op jit(solution)/shard_map/pallas_call | solution.py:25
  53.8 1.5 %collective-permute-start.6 = (f32[2,5,16,128]{3,2,1,0:T(8,128)S(1)}, f32[2,5,16,128]{3,2,1,0:T(8,128)S(1)}, u32[]{:S(2)}, u32[]{:S(2)}) collective-permute-start(f32[2,5,16,128]{3,2,1,0:T(8,128)S(1)} %shard_map.102.pair_ref), channel_id=1, source_target_pairs={{0,2},{1,3},{2,0},{3,1},{4,6},{5,7},{6,4},{7,5},{8,10},{9,11},{10,... | collective-permute-start | bytes 245768 | tf_op jit(solution)/shard_map/ppermute | solution.py:446
  55.3 0.7 %shard_map.103.res_in_hbm = f32[8,5,16,128]{3,2,1,0:T(8,128)} custom-call(f32[8,5,16,128]{3,2,1,0:T(8,128)S(1)} %get-tuple-element.33.res_ref), custom_call_target="tpu_custom_call" | custom-call | flops 1000000000 | bytes 1000000 | tf_op jit(solution)/shard_map/pallas_call | solution.py:25
  56.0 2.3 %collective-permute-done.6.pair_other_ref = f32[2,5,16,128]{3,2,1,0:T(8,128)S(1)} collective-permute-done((f32[2,5,16,128]{3,2,1,0:T(8,128)S(1)}, f32[2,5,16,128]{3,2,1,0:T(8,128)S(1)}, u32[]{:S(2)}, u32[]{:S(2)}) %collective-permute-start.6) | collective-permute-done | bytes 81952 | tf_op jit(solution)/shard_map/ppermute | solution.py:446
  58.3 2.3 %shard_map.104 = (f32[8,5,16,128]{3,2,1,0:T(8,128)}, f32[8,5,16,128]{3,2,1,0:T(8,128)}) custom-call(f32[16,128]{1,0:T(8,128)S(1)} %get-tuple-element.20.live_ref, f32[5,5,16,128]{3,2,1,0:T(8,128)S(1)} %get-tuple-element.32.low0_ref, f32[8,5,16,128]{3,2,1,0:T(8,128)S(1)} %get-tuple-element.30.cur_ref, ...), custom_call_target="tpu_custom_call", output_to_operand_aliasing={{1}: (14, {})} | custom-call | flops 1000000000 | bytes 1000000 | tf_op jit(solution)/shard_map/pallas_call | solution.py:25
Async XLA Ops:
  0.6 6.3 %copy-start.6 = (f32[1,8,5,16,128]{4,3,2,1,0:T(8,128)S(1)}, f32[1,8,5,16,128]{4,3,2,1,0:T(8,128)}, u32[]{:S(2)}) copy-start(f32[1,8,5,16,128]{4,3,2,1,0:T(8,128)} %param.8) | copy-start | bytes 983044
  5.8 0.7 %copy-start.11 = (f32[2,8,16,128]{3,2,1,0:T(8,128)}, f32[2,8,16,128]{3,2,1,0:T(8,128)S(1)}, u32[]{:S(2)}) copy-start(f32[2,8,16,128]{3,2,1,0:T(8,128)S(1)} %get-tuple-element.21.pick_ref) | copy-start | bytes 393220
  6.4 10.5 %collective-permute-start.1 = (f32[3,5,5,16,128]{4,3,2,1,0:T(8,128)}, f32[3,5,5,16,128]{4,3,2,1,0:T(8,128)}, u32[]{:S(2)}, u32[]{:S(2)}) collective-permute-start(f32[3,5,5,16,128]{4,3,2,1,0:T(8,128)} %get-tuple-element.22.mats_ref.mine_ref), channel_id=1, source_target_pairs={{0,1},{1,0},{2,3},{3,2},{4,5},{5,4},{6,7},{7,6},{8,9},{9,8},{10,11... | collective-permute-start | bytes 1843208 | tf_op jit(solution)/shard_map/ppermute | solution.py:446
  8.7 13.7 %all-to-all-start = ((f32[8,16,128]{2,1,0:T(8,128)}), f32[8,16,128]{2,1,0:T(8,128)S(1)}, u32[]{:S(2)}, u32[]{:S(2)}) async-start(f32[8,16,128]{2,1,0:T(8,128)} %get-tuple-element.24), calls=%async_computation | async-start | bytes 131072 | tf_op jit(solution)/shard_map/all_to_all | solution.py:449
  15.6 3.3 %collective-permute-start = (f32[5,16,128]{2,1,0:T(8,128)}, f32[5,16,128]{2,1,0:T(8,128)S(1)}, u32[]{:S(2)}, u32[]{:S(2)}) collective-permute-start(f32[5,16,128]{2,1,0:T(8,128)} %get-tuple-element.23), channel_id=1, source_target_pairs={{1,0},{2,1},{3,2},{0,3},{5,4},{6,5},{7,6},{4,7},{9,8},{10,9},{11,1... | collective-permute-start | bytes 122888 | tf_op jit(solution)/shard_map/ppermute | solution.py:461
  18.9 0.6 %copy-start.14 = (f32[5,16,128]{2,1,0:T(8,128)}, f32[5,16,128]{2,1,0:T(8,128)S(1)}, u32[]{:S(2)}) copy-start(f32[5,16,128]{2,1,0:T(8,128)S(1)} %collective-permute-done.above_ref) | copy-start | bytes 122884
  22.5 1.4 %copy-start = (f32[1,8,5,5,16,128]{5,4,3,2,1,0:T(8,128)S(1)}, f32[1,8,5,5,16,128]{5,4,3,2,1,0:T(8,128)}, u32[]{:S(2)}) copy-start(f32[1,8,5,5,16,128]{5,4,3,2,1,0:T(8,128)} %param.13) | copy-start | bytes 4915204
  23.9 1.4 %copy-start.2 = (f32[1,8,5,5,16,128]{5,4,3,2,1,0:T(8,128)S(1)}, f32[1,8,5,5,16,128]{5,4,3,2,1,0:T(8,128)}, u32[]{:S(2)}) copy-start(f32[1,8,5,5,16,128]{5,4,3,2,1,0:T(8,128)} %param.10) | copy-start | bytes 4915204
  25.3 1.0 %copy-start.7 = (f32[1,8,5,16,128]{4,3,2,1,0:T(8,128)S(1)}, f32[1,8,5,16,128]{4,3,2,1,0:T(8,128)}, u32[]{:S(2)}) copy-start(f32[1,8,5,16,128]{4,3,2,1,0:T(8,128)} %param.8) | copy-start | bytes 983044
  26.3 1.0 %copy-start.9 = (f32[1,8,5,16,128]{4,3,2,1,0:T(8,128)S(1)}, f32[1,8,5,16,128]{4,3,2,1,0:T(8,128)}, u32[]{:S(2)}) copy-start(f32[1,8,5,16,128]{4,3,2,1,0:T(8,128)} %param.9) | copy-start | bytes 983044
  27.3 0.9 %copy-start.12 = (f32[2,8,16,128]{3,2,1,0:T(8,128)S(1)}, f32[2,8,16,128]{3,2,1,0:T(8,128)}, u32[]{:S(2)}) copy-start(f32[2,8,16,128]{3,2,1,0:T(8,128)} %copy-done.11) | copy-start | bytes 393220
  28.2 0.8 %copy-start.15 = (f32[5,16,128]{2,1,0:T(8,128)S(1)}, f32[5,16,128]{2,1,0:T(8,128)}, u32[]{:S(2)}) copy-start(f32[5,16,128]{2,1,0:T(8,128)} %copy-done.14) | copy-start | bytes 122884
  29.9 8.5 %copy-start.8 = (f32[1,8,5,16,128]{4,3,2,1,0:T(8,128)S(1)}, f32[1,8,5,16,128]{4,3,2,1,0:T(8,128)}, u32[]{:S(2)}) copy-start(f32[1,8,5,16,128]{4,3,2,1,0:T(8,128)} %param.8) | copy-start | bytes 983044
  29.9 8.5 %copy-start.16 = (f32[5,16,128]{2,1,0:T(8,128)S(1)}, f32[5,16,128]{2,1,0:T(8,128)}, u32[]{:S(2)}) copy-start(f32[5,16,128]{2,1,0:T(8,128)} %copy-done.14) | copy-start | bytes 122884
  29.9 1.6 %collective-permute-start.2 = (f32[2,5,16,128]{3,2,1,0:T(8,128)S(1)}, f32[2,5,16,128]{3,2,1,0:T(8,128)S(1)}, u32[]{:S(2)}, u32[]{:S(2)}) collective-permute-start(f32[2,5,16,128]{3,2,1,0:T(8,128)S(1)} %get-tuple-element.28.ends_ref), channel_id=1, source_target_pairs={{0,1},{1,0},{2,3},{3,2},{4,5},{5,4},{6,7},{7,6},{8,9},{9,8},{10,11... | collective-permute-start | bytes 245768 | tf_op jit(solution)/shard_map/ppermute | solution.py:446
  30.0 8.4 %collective-permute-start.4 = (f32[5,5,16,128]{3,2,1,0:T(8,128)S(1)}, f32[5,5,16,128]{3,2,1,0:T(8,128)S(1)}, u32[]{:S(2)}, u32[]{:S(2)}) collective-permute-start(f32[5,5,16,128]{3,2,1,0:T(8,128)S(1)} %shard_map.97.beta_ref), channel_id=1, source_target_pairs={{0,2},{1,3},{2,0},{3,1},{4,6},{5,7},{6,4},{7,5},{8,10},{9,11},{10,... | collective-permute-start | bytes 614408 | tf_op jit(solution)/shard_map/ppermute | solution.py:446
  31.5 18.4 %copy-start.5 = (f32[1,8,5,5,16,128]{5,4,3,2,1,0:T(8,128)S(1)}, f32[1,8,5,5,16,128]{5,4,3,2,1,0:T(8,128)}, u32[]{:S(2)}) copy-start(f32[1,8,5,5,16,128]{5,4,3,2,1,0:T(8,128)} %param.12) | copy-start | bytes 4915204
  33.0 5.4 %collective-permute-start.3 = (f32[1,5,16,128]{3,2,1,0:T(8,128)S(1)}, f32[1,5,16,128]{3,2,1,0:T(8,128)S(1)}, u32[]{:S(2)}, u32[]{:S(2)}) collective-permute-start(f32[1,5,16,128]{3,2,1,0:T(8,128)S(1)} %shard_map.99.pair_ref), channel_id=1, source_target_pairs={{0,2},{1,3},{2,0},{3,1},{4,6},{5,7},{6,4},{7,5},{8,10},{9,11},{10,... | collective-permute-start | bytes 122888 | tf_op jit(solution)/shard_map/ppermute | solution.py:446
  38.4 11.6 %copy-start.1 = (f32[1,8,5,5,16,128]{5,4,3,2,1,0:T(8,128)S(1)}, f32[1,8,5,5,16,128]{5,4,3,2,1,0:T(8,128)}, u32[]{:S(2)}) copy-start(f32[1,8,5,5,16,128]{5,4,3,2,1,0:T(8,128)} %param.13) | copy-start | bytes 4915204
  38.4 11.6 %copy-start.3 = (f32[1,8,5,5,16,128]{5,4,3,2,1,0:T(8,128)S(1)}, f32[1,8,5,5,16,128]{5,4,3,2,1,0:T(8,128)}, u32[]{:S(2)}) copy-start(f32[1,8,5,5,16,128]{5,4,3,2,1,0:T(8,128)} %param.10) | copy-start | bytes 4915204
  38.4 11.6 %copy-start.4 = (f32[1,8,5,5,16,128]{5,4,3,2,1,0:T(8,128)S(1)}, f32[1,8,5,5,16,128]{5,4,3,2,1,0:T(8,128)}, u32[]{:S(2)}) copy-start(f32[1,8,5,5,16,128]{5,4,3,2,1,0:T(8,128)} %param.11) | copy-start | bytes 4915204
  38.4 11.6 %copy-start.10 = (f32[1,8,5,16,128]{4,3,2,1,0:T(8,128)S(1)}, f32[1,8,5,16,128]{4,3,2,1,0:T(8,128)}, u32[]{:S(2)}) copy-start(f32[1,8,5,16,128]{4,3,2,1,0:T(8,128)} %param.9) | copy-start | bytes 983044
  38.4 11.6 %copy-start.13 = (f32[2,8,16,128]{3,2,1,0:T(8,128)S(1)}, f32[2,8,16,128]{3,2,1,0:T(8,128)}, u32[]{:S(2)}) copy-start(f32[2,8,16,128]{3,2,1,0:T(8,128)} %copy-done.11) | copy-start | bytes 393220
  51.1 1.4 %collective-permute-start.5 = (f32[3,5,16,128]{3,2,1,0:T(8,128)S(1)}, f32[3,5,16,128]{3,2,1,0:T(8,128)S(1)}, u32[]{:S(2)}, u32[]{:S(2)}) collective-permute-start(f32[3,5,16,128]{3,2,1,0:T(8,128)S(1)} %get-tuple-element.35.ends_ref), channel_id=1, source_target_pairs={{0,1},{1,0},{2,3},{3,2},{4,5},{5,4},{6,7},{7,6},{8,9},{9,8},{10,11... | collective-permute-start | bytes 368648 | tf_op jit(solution)/shard_map/ppermute | solution.py:446
  53.8 4.6 %collective-permute-start.6 = (f32[2,5,16,128]{3,2,1,0:T(8,128)S(1)}, f32[2,5,16,128]{3,2,1,0:T(8,128)S(1)}, u32[]{:S(2)}, u32[]{:S(2)}) collective-permute-start(f32[2,5,16,128]{3,2,1,0:T(8,128)S(1)} %shard_map.102.pair_ref), channel_id=1, source_target_pairs={{0,2},{1,3},{2,0},{3,1},{4,6},{5,7},{6,4},{7,5},{8,10},{9,11},{10,... | collective-permute-start | bytes 245768 | tf_op jit(solution)/shard_map/ppermute | solution.py:446

commit v5 on v4

--- a/solution.py
+++ b/solution.py
@@ -10,7 +10,6 @@
 COUPLE = 0.25
 
 VMEM = pl.BlockSpec(memory_space=pltpu.VMEM)
-ANY = pl.BlockSpec(memory_space=pl.ANY)
 HBM = pl.BlockSpec(memory_space=pltpu.HBM)
 
 
@@ -19,20 +18,24 @@
 
     def run(*arrays):
         arrays = [
-            pltpu.with_memory_space_constraint(a, pltpu.HBM) if i in far else a
+            pltpu.with_memory_space_constraint(a, pltpu.HBM if i in far else pltpu.VMEM)
             for i, a in enumerate(arrays)
         ]
+        specs = out_specs or [VMEM] * len(shapes)
         return pl.pallas_call(
             kernel,
-            out_shape=[jax.ShapeDtypeStruct(s, jnp.float32) for s in shapes],
-            in_specs=[
-                HBM if i in far else ANY if i in alias else VMEM for i in range(len(arrays))
+            out_shape=[
+                pltpu.VMEM(s, jnp.float32) if spec is VMEM else jax.ShapeDtypeStruct(s, jnp.float32)
+                for s, spec in zip(shapes, specs)
             ],
-            out_specs=out_specs or [VMEM] * len(shapes),
+            in_specs=[HBM if i in far else VMEM for i in range(len(arrays))],
+            out_specs=specs,
             scratch_shapes=list(scratch),
             input_output_aliases=alias,
-            compiler_params=pltpu.CompilerParams(vmem_limit_bytes=12 * 2**20),
-            cost_estimate=pl.CostEstimate(flops=flops, bytes_accessed=flops // 10**3, transcendentals=0),
+            compiler_params=pltpu.CompilerParams(vmem_limit_bytes=8 * 2**20),
+            cost_estimate=pl.CostEstimate(
+                flops=flops, bytes_accessed=flops // 10**3, transcendentals=0
+            ),
         )(*arrays)
 
     return run
@@ -97,10 +100,23 @@
     return [jnp.where(inner, x, 0.0) for x in values]
 
 
-def pack_kernel(mats_ref, flow_ref, tile_ref, first_ref):
-    del mats_ref
-    put(first_ref, cell(flow_ref, 0))
-    pack_faces(lambda j, v: flow_ref[j, v], flow_ref.shape[0], tile_ref)
+def pack_kernel(live_ref, flow_ref, tile_ref, cur_ref, first_ref):
+    planes = flow_ref.shape[0]
+    for j in range(planes):
+        put(cur_ref, masked(live_ref, cell(flow_ref, j)), j)
+    put(first_ref, masked(live_ref, cell(flow_ref, 0)))
+    pack_faces(lambda j, v: cur_ref[j, v], planes, tile_ref)
+
+
+def load_kernel(diag_hbm, force_hbm, diag_ref, force_ref, sems):
+    copies = [
+        pltpu.make_async_copy(diag_hbm, diag_ref, sems.at[0]),
+        pltpu.make_async_copy(force_hbm, force_ref, sems.at[1]),
+    ]
+    for copy in copies:
+        copy.start()
+    for copy in copies:
+        copy.wait()
 
 
 def neighbours(x):
@@ -128,8 +144,8 @@
 
 def matrix_kernel(
     depth_hbm, east_hbm, inv_hbm, low_hbm, up_hbm,
-    e_ref, f_ref, mats_ref, live_ref, pick_ref,
-    inv_ref, low_ref, up_ref, y_ref, depth_ref, east_ref, sems, small_sems,
+    inv_ref, low_ref, up_ref, e_ref, f_ref, mats_ref, live_ref, pick_ref,
+    y_ref, depth_ref, east_ref, sems, small_sems,
 ):
     planes = inv_ref.shape[0]
 
@@ -210,9 +226,8 @@
     row = iota(0)
     live_ref[...] = jnp.where(row < depth_ref[zone], 1.0, 0.0)
     for w in range(pick_ref.shape[1]):
-        rows = row < depth_ref[w]
-        pick_ref[0, w] = jnp.where(rows & (east_ref[w] == zone), 1.0, 0.0)
-        pick_ref[1, w] = jnp.where(rows & (east_ref[zone] == w), 1.0, 0.0)
+        pick_ref[0, w] = jnp.where((row >= 0) & (east_ref[w] == zone), 1.0, 0.0)
+        pick_ref[1, w] = jnp.where((row >= 0) & (east_ref[zone] == w), 1.0, 0.0)
 
 
 def by_place(mine_refs, other_refs, run):
@@ -227,17 +242,22 @@
         run(*other_refs, *mine_refs)
 
 
-def beta_kernel(mine_ref, other_ref, beta_ref):
-    def run(lo, hi):
-        d_hi, n_lo = block(hi, 1), block(lo, 2)
-        for q in range(5):
-            m_col = [lo[0, r, q] for r in range(5)]
-            d_col = [lo[1, r, q] for r in range(5)]
-            out = add(d_col, matvec(n_lo, matvec(d_hi, m_col)))
-            for r in range(5):
-                beta_ref[r, q] = out[r]
-
-    by_place([mine_ref], [other_ref], run)
+def beta_kernel(mine_ref, other_ref, half_ref):
+    odd = lax.axis_index("ja") % 2
+    for side in range(2):
+        lo, hi = (mine_ref, other_ref) if side == 0 else (other_ref, mine_ref)
+        rows = pl.ds(8 * side, 8)
+
+        @pl.when(odd == side)
+        def _():
+            d_hi = [[hi[1, r, c, rows] for c in range(5)] for r in range(5)]
+            n_lo = [[lo[2, r, c, rows] for c in range(5)] for r in range(5)]
+            for q in range(5):
+                m_col = [lo[0, r, q, rows] for r in range(5)]
+                d_col = [lo[1, r, q, rows] for r in range(5)]
+                out = add(d_col, matvec(n_lo, matvec(d_hi, m_col)))
+                for r in range(5):
+                    half_ref[r, q] = out[r]
 
 
 def sweeps(s_ref, e_ref, f_ref, y_ref, ends_ref, last):
@@ -254,17 +274,17 @@
 
 
 def local_kernel(
-    beta_ref, live_ref, pick_ref, tiles_ref, cur_ref, above_ref, force_ref, diag_ref, inv_ref,
+    half_ref, live_ref, pick_ref, tiles_ref, cur_ref, above_ref, force_ref, diag_ref, inv_ref,
     e_ref, f_ref,
-    s_ref, ends_ref, y_ref,
-):
-    del beta_ref
+    s_ref, ends_ref, half_out_ref, y_ref,
+):
+    for r in range(5):
+        put(half_out_ref, cell(half_ref, r), r)
     planes = cur_ref.shape[0]
     ghosts = ghosts_of(pick_ref, tiles_ref)
-    before, here = None, masked(live_ref, cell(cur_ref, 0))
+    before, here = None, cell(cur_ref, 0)
     for j in range(planes):
         after = cell(cur_ref, j + 1) if j < planes - 1 else has_above(cell(above_ref))
-        after = masked(live_ref, after)
         own = matvec(block(diag_ref, j), here)
         res = []
         for v in range(5):
@@ -276,18 +296,14 @@
         linked = [x * (1.0 / OMEGA) for x in linked]
         put(s_ref, add(matvec(block(inv_ref, j), masked(live_ref, res)), linked), j)
         before, here = here, after
-    sweeps(s_ref, e_ref, f_ref, y_ref, ends_ref, masked(live_ref, cell(cur_ref, planes - 1)))
-
-
-def second_kernel(
-    live_ref, pick_ref, tiles_ref, cur_ref, above_ref, force_ref, diag_ref, low_ref, up_ref,
-    inv_ref, e_ref, f_ref,
-    res_ref, s_ref, ends_ref, low0_ref, y_ref,
+    sweeps(s_ref, e_ref, f_ref, y_ref, ends_ref, cell(cur_ref, planes - 1))
+
+
+def residual_kernel(
+    live_ref, cur_ref, above_ref, force_ref, diag_ref, low_ref, up_ref, inv_ref,
+    res_ref, s_ref,
 ):
     planes = cur_ref.shape[0]
-    ghosts = ghosts_of(pick_ref, tiles_ref)
-    for r in range(5):
-        put(low0_ref, cell(low_ref, 0, r), r)
     for j in range(planes):
         here = cell(cur_ref, j)
         applied = matvec(block(diag_ref, j), here)
@@ -298,12 +314,23 @@
         upper = matvec(block(up_ref, j), above)
         res = []
         for v in range(5):
-            sides = neighbours(here[v]) + ghost_at(ghosts, j, v)
-            all_of = applied[v] - upper[v] - COUPLE * sides
+            all_of = applied[v] - upper[v] - COUPLE * neighbours(here[v])
             res.append(force_ref[j, v] - all_of)
         res = masked(live_ref, res)
         put(res_ref, res, j)
         put(s_ref, matvec(block(inv_ref, j), res), j)
+
+
+def ghost_kernel(
+    live_ref, pick_ref, tiles_ref, cur_ref, res0_ref, s0_ref, inv_ref, e_ref, f_ref,
+    res_ref, s_ref, ends_ref, y_ref,
+):
+    planes = cur_ref.shape[0]
+    ghosts = jnp.where(live_ref[...] > 0.0, COUPLE * ghosts_of(pick_ref, tiles_ref), 0.0)
+    for j in range(planes):
+        extra = [ghost_at(ghosts, j, v) for v in range(5)]
+        put(res_ref, add(cell(res0_ref, j), extra), j)
+        put(s_ref, add(cell(s0_ref, j), matvec(block(inv_ref, j), extra)), j)
     last = cell(cur_ref, planes - 1)
     sweeps(s_ref, e_ref, f_ref, y_ref, ends_ref, last)
     put(ends_ref, last, 2)
@@ -336,25 +363,29 @@
 
 def inflows(
     ends_ref, ends_other_ref, mats_ref, mats_other_ref, pair_ref, pair_other_ref,
-    beta_ref, inflow_ref,
+    half_ref, half_other_ref, inflow_ref,
 ):
     ja = lax.axis_index("ja")
     zeros = [jnp.zeros((16, 128), jnp.float32)] * 5
 
-    def far():
-        return add(cell(pair_other_ref, 0), matvec(block(beta_ref), cell(pair_ref, 0)))
+    def far(top_ref, bottom_ref):
+        beta = [
+            [jnp.concatenate([top_ref[r, c], bottom_ref[r, c]], axis=0) for c in range(5)]
+            for r in range(5)
+        ]
+        return add(cell(pair_other_ref, 0), matvec(beta, cell(pair_ref, 0)))
 
     @pl.when(ja == 0)
     def _():
         put(inflow_ref, zeros, 0)
         b = add(cell(ends_other_ref, 1), matvec(block(mats_other_ref, 1), cell(ends_ref, 0)))
-        b = add(b, matvec(block(mats_other_ref, 2), far()))
+        b = add(b, matvec(block(mats_other_ref, 2), far(half_ref, half_other_ref)))
         put(inflow_ref, b, 1)
 
     @pl.when(ja == 1)
     def _():
         put(inflow_ref, cell(ends_other_ref, 0), 0)
-        put(inflow_ref, far(), 1)
+        put(inflow_ref, far(half_other_ref, half_ref), 1)
 
     @pl.when(ja == 2)
     def _():
@@ -372,32 +403,32 @@
 
 
 def final_kernel(
-    live_ref, cur_ref, above_ref, s_ref, e_ref, f_ref,
+    cur_ref, above_ref, s_ref, e_ref, f_ref,
     ends_ref, ends_other_ref, mats_ref, mats_other_ref, pair_ref, pair_other_ref,
-    beta_ref,
+    half_ref, half_other_ref,
     new_ref, above_new_ref, tile_ref, y_ref, inflow_ref,
 ):
     planes = cur_ref.shape[0]
     inflows(
         ends_ref, ends_other_ref, mats_ref, mats_other_ref, pair_ref, pair_other_ref,
-        beta_ref, inflow_ref,
+        half_ref, half_other_ref, inflow_ref,
     )
     value = cell(inflow_ref, 0)
     for j in range(planes):
         value = add(cell(s_ref, j), matvec(block(e_ref, j), value))
         put(y_ref, value, j)
     value = cell(inflow_ref, 1)
-    put(above_new_ref, add(masked(live_ref, has_above(cell(above_ref))), value))
+    put(above_new_ref, add(has_above(cell(above_ref)), value))
     for j in range(planes - 1, -1, -1):
         value = add(cell(y_ref, j), matvec(block(f_ref, j), value))
-        put(new_ref, add(masked(live_ref, cell(cur_ref, j)), value), j)
+        put(new_ref, add(cell(cur_ref, j), value), j)
     pack_faces(lambda j, v: new_ref[j, v], planes, tile_ref)
 
 
 def last_kernel(
-    live_ref, low0_ref, cur_ref, res_ref, s_ref, e_ref, f_ref,
+    live_ref, low_ref, cur_ref, res_ref, s_ref, e_ref, f_ref,
     ends_ref, ends_other_ref, mats_ref, mats_other_ref, pair_ref, pair_other_ref,
-    beta_ref,
+    half_ref, half_other_ref,
     res_in_hbm,
     new_hbm, res_hbm, y_ref, inflow_ref, new_ref, res0_ref, sems,
 ):
@@ -408,12 +439,12 @@
         jnp.where(ja == 0, 0.0, jnp.where(ja == 2, pair_other_ref[1, v], ends_other_ref[2, v]))
         for v in range(5)
     ]
-    put(res0_ref, add(cell(res_ref, 0), masked(live_ref, matvec(block(low0_ref), before))))
+    put(res0_ref, add(cell(res_ref, 0), masked(live_ref, matvec(block(low_ref, 0), before))))
     copies = [pltpu.make_async_copy(res0_ref, res_hbm.at[0], sems.at[planes])]
     copies[0].start()
     inflows(
         ends_ref, ends_other_ref, mats_ref, mats_other_ref, pair_ref, pair_other_ref,
-        beta_ref, inflow_ref,
+        half_ref, half_other_ref, inflow_ref,
     )
     value = cell(inflow_ref, 0)
     for j in range(planes):
@@ -448,38 +479,43 @@
     def faces(x):
         return lax.all_to_all(x, "zone", 0, 0, tiled=True)
 
-    e, f, mats, live, pick = call(
+    inv, low, up, e, f, mats, live, pick = call(
         matrix_kernel,
-        [blocks, blocks, (3, *matrix), state[2:], (2, *tiles)],
-        [buffer(*blocks)] * 4
+        [blocks] * 5 + [(3, *matrix), state[2:], (2, *tiles)],
+        [buffer(*blocks)]
         + [pltpu.SMEM((zones,), jnp.int32)] * 2
         + [pltpu.SemaphoreType.DMA((3, planes)), pltpu.SemaphoreType.DMA((2,))],
         flops=5 * 10**9,
         far=(0, 1, 2, 3, 4),
     )(zone_depth, east_zone, inv, low, up)
-    tile, first = call(pack_kernel, [tiles, plane], flops=2 * 10**10)(mats, current)
+    tile, current, first = call(pack_kernel, [tiles, state, plane])(live, current)
     above = lax.ppermute(first, "ja", [((p + 1) % parts, p) for p in range(parts)])
     mats_other = swap(mats, 1)
     got = faces(tile)
-    beta = call(beta_kernel, [matrix], flops=10**5)(mats, mats_other)[0]
-    s, ends = call(local_kernel, [state, (2, *plane)], work)(
-        beta, live, pick, got, current, above, force, diag, inv, e, f
-    )
-    beta = swap(beta, 2)
+    diag, force = call(
+        load_kernel, [blocks, state], [pltpu.SemaphoreType.DMA((2,))], far=(0, 1)
+    )(diag, force)
+    half = call(beta_kernel, [(*matrix[:2], 8, matrix[3])], flops=10**5)(mats, mats_other)[0]
+    half = swap(half, 2)
+    s, ends, half = call(local_kernel, [state, (2, *plane), half.shape], work)(
+        half, live, pick, got, current, above, force, diag, inv, e, f
+    )
     ends_other = swap(ends, 1)
+    half_other = swap(half, 1)
     pair = call(mid_kernel, [(1, *plane)])(ends, ends_other, mats, mats_other)[0]
     pair_other = swap(pair, 2)
     flows = [buffer(2, *plane)]
     current, above, tile = call(final_kernel, [state, plane, tiles], work + flows)(
-        live, current, above, s, e, f,
-        ends, ends_other, mats, mats_other, pair, pair_other, beta,
+        current, above, s, e, f,
+        ends, ends_other, mats, mats_other, pair, pair_other, half, half_other,
     )
 
     got = faces(tile)
-    residual, s, ends, low0 = call(
-        second_kernel, [state, state, (3, *plane), matrix], work
-    )(
-        live, pick, got, current, above, force, diag, low, up, inv, e, f
+    residual, s = call(residual_kernel, [state, state])(
+        live, current, above, force, diag, low, up, inv
+    )
+    residual, s, ends = call(ghost_kernel, [state, state, (3, *plane)], work)(
+        live, pick, got, current, residual, s, inv, e, f
     )
     ends_other = swap(ends, 1)
     pair = call(mid_kernel, [(2, *plane)])(ends, ends_other, mats, mats_other)[0]
@@ -490,10 +526,11 @@
         [state, state],
         work + flows + work + [buffer(*plane), pltpu.SemaphoreType.DMA((planes + 1,))],
         out_specs=[HBM, HBM],
-        alias={14: 1},
+        far=(15,),
+        alias={15: 1},
     )(
-        live, low0, current, residual, s, e, f,
-        ends, ends_other, mats, mats_other, pair, pair_other, beta, written,
+        live, low, current, residual, s, e, f,
+        ends, ends_other, mats, mats_other, pair, pair_other, half, half_other, written,
     )
     return (current[None], residual[None])
 

time: 61.2 us -> 77.1 us (1.26)
  local copies, waits for them, and re-layouts: 7.81 us -> 28.3 us
  blocking collectives: 9.69 us -> 0 us
  starting transfers between devices: 13.1 us -> 18.6 us
  waiting for transfers between devices: 11.3 us -> 7.37 us
  Pallas kernels: 17.9 us -> 20.9 us
    unnamed x34 -> x78, local copies, waits for them, and re-layouts: 7.81 us -> 28.3 us
    all_to_all x1 -> x0, blocking collectives: 9.69 us -> none  [faces(): return lax.all_to_all(x, 'zone', 0, 0, tiled=True)]
    all_to_all x1 -> x2, starting transfers between devices: 6.83 us -> 13.3 us  [faces(): return lax.all_to_all(x, 'zone', 0, 0, tiled=True)]
    all_to_all x1 -> x2, waiting for transfers between devices: 2.97 us -> 0.02 us  [faces(): return lax.all_to_all(x, 'zone', 0, 0, tiled=True)]
    pallas_call x10 -> x12, Pallas kernels: 17.9 us -> 20.9 us  [run(): pl.pallas_call(kernel, out_shape=[pltpu.VMEM(s, jnp.float32) if spec is V...]
    ppermute x1, starting transfers between devices: 1.32 us -> 0.01 us  [per_device(): lax.ppermute(first, 'ja', [((p + 1) % parts, p) for p in range(parts)])]
    ppermute x6 -> x7, starting transfers between devices: 4.96 us -> 5.35 us  [swap(): return lax.ppermute(x, 'ja', [(p, p ^ bit) for p in range(parts)])]
    ppermute x6 -> x7, waiting for transfers between devices: 7.74 us -> 7.35 us  [swap(): return lax.ppermute(x, 'ja', [(p, p ^ bit) for p in range(parts)])]
  transfers between devices with their start and end apart: 8 -> 10, of which waited for: 5 -> 4; matrix products, arithmetic and copies ran while one was open for 0% -> 0% of each run, Pallas kernels for 9% -> 10%
where the time goes in v5:
time: 77.1 us; the launch traced here: 75.9 us
  local copies, waits for them, and re-layouts  28.3 us (37%)
  Pallas kernels  20.9 us (27%)
  starting transfers between devices  18.6 us (24%)
  waiting for transfers between devices  7.37 us (10%)
  between operations  0.81 us (1%)
    unnamed x78, local copies, waits for them, and re-layouts  28.3 us
    pallas_call x12, Pallas kernels, run(): pl.pallas_call(kernel, out_shape=[pltpu.VMEM(s, jnp.float32) if spec is V...  20.9 us
    all_to_all x2, starting transfers between devices, faces(): return lax.all_to_all(x, 'zone', 0, 0, tiled=True)  13.3 us
    ppermute x7, waiting for transfers between devices, swap(): return lax.ppermute(x, 'ja', [(p, p ^ bit) for p in range(parts)])  7.35 us
    ppermute x7, starting transfers between devices, swap(): return lax.ppermute(x, 'ja', [(p, p ^ bit) for p in range(parts)])  5.35 us
  transfers between devices with their start and end apart: 10, of which 4 were waited for; matrix products, arithmetic and copies ran while one was open for 0% of the time, Pallas kernels for 10%

profile of v5, /device:TPU:0, one launch (start us, length us, event | category | flops | bytes accessed | tf_op | source)
XLA Modules:
  0.0 75.9 jit_solution(3470191421574977438)
XLA Ops:
  0.6 5.1 %shard_map.95 = (f32[8,5,5,16,128]{4,3,2,1,0:T(8,128)S(1)}, f32[8,5,5,16,128]{4,3,2,1,0:T(8,128)S(1)}, f32[8,5,5,16,128]{4,3,2,1,0:T(8,128)S(1)}, f32[8,5,5,16,1...) custom-call(s32[8]{0:T(128)} %depth_hbm.1, ...), custom_call_target="tpu_custom_call" | custom-call | flops 5000000000 | bytes 5000000 | tf_op jit(solution)/shard_map/pallas_call | solution.py:25
  5.8 1.2 %copy-done = f32[8,5,5,16,128]{4,3,2,1,0:T(8,128)} copy-done((f32[8,5,5,16,128]{4,3,2,1,0:T(8,128)}, f32[8,5,5,16,128]{4,3,2,1,0:T(8,128)S(1)}, u32[]{:S(2)}) %copy-start) | copy-done | bytes 1638424
  7.0 0.5 collective-permute-start.1
  7.4 0.0 copy-done.37
  7.4 1.3 %shard_map.96 = (f32[8,16,128]{2,1,0:T(8,128)}, f32[8,5,16,128]{3,2,1,0:T(8,128)S(1)}, f32[5,16,128]{2,1,0:T(8,128)S(1)}) custom-call(f32[16,128]{1,0:T(8,128)S(1)} %get-tuple-element.28.live_ref, f32[8,5,16,128]{3,2,1,0:T(8,128)S(1)} %bitcast.8), custom_call_target="tpu_custom_call" | custom-call | flops 1000000000 | bytes 1000000 | tf_op jit(solution)/shard_map/pallas_call | solution.py:25
  8.7 0.7 copy-done.16
  9.4 0.6 copy-done.38
  10.0 7.3 %all-to-all-start = ((f32[8,16,128]{2,1,0:T(8,128)}), f32[8,16,128]{2,1,0:T(8,128)S(1)}, u32[]{:S(2)}, u32[]{:S(2)}) async-start(f32[8,16,128]{2,1,0:T(8,128)} %get-tuple-element.34), calls=%async_computation | async-start | bytes 131072 | tf_op jit(solution)/shard_map/all_to_all | solution.py:480
  17.3 0.0 collective-permute-done.1.other_ref.mats_other_ref
  17.3 2.0 %shard_map.97 = f32[5,5,8,128]{3,2,1,0:T(8,128)} custom-call(f32[3,5,5,16,128]{4,3,2,1,0:T(8,128)} %get-tuple-element.32.mine_ref.mats_ref, f32[3,5,5,16,128]{4,3,2,1,0:T(8,128)} %collective-permute-done.1.other_ref.mats_other_ref), custom_call_target="tpu_custom_call" | custom-call | flops 100000 | bytes 100 | tf_op jit(solution)/shard_map/pallas_call | solution.py:25
  19.3 1.5 %collective-permute-start.2 = (f32[5,5,8,128]{3,2,1,0:T(8,128)}, f32[5,5,8,128]{3,2,1,0:T(8,128)}, u32[]{:S(2)}, u32[]{:S(2)}) collective-permute-start(f32[5,5,8,128]{3,2,1,0:T(8,128)} %shard_map.97), channel_id=1, source_target_pairs={{0,2},{1,3},{2,0},{3,1},{4,6},{5,7},{6,4},{7,5},{8,10},{9,11},{10,... | collective-permute-start | bytes 307208 | tf_op jit(solution)/shard_map/ppermute | solution.py:477
  20.8 0.0 collective-permute-start
  20.8 1.5 %shard_map.98 = (f32[8,5,5,16,128]{4,3,2,1,0:T(8,128)S(1)}, f32[8,5,16,128]{3,2,1,0:T(8,128)S(1)}) custom-call(f32[8,5,5,16,128]{4,3,2,1,0:T(8,128)} %bitcast.13, f32[8,5,16,128]{3,2,1,0:T(8,128)} %bitcast.14), custom_call_target="tpu_custom_call" | custom-call | flops 1000000000 | bytes 1000000 | tf_op jit(solution)/shard_map/pallas_call | solution.py:25
  22.3 1.2 %copy-done.4 = f32[8,5,5,16,128]{4,3,2,1,0:T(8,128)} copy-done((f32[8,5,5,16,128]{4,3,2,1,0:T(8,128)}, f32[8,5,5,16,128]{4,3,2,1,0:T(8,128)S(1)}, u32[]{:S(2)}) %copy-start.4) | copy-done | bytes 1638424
  23.5 0.7 copy-done.19
  24.2 0.0 collective-permute-done.above_ref
  24.2 0.0 all-to-all-done.tiles_ref
  24.2 0.6 copy-done.28
  24.8 0.0 collective-permute-done.2.half_ref
  24.8 1.4 %copy-done.1 = f32[8,5,5,16,128]{4,3,2,1,0:T(8,128)S(1)} copy-done((f32[8,5,5,16,128]{4,3,2,1,0:T(8,128)S(1)}, f32[8,5,5,16,128]{4,3,2,1,0:T(8,128)}, u32[]{:S(2)}) %copy-start.1) | copy-done | bytes 1638424
  26.3 1.4 %copy-done.5 = f32[8,5,5,16,128]{4,3,2,1,0:T(8,128)S(1)} copy-done((f32[8,5,5,16,128]{4,3,2,1,0:T(8,128)S(1)}, f32[8,5,5,16,128]{4,3,2,1,0:T(8,128)}, u32[]{:S(2)}) %copy-start.5) | copy-done | bytes 1638424
  27.7 1.0 %copy-done.17 = f32[8,5,16,128]{3,2,1,0:T(8,128)S(1)} copy-done((f32[8,5,16,128]{3,2,1,0:T(8,128)S(1)}, f32[8,5,16,128]{3,2,1,0:T(8,128)}, u32[]{:S(2)}) %copy-start.17) | copy-done | bytes 327704
  28.7 1.0 %copy-done.20 = f32[8,5,16,128]{3,2,1,0:T(8,128)S(1)} copy-done((f32[8,5,16,128]{3,2,1,0:T(8,128)S(1)}, f32[8,5,16,128]{3,2,1,0:T(8,128)}, u32[]{:S(2)}) %copy-start.20) | copy-done | bytes 327704
  29.6 0.8 %copy-done.29 = f32[8,16,128]{2,1,0:T(8,128)S(1)} copy-done((f32[8,16,128]{2,1,0:T(8,128)S(1)}, f32[8,16,128]{2,1,0:T(8,128)}, u32[]{:S(2)}) %copy-start.29) | copy-done | bytes 65560
  30.5 0.7 copy-done.31
  31.2 1.8 %shard_map.99 = (f32[8,5,16,128]{3,2,1,0:T(8,128)S(1)}, f32[2,5,16,128]{3,2,1,0:T(8,128)S(1)}, f32[5,5,8,128]{3,2,1,0:T(8,128)S(1)}) custom-call(f32[5,5,8,128]{3,2,1,0:T(8,128)} %collective-permute-done.2.half_ref, f32[16,128]{1,0:T(8,128)S(1)} %copy-done.31, f32[2,8,16,128]{3,2,1,0:T(8,128)S(1)} %get-tuple-element.33.pick_ref, ...), custom_call_target="tpu_custom_call" | custom-call | flops 1000000000 | bytes 1000000 | tf_op jit(solution)/shard_map/pallas_call | solution.py:25
  33.0 0.6 collective-permute-start.3
  33.5 0.1 collective-permute-start.5
  33.6 0.8 %collective-permute-done.3.ends_other_ref = f32[2,5,16,128]{3,2,1,0:T(8,128)S(1)} collective-permute-done((f32[2,5,16,128]{3,2,1,0:T(8,128)S(1)}, f32[2,5,16,128]{3,2,1,0:T(8,128)S(1)}, u32[]{:S(2)}, u32[]{:S(2)}) %collective-permute-start.3) | collective-permute-done | bytes 81952 | tf_op jit(solution)/shard_map/ppermute | solution.py:477
  34.4 1.3 %shard_map.100.pair_ref = f32[1,5,16,128]{3,2,1,0:T(8,128)S(1)} custom-call(f32[2,5,16,128]{3,2,1,0:T(8,128)S(1)} %get-tuple-element.41.ends_ref, f32[2,5,16,128]{3,2,1,0:T(8,128)S(1)} %collective-permute-done.3.ends_other_ref, f32[3,5,5,16,128]{4,3,2,1,0:T(8,128)} %get-tuple-element.32.mine_ref.mats_ref, ...), custom_call_target="tpu_custom_call" | custom-call | flops 1000000000 | bytes 1000000 | tf_op jit(solution)/shard_map/pallas_call | solution.py:25
  35.7 1.4 %collective-permute-start.4 = (f32[1,5,16,128]{3,2,1,0:T(8,128)S(1)}, f32[1,5,16,128]{3,2,1,0:T(8,128)S(1)}, u32[]{:S(2)}, u32[]{:S(2)}) collective-permute-start(f32[1,5,16,128]{3,2,1,0:T(8,128)S(1)} %shard_map.100.pair_ref), channel_id=1, source_target_pairs={{0,2},{1,3},{2,0},{3,1},{4,6},{5,7},{6,4},{7,5},{8,10},{9,11},{10,... | collective-permute-start | bytes 122888 | tf_op jit(solution)/shard_map/ppermute | solution.py:477
  37.2 0.0 collective-permute-done.5.half_other_ref
  37.2 2.6 %collective-permute-done.4.pair_other_ref = f32[1,5,16,128]{3,2,1,0:T(8,128)S(1)} collective-permute-done((f32[1,5,16,128]{3,2,1,0:T(8,128)S(1)}, f32[1,5,16,128]{3,2,1,0:T(8,128)S(1)}, u32[]{:S(2)}, u32[]{:S(2)}) %collective-permute-start.4) | collective-permute-done | bytes 40992 | tf_op jit(solution)/shard_map/ppermute | solution.py:477
  39.8 1.7 %shard_map.101 = (f32[8,5,16,128]{3,2,1,0:T(8,128)S(1)}, f32[5,16,128]{2,1,0:T(8,128)S(1)}, f32[8,16,128]{2,1,0:T(8,128)S(1)}) custom-call(f32[8,5,16,128]{3,2,1,0:T(8,128)S(1)} %copy-done.18, f32[5,16,128]{2,1,0:T(8,128)S(1)} %collective-permute-done.above_ref, f32[8,5,16,128]{3,2,1,0:T(8,128)S(1)} %get-tuple-element.40.s_ref, ...), custom_call_target="tpu_custom_call" | custom-call | flops 1000000000 | bytes 1000000 | tf_op jit(solution)/shard_map/pallas_call | solution.py:25
  41.5 0.0 copy-start.10
  41.5 0.7 copy-done.10
  42.2 0.6 copy-done.34
  42.8 0.6 copy-done.35
  43.5 6.0 %all-to-all-start.1 = ((f32[8,16,128]{2,1,0:T(8,128)}), f32[8,16,128]{2,1,0:T(8,128)}, u32[]{:S(2)}, u32[]{:S(2)}) async-start(f32[8,16,128]{2,1,0:T(8,128)} %copy-done.34), calls=%async_computation.1 | async-start | bytes 131072 | tf_op jit(solution)/shard_map/all_to_all | solution.py:480
  49.5 1.4 %copy-done.2 = f32[8,5,5,16,128]{4,3,2,1,0:T(8,128)S(1)} copy-done((f32[8,5,5,16,128]{4,3,2,1,0:T(8,128)S(1)}, f32[8,5,5,16,128]{4,3,2,1,0:T(8,128)}, u32[]{:S(2)}) %copy-start.2) | copy-done | bytes 1638424
  50.9 1.4 %copy-done.6 = f32[8,5,5,16,128]{4,3,2,1,0:T(8,128)S(1)} copy-done((f32[8,5,5,16,128]{4,3,2,1,0:T(8,128)S(1)}, f32[8,5,5,16,128]{4,3,2,1,0:T(8,128)}, u32[]{:S(2)}) %copy-start.6) | copy-done | bytes 1638424
  52.3 1.4 %copy-done.8 = f32[8,5,5,16,128]{4,3,2,1,0:T(8,128)S(1)} copy-done((f32[8,5,5,16,128]{4,3,2,1,0:T(8,128)S(1)}, f32[8,5,5,16,128]{4,3,2,1,0:T(8,128)}, u32[]{:S(2)}) %copy-start.8) | copy-done | bytes 1638424
  53.8 1.0 %copy-done.11 = f32[8,5,16,128]{3,2,1,0:T(8,128)S(1)} copy-done((f32[8,5,16,128]{3,2,1,0:T(8,128)S(1)}, f32[8,5,16,128]{3,2,1,0:T(8,128)}, u32[]{:S(2)}) %copy-start.11) | copy-done | bytes 327704
  54.7 1.4 %copy-done.15 = f32[8,5,5,16,128]{4,3,2,1,0:T(8,128)S(1)} copy-done((f32[8,5,5,16,128]{4,3,2,1,0:T(8,128)S(1)}, f32[8,5,5,16,128]{4,3,2,1,0:T(8,128)}, u32[]{:S(2)}) %copy-start.15) | copy-done | bytes 1638424
  56.2 1.0 %copy-done.21 = f32[8,5,16,128]{3,2,1,0:T(8,128)S(1)} copy-done((f32[8,5,16,128]{3,2,1,0:T(8,128)S(1)}, f32[8,5,16,128]{3,2,1,0:T(8,128)}, u32[]{:S(2)}) %copy-start.21) | copy-done | bytes 327704
  57.1 0.7 copy-done.32
  57.8 0.8 %copy-done.36 = f32[5,16,128]{2,1,0:T(8,128)S(1)} copy-done((f32[5,16,128]{2,1,0:T(8,128)S(1)}, f32[5,16,128]{2,1,0:T(8,128)}, u32[]{:S(2)}) %copy-start.36) | copy-done | bytes 40984
  58.6 0.6 shard_map.102
  59.2 0.0 copy-start.24
  59.2 0.7 copy-done.24
  59.9 0.7 copy-done.26
  60.7 0.0 all-to-all-done.1.tiles_ref
  60.7 1.4 %copy-done.3 = f32[8,5,5,16,128]{4,3,2,1,0:T(8,128)S(1)} copy-done((f32[8,5,5,16,128]{4,3,2,1,0:T(8,128)S(1)}, f32[8,5,5,16,128]{4,3,2,1,0:T(8,128)}, u32[]{:S(2)}) %copy-start.3) | copy-done | bytes 1638424
  62.1 1.0 %copy-done.12 = f32[8,5,16,128]{3,2,1,0:T(8,128)S(1)} copy-done((f32[8,5,16,128]{3,2,1,0:T(8,128)S(1)}, f32[8,5,16,128]{3,2,1,0:T(8,128)}, u32[]{:S(2)}) %copy-start.12) | copy-done | bytes 327704
  63.1 1.0 %copy-done.25 = f32[8,5,16,128]{3,2,1,0:T(8,128)S(1)} copy-done((f32[8,5,16,128]{3,2,1,0:T(8,128)S(1)}, f32[8,5,16,128]{3,2,1,0:T(8,128)}, u32[]{:S(2)}) %copy-start.25) | copy-done | bytes 327704
  64.1 1.0 %copy-done.27 = f32[8,5,16,128]{3,2,1,0:T(8,128)S(1)} copy-done((f32[8,5,16,128]{3,2,1,0:T(8,128)S(1)}, f32[8,5,16,128]{3,2,1,0:T(8,128)}, u32[]{:S(2)}) %copy-start.27) | copy-done | bytes 327704
  65.0 1.3 %shard_map.103 = (f32[8,5,16,128]{3,2,1,0:T(8,128)S(1)}, f32[8,5,16,128]{3,2,1,0:T(8,128)S(1)}, f32[3,5,16,128]{3,2,1,0:T(8,128)S(1)}) custom-call(f32[16,128]{1,0:T(8,128)S(1)} %copy-done.33, f32[2,8,16,128]{3,2,1,0:T(8,128)S(1)} %get-tuple-element.33.pick_ref, f32[8,16,128]{2,1,0:T(8,128)} %all-to-all-done.1.tiles_ref, f32[8,5,16,128]{3,2,1,0:T(8,128)S(1)} %copy-done.12, ...), custom_call_target="tpu_custom_call" | custom-call | flops 1000000000 | bytes 1000000 | tf_op jit(solution)/shard_map/pallas_call | solution.py:25
  66.4 0.1 collective-permute-start.6
  66.4 1.3 %collective-permute-done.6.ends_other_ref = f32[3,5,16,128]{3,2,1,0:T(8,128)S(1)} collective-permute-done((f32[3,5,16,128]{3,2,1,0:T(8,128)S(1)}, f32[3,5,16,128]{3,2,1,0:T(8,128)S(1)}, u32[]{:S(2)}, u32[]{:S(2)}) %collective-permute-start.6) | collective-permute-done | bytes 122912 | tf_op jit(solution)/shard_map/ppermute | solution.py:477
  67.8 1.3 %shard_map.104.pair_ref = f32[2,5,16,128]{3,2,1,0:T(8,128)S(1)} custom-call(f32[3,5,16,128]{3,2,1,0:T(8,128)S(1)} %get-tuple-element.51.ends_ref, f32[3,5,16,128]{3,2,1,0:T(8,128)S(1)} %collective-permute-done.6.ends_other_ref, f32[3,5,5,16,128]{4,3,2,1,0:T(8,128)} %get-tuple-element.32.mine_ref.mats_ref, ...), custom_call_target="tpu_custom_call" | custom-call | flops 1000000000 | bytes 1000000 | tf_op jit(solution)/shard_map/pallas_call | solution.py:25
  69.1 1.3 %collective-permute-start.7 = (f32[2,5,16,128]{3,2,1,0:T(8,128)S(1)}, f32[2,5,16,128]{3,2,1,0:T(8,128)S(1)}, u32[]{:S(2)}, u32[]{:S(2)}) collective-permute-start(f32[2,5,16,128]{3,2,1,0:T(8,128)S(1)} %shard_map.104.pair_ref), channel_id=1, source_target_pairs={{0,2},{1,3},{2,0},{3,1},{4,6},{5,7},{6,4},{7,5},{8,10},{9,11},{10,... | collective-permute-start | bytes 245768 | tf_op jit(solution)/shard_map/ppermute | solution.py:477
  70.3 0.7 shard_map.105.res_in_hbm
  71.1 2.6 %collective-permute-done.7.pair_other_ref = f32[2,5,16,128]{3,2,1,0:T(8,128)S(1)} collective-permute-done((f32[2,5,16,128]{3,2,1,0:T(8,128)S(1)}, f32[2,5,16,128]{3,2,1,0:T(8,128)S(1)}, u32[]{:S(2)}, u32[]{:S(2)}) %collective-permute-start.7) | collective-permute-done | bytes 81952 | tf_op jit(solution)/shard_map/ppermute | solution.py:477
  73.6 2.3 %shard_map.106 = (f32[8,5,16,128]{3,2,1,0:T(8,128)}, f32[8,5,16,128]{3,2,1,0:T(8,128)}) custom-call(f32[16,128]{1,0:T(8,128)S(1)} %copy-done.33, f32[8,5,5,16,128]{4,3,2,1,0:T(8,128)S(1)} %copy-done.9, f32[8,5,16,128]{3,2,1,0:T(8,128)S(1)} %copy-done.13, f32[8,5,16,128]{3,2,1,0:T(8,128)S(1)} %get-tuple-element.49.res_ref, ...), custom_call_target="tpu_custom_call", output_to_operand_aliasing={{1}: (15, {})} | custom-call | flops 1000000000 | bytes 1000000 | tf_op jit(solution)/shard_map/pallas_call | solution.py:25
  (46 shorter events, 0.1 us)
Async XLA Ops:
  0.6 6.8 %copy-start.37 = (f32[1,8,5,16,128]{4,3,2,1,0:T(8,128)S(1)}, f32[1,8,5,16,128]{4,3,2,1,0:T(8,128)}, u32[]{:S(2)}) copy-start(f32[1,8,5,16,128]{4,3,2,1,0:T(8,128)} %param.8) | copy-start | bytes 983044
  5.8 1.2 %copy-start = (f32[8,5,5,16,128]{4,3,2,1,0:T(8,128)}, f32[8,5,5,16,128]{4,3,2,1,0:T(8,128)S(1)}, u32[]{:S(2)}) copy-start(f32[8,5,5,16,128]{4,3,2,1,0:T(8,128)S(1)} %get-tuple-element.37.inv_ref) | copy-start | bytes 4915204
  7.0 1.7 %copy-start.7 = (f32[8,5,5,16,128]{4,3,2,1,0:T(8,128)}, f32[8,5,5,16,128]{4,3,2,1,0:T(8,128)S(1)}, u32[]{:S(2)}) copy-start(f32[8,5,5,16,128]{4,3,2,1,0:T(8,128)S(1)} %get-tuple-element.29.low_ref) | copy-start | bytes 4915204
  7.0 1.7 %copy-start.14 = (f32[8,5,5,16,128]{4,3,2,1,0:T(8,128)}, f32[8,5,5,16,128]{4,3,2,1,0:T(8,128)S(1)}, u32[]{:S(2)}) copy-start(f32[8,5,5,16,128]{4,3,2,1,0:T(8,128)S(1)} %get-tuple-element.46.up_ref) | copy-start | bytes 4915204
  7.0 1.7 %copy-start.30 = (f32[16,128]{1,0:T(8,128)}, f32[16,128]{1,0:T(8,128)S(1)}, u32[]{:S(2)}) copy-start(f32[16,128]{1,0:T(8,128)S(1)} %get-tuple-element.28.live_ref) | copy-start | bytes 24580
  7.0 10.3 %collective-permute-start.1 = (f32[3,5,5,16,128]{4,3,2,1,0:T(8,128)}, f32[3,5,5,16,128]{4,3,2,1,0:T(8,128)}, u32[]{:S(2)}, u32[]{:S(2)}) collective-permute-start(f32[3,5,5,16,128]{4,3,2,1,0:T(8,128)} %get-tuple-element.32.mine_ref.mats_ref), channel_id=1, source_target_pairs={{0,1},{1,0},{2,3},{3,2},{4,5},{5,4},{6,7},{7,6},{8,9},{9,8},{10,11... | collective-permute-start | bytes 1843208 | tf_op jit(solution)/shard_map/ppermute | solution.py:477
  8.7 0.7 copy-start.16
  9.4 0.6 copy-start.38
  10.0 14.2 %all-to-all-start = ((f32[8,16,128]{2,1,0:T(8,128)}), f32[8,16,128]{2,1,0:T(8,128)S(1)}, u32[]{:S(2)}, u32[]{:S(2)}) async-start(f32[8,16,128]{2,1,0:T(8,128)} %get-tuple-element.34), calls=%async_computation | async-start | bytes 131072 | tf_op jit(solution)/shard_map/all_to_all | solution.py:480
  19.3 5.5 %collective-permute-start.2 = (f32[5,5,8,128]{3,2,1,0:T(8,128)}, f32[5,5,8,128]{3,2,1,0:T(8,128)}, u32[]{:S(2)}, u32[]{:S(2)}) collective-permute-start(f32[5,5,8,128]{3,2,1,0:T(8,128)} %shard_map.97), channel_id=1, source_target_pairs={{0,2},{1,3},{2,0},{3,1},{4,6},{5,7},{6,4},{7,5},{8,10},{9,11},{10,... | collective-permute-start | bytes 307208 | tf_op jit(solution)/shard_map/ppermute | solution.py:477
  20.8 3.4 %collective-permute-start = (f32[5,16,128]{2,1,0:T(8,128)}, f32[5,16,128]{2,1,0:T(8,128)S(1)}, u32[]{:S(2)}, u32[]{:S(2)}) collective-permute-start(f32[5,16,128]{2,1,0:T(8,128)} %copy-done.38), channel_id=1, source_target_pairs={{1,0},{2,1},{3,2},{0,3},{5,4},{6,5},{7,6},{4,7},{9,8},{10,9},{11,1... | collective-permute-start | bytes 122888 | tf_op jit(solution)/shard_map/ppermute | solution.py:492
  22.3 1.2 %copy-start.4 = (f32[8,5,5,16,128]{4,3,2,1,0:T(8,128)}, f32[8,5,5,16,128]{4,3,2,1,0:T(8,128)S(1)}, u32[]{:S(2)}) copy-start(f32[8,5,5,16,128]{4,3,2,1,0:T(8,128)S(1)} %get-tuple-element.36.diag_ref) | copy-start | bytes 4915204
  23.5 0.7 copy-start.19
  24.2 0.6 copy-start.28
  24.8 1.4 %copy-start.1 = (f32[8,5,5,16,128]{4,3,2,1,0:T(8,128)S(1)}, f32[8,5,5,16,128]{4,3,2,1,0:T(8,128)}, u32[]{:S(2)}) copy-start(f32[8,5,5,16,128]{4,3,2,1,0:T(8,128)} %copy-done) | copy-start | bytes 4915204
  26.3 1.4 %copy-start.5 = (f32[8,5,5,16,128]{4,3,2,1,0:T(8,128)S(1)}, f32[8,5,5,16,128]{4,3,2,1,0:T(8,128)}, u32[]{:S(2)}) copy-start(f32[8,5,5,16,128]{4,3,2,1,0:T(8,128)} %copy-done.4) | copy-start | bytes 4915204
  27.7 1.0 %copy-start.17 = (f32[8,5,16,128]{3,2,1,0:T(8,128)S(1)}, f32[8,5,16,128]{3,2,1,0:T(8,128)}, u32[]{:S(2)}) copy-start(f32[8,5,16,128]{3,2,1,0:T(8,128)} %copy-done.16) | copy-start | bytes 983044
  28.7 1.0 %copy-start.20 = (f32[8,5,16,128]{3,2,1,0:T(8,128)S(1)}, f32[8,5,16,128]{3,2,1,0:T(8,128)}, u32[]{:S(2)}) copy-start(f32[8,5,16,128]{3,2,1,0:T(8,128)} %copy-done.19) | copy-start | bytes 983044
  29.6 0.8 %copy-start.29 = (f32[8,16,128]{2,1,0:T(8,128)S(1)}, f32[8,16,128]{2,1,0:T(8,128)}, u32[]{:S(2)}) copy-start(f32[8,16,128]{2,1,0:T(8,128)} %copy-done.28) | copy-start | bytes 196612
  30.5 0.7 copy-start.31
  33.0 1.5 %collective-permute-start.3 = (f32[2,5,16,128]{3,2,1,0:T(8,128)S(1)}, f32[2,5,16,128]{3,2,1,0:T(8,128)S(1)}, u32[]{:S(2)}, u32[]{:S(2)}) collective-permute-start(f32[2,5,16,128]{3,2,1,0:T(8,128)S(1)} %get-tuple-element.41.ends_ref), channel_id=1, source_target_pairs={{0,1},{1,0},{2,3},{3,2},{4,5},{5,4},{6,7},{7,6},{8,9},{9,8},{10,11... | collective-permute-start | bytes 245768 | tf_op jit(solution)/shard_map/ppermute | solution.py:477
  33.5 6.3 %copy-start.18 = (f32[8,5,16,128]{3,2,1,0:T(8,128)S(1)}, f32[8,5,16,128]{3,2,1,0:T(8,128)}, u32[]{:S(2)}) copy-start(f32[8,5,16,128]{3,2,1,0:T(8,128)} %copy-done.16) | copy-start | bytes 983044
  33.5 3.6 %collective-permute-start.5 = (f32[5,5,8,128]{3,2,1,0:T(8,128)S(1)}, f32[5,5,8,128]{3,2,1,0:T(8,128)S(1)}, u32[]{:S(2)}, u32[]{:S(2)}) collective-permute-start(f32[5,5,8,128]{3,2,1,0:T(8,128)S(1)} %get-tuple-element.42.half_ref), channel_id=1, source_target_pairs={{0,1},{1,0},{2,3},{3,2},{4,5},{5,4},{6,7},{7,6},{8,9},{9,8},{10,11... | collective-permute-start | bytes 307208 | tf_op jit(solution)/shard_map/ppermute | solution.py:477
  35.7 4.1 %collective-permute-start.4 = (f32[1,5,16,128]{3,2,1,0:T(8,128)S(1)}, f32[1,5,16,128]{3,2,1,0:T(8,128)S(1)}, u32[]{:S(2)}, u32[]{:S(2)}) collective-permute-start(f32[1,5,16,128]{3,2,1,0:T(8,128)S(1)} %shard_map.100.pair_ref), channel_id=1, source_target_pairs={{0,2},{1,3},{2,0},{3,1},{4,6},{5,7},{6,4},{7,5},{8,10},{9,11},{10,... | collective-permute-start | bytes 122888 | tf_op jit(solution)/shard_map/ppermute | solution.py:477
  37.2 4.3 %copy-start.22 = (f32[5,5,8,128]{3,2,1,0:T(8,128)}, f32[5,5,8,128]{3,2,1,0:T(8,128)S(1)}, u32[]{:S(2)}) copy-start(f32[5,5,8,128]{3,2,1,0:T(8,128)S(1)} %collective-permute-done.5.half_other_ref) | copy-start | bytes 307204
  41.5 0.7 copy-start.10
  42.2 0.6 copy-start.34
  42.8 0.6 copy-start.35
  43.5 17.2 %all-to-all-start.1 = ((f32[8,16,128]{2,1,0:T(8,128)}), f32[8,16,128]{2,1,0:T(8,128)}, u32[]{:S(2)}, u32[]{:S(2)}) async-start(f32[8,16,128]{2,1,0:T(8,128)} %copy-done.34), calls=%async_computation.1 | async-start | bytes 131072 | tf_op jit(solution)/shard_map/all_to_all | solution.py:480
  49.5 1.4 %copy-start.2 = (f32[8,5,5,16,128]{4,3,2,1,0:T(8,128)S(1)}, f32[8,5,5,16,128]{4,3,2,1,0:T(8,128)}, u32[]{:S(2)}) copy-start(f32[8,5,5,16,128]{4,3,2,1,0:T(8,128)} %copy-done) | copy-start | bytes 4915204
  50.9 1.4 %copy-start.6 = (f32[8,5,5,16,128]{4,3,2,1,0:T(8,128)S(1)}, f32[8,5,5,16,128]{4,3,2,1,0:T(8,128)}, u32[]{:S(2)}) copy-start(f32[8,5,5,16,128]{4,3,2,1,0:T(8,128)} %copy-done.4) | copy-start | bytes 4915204
  52.3 1.4 %copy-start.8 = (f32[8,5,5,16,128]{4,3,2,1,0:T(8,128)S(1)}, f32[8,5,5,16,128]{4,3,2,1,0:T(8,128)}, u32[]{:S(2)}) copy-start(f32[8,5,5,16,128]{4,3,2,1,0:T(8,128)} %copy-done.7) | copy-start | bytes 4915204
  53.8 1.0 %copy-start.11 = (f32[8,5,16,128]{3,2,1,0:T(8,128)S(1)}, f32[8,5,16,128]{3,2,1,0:T(8,128)}, u32[]{:S(2)}) copy-start(f32[8,5,16,128]{3,2,1,0:T(8,128)} %copy-done.10) | copy-start | bytes 983044
  54.7 1.4 %copy-start.15 = (f32[8,5,5,16,128]{4,3,2,1,0:T(8,128)S(1)}, f32[8,5,5,16,128]{4,3,2,1,0:T(8,128)}, u32[]{:S(2)}) copy-start(f32[8,5,5,16,128]{4,3,2,1,0:T(8,128)} %copy-done.14) | copy-start | bytes 4915204
  56.2 1.0 %copy-start.21 = (f32[8,5,16,128]{3,2,1,0:T(8,128)S(1)}, f32[8,5,16,128]{3,2,1,0:T(8,128)}, u32[]{:S(2)}) copy-start(f32[8,5,16,128]{3,2,1,0:T(8,128)} %copy-done.19) | copy-start | bytes 983044
  57.1 0.7 copy-start.32
  57.8 0.8 %copy-start.36 = (f32[5,16,128]{2,1,0:T(8,128)S(1)}, f32[5,16,128]{2,1,0:T(8,128)}, u32[]{:S(2)}) copy-start(f32[5,16,128]{2,1,0:T(8,128)} %copy-done.35) | copy-start | bytes 122884
  58.6 2.1 %copy-start.33 = (f32[16,128]{1,0:T(8,128)S(1)}, f32[16,128]{1,0:T(8,128)}, u32[]{:S(2)}) copy-start(f32[16,128]{1,0:T(8,128)} %copy-done.30) | copy-start | bytes 24580
  59.2 0.7 copy-start.24
  59.9 0.7 copy-start.26
  60.7 1.4 %copy-start.3 = (f32[8,5,5,16,128]{4,3,2,1,0:T(8,128)S(1)}, f32[8,5,5,16,128]{4,3,2,1,0:T(8,128)}, u32[]{:S(2)}) copy-start(f32[8,5,5,16,128]{4,3,2,1,0:T(8,128)} %copy-done) | copy-start | bytes 4915204
  62.1 1.0 %copy-start.12 = (f32[8,5,16,128]{3,2,1,0:T(8,128)S(1)}, f32[8,5,16,128]{3,2,1,0:T(8,128)}, u32[]{:S(2)}) copy-start(f32[8,5,16,128]{3,2,1,0:T(8,128)} %copy-done.10) | copy-start | bytes 983044
  63.1 1.0 %copy-start.25 = (f32[8,5,16,128]{3,2,1,0:T(8,128)S(1)}, f32[8,5,16,128]{3,2,1,0:T(8,128)}, u32[]{:S(2)}) copy-start(f32[8,5,16,128]{3,2,1,0:T(8,128)} %copy-done.24) | copy-start | bytes 983044
  64.0 1.0 %copy-start.27 = (f32[8,5,16,128]{3,2,1,0:T(8,128)S(1)}, f32[8,5,16,128]{3,2,1,0:T(8,128)}, u32[]{:S(2)}) copy-start(f32[8,5,16,128]{3,2,1,0:T(8,128)} %copy-done.26) | copy-start | bytes 983044
  66.4 1.4 %collective-permute-start.6 = (f32[3,5,16,128]{3,2,1,0:T(8,128)S(1)}, f32[3,5,16,128]{3,2,1,0:T(8,128)S(1)}, u32[]{:S(2)}, u32[]{:S(2)}) collective-permute-start(f32[3,5,16,128]{3,2,1,0:T(8,128)S(1)} %get-tuple-element.51.ends_ref), channel_id=1, source_target_pairs={{0,1},{1,0},{2,3},{3,2},{4,5},{5,4},{6,7},{7,6},{8,9},{9,8},{10,11... | collective-permute-start | bytes 368648 | tf_op jit(solution)/shard_map/ppermute | solution.py:477
  69.1 4.6 %collective-permute-start.7 = (f32[2,5,16,128]{3,2,1,0:T(8,128)S(1)}, f32[2,5,16,128]{3,2,1,0:T(8,128)S(1)}, u32[]{:S(2)}, u32[]{:S(2)}) collective-permute-start(f32[2,5,16,128]{3,2,1,0:T(8,128)S(1)} %shard_map.104.pair_ref), channel_id=1, source_target_pairs={{0,2},{1,3},{2,0},{3,1},{4,6},{5,7},{6,4},{7,5},{8,10},{9,11},{10,... | collective-permute-start | bytes 245768 | tf_op jit(solution)/shard_map/ppermute | solution.py:477
  70.3 3.3 %copy-start.9 = (f32[8,5,5,16,128]{4,3,2,1,0:T(8,128)S(1)}, f32[8,5,5,16,128]{4,3,2,1,0:T(8,128)}, u32[]{:S(2)}) copy-start(f32[8,5,5,16,128]{4,3,2,1,0:T(8,128)} %copy-done.7) | copy-start | bytes 4915204
  70.3 3.3 %copy-start.13 = (f32[8,5,16,128]{3,2,1,0:T(8,128)S(1)}, f32[8,5,16,128]{3,2,1,0:T(8,128)}, u32[]{:S(2)}) copy-start(f32[8,5,16,128]{3,2,1,0:T(8,128)} %copy-done.10) | copy-start | bytes 983044
  70.3 3.3 %copy-start.23 = (f32[5,5,8,128]{3,2,1,0:T(8,128)S(1)}, f32[5,5,8,128]{3,2,1,0:T(8,128)}, u32[]{:S(2)}) copy-start(f32[5,5,8,128]{3,2,1,0:T(8,128)} %copy-done.22) | copy-start | bytes 307204

commit v6 on v4

--- a/solution.py
+++ b/solution.py
@@ -31,7 +31,7 @@
             out_specs=out_specs or [VMEM] * len(shapes),
             scratch_shapes=list(scratch),
             input_output_aliases=alias,
-            compiler_params=pltpu.CompilerParams(vmem_limit_bytes=12 * 2**20),
+            compiler_params=pltpu.CompilerParams(vmem_limit_bytes=8 * 2**20),
             cost_estimate=pl.CostEstimate(flops=flops, bytes_accessed=flops // 10**3, transcendentals=0),
         )(*arrays)
 
@@ -97,8 +97,7 @@
     return [jnp.where(inner, x, 0.0) for x in values]
 
 
-def pack_kernel(mats_ref, flow_ref, tile_ref, first_ref):
-    del mats_ref
+def pack_kernel(flow_ref, tile_ref, first_ref):
     put(first_ref, cell(flow_ref, 0))
     pack_faces(lambda j, v: flow_ref[j, v], flow_ref.shape[0], tile_ref)
 
@@ -127,26 +126,15 @@
 
 
 def matrix_kernel(
-    depth_hbm, east_hbm, inv_hbm, low_hbm, up_hbm,
+    depth_hbm, east_hbm, tiles_ref, inv_ref, low_ref, up_ref,
     e_ref, f_ref, mats_ref, live_ref, pick_ref,
-    inv_ref, low_ref, up_ref, y_ref, depth_ref, east_ref, sems, small_sems,
-):
+    y_ref, depth_ref, east_ref, sems,
+):
+    del tiles_ref
     planes = inv_ref.shape[0]
-
-    def copies(j):
-        return [
-            pltpu.make_async_copy(src.at[j], dst.at[j], sems.at[i, j])
-            for i, (src, dst) in enumerate(
-                [(inv_hbm, inv_ref), (low_hbm, low_ref), (up_hbm, up_ref)]
-            )
-        ]
-
-    for j in range(planes):
-        for copy in copies(j):
-            copy.start()
     scalars = [
-        pltpu.make_async_copy(depth_hbm, depth_ref, small_sems.at[0]),
-        pltpu.make_async_copy(east_hbm, east_ref, small_sems.at[1]),
+        pltpu.make_async_copy(depth_hbm, depth_ref, sems.at[0]),
+        pltpu.make_async_copy(east_hbm, east_ref, sems.at[1]),
     ]
     for copy in scalars:
         copy.start()
@@ -171,8 +159,6 @@
                 put_col(out_ref, [OMEGA * x for x in product], q, j, rows)
 
     def forward(j, carry):
-        for copy in copies(j):
-            copy.wait()
         for rows in halves:
             products(j, rows)
             e = mat(e_ref, j, rows)
@@ -180,8 +166,6 @@
                 put_col(y_ref, matvec(e, col(y_ref, q, j - 1, rows)), q, j, rows)
         return carry
 
-    for copy in copies(0):
-        copy.wait()
     for rows in halves:
         products(0, rows)
         for q in range(5):
@@ -254,11 +238,13 @@
 
 
 def local_kernel(
-    beta_ref, live_ref, pick_ref, tiles_ref, cur_ref, above_ref, force_ref, diag_ref, inv_ref,
+    mats_ref, live_ref, pick_ref, tiles_ref, cur_ref, above_ref, force_ref, diag_ref, inv_ref,
     e_ref, f_ref,
-    s_ref, ends_ref, y_ref,
-):
-    del beta_ref
+    s_ref, ends_ref, mats_out_ref, y_ref,
+):
+    for i in range(3):
+        for r in range(5):
+            put(mats_out_ref, cell(mats_ref, i, r), i, r)
     planes = cur_ref.shape[0]
     ghosts = ghosts_of(pick_ref, tiles_ref)
     before, here = None, masked(live_ref, cell(cur_ref, 0))
@@ -280,10 +266,11 @@
 
 
 def second_kernel(
-    live_ref, pick_ref, tiles_ref, cur_ref, above_ref, force_ref, diag_ref, low_ref, up_ref,
+    beta_ref, live_ref, pick_ref, tiles_ref, cur_ref, above_ref, force_ref, diag_ref, low_ref, up_ref,
     inv_ref, e_ref, f_ref,
     res_ref, s_ref, ends_ref, low0_ref, y_ref,
 ):
+    del beta_ref
     planes = cur_ref.shape[0]
     ghosts = ghosts_of(pick_ref, tiles_ref)
     for r in range(5):
@@ -334,15 +321,16 @@
     by_place([ends_ref, mats_ref], [ends_other_ref, mats_other_ref], run)
 
 
+def raise_kernel(pair_ref, pair_other_ref, beta_ref, raised_ref):
+    beyond = add(cell(pair_ref, 0), matvec(block(beta_ref), cell(pair_other_ref, 0)))
+    put(raised_ref, beyond, 0)
+
+
 def inflows(
-    ends_ref, ends_other_ref, mats_ref, mats_other_ref, pair_ref, pair_other_ref,
-    beta_ref, inflow_ref,
+    ends_ref, ends_other_ref, mats_ref, mats_other_ref, pair_ref, pair_other_ref, far, inflow_ref
 ):
     ja = lax.axis_index("ja")
     zeros = [jnp.zeros((16, 128), jnp.float32)] * 5
-
-    def far():
-        return add(cell(pair_other_ref, 0), matvec(block(beta_ref), cell(pair_ref, 0)))
 
     @pl.when(ja == 0)
     def _():
@@ -373,14 +361,13 @@
 
 def final_kernel(
     live_ref, cur_ref, above_ref, s_ref, e_ref, f_ref,
-    ends_ref, ends_other_ref, mats_ref, mats_other_ref, pair_ref, pair_other_ref,
-    beta_ref,
+    ends_ref, ends_other_ref, mats_ref, mats_other_ref, pair_ref, pair_other_ref, raised_ref,
     new_ref, above_new_ref, tile_ref, y_ref, inflow_ref,
 ):
     planes = cur_ref.shape[0]
     inflows(
         ends_ref, ends_other_ref, mats_ref, mats_other_ref, pair_ref, pair_other_ref,
-        beta_ref, inflow_ref,
+        lambda: cell(raised_ref, 0), inflow_ref,
     )
     value = cell(inflow_ref, 0)
     for j in range(planes):
@@ -411,9 +398,13 @@
     put(res0_ref, add(cell(res_ref, 0), masked(live_ref, matvec(block(low0_ref), before))))
     copies = [pltpu.make_async_copy(res0_ref, res_hbm.at[0], sems.at[planes])]
     copies[0].start()
+
+    def far():
+        return add(cell(pair_other_ref, 0), matvec(block(beta_ref), cell(pair_ref, 0)))
+
     inflows(
         ends_ref, ends_other_ref, mats_ref, mats_other_ref, pair_ref, pair_other_ref,
-        beta_ref, inflow_ref,
+        far, inflow_ref,
     )
     value = cell(inflow_ref, 0)
     for j in range(planes):
@@ -448,38 +439,40 @@
     def faces(x):
         return lax.all_to_all(x, "zone", 0, 0, tiled=True)
 
+    tile, first = call(pack_kernel, [tiles, plane], flops=2 * 10**10)(current)
+    above = lax.ppermute(first, "ja", [((p + 1) % parts, p) for p in range(parts)])
+    got = faces(tile)
     e, f, mats, live, pick = call(
         matrix_kernel,
         [blocks, blocks, (3, *matrix), state[2:], (2, *tiles)],
-        [buffer(*blocks)] * 4
+        [buffer(*blocks)]
         + [pltpu.SMEM((zones,), jnp.int32)] * 2
-        + [pltpu.SemaphoreType.DMA((3, planes)), pltpu.SemaphoreType.DMA((2,))],
+        + [pltpu.SemaphoreType.DMA((2,))],
         flops=5 * 10**9,
-        far=(0, 1, 2, 3, 4),
-    )(zone_depth, east_zone, inv, low, up)
-    tile, first = call(pack_kernel, [tiles, plane], flops=2 * 10**10)(mats, current)
-    above = lax.ppermute(first, "ja", [((p + 1) % parts, p) for p in range(parts)])
+        far=(0, 1),
+    )(zone_depth, east_zone, got, inv, low, up)
+    s, ends, mats = call(local_kernel, [state, (2, *plane), mats.shape], work)(
+        mats, live, pick, got, current, above, force, diag, inv, e, f
+    )
+    ends_other = swap(ends, 1)
     mats_other = swap(mats, 1)
-    got = faces(tile)
+    pair = call(mid_kernel, [(1, *plane)], flops=10**5)(ends, ends_other, mats, mats_other)[0]
     beta = call(beta_kernel, [matrix], flops=10**5)(mats, mats_other)[0]
-    s, ends = call(local_kernel, [state, (2, *plane)], work)(
-        beta, live, pick, got, current, above, force, diag, inv, e, f
-    )
+    pair_other = swap(pair, 2)
+    raised = call(raise_kernel, [(1, *plane)], flops=10**5)(pair, pair_other, beta)[0]
+    raised = swap(raised, 2)
     beta = swap(beta, 2)
-    ends_other = swap(ends, 1)
-    pair = call(mid_kernel, [(1, *plane)])(ends, ends_other, mats, mats_other)[0]
-    pair_other = swap(pair, 2)
     flows = [buffer(2, *plane)]
     current, above, tile = call(final_kernel, [state, plane, tiles], work + flows)(
         live, current, above, s, e, f,
-        ends, ends_other, mats, mats_other, pair, pair_other, beta,
+        ends, ends_other, mats, mats_other, pair, pair_other, raised,
     )
 
     got = faces(tile)
     residual, s, ends, low0 = call(
         second_kernel, [state, state, (3, *plane), matrix], work
     )(
-        live, pick, got, current, above, force, diag, low, up, inv, e, f
+        beta, live, pick, got, current, above, force, diag, low, up, inv, e, f
     )
     ends_other = swap(ends, 1)
     pair = call(mid_kernel, [(2, *plane)])(ends, ends_other, mats, mats_other)[0]

time: 61.2 us -> 51.1 us (0.83)
  Pallas kernels: 17.9 us -> 8.08 us
  local copies, waits for them, and re-layouts: 7.81 us -> 2.42 us
  waiting for transfers between devices: 11.3 us -> 16.1 us
  starting transfers between devices: 13.1 us -> 14 us
    pallas_call x10 -> x11, Pallas kernels: 17.9 us -> 8.08 us  [run(): pl.pallas_call(kernel, out_shape=[jax.ShapeDtypeStruct(s, jnp.float32) fo...]
    unnamed x34 -> x16, local copies, waits for them, and re-layouts: 7.81 us -> 2.42 us
    all_to_all x1, waiting for transfers between devices: 2.97 us -> 6.25 us  [faces(): return lax.all_to_all(x, 'zone', 0, 0, tiled=True)]
    ppermute x6 -> x7, waiting for transfers between devices: 7.74 us -> 9.85 us  [swap(): return lax.ppermute(x, 'ja', [(p, p ^ bit) for p in range(parts)])]
    ppermute x6 -> x7, starting transfers between devices: 4.96 us -> 5.96 us  [swap(): return lax.ppermute(x, 'ja', [(p, p ^ bit) for p in range(parts)])]
    ppermute x1, starting transfers between devices: 1.32 us -> 0.65 us  [per_device(): lax.ppermute(first, 'ja', [((p + 1) % parts, p) for p in range(parts)])]
  transfers between devices with their start and end apart: 8 -> 9, of which waited for: 5 -> 6; matrix products, arithmetic and copies ran while one was open for 0% -> 0% of each run, Pallas kernels for 9% -> 8%
where the time goes in v6:
time: 51.1 us; the launch traced here: 50.8 us
  waiting for transfers between devices  16.1 us (32%)
  starting transfers between devices  14 us (27%)
  blocking collectives  9.42 us (18%)
  Pallas kernels  8.08 us (16%)
  local copies, waits for them, and re-layouts  2.42 us (5%)
  between operations  0.76 us (1%)
    ppermute x7, waiting for transfers between devices, swap(): return lax.ppermute(x, 'ja', [(p, p ^ bit) for p in range(parts)])  9.85 us
    all_to_all x1, blocking collectives, faces(): return lax.all_to_all(x, 'zone', 0, 0, tiled=True)  9.42 us
    pallas_call x11, Pallas kernels, run(): pl.pallas_call(kernel, out_shape=[jax.ShapeDtypeStruct(s, jnp.float32) fo...  8.08 us
    all_to_all x1, starting transfers between devices, faces(): return lax.all_to_all(x, 'zone', 0, 0, tiled=True)  7.41 us
    all_to_all x1, waiting for transfers between devices, faces(): return lax.all_to_all(x, 'zone', 0, 0, tiled=True)  6.25 us
    ppermute x7, starting transfers between devices, swap(): return lax.ppermute(x, 'ja', [(p, p ^ bit) for p in range(parts)])  5.96 us
    unnamed x16, local copies, waits for them, and re-layouts  2.42 us
  transfers between devices with their start and end apart: 9, of which 6 were waited for; matrix products, arithmetic and copies ran while one was open for 0% of the time, Pallas kernels for 8%

profile of v6, /device:TPU:0, one launch (start us, length us, event | category | flops | bytes accessed | tf_op | source)
XLA Modules:
  0.0 50.8 jit_solution(13833354781279809904)
XLA Ops:
  0.6 0.0 copy-start.6
  0.6 1.0 %copy-done.6 = f32[1,8,5,16,128]{4,3,2,1,0:T(8,128)S(1)} copy-done((f32[1,8,5,16,128]{4,3,2,1,0:T(8,128)S(1)}, f32[1,8,5,16,128]{4,3,2,1,0:T(8,128)}, u32[]{:S(2)}) %copy-start.6) | copy-done | bytes 327704
  1.6 0.0 copy-start
  1.6 0.0 copy-start.2
  1.6 0.8 %shard_map.95 = (f32[8,16,128]{2,1,0:T(8,128)}, f32[5,16,128]{2,1,0:T(8,128)S(1)}) custom-call(f32[8,5,16,128]{3,2,1,0:T(8,128)S(1)} %bitcast.19), custom_call_target="tpu_custom_call" | custom-call | flops 20000000000 | bytes 20000000 | tf_op jit(solution)/shard_map/pallas_call | solution.py:25
  2.4 7.4 %all-to-all-start = ((f32[8,16,128]{2,1,0:T(8,128)}), f32[8,16,128]{2,1,0:T(8,128)S(1)}, u32[]{:S(2)}, u32[]{:S(2)}) async-start(f32[8,16,128]{2,1,0:T(8,128)} %get-tuple-element.21), calls=%async_computation | async-start | bytes 131072 | tf_op jit(solution)/shard_map/all_to_all | solution.py:440
  9.8 0.7 %collective-permute-start = (f32[5,16,128]{2,1,0:T(8,128)S(1)}, f32[5,16,128]{2,1,0:T(8,128)S(1)}, u32[]{:S(2)}, u32[]{:S(2)}) collective-permute-start(f32[5,16,128]{2,1,0:T(8,128)S(1)} %get-tuple-element.25), channel_id=1, source_target_pairs={{1,0},{2,1},{3,2},{0,3},{5,4},{6,5},{7,6},{4,7},{9,8},{10,9},{11,1... | collective-permute-start | bytes 122888 | tf_op jit(solution)/shard_map/ppermute | solution.py:443
  10.5 6.3 %all-to-all-done.tiles_ref = f32[8,16,128]{2,1,0:T(8,128)S(1)} async-done(((f32[8,16,128]{2,1,0:T(8,128)}), f32[8,16,128]{2,1,0:T(8,128)S(1)}, u32[]{:S(2)}, u32[]{:S(2)}) %all-to-all-start) | async-done | bytes 65568 | tf_op jit(solution)/shard_map/all_to_all | solution.py:440
  16.7 0.0 copy-done
  16.7 0.0 copy-done.2
  16.7 0.0 copy-start.3
  16.7 1.4 %copy-done.3 = f32[1,8,5,5,16,128]{5,4,3,2,1,0:T(8,128)S(1)} copy-done((f32[1,8,5,5,16,128]{5,4,3,2,1,0:T(8,128)S(1)}, f32[1,8,5,5,16,128]{5,4,3,2,1,0:T(8,128)}, u32[]{:S(2)}) %copy-start.3) | copy-done | bytes 1638424
  18.1 0.0 copy-start.1
  18.1 0.0 copy-start.5
  18.2 0.0 copy-start.7
  18.2 2.8 %shard_map.96 = (f32[8,5,5,16,128]{4,3,2,1,0:T(8,128)S(1)}, f32[8,5,5,16,128]{4,3,2,1,0:T(8,128)S(1)}, f32[3,5,5,16,128]{4,3,2,1,0:T(8,128)S(1)}, f32[16,128]{1,0:T(8,128)S(1)}, f32[2,8,16,128]{3,2,1,0:T(8,128)S(1)}) custom-call(s32[8]{0:T(128)} %depth_hbm.1, s32[8]{0:T(128)} %east_hbm.1, f32[8,16,128]{2,1,0:T(8,128)S(1)} %all-to-all-done.tiles_ref, ...), custom_call_target="tpu_custom_call" | custom-call | flops 5000000000 | bytes 5000000 | tf_op jit(solution)/shard_map/pallas_call | solution.py:25
  21.0 0.0 collective-permute-done.above_ref
  21.0 0.0 copy-done.1
  21.0 0.0 copy-done.5
  21.0 0.0 copy-done.7
  21.0 1.0 %shard_map.97 = (f32[8,5,16,128]{3,2,1,0:T(8,128)S(1)}, f32[2,5,16,128]{3,2,1,0:T(8,128)S(1)}, f32[3,5,5,16,128]{4,3,2,1,0:T(8,128)S(1)}) custom-call(f32[3,5,5,16,128]{4,3,2,1,0:T(8,128)S(1)} %get-tuple-element.23.mats_ref, f32[16,128]{1,0:T(8,128)S(1)} %get-tuple-element.22.live_ref, f32[2,8,16,128]{3,2,1,0:T(8,128)S(1)} %get-tuple-element.24.pick_ref, ...), custom_call_target="tpu_custom_call" | custom-call | flops 1000000000 | bytes 1000000 | tf_op jit(solution)/shard_map/pallas_call | solution.py:25
  22.0 0.1 collective-permute-start.1
  22.1 0.5 collective-permute-start.3
  22.6 1.6 %collective-permute-done.3.ends_other_ref = f32[2,5,16,128]{3,2,1,0:T(8,128)S(1)} collective-permute-done((f32[2,5,16,128]{3,2,1,0:T(8,128)S(1)}, f32[2,5,16,128]{3,2,1,0:T(8,128)S(1)}, u32[]{:S(2)}, u32[]{:S(2)}) %collective-permute-start.3) | collective-permute-done | bytes 81952 | tf_op jit(solution)/shard_map/ppermute | solution.py:437
  24.2 0.0 collective-permute-done.1.other_ref.mats_other_ref
  24.3 1.6 %collective-permute-start.4 = (f32[1,5,16,128]{3,2,1,0:T(8,128)S(1)}, f32[1,5,16,128]{3,2,1,0:T(8,128)S(1)}, u32[]{:S(2)}, u32[]{:S(2)}) collective-permute-start(f32[1,5,16,128]{3,2,1,0:T(8,128)S(1)} %shard_map.99.pair_ref), channel_id=1, source_target_pairs={{0,2},{1,3},{2,0},{3,1},{4,6},{5,7},{6,4},{7,5},{8,10},{9,11},{10,... | collective-permute-start | bytes 122888 | tf_op jit(solution)/shard_map/ppermute | solution.py:437
  25.8 0.2 shard_map.98.beta_ref
  26.0 2.3 %collective-permute-done.4.pair_other_ref = f32[1,5,16,128]{3,2,1,0:T(8,128)S(1)} collective-permute-done((f32[1,5,16,128]{3,2,1,0:T(8,128)S(1)}, f32[1,5,16,128]{3,2,1,0:T(8,128)S(1)}, u32[]{:S(2)}, u32[]{:S(2)}) %collective-permute-start.4) | collective-permute-done | bytes 40992 | tf_op jit(solution)/shard_map/ppermute | solution.py:437
  28.4 1.6 %collective-permute-start.5 = (f32[1,5,16,128]{3,2,1,0:T(8,128)S(1)}, f32[1,5,16,128]{3,2,1,0:T(8,128)S(1)}, u32[]{:S(2)}, u32[]{:S(2)}) collective-permute-start(f32[1,5,16,128]{3,2,1,0:T(8,128)S(1)} %shard_map.100), channel_id=1, source_target_pairs={{0,2},{1,3},{2,0},{3,1},{4,6},{5,7},{6,4},{7,5},{8,10},{9,11},{10,... | collective-permute-start | bytes 122888 | tf_op jit(solution)/shard_map/ppermute | solution.py:437
  29.9 0.5 %collective-permute-start.2 = (f32[5,5,16,128]{3,2,1,0:T(8,128)S(1)}, f32[5,5,16,128]{3,2,1,0:T(8,128)S(1)}, u32[]{:S(2)}, u32[]{:S(2)}) collective-permute-start(f32[5,5,16,128]{3,2,1,0:T(8,128)S(1)} %shard_map.98.beta_ref), channel_id=1, source_target_pairs={{0,2},{1,3},{2,0},{3,1},{4,6},{5,7},{6,4},{7,5},{8,10},{9,11},{10,... | collective-permute-start | bytes 614408 | tf_op jit(solution)/shard_map/ppermute | solution.py:437
  30.4 2.4 %collective-permute-done.5.raised_ref = f32[1,5,16,128]{3,2,1,0:T(8,128)S(1)} collective-permute-done((f32[1,5,16,128]{3,2,1,0:T(8,128)S(1)}, f32[1,5,16,128]{3,2,1,0:T(8,128)S(1)}, u32[]{:S(2)}, u32[]{:S(2)}) %collective-permute-start.5) | collective-permute-done | bytes 40992 | tf_op jit(solution)/shard_map/ppermute | solution.py:437
  32.8 0.0 copy-start.4
  32.8 0.5 shard_map.101
  33.3 9.4 %all_to_all.10.tiles_ref = f32[8,16,128]{2,1,0:T(8,128)S(1)} all-to-all(f32[8,16,128]{2,1,0:T(8,128)S(1)} %get-tuple-element.31), channel_id=1, replica_groups=mesh['zone'=8,'ja'=4] {'zone'}, dimensions={0} | all-to-all | bytes 131072 | tf_op jit(solution)/shard_map/all_to_all | solution.py:440
  42.7 0.0 collective-permute-done.2.beta_ref
  42.7 0.0 copy-done.4
  42.7 1.0 %shard_map.102 = (f32[8,5,16,128]{3,2,1,0:T(8,128)S(1)}, f32[8,5,16,128]{3,2,1,0:T(8,128)S(1)}, f32[3,5,16,128]{3,2,1,0:T(8,128)S(1)}, f32[5,5,16,128]{3,2,1,0:T(8,128)S(1)}) custom-call(f32[5,5,16,128]{3,2,1,0:T(8,128)S(1)} %collective-permute-done.2.beta_ref, f32[16,128]{1,0:T(8,128)S(1)} %get-tuple-element.22.live_ref, ...), custom_call_target="tpu_custom_call" | custom-call | flops 1000000000 | bytes 1000000 | tf_op jit(solution)/shard_map/pallas_call | solution.py:25
  43.7 0.1 collective-permute-start.6
  43.8 1.3 %collective-permute-done.6.ends_other_ref = f32[3,5,16,128]{3,2,1,0:T(8,128)S(1)} collective-permute-done((f32[3,5,16,128]{3,2,1,0:T(8,128)S(1)}, f32[3,5,16,128]{3,2,1,0:T(8,128)S(1)}, u32[]{:S(2)}, u32[]{:S(2)}) %collective-permute-start.6) | collective-permute-done | bytes 122912 | tf_op jit(solution)/shard_map/ppermute | solution.py:437
  45.2 1.7 %collective-permute-start.7 = (f32[2,5,16,128]{3,2,1,0:T(8,128)S(1)}, f32[2,5,16,128]{3,2,1,0:T(8,128)S(1)}, u32[]{:S(2)}, u32[]{:S(2)}) collective-permute-start(f32[2,5,16,128]{3,2,1,0:T(8,128)S(1)} %shard_map.103.pair_ref), channel_id=1, source_target_pairs={{0,2},{1,3},{2,0},{3,1},{4,6},{5,7},{6,4},{7,5},{8,10},{9,11},{10,... | collective-permute-start | bytes 245768 | tf_op jit(solution)/shard_map/ppermute | solution.py:437
  46.8 0.7 %shard_map.104.res_in_hbm = f32[8,5,16,128]{3,2,1,0:T(8,128)} custom-call(f32[8,5,16,128]{3,2,1,0:T(8,128)S(1)} %get-tuple-element.35.res_ref), custom_call_target="tpu_custom_call" | custom-call | flops 1000000000 | bytes 1000000 | tf_op jit(solution)/shard_map/pallas_call | solution.py:25
  47.6 2.2 %collective-permute-done.7.pair_other_ref = f32[2,5,16,128]{3,2,1,0:T(8,128)S(1)} collective-permute-done((f32[2,5,16,128]{3,2,1,0:T(8,128)S(1)}, f32[2,5,16,128]{3,2,1,0:T(8,128)S(1)}, u32[]{:S(2)}, u32[]{:S(2)}) %collective-permute-start.7) | collective-permute-done | bytes 81952 | tf_op jit(solution)/shard_map/ppermute | solution.py:437
  49.7 1.1 %shard_map.105 = (f32[8,5,16,128]{3,2,1,0:T(8,128)}, f32[8,5,16,128]{3,2,1,0:T(8,128)}) custom-call(f32[16,128]{1,0:T(8,128)S(1)} %get-tuple-element.22.live_ref, f32[5,5,16,128]{3,2,1,0:T(8,128)S(1)} %get-tuple-element.34.low0_ref, f32[8,5,16,128]{3,2,1,0:T(8,128)S(1)} %get-tuple-element.32.cur_ref, ...), custom_call_target="tpu_custom_call", output_to_operand_aliasing={{1}: (14, {})} | custom-call | flops 1000000000 | bytes 1000000 | tf_op jit(solution)/shard_map/pallas_call | solution.py:25
  (3 shorter events, 0.1 us)
Async XLA Ops:
  0.6 1.0 %copy-start.6 = (f32[1,8,5,16,128]{4,3,2,1,0:T(8,128)S(1)}, f32[1,8,5,16,128]{4,3,2,1,0:T(8,128)}, u32[]{:S(2)}) copy-start(f32[1,8,5,16,128]{4,3,2,1,0:T(8,128)} %param.8) | copy-start | bytes 983044
  1.6 15.1 %copy-start = (f32[1,8,5,5,16,128]{5,4,3,2,1,0:T(8,128)S(1)}, f32[1,8,5,5,16,128]{5,4,3,2,1,0:T(8,128)}, u32[]{:S(2)}) copy-start(f32[1,8,5,5,16,128]{5,4,3,2,1,0:T(8,128)} %param.13) | copy-start | bytes 4915204
  1.6 15.1 %copy-start.2 = (f32[1,8,5,5,16,128]{5,4,3,2,1,0:T(8,128)S(1)}, f32[1,8,5,5,16,128]{5,4,3,2,1,0:T(8,128)}, u32[]{:S(2)}) copy-start(f32[1,8,5,5,16,128]{5,4,3,2,1,0:T(8,128)} %param.11) | copy-start | bytes 4915204
  2.4 14.3 %all-to-all-start = ((f32[8,16,128]{2,1,0:T(8,128)}), f32[8,16,128]{2,1,0:T(8,128)S(1)}, u32[]{:S(2)}, u32[]{:S(2)}) async-start(f32[8,16,128]{2,1,0:T(8,128)} %get-tuple-element.21), calls=%async_computation | async-start | bytes 131072 | tf_op jit(solution)/shard_map/all_to_all | solution.py:440
  9.8 11.2 %collective-permute-start = (f32[5,16,128]{2,1,0:T(8,128)S(1)}, f32[5,16,128]{2,1,0:T(8,128)S(1)}, u32[]{:S(2)}, u32[]{:S(2)}) collective-permute-start(f32[5,16,128]{2,1,0:T(8,128)S(1)} %get-tuple-element.25), channel_id=1, source_target_pairs={{1,0},{2,1},{3,2},{0,3},{5,4},{6,5},{7,6},{4,7},{9,8},{10,9},{11,1... | collective-permute-start | bytes 122888 | tf_op jit(solution)/shard_map/ppermute | solution.py:443
  16.7 1.4 %copy-start.3 = (f32[1,8,5,5,16,128]{5,4,3,2,1,0:T(8,128)S(1)}, f32[1,8,5,5,16,128]{5,4,3,2,1,0:T(8,128)}, u32[]{:S(2)}) copy-start(f32[1,8,5,5,16,128]{5,4,3,2,1,0:T(8,128)} %param.12) | copy-start | bytes 4915204
  18.1 2.8 %copy-start.1 = (f32[1,8,5,5,16,128]{5,4,3,2,1,0:T(8,128)S(1)}, f32[1,8,5,5,16,128]{5,4,3,2,1,0:T(8,128)}, u32[]{:S(2)}) copy-start(f32[1,8,5,5,16,128]{5,4,3,2,1,0:T(8,128)} %param.10) | copy-start | bytes 4915204
  18.1 2.8 %copy-start.5 = (f32[1,8,5,16,128]{4,3,2,1,0:T(8,128)S(1)}, f32[1,8,5,16,128]{4,3,2,1,0:T(8,128)}, u32[]{:S(2)}) copy-start(f32[1,8,5,16,128]{4,3,2,1,0:T(8,128)} %param.9) | copy-start | bytes 983044
  18.2 2.9 %copy-start.7 = (f32[1,8,5,16,128]{4,3,2,1,0:T(8,128)S(1)}, f32[1,8,5,16,128]{4,3,2,1,0:T(8,128)}, u32[]{:S(2)}) copy-start(f32[1,8,5,16,128]{4,3,2,1,0:T(8,128)} %param.8) | copy-start | bytes 983044
  22.0 2.2 %collective-permute-start.1 = (f32[3,5,5,16,128]{4,3,2,1,0:T(8,128)S(1)}, f32[3,5,5,16,128]{4,3,2,1,0:T(8,128)S(1)}, u32[]{:S(2)}, u32[]{:S(2)}) collective-permute-start(f32[3,5,5,16,128]{4,3,2,1,0:T(8,128)S(1)} %get-tuple-element.28.mine_ref.mats_ref), channel_id=1, source_target_pairs={{0,1},{1,0},{2,3},{3,2},{4,5},{5,4},{6,7},{7,6},{8,9},{9,8},{10,11... | collective-permute-start | bytes 1843208 | tf_op jit(solution)/shard_map/ppermute | solution.py:437
  22.1 2.1 %collective-permute-start.3 = (f32[2,5,16,128]{3,2,1,0:T(8,128)S(1)}, f32[2,5,16,128]{3,2,1,0:T(8,128)S(1)}, u32[]{:S(2)}, u32[]{:S(2)}) collective-permute-start(f32[2,5,16,128]{3,2,1,0:T(8,128)S(1)} %get-tuple-element.30.ends_ref), channel_id=1, source_target_pairs={{0,1},{1,0},{2,3},{3,2},{4,5},{5,4},{6,7},{7,6},{8,9},{9,8},{10,11... | collective-permute-start | bytes 245768 | tf_op jit(solution)/shard_map/ppermute | solution.py:437
  24.3 4.1 %collective-permute-start.4 = (f32[1,5,16,128]{3,2,1,0:T(8,128)S(1)}, f32[1,5,16,128]{3,2,1,0:T(8,128)S(1)}, u32[]{:S(2)}, u32[]{:S(2)}) collective-permute-start(f32[1,5,16,128]{3,2,1,0:T(8,128)S(1)} %shard_map.99.pair_ref), channel_id=1, source_target_pairs={{0,2},{1,3},{2,0},{3,1},{4,6},{5,7},{6,4},{7,5},{8,10},{9,11},{10,... | collective-permute-start | bytes 122888 | tf_op jit(solution)/shard_map/ppermute | solution.py:437
  28.4 4.5 %collective-permute-start.5 = (f32[1,5,16,128]{3,2,1,0:T(8,128)S(1)}, f32[1,5,16,128]{3,2,1,0:T(8,128)S(1)}, u32[]{:S(2)}, u32[]{:S(2)}) collective-permute-start(f32[1,5,16,128]{3,2,1,0:T(8,128)S(1)} %shard_map.100), channel_id=1, source_target_pairs={{0,2},{1,3},{2,0},{3,1},{4,6},{5,7},{6,4},{7,5},{8,10},{9,11},{10,... | collective-permute-start | bytes 122888 | tf_op jit(solution)/shard_map/ppermute | solution.py:437
  29.9 12.8 %collective-permute-start.2 = (f32[5,5,16,128]{3,2,1,0:T(8,128)S(1)}, f32[5,5,16,128]{3,2,1,0:T(8,128)S(1)}, u32[]{:S(2)}, u32[]{:S(2)}) collective-permute-start(f32[5,5,16,128]{3,2,1,0:T(8,128)S(1)} %shard_map.98.beta_ref), channel_id=1, source_target_pairs={{0,2},{1,3},{2,0},{3,1},{4,6},{5,7},{6,4},{7,5},{8,10},{9,11},{10,... | collective-permute-start | bytes 614408 | tf_op jit(solution)/shard_map/ppermute | solution.py:437
  32.8 9.9 %copy-start.4 = (f32[1,8,5,5,16,128]{5,4,3,2,1,0:T(8,128)S(1)}, f32[1,8,5,5,16,128]{5,4,3,2,1,0:T(8,128)}, u32[]{:S(2)}) copy-start(f32[1,8,5,5,16,128]{5,4,3,2,1,0:T(8,128)} %param.12) | copy-start | bytes 4915204
  43.7 1.4 %collective-permute-start.6 = (f32[3,5,16,128]{3,2,1,0:T(8,128)S(1)}, f32[3,5,16,128]{3,2,1,0:T(8,128)S(1)}, u32[]{:S(2)}, u32[]{:S(2)}) collective-permute-start(f32[3,5,16,128]{3,2,1,0:T(8,128)S(1)} %get-tuple-element.37.ends_ref), channel_id=1, source_target_pairs={{0,1},{1,0},{2,3},{3,2},{4,5},{5,4},{6,7},{7,6},{8,9},{9,8},{10,11... | collective-permute-start | bytes 368648 | tf_op jit(solution)/shard_map/ppermute | solution.py:437
  45.2 4.6 %collective-permute-start.7 = (f32[2,5,16,128]{3,2,1,0:T(8,128)S(1)}, f32[2,5,16,128]{3,2,1,0:T(8,128)S(1)}, u32[]{:S(2)}, u32[]{:S(2)}) collective-permute-start(f32[2,5,16,128]{3,2,1,0:T(8,128)S(1)} %shard_map.103.pair_ref), channel_id=1, source_target_pairs={{0,2},{1,3},{2,0},{3,1},{4,6},{5,7},{6,4},{7,5},{8,10},{9,11},{10,... | collective-permute-start | bytes 245768 | tf_op jit(solution)/shard_map/ppermute | solution.py:437

commit v7 on v6

--- a/solution.py
+++ b/solution.py
@@ -97,8 +97,12 @@
     return [jnp.where(inner, x, 0.0) for x in values]
 
 
-def pack_kernel(flow_ref, tile_ref, first_ref):
+def first_kernel(tiles_ref, flow_ref, first_ref):
+    del tiles_ref
     put(first_ref, cell(flow_ref, 0))
+
+
+def pack_kernel(flow_ref, tile_ref):
     pack_faces(lambda j, v: flow_ref[j, v], flow_ref.shape[0], tile_ref)
 
 
@@ -211,17 +215,22 @@
         run(*other_refs, *mine_refs)
 
 
-def beta_kernel(mine_ref, other_ref, beta_ref):
-    def run(lo, hi):
-        d_hi, n_lo = block(hi, 1), block(lo, 2)
-        for q in range(5):
-            m_col = [lo[0, r, q] for r in range(5)]
-            d_col = [lo[1, r, q] for r in range(5)]
-            out = add(d_col, matvec(n_lo, matvec(d_hi, m_col)))
-            for r in range(5):
-                beta_ref[r, q] = out[r]
-
-    by_place([mine_ref], [other_ref], run)
+def beta_kernel(mine_ref, other_ref, half_ref):
+    odd = lax.axis_index("ja") % 2
+    for side in range(2):
+        lo, hi = (mine_ref, other_ref) if side == 0 else (other_ref, mine_ref)
+        rows = pl.ds(8 * side, 8)
+
+        @pl.when(odd == side)
+        def _():
+            d_hi = [[hi[1, r, c, rows] for c in range(5)] for r in range(5)]
+            n_lo = [[lo[2, r, c, rows] for c in range(5)] for r in range(5)]
+            for q in range(5):
+                m_col = [lo[0, r, q, rows] for r in range(5)]
+                d_col = [lo[1, r, q, rows] for r in range(5)]
+                out = add(d_col, matvec(n_lo, matvec(d_hi, m_col)))
+                for r in range(5):
+                    half_ref[r, q] = out[r]
 
 
 def sweeps(s_ref, e_ref, f_ref, y_ref, ends_ref, last):
@@ -238,13 +247,10 @@
 
 
 def local_kernel(
-    mats_ref, live_ref, pick_ref, tiles_ref, cur_ref, above_ref, force_ref, diag_ref, inv_ref,
+    live_ref, pick_ref, tiles_ref, cur_ref, above_ref, force_ref, diag_ref, inv_ref,
     e_ref, f_ref,
-    s_ref, ends_ref, mats_out_ref, y_ref,
-):
-    for i in range(3):
-        for r in range(5):
-            put(mats_out_ref, cell(mats_ref, i, r), i, r)
+    s_ref, ends_ref, y_ref,
+):
     planes = cur_ref.shape[0]
     ghosts = ghosts_of(pick_ref, tiles_ref)
     before, here = None, masked(live_ref, cell(cur_ref, 0))
@@ -266,11 +272,11 @@
 
 
 def second_kernel(
-    beta_ref, live_ref, pick_ref, tiles_ref, cur_ref, above_ref, force_ref, diag_ref, low_ref, up_ref,
+    half_ref, live_ref, pick_ref, tiles_ref, cur_ref, above_ref, force_ref, diag_ref, low_ref, up_ref,
     inv_ref, e_ref, f_ref,
     res_ref, s_ref, ends_ref, low0_ref, y_ref,
 ):
-    del beta_ref
+    del half_ref
     planes = cur_ref.shape[0]
     ghosts = ghosts_of(pick_ref, tiles_ref)
     for r in range(5):
@@ -321,9 +327,22 @@
     by_place([ends_ref, mats_ref], [ends_other_ref, mats_other_ref], run)
 
 
-def raise_kernel(pair_ref, pair_other_ref, beta_ref, raised_ref):
-    beyond = add(cell(pair_ref, 0), matvec(block(beta_ref), cell(pair_other_ref, 0)))
-    put(raised_ref, beyond, 0)
+def raise_kernel(pair_ref, pair_other_ref, half_ref, raised_ref):
+    odd = lax.axis_index("ja") % 2
+    for side in range(2):
+        rows = pl.ds(8 * side, 8)
+
+        @pl.when(odd == side)
+        def _():
+            inflow = [pair_ref[0, v, rows] for v in range(5)]
+            alpha = [pair_other_ref[0, v, rows] for v in range(5)]
+            put(raised_ref, add(alpha, matvec(block(half_ref), inflow)))
+
+
+def join(mine_ref, other_ref, *at):
+    mine, other = mine_ref[at], other_ref[at]
+    odd = lax.axis_index("ja") % 2 == 1
+    return jnp.concatenate([jnp.where(odd, other, mine), jnp.where(odd, mine, other)], axis=0)
 
 
 def inflows(
@@ -361,13 +380,14 @@
 
 def final_kernel(
     live_ref, cur_ref, above_ref, s_ref, e_ref, f_ref,
-    ends_ref, ends_other_ref, mats_ref, mats_other_ref, pair_ref, pair_other_ref, raised_ref,
+    ends_ref, ends_other_ref, mats_ref, mats_other_ref, pair_ref, pair_other_ref,
+    raised_ref, raised_other_ref,
     new_ref, above_new_ref, tile_ref, y_ref, inflow_ref,
 ):
     planes = cur_ref.shape[0]
     inflows(
         ends_ref, ends_other_ref, mats_ref, mats_other_ref, pair_ref, pair_other_ref,
-        lambda: cell(raised_ref, 0), inflow_ref,
+        lambda: [join(raised_ref, raised_other_ref, v) for v in range(5)], inflow_ref,
     )
     value = cell(inflow_ref, 0)
     for j in range(planes):
@@ -384,8 +404,7 @@
 def last_kernel(
     live_ref, low0_ref, cur_ref, res_ref, s_ref, e_ref, f_ref,
     ends_ref, ends_other_ref, mats_ref, mats_other_ref, pair_ref, pair_other_ref,
-    beta_ref,
-    res_in_hbm,
+    half_ref, half_other_ref, res_in_hbm,
     new_hbm, res_hbm, y_ref, inflow_ref, new_ref, res0_ref, sems,
 ):
     del res_in_hbm
@@ -400,7 +419,8 @@
     copies[0].start()
 
     def far():
-        return add(cell(pair_other_ref, 0), matvec(block(beta_ref), cell(pair_ref, 0)))
+        beta = [[join(half_ref, half_other_ref, r, c) for c in range(5)] for r in range(5)]
+        return add(cell(pair_other_ref, 0), matvec(beta, cell(pair_ref, 0)))
 
     inflows(
         ends_ref, ends_other_ref, mats_ref, mats_other_ref, pair_ref, pair_other_ref,
@@ -439,9 +459,10 @@
     def faces(x):
         return lax.all_to_all(x, "zone", 0, 0, tiled=True)
 
-    tile, first = call(pack_kernel, [tiles, plane], flops=2 * 10**10)(current)
+    tile = call(pack_kernel, [tiles], flops=2 * 10**10)(current)[0]
+    got = faces(tile)
+    first = call(first_kernel, [plane], flops=10**5)(got, current)[0]
     above = lax.ppermute(first, "ja", [((p + 1) % parts, p) for p in range(parts)])
-    got = faces(tile)
     e, f, mats, live, pick = call(
         matrix_kernel,
         [blocks, blocks, (3, *matrix), state[2:], (2, *tiles)],
@@ -451,28 +472,29 @@
         flops=5 * 10**9,
         far=(0, 1),
     )(zone_depth, east_zone, got, inv, low, up)
-    s, ends, mats = call(local_kernel, [state, (2, *plane), mats.shape], work)(
-        mats, live, pick, got, current, above, force, diag, inv, e, f
+    mats_other = swap(mats, 1)
+    s, ends = call(local_kernel, [state, (2, *plane)], work, flops=2 * 10**10)(
+        live, pick, got, current, above, force, diag, inv, e, f
     )
     ends_other = swap(ends, 1)
-    mats_other = swap(mats, 1)
+    half = call(beta_kernel, [(*matrix[:2], 8, matrix[3])], flops=10**5)(mats, mats_other)[0]
+    half = swap(half, 2)
     pair = call(mid_kernel, [(1, *plane)], flops=10**5)(ends, ends_other, mats, mats_other)[0]
-    beta = call(beta_kernel, [matrix], flops=10**5)(mats, mats_other)[0]
     pair_other = swap(pair, 2)
-    raised = call(raise_kernel, [(1, *plane)], flops=10**5)(pair, pair_other, beta)[0]
-    raised = swap(raised, 2)
-    beta = swap(beta, 2)
+    raised = call(raise_kernel, [(plane[0], 8, plane[2])], flops=10**5)(pair, pair_other, half)[0]
+    raised_other = swap(raised, 1)
+    half_other = swap(half, 1)
     flows = [buffer(2, *plane)]
     current, above, tile = call(final_kernel, [state, plane, tiles], work + flows)(
         live, current, above, s, e, f,
-        ends, ends_other, mats, mats_other, pair, pair_other, raised,
+        ends, ends_other, mats, mats_other, pair, pair_other, raised, raised_other,
     )
 
     got = faces(tile)
     residual, s, ends, low0 = call(
         second_kernel, [state, state, (3, *plane), matrix], work
     )(
-        beta, live, pick, got, current, above, force, diag, low, up, inv, e, f
+        half_other, live, pick, got, current, above, force, diag, low, up, inv, e, f
     )
     ends_other = swap(ends, 1)
     pair = call(mid_kernel, [(2, *plane)])(ends, ends_other, mats, mats_other)[0]
@@ -483,10 +505,10 @@
         [state, state],
         work + flows + work + [buffer(*plane), pltpu.SemaphoreType.DMA((planes + 1,))],
         out_specs=[HBM, HBM],
-        alias={14: 1},
+        alias={15: 1},
     )(
         live, low0, current, residual, s, e, f,
-        ends, ends_other, mats, mats_other, pair, pair_other, beta, written,
+        ends, ends_other, mats, mats_other, pair, pair_other, half, half_other, written,
     )
     return (current[None], residual[None])
 

time: 51.1 us -> 59.1 us (1.16)
  local copies, waits for them, and re-layouts: 2.42 us -> 11.7 us
  starting transfers between devices: 14 us -> 8.07 us
  blocking collectives: 9.42 us -> 14.2 us
    unnamed x16 -> x44, local copies, waits for them, and re-layouts: 2.42 us -> 11.7 us
    all_to_all x1, blocking collectives: 9.42 us -> 14.2 us  [faces(): return lax.all_to_all(x, 'zone', 0, 0, tiled=True)]
    all_to_all x1, starting transfers between devices: 7.41 us -> 3.35 us  [faces(): return lax.all_to_all(x, 'zone', 0, 0, tiled=True)]
    ppermute x7 -> x8, starting transfers between devices: 5.96 us -> 4.72 us  [swap(): return lax.ppermute(x, 'ja', [(p, p ^ bit) for p in range(parts)])]
    all_to_all x1, waiting for transfers between devices: 6.25 us -> 5.47 us  [faces(): return lax.all_to_all(x, 'zone', 0, 0, tiled=True)]
    ppermute x1, starting transfers between devices: 0.65 us -> 0.01 us  [per_device(): lax.ppermute(first, 'ja', [((p + 1) % parts, p) for p in range(parts)])]
    ppermute x7 -> x8, waiting for transfers between devices: 9.85 us -> 10.4 us  [swap(): return lax.ppermute(x, 'ja', [(p, p ^ bit) for p in range(parts)])]
    pallas_call x11 -> x12, Pallas kernels: 8.08 us -> 7.84 us  [run(): pl.pallas_call(kernel, out_shape=[jax.ShapeDtypeStruct(s, jnp.float32) fo...]
  transfers between devices with their start and end apart: 9 -> 10, of which waited for: 6 -> 7; matrix products, arithmetic and copies ran while one was open for 0% -> 0% of each run, Pallas kernels for 8% -> 8%
where the time goes in v7:
time: 59.1 us; the launch traced here: 58.6 us
  waiting for transfers between devices  15.9 us (27%)
  blocking collectives  14.2 us (24%)
  local copies, waits for them, and re-layouts  11.7 us (20%)
  starting transfers between devices  8.07 us (14%)
  Pallas kernels  7.84 us (13%)
  between operations  0.83 us (1%)
    all_to_all x1, blocking collectives, faces(): return lax.all_to_all(x, 'zone', 0, 0, tiled=True)  14.2 us
    unnamed x44, local copies, waits for them, and re-layouts  11.7 us
    ppermute x8, waiting for transfers between devices, swap(): return lax.ppermute(x, 'ja', [(p, p ^ bit) for p in range(parts)])  10.4 us
    pallas_call x12, Pallas kernels, run(): pl.pallas_call(kernel, out_shape=[jax.ShapeDtypeStruct(s, jnp.float32) fo...  7.84 us
    all_to_all x1, waiting for transfers between devices, faces(): return lax.all_to_all(x, 'zone', 0, 0, tiled=True)  5.47 us
    ppermute x8, starting transfers between devices, swap(): return lax.ppermute(x, 'ja', [(p, p ^ bit) for p in range(parts)])  4.72 us
    all_to_all x1, starting transfers between devices, faces(): return lax.all_to_all(x, 'zone', 0, 0, tiled=True)  3.35 us
  transfers between devices with their start and end apart: 10, of which 7 were waited for; matrix products, arithmetic and copies ran while one was open for 0% of the time, Pallas kernels for 8%

profile of v7, /device:TPU:0, one launch (start us, length us, event | category | flops | bytes accessed | tf_op | source)
XLA Modules:
  0.0 58.6 jit_solution(3385104607632640284)
XLA Ops:
  0.6 0.0 copy-start.14
  0.6 1.0 %copy-done.14 = f32[1,8,5,16,128]{4,3,2,1,0:T(8,128)S(1)} copy-done((f32[1,8,5,16,128]{4,3,2,1,0:T(8,128)S(1)}, f32[1,8,5,16,128]{4,3,2,1,0:T(8,128)}, u32[]{:S(2)}) %copy-start.14) | copy-done | bytes 327704
  1.6 0.0 copy-start.4
  1.6 0.0 copy-start.6
  1.6 0.0 copy-start.8
  1.6 0.1 shard_map.95
  1.8 14.2 %all_to_all.10.tiles_ref = f32[8,16,128]{2,1,0:T(8,128)S(1)} all-to-all(f32[8,16,128]{2,1,0:T(8,128)S(1)} %shard_map.95), channel_id=1, replica_groups=mesh['zone'=8,'ja'=4] {'zone'}, dimensions={0} | all-to-all | bytes 131072 | tf_op jit(solution)/shard_map/all_to_all | solution.py:460
  16.0 0.0 collective-permute-start.3
  16.0 0.0 copy-done.4
  16.0 0.0 copy-done.6
  16.0 0.0 copy-done.8
  16.0 0.0 copy-start.10
  16.1 0.0 copy-start.15
  16.1 0.0 copy-start.16
  16.1 2.8 %shard_map.96 = (f32[8,5,5,16,128]{4,3,2,1,0:T(8,128)S(1)}, f32[8,5,5,16,128]{4,3,2,1,0:T(8,128)S(1)}, f32[3,5,5,16,128]{4,3,2,1,0:T(8,128)S(1)}, f32[16,128]{1,0:T(8,128)S(1)}, f32[2,8,16,128]{3,2,1,0:T(8,128)S(1)}) custom-call(s32[8]{0:T(128)} %depth_hbm.1, s32[8]{0:T(128)} %east_hbm.1, f32[8,16,128]{2,1,0:T(8,128)S(1)} %all_to_all.10.tiles_ref, ...), custom_call_target="tpu_custom_call" | custom-call | flops 5000000000 | bytes 5000000 | tf_op jit(solution)/shard_map/pallas_call | solution.py:25
  18.9 0.0 copy-start.18
  18.9 0.0 copy-start
  18.9 0.6 collective-permute-start
  19.5 0.0 collective-permute-done.3.above_ref
  19.5 0.0 copy-done.10
  19.5 0.0 copy-done.15
  19.5 0.0 copy-done.16
  19.5 0.9 %shard_map.99 = (f32[8,5,16,128]{3,2,1,0:T(8,128)S(1)}, f32[2,5,16,128]{3,2,1,0:T(8,128)S(1)}) custom-call(f32[16,128]{1,0:T(8,128)S(1)} %get-tuple-element.18.live_ref, f32[2,8,16,128]{3,2,1,0:T(8,128)S(1)} %get-tuple-element.20.pick_ref, f32[8,16,128]{2,1,0:T(8,128)S(1)} %all_to_all.10.tiles_ref, f32[8,5,16,128]{3,2,1,0:T(8,128)S(1)} %bitcast.19, ...), custom_call_target="tpu_custom_call" | custom-call | flops 20000000000 | bytes 20000000 | tf_op jit(solution)/shard_map/pallas_call | solution.py:25
  20.4 0.0 copy-done.18
  20.4 0.1 collective-permute-start.4
  20.5 0.6 %collective-permute-done.other_ref.mats_other_ref = f32[3,5,5,16,128]{4,3,2,1,0:T(8,128)S(1)} collective-permute-done((f32[3,5,5,16,128]{4,3,2,1,0:T(8,128)S(1)}, f32[3,5,5,16,128]{4,3,2,1,0:T(8,128)S(1)}, u32[]{:S(2)}, u32[]{:S(2)}) %collective-permute-start) | collective-permute-done | bytes 614432 | tf_op jit(solution)/shard_map/ppermute | solution.py:457
  21.1 0.0 copy-start.2
  21.1 0.1 shard_map.97
  21.2 1.6 %collective-permute-start.1 = (f32[5,5,8,128]{3,2,1,0:T(8,128)S(1)}, f32[5,5,8,128]{3,2,1,0:T(8,128)S(1)}, u32[]{:S(2)}, u32[]{:S(2)}) collective-permute-start(f32[5,5,8,128]{3,2,1,0:T(8,128)S(1)} %shard_map.97), channel_id=1, source_target_pairs={{0,2},{1,3},{2,0},{3,1},{4,6},{5,7},{6,4},{7,5},{8,10},{9,11},{10,... | collective-permute-start | bytes 307208 | tf_op jit(solution)/shard_map/ppermute | solution.py:457
  22.8 0.0 collective-permute-done.4.ends_other_ref
  22.8 0.6 %collective-permute-start.5 = (f32[1,5,16,128]{3,2,1,0:T(8,128)S(1)}, f32[1,5,16,128]{3,2,1,0:T(8,128)S(1)}, u32[]{:S(2)}, u32[]{:S(2)}) collective-permute-start(f32[1,5,16,128]{3,2,1,0:T(8,128)S(1)} %shard_map.100.pair_ref), channel_id=1, source_target_pairs={{0,2},{1,3},{2,0},{3,1},{4,6},{5,7},{6,4},{7,5},{8,10},{9,11},{10,... | collective-permute-start | bytes 122888 | tf_op jit(solution)/shard_map/ppermute | solution.py:457
  23.4 3.9 %collective-permute-done.5.pair_other_ref = f32[1,5,16,128]{3,2,1,0:T(8,128)S(1)} collective-permute-done((f32[1,5,16,128]{3,2,1,0:T(8,128)S(1)}, f32[1,5,16,128]{3,2,1,0:T(8,128)S(1)}, u32[]{:S(2)}, u32[]{:S(2)}) %collective-permute-start.5) | collective-permute-done | bytes 40992 | tf_op jit(solution)/shard_map/ppermute | solution.py:457
  27.3 0.0 collective-permute-done.1.half_ref
  27.4 0.1 collective-permute-start.6
  27.4 1.2 %collective-permute-done.6.raised_other_ref = f32[5,8,128]{2,1,0:T(8,128)S(1)} collective-permute-done((f32[5,8,128]{2,1,0:T(8,128)S(1)}, f32[5,8,128]{2,1,0:T(8,128)S(1)}, u32[]{:S(2)}, u32[]{:S(2)}) %collective-permute-start.6) | collective-permute-done | bytes 20512 | tf_op jit(solution)/shard_map/ppermute | solution.py:457
  28.6 0.0 copy-done
  28.6 1.0 %shard_map.102 = (f32[8,5,16,128]{3,2,1,0:T(8,128)S(1)}, f32[5,16,128]{2,1,0:T(8,128)S(1)}, f32[8,16,128]{2,1,0:T(8,128)}) custom-call(f32[16,128]{1,0:T(8,128)S(1)} %get-tuple-element.18.live_ref, f32[8,5,16,128]{3,2,1,0:T(8,128)S(1)} %bitcast.20, f32[5,16,128]{2,1,0:T(8,128)S(1)} %collective-permute-done.3.above_ref, ...), custom_call_target="tpu_custom_call" | custom-call | flops 1000000000 | bytes 1000000 | tf_op jit(solution)/shard_map/pallas_call | solution.py:25
  29.6 0.0 copy-done.2
  29.6 0.0 copy-start.12
  29.6 0.7 %copy-done.12 = f32[8,5,16,128]{3,2,1,0:T(8,128)} copy-done((f32[8,5,16,128]{3,2,1,0:T(8,128)}, f32[8,5,16,128]{3,2,1,0:T(8,128)S(1)}, u32[]{:S(2)}) %copy-start.12) | copy-done | bytes 327704
  30.4 0.0 copy-start.20
  30.4 0.6 %copy-done.20 = f32[5,16,128]{2,1,0:T(8,128)} copy-done((f32[5,16,128]{2,1,0:T(8,128)}, f32[5,16,128]{2,1,0:T(8,128)S(1)}, u32[]{:S(2)}) %copy-start.20) | copy-done | bytes 40984
  31.0 3.3 %all-to-all-start.1 = ((f32[8,16,128]{2,1,0:T(8,128)}), f32[8,16,128]{2,1,0:T(8,128)S(1)}, u32[]{:S(2)}, u32[]{:S(2)}) async-start(f32[8,16,128]{2,1,0:T(8,128)} %get-tuple-element.25), calls=%async_computation.1 | async-start | bytes 131072 | tf_op jit(solution)/shard_map/all_to_all | solution.py:460
  34.3 0.2 collective-permute-start.2
  34.5 1.2 %collective-permute-done.2.half_ref.half_other_ref = f32[5,5,8,128]{3,2,1,0:T(8,128)S(1)} collective-permute-done((f32[5,5,8,128]{3,2,1,0:T(8,128)S(1)}, f32[5,5,8,128]{3,2,1,0:T(8,128)S(1)}, u32[]{:S(2)}, u32[]{:S(2)}) %collective-permute-start.2) | collective-permute-done | bytes 102432 | tf_op jit(solution)/shard_map/ppermute | solution.py:457
  35.7 5.5 %all-to-all-done.1.tiles_ref = f32[8,16,128]{2,1,0:T(8,128)S(1)} async-done(((f32[8,16,128]{2,1,0:T(8,128)}), f32[8,16,128]{2,1,0:T(8,128)S(1)}, u32[]{:S(2)}, u32[]{:S(2)}) %all-to-all-start.1) | async-done | bytes 65568 | tf_op jit(solution)/shard_map/all_to_all | solution.py:460
  41.2 1.4 %copy-done.5 = f32[1,8,5,5,16,128]{5,4,3,2,1,0:T(8,128)S(1)} copy-done((f32[1,8,5,5,16,128]{5,4,3,2,1,0:T(8,128)S(1)}, f32[1,8,5,5,16,128]{5,4,3,2,1,0:T(8,128)}, u32[]{:S(2)}) %copy-start.5) | copy-done | bytes 1638424
  42.6 0.0 copy-start.7
  42.6 1.4 %copy-done.7 = f32[1,8,5,5,16,128]{5,4,3,2,1,0:T(8,128)S(1)} copy-done((f32[1,8,5,5,16,128]{5,4,3,2,1,0:T(8,128)S(1)}, f32[1,8,5,5,16,128]{5,4,3,2,1,0:T(8,128)}, u32[]{:S(2)}) %copy-start.7) | copy-done | bytes 1638424
  44.0 1.4 %copy-done.9 = f32[1,8,5,5,16,128]{5,4,3,2,1,0:T(8,128)S(1)} copy-done((f32[1,8,5,5,16,128]{5,4,3,2,1,0:T(8,128)S(1)}, f32[1,8,5,5,16,128]{5,4,3,2,1,0:T(8,128)}, u32[]{:S(2)}) %copy-start.9) | copy-done | bytes 1638424
  45.5 1.4 %copy-done.11 = f32[1,8,5,5,16,128]{5,4,3,2,1,0:T(8,128)S(1)} copy-done((f32[1,8,5,5,16,128]{5,4,3,2,1,0:T(8,128)S(1)}, f32[1,8,5,5,16,128]{5,4,3,2,1,0:T(8,128)}, u32[]{:S(2)}) %copy-start.11) | copy-done | bytes 1638424
  46.9 1.0 %copy-done.13 = f32[8,5,16,128]{3,2,1,0:T(8,128)S(1)} copy-done((f32[8,5,16,128]{3,2,1,0:T(8,128)S(1)}, f32[8,5,16,128]{3,2,1,0:T(8,128)}, u32[]{:S(2)}) %copy-start.13) | copy-done | bytes 327704
  47.9 1.0 %copy-done.17 = f32[1,8,5,16,128]{4,3,2,1,0:T(8,128)S(1)} copy-done((f32[1,8,5,16,128]{4,3,2,1,0:T(8,128)S(1)}, f32[1,8,5,16,128]{4,3,2,1,0:T(8,128)}, u32[]{:S(2)}) %copy-start.17) | copy-done | bytes 327704
  48.9 0.9 %copy-done.19 = f32[2,8,16,128]{3,2,1,0:T(8,128)S(1)} copy-done((f32[2,8,16,128]{3,2,1,0:T(8,128)S(1)}, f32[2,8,16,128]{3,2,1,0:T(8,128)}, u32[]{:S(2)}) %copy-start.19) | copy-done | bytes 131096
  49.8 0.8 %copy-done.21 = f32[5,16,128]{2,1,0:T(8,128)S(1)} copy-done((f32[5,16,128]{2,1,0:T(8,128)S(1)}, f32[5,16,128]{2,1,0:T(8,128)}, u32[]{:S(2)}) %copy-start.21) | copy-done | bytes 40984
  50.5 1.0 %shard_map.103 = (f32[8,5,16,128]{3,2,1,0:T(8,128)S(1)}, f32[8,5,16,128]{3,2,1,0:T(8,128)S(1)}, f32[3,5,16,128]{3,2,1,0:T(8,128)S(1)}, f32[5,5,16,128]{3,2,1,0:T(8,128)S(1)}) custom-call(f32[5,5,8,128]{3,2,1,0:T(8,128)S(1)} %collective-permute-done.2.half_ref.half_other_ref, f32[16,128]{1,0:T(8,128)S(1)} %get-tuple-element.18.live_ref, ...), custom_call_target="tpu_custom_call" | custom-call | flops 1000000000 | bytes 1000000 | tf_op jit(solution)/shard_map/pallas_call | solution.py:25
  51.5 0.1 collective-permute-start.7
  51.6 1.3 %collective-permute-done.7.ends_other_ref = f32[3,5,16,128]{3,2,1,0:T(8,128)S(1)} collective-permute-done((f32[3,5,16,128]{3,2,1,0:T(8,128)S(1)}, f32[3,5,16,128]{3,2,1,0:T(8,128)S(1)}, u32[]{:S(2)}, u32[]{:S(2)}) %collective-permute-start.7) | collective-permute-done | bytes 122912 | tf_op jit(solution)/shard_map/ppermute | solution.py:457
  52.9 0.0 copy-done.1
  52.9 0.0 copy-done.3
  53.0 1.6 %collective-permute-start.8 = (f32[2,5,16,128]{3,2,1,0:T(8,128)S(1)}, f32[2,5,16,128]{3,2,1,0:T(8,128)S(1)}, u32[]{:S(2)}, u32[]{:S(2)}) collective-permute-start(f32[2,5,16,128]{3,2,1,0:T(8,128)S(1)} %shard_map.104.pair_ref), channel_id=1, source_target_pairs={{0,2},{1,3},{2,0},{3,1},{4,6},{5,7},{6,4},{7,5},{8,10},{9,11},{10,... | collective-permute-start | bytes 245768 | tf_op jit(solution)/shard_map/ppermute | solution.py:457
  54.5 0.7 %shard_map.105.res_in_hbm = f32[8,5,16,128]{3,2,1,0:T(8,128)} custom-call(f32[8,5,16,128]{3,2,1,0:T(8,128)S(1)} %get-tuple-element.29.res_ref), custom_call_target="tpu_custom_call" | custom-call | flops 1000000000 | bytes 1000000 | tf_op jit(solution)/shard_map/pallas_call | solution.py:25
  55.2 2.3 %collective-permute-done.8.pair_other_ref = f32[2,5,16,128]{3,2,1,0:T(8,128)S(1)} collective-permute-done((f32[2,5,16,128]{3,2,1,0:T(8,128)S(1)}, f32[2,5,16,128]{3,2,1,0:T(8,128)S(1)}, u32[]{:S(2)}, u32[]{:S(2)}) %collective-permute-start.8) | collective-permute-done | bytes 81952 | tf_op jit(solution)/shard_map/ppermute | solution.py:457
  57.5 1.1 %shard_map.106 = (f32[8,5,16,128]{3,2,1,0:T(8,128)}, f32[8,5,16,128]{3,2,1,0:T(8,128)}) custom-call(f32[16,128]{1,0:T(8,128)S(1)} %get-tuple-element.18.live_ref, f32[5,5,16,128]{3,2,1,0:T(8,128)S(1)} %get-tuple-element.28.low0_ref, f32[8,5,16,128]{3,2,1,0:T(8,128)S(1)} %copy-done.13, ...), custom_call_target="tpu_custom_call", output_to_operand_aliasing={{1}: (15, {})} | custom-call | flops 1000000000 | bytes 1000000 | tf_op jit(solution)/shard_map/pallas_call | solution.py:25
  (13 shorter events, 0.1 us)
Async XLA Ops:
  0.6 1.0 %copy-start.14 = (f32[1,8,5,16,128]{4,3,2,1,0:T(8,128)S(1)}, f32[1,8,5,16,128]{4,3,2,1,0:T(8,128)}, u32[]{:S(2)}) copy-start(f32[1,8,5,16,128]{4,3,2,1,0:T(8,128)} %param.8) | copy-start | bytes 983044
  1.6 14.4 %copy-start.4 = (f32[1,8,5,5,16,128]{5,4,3,2,1,0:T(8,128)S(1)}, f32[1,8,5,5,16,128]{5,4,3,2,1,0:T(8,128)}, u32[]{:S(2)}) copy-start(f32[1,8,5,5,16,128]{5,4,3,2,1,0:T(8,128)} %param.13) | copy-start | bytes 4915204
  1.6 14.4 %copy-start.6 = (f32[1,8,5,5,16,128]{5,4,3,2,1,0:T(8,128)S(1)}, f32[1,8,5,5,16,128]{5,4,3,2,1,0:T(8,128)}, u32[]{:S(2)}) copy-start(f32[1,8,5,5,16,128]{5,4,3,2,1,0:T(8,128)} %param.11) | copy-start | bytes 4915204
  1.6 14.4 %copy-start.8 = (f32[1,8,5,5,16,128]{5,4,3,2,1,0:T(8,128)S(1)}, f32[1,8,5,5,16,128]{5,4,3,2,1,0:T(8,128)}, u32[]{:S(2)}) copy-start(f32[1,8,5,5,16,128]{5,4,3,2,1,0:T(8,128)} %param.12) | copy-start | bytes 4915204
  16.0 3.5 %collective-permute-start.3 = (f32[5,16,128]{2,1,0:T(8,128)S(1)}, f32[5,16,128]{2,1,0:T(8,128)S(1)}, u32[]{:S(2)}, u32[]{:S(2)}) collective-permute-start(f32[5,16,128]{2,1,0:T(8,128)S(1)} %shard_map.98), channel_id=1, source_target_pairs={{1,0},{2,1},{3,2},{0,3},{5,4},{6,5},{7,6},{4,7},{9,8},{10,9},{11,1... | collective-permute-start | bytes 122888 | tf_op jit(solution)/shard_map/ppermute | solution.py:465
  16.0 3.4 %copy-start.10 = (f32[1,8,5,5,16,128]{5,4,3,2,1,0:T(8,128)S(1)}, f32[1,8,5,5,16,128]{5,4,3,2,1,0:T(8,128)}, u32[]{:S(2)}) copy-start(f32[1,8,5,5,16,128]{5,4,3,2,1,0:T(8,128)} %param.10) | copy-start | bytes 4915204
  16.1 3.4 %copy-start.15 = (f32[1,8,5,16,128]{4,3,2,1,0:T(8,128)S(1)}, f32[1,8,5,16,128]{4,3,2,1,0:T(8,128)}, u32[]{:S(2)}) copy-start(f32[1,8,5,16,128]{4,3,2,1,0:T(8,128)} %param.8) | copy-start | bytes 983044
  16.1 3.4 %copy-start.16 = (f32[1,8,5,16,128]{4,3,2,1,0:T(8,128)S(1)}, f32[1,8,5,16,128]{4,3,2,1,0:T(8,128)}, u32[]{:S(2)}) copy-start(f32[1,8,5,16,128]{4,3,2,1,0:T(8,128)} %param.9) | copy-start | bytes 983044
  18.9 1.5 %copy-start.18 = (f32[2,8,16,128]{3,2,1,0:T(8,128)}, f32[2,8,16,128]{3,2,1,0:T(8,128)S(1)}, u32[]{:S(2)}) copy-start(f32[2,8,16,128]{3,2,1,0:T(8,128)S(1)} %get-tuple-element.20.pick_ref) | copy-start | bytes 393220
  18.9 9.7 %copy-start = (f32[3,5,5,16,128]{4,3,2,1,0:T(8,128)}, f32[3,5,5,16,128]{4,3,2,1,0:T(8,128)S(1)}, u32[]{:S(2)}) copy-start(f32[3,5,5,16,128]{4,3,2,1,0:T(8,128)S(1)} %get-tuple-element.19.mine_ref.mats_ref) | copy-start | bytes 1843204
  18.9 2.2 %collective-permute-start = (f32[3,5,5,16,128]{4,3,2,1,0:T(8,128)S(1)}, f32[3,5,5,16,128]{4,3,2,1,0:T(8,128)S(1)}, u32[]{:S(2)}, u32[]{:S(2)}) collective-permute-start(f32[3,5,5,16,128]{4,3,2,1,0:T(8,128)S(1)} %get-tuple-element.19.mine_ref.mats_ref), channel_id=1, source_target_pairs={{0,1},{1,0},{2,3},{3,2},{4,5},{5,4},{6,7},{7,6},{8,9},{9,8},{10,11... | collective-permute-start | bytes 1843208 | tf_op jit(solution)/shard_map/ppermute | solution.py:457
  20.4 2.4 %collective-permute-start.4 = (f32[2,5,16,128]{3,2,1,0:T(8,128)S(1)}, f32[2,5,16,128]{3,2,1,0:T(8,128)S(1)}, u32[]{:S(2)}, u32[]{:S(2)}) collective-permute-start(f32[2,5,16,128]{3,2,1,0:T(8,128)S(1)} %get-tuple-element.24.ends_ref), channel_id=1, source_target_pairs={{0,1},{1,0},{2,3},{3,2},{4,5},{5,4},{6,7},{7,6},{8,9},{9,8},{10,11... | collective-permute-start | bytes 245768 | tf_op jit(solution)/shard_map/ppermute | solution.py:457
  21.1 8.5 %copy-start.2 = (f32[3,5,5,16,128]{4,3,2,1,0:T(8,128)}, f32[3,5,5,16,128]{4,3,2,1,0:T(8,128)S(1)}, u32[]{:S(2)}) copy-start(f32[3,5,5,16,128]{4,3,2,1,0:T(8,128)S(1)} %collective-permute-done.other_ref.mats_other_ref) | copy-start | bytes 1843204
  21.2 6.1 %collective-permute-start.1 = (f32[5,5,8,128]{3,2,1,0:T(8,128)S(1)}, f32[5,5,8,128]{3,2,1,0:T(8,128)S(1)}, u32[]{:S(2)}, u32[]{:S(2)}) collective-permute-start(f32[5,5,8,128]{3,2,1,0:T(8,128)S(1)} %shard_map.97), channel_id=1, source_target_pairs={{0,2},{1,3},{2,0},{3,1},{4,6},{5,7},{6,4},{7,5},{8,10},{9,11},{10,... | collective-permute-start | bytes 307208 | tf_op jit(solution)/shard_map/ppermute | solution.py:457
  22.8 4.5 %collective-permute-start.5 = (f32[1,5,16,128]{3,2,1,0:T(8,128)S(1)}, f32[1,5,16,128]{3,2,1,0:T(8,128)S(1)}, u32[]{:S(2)}, u32[]{:S(2)}) collective-permute-start(f32[1,5,16,128]{3,2,1,0:T(8,128)S(1)} %shard_map.100.pair_ref), channel_id=1, source_target_pairs={{0,2},{1,3},{2,0},{3,1},{4,6},{5,7},{6,4},{7,5},{8,10},{9,11},{10,... | collective-permute-start | bytes 122888 | tf_op jit(solution)/shard_map/ppermute | solution.py:457
  27.4 1.3 %collective-permute-start.6 = (f32[5,8,128]{2,1,0:T(8,128)S(1)}, f32[5,8,128]{2,1,0:T(8,128)S(1)}, u32[]{:S(2)}, u32[]{:S(2)}) collective-permute-start(f32[5,8,128]{2,1,0:T(8,128)S(1)} %shard_map.101.raised_ref), channel_id=1, source_target_pairs={{0,1},{1,0},{2,3},{3,2},{4,5},{5,4},{6,7},{7,6},{8,9},{9,8},{10,11... | collective-permute-start | bytes 61448 | tf_op jit(solution)/shard_map/ppermute | solution.py:457
  29.6 0.7 %copy-start.12 = (f32[8,5,16,128]{3,2,1,0:T(8,128)}, f32[8,5,16,128]{3,2,1,0:T(8,128)S(1)}, u32[]{:S(2)}) copy-start(f32[8,5,16,128]{3,2,1,0:T(8,128)S(1)} %get-tuple-element.26.cur_ref) | copy-start | bytes 983044
  30.4 0.6 %copy-start.20 = (f32[5,16,128]{2,1,0:T(8,128)}, f32[5,16,128]{2,1,0:T(8,128)S(1)}, u32[]{:S(2)}) copy-start(f32[5,16,128]{2,1,0:T(8,128)S(1)} %get-tuple-element.27.above_ref) | copy-start | bytes 122884
  31.0 10.2 %all-to-all-start.1 = ((f32[8,16,128]{2,1,0:T(8,128)}), f32[8,16,128]{2,1,0:T(8,128)S(1)}, u32[]{:S(2)}, u32[]{:S(2)}) async-start(f32[8,16,128]{2,1,0:T(8,128)} %get-tuple-element.25), calls=%async_computation.1 | async-start | bytes 131072 | tf_op jit(solution)/shard_map/all_to_all | solution.py:460
  34.3 1.4 %collective-permute-start.2 = (f32[5,5,8,128]{3,2,1,0:T(8,128)S(1)}, f32[5,5,8,128]{3,2,1,0:T(8,128)S(1)}, u32[]{:S(2)}, u32[]{:S(2)}) collective-permute-start(f32[5,5,8,128]{3,2,1,0:T(8,128)S(1)} %collective-permute-done.1.half_ref), channel_id=1, source_target_pairs={{0,1},{1,0},{2,3},{3,2},{4,5},{5,4},{6,7},{7,6},{8,9},{9,8},{10,11... | collective-permute-start | bytes 307208 | tf_op jit(solution)/shard_map/ppermute | solution.py:457
  41.2 1.4 %copy-start.5 = (f32[1,8,5,5,16,128]{5,4,3,2,1,0:T(8,128)S(1)}, f32[1,8,5,5,16,128]{5,4,3,2,1,0:T(8,128)}, u32[]{:S(2)}) copy-start(f32[1,8,5,5,16,128]{5,4,3,2,1,0:T(8,128)} %param.13) | copy-start | bytes 4915204
  42.6 1.4 %copy-start.7 = (f32[1,8,5,5,16,128]{5,4,3,2,1,0:T(8,128)S(1)}, f32[1,8,5,5,16,128]{5,4,3,2,1,0:T(8,128)}, u32[]{:S(2)}) copy-start(f32[1,8,5,5,16,128]{5,4,3,2,1,0:T(8,128)} %param.11) | copy-start | bytes 4915204
  44.0 1.4 %copy-start.9 = (f32[1,8,5,5,16,128]{5,4,3,2,1,0:T(8,128)S(1)}, f32[1,8,5,5,16,128]{5,4,3,2,1,0:T(8,128)}, u32[]{:S(2)}) copy-start(f32[1,8,5,5,16,128]{5,4,3,2,1,0:T(8,128)} %param.12) | copy-start | bytes 4915204
  45.5 1.4 %copy-start.11 = (f32[1,8,5,5,16,128]{5,4,3,2,1,0:T(8,128)S(1)}, f32[1,8,5,5,16,128]{5,4,3,2,1,0:T(8,128)}, u32[]{:S(2)}) copy-start(f32[1,8,5,5,16,128]{5,4,3,2,1,0:T(8,128)} %param.10) | copy-start | bytes 4915204
  46.9 1.0 %copy-start.13 = (f32[8,5,16,128]{3,2,1,0:T(8,128)S(1)}, f32[8,5,16,128]{3,2,1,0:T(8,128)}, u32[]{:S(2)}) copy-start(f32[8,5,16,128]{3,2,1,0:T(8,128)} %copy-done.12) | copy-start | bytes 983044
  47.9 1.0 %copy-start.17 = (f32[1,8,5,16,128]{4,3,2,1,0:T(8,128)S(1)}, f32[1,8,5,16,128]{4,3,2,1,0:T(8,128)}, u32[]{:S(2)}) copy-start(f32[1,8,5,16,128]{4,3,2,1,0:T(8,128)} %param.9) | copy-start | bytes 983044
  48.9 0.9 %copy-start.19 = (f32[2,8,16,128]{3,2,1,0:T(8,128)S(1)}, f32[2,8,16,128]{3,2,1,0:T(8,128)}, u32[]{:S(2)}) copy-start(f32[2,8,16,128]{3,2,1,0:T(8,128)} %copy-done.18) | copy-start | bytes 393220
  49.8 0.8 %copy-start.21 = (f32[5,16,128]{2,1,0:T(8,128)S(1)}, f32[5,16,128]{2,1,0:T(8,128)}, u32[]{:S(2)}) copy-start(f32[5,16,128]{2,1,0:T(8,128)} %copy-done.20) | copy-start | bytes 122884
  50.5 2.4 %copy-start.1 = (f32[3,5,5,16,128]{4,3,2,1,0:T(8,128)S(1)}, f32[3,5,5,16,128]{4,3,2,1,0:T(8,128)}, u32[]{:S(2)}) copy-start(f32[3,5,5,16,128]{4,3,2,1,0:T(8,128)} %copy-done) | copy-start | bytes 1843204
  50.5 2.4 %copy-start.3 = (f32[3,5,5,16,128]{4,3,2,1,0:T(8,128)S(1)}, f32[3,5,5,16,128]{4,3,2,1,0:T(8,128)}, u32[]{:S(2)}) copy-start(f32[3,5,5,16,128]{4,3,2,1,0:T(8,128)} %copy-done.2) | copy-start | bytes 1843204
  51.5 1.4 %collective-permute-start.7 = (f32[3,5,16,128]{3,2,1,0:T(8,128)S(1)}, f32[3,5,16,128]{3,2,1,0:T(8,128)S(1)}, u32[]{:S(2)}, u32[]{:S(2)}) collective-permute-start(f32[3,5,16,128]{3,2,1,0:T(8,128)S(1)} %get-tuple-element.31.ends_ref), channel_id=1, source_target_pairs={{0,1},{1,0},{2,3},{3,2},{4,5},{5,4},{6,7},{7,6},{8,9},{9,8},{10,11... | collective-permute-start | bytes 368648 | tf_op jit(solution)/shard_map/ppermute | solution.py:457
  53.0 4.6 %collective-permute-start.8 = (f32[2,5,16,128]{3,2,1,0:T(8,128)S(1)}, f32[2,5,16,128]{3,2,1,0:T(8,128)S(1)}, u32[]{:S(2)}, u32[]{:S(2)}) collective-permute-start(f32[2,5,16,128]{3,2,1,0:T(8,128)S(1)} %shard_map.104.pair_ref), channel_id=1, source_target_pairs={{0,2},{1,3},{2,0},{3,1},{4,6},{5,7},{6,4},{7,5},{8,10},{9,11},{10,... | collective-permute-start | bytes 245768 | tf_op jit(solution)/shard_map/ppermute | solution.py:457

commit v8 on v7

--- a/solution.py
+++ b/solution.py
@@ -83,8 +83,7 @@
             here = (lane == q) | (lane == (q - 1) % 128)
             x = load(j, v)
             tile = jnp.where(here, pltpu.roll(x, q, 1) if q else x, tile)
-    for w in range(tile_ref.shape[0]):
-        tile_ref[w] = tile
+    tile_ref[0] = tile
 
 
 def masked(live_ref, values):
@@ -97,13 +96,17 @@
     return [jnp.where(inner, x, 0.0) for x in values]
 
 
-def first_kernel(tiles_ref, flow_ref, first_ref):
-    del tiles_ref
+def pack_kernel(flow_ref, tile_ref, first_ref):
     put(first_ref, cell(flow_ref, 0))
-
-
-def pack_kernel(flow_ref, tile_ref):
     pack_faces(lambda j, v: flow_ref[j, v], flow_ref.shape[0], tile_ref)
+
+
+def merge_kernel(own_ref, got_ref, after_ref, out_ref):
+    del after_ref
+    count = own_ref.shape[0]
+    for w in range(count):
+        out_ref[w] = own_ref[w]
+        out_ref[count + w] = got_ref[w]
 
 
 def neighbours(x):
@@ -114,11 +117,13 @@
     return total + jnp.where(row == 15, 0.0, pltpu.roll(x, 15, 0))
 
 
-def ghosts_of(pick_ref, tiles_ref):
+def ghosts_of(pick_ref, own_ref, got_ref):
     low = high = jnp.zeros((16, 128), jnp.float32)
-    for w in range(tiles_ref.shape[0]):
-        low = jnp.where(pick_ref[0, w] > 0.0, tiles_ref[w], low)
-        high = jnp.where(pick_ref[1, w] > 0.0, tiles_ref[w], high)
+    count = own_ref.shape[0]
+    for w in range(2 * count):
+        tile = own_ref[w] if w < count else got_ref[w - count]
+        low = jnp.where(pick_ref[0, w] > 0.0, tile, low)
+        high = jnp.where(pick_ref[1, w] > 0.0, tile, high)
     return jnp.where(iota(1) % 2 == 0, pltpu.roll(low, 1, 1), pltpu.roll(high, 127, 1))
 
 
@@ -129,61 +134,81 @@
     return jnp.where((lane == 0) | (lane == 127), turned, 0.0)
 
 
-def matrix_kernel(
-    depth_hbm, east_hbm, tiles_ref, inv_ref, low_ref, up_ref,
-    e_ref, f_ref, mats_ref, live_ref, pick_ref,
-    y_ref, depth_ref, east_ref, sems,
-):
-    del tiles_ref
-    planes = inv_ref.shape[0]
+HALVES = [pl.ds(0, 8), pl.ds(8, 8)]
+
+
+def col(ref, q, j, rows):
+    return [ref[j, r, q, rows] for r in range(5)]
+
+
+def put_col(ref, values, q, j, rows):
+    for r in range(5):
+        ref[j, r, q, rows] = values[r]
+
+
+def mat(ref, j, rows):
+    return [[ref[j, r, c, rows] for c in range(5)] for r in range(5)]
+
+
+def product_kernel(
+    depth_hbm, east_hbm, tile_ref, inv_ref, low_ref, up_ref,
+    e_ref, f_ref, live_ref, pick_ref,
+    depth_ref, east_ref, sems,
+):
+    del tile_ref
     scalars = [
         pltpu.make_async_copy(depth_hbm, depth_ref, sems.at[0]),
         pltpu.make_async_copy(east_hbm, east_ref, sems.at[1]),
     ]
     for copy in scalars:
         copy.start()
-    last = planes - 1
-    halves = [pl.ds(0, 8), pl.ds(8, 8)]
-
-    def col(ref, q, j, rows):
-        return [ref[j, r, q, rows] for r in range(5)]
-
-    def put_col(ref, values, q, j, rows):
-        for r in range(5):
-            ref[j, r, q, rows] = values[r]
-
-    def mat(ref, j, rows):
-        return [[ref[j, r, c, rows] for c in range(5)] for r in range(5)]
-
-    def products(j, rows):
-        inv = mat(inv_ref, j, rows)
-        for jac_ref, out_ref in ((low_ref, e_ref), (up_ref, f_ref)):
-            for q in range(5):
-                product = matvec(inv, col(jac_ref, q, j, rows))
-                put_col(out_ref, [OMEGA * x for x in product], q, j, rows)
+
+    def products(j, carry):
+        for rows in HALVES:
+            inv = mat(inv_ref, j, rows)
+            for jac_ref, out_ref in ((low_ref, e_ref), (up_ref, f_ref)):
+                for q in range(5):
+                    product = matvec(inv, col(jac_ref, q, j, rows))
+                    put_col(out_ref, [OMEGA * x for x in product], q, j, rows)
+        return carry
+
+    lax.fori_loop(0, inv_ref.shape[0], products, 0)
+    for copy in scalars:
+        copy.wait()
+    zone = lax.axis_index("zone")
+    row = iota(0)
+    live_ref[...] = jnp.where(row < depth_ref[zone], 1.0, 0.0)
+    for i in range(pick_ref.shape[1]):
+        w = zone ^ i
+        rows = row < depth_ref[w]
+        pick_ref[0, i] = jnp.where(rows & (east_ref[w] == zone), 1.0, 0.0)
+        pick_ref[1, i] = jnp.where(rows & (east_ref[zone] == w), 1.0, 0.0)
+
+
+def matrix_kernel(tiles_ref, e_ref, f_ref, mats_ref, y_ref):
+    del tiles_ref
+    last = e_ref.shape[0] - 1
+    for rows in HALVES:
+        for q in range(5):
+            put_col(y_ref, col(e_ref, q, 0, rows), q, 0, rows)
 
     def forward(j, carry):
-        for rows in halves:
-            products(j, rows)
+        for rows in HALVES:
             e = mat(e_ref, j, rows)
             for q in range(5):
                 put_col(y_ref, matvec(e, col(y_ref, q, j - 1, rows)), q, j, rows)
         return carry
 
-    for rows in halves:
-        products(0, rows)
-        for q in range(5):
-            put_col(y_ref, col(e_ref, q, 0, rows), q, 0, rows)
-    lax.fori_loop(1, planes, forward, 0)
-    for rows in halves:
+    lax.fori_loop(1, last + 1, forward, 0)
+    for rows in HALVES:
         for q in range(5):
             put_col(mats_ref, col(y_ref, q, last, rows), q, 0, rows)
             put_col(mats_ref, col(y_ref, q, last, rows), q, 1, rows)
             put_col(mats_ref, col(f_ref, q, last, rows), q, 2, rows)
 
     def backward(step, carry):
-        j = planes - 2 - step
-        for rows in halves:
+        j = last - 1 - step
+        for rows in HALVES:
             f = mat(f_ref, j, rows)
             for q in range(5):
                 turned = matvec(f, col(mats_ref, q, 1, rows))
@@ -191,16 +216,7 @@
                 put_col(mats_ref, matvec(f, col(mats_ref, q, 2, rows)), q, 2, rows)
         return carry
 
-    lax.fori_loop(0, planes - 1, backward, 0)
-    for copy in scalars:
-        copy.wait()
-    zone = lax.axis_index("zone")
-    row = iota(0)
-    live_ref[...] = jnp.where(row < depth_ref[zone], 1.0, 0.0)
-    for w in range(pick_ref.shape[1]):
-        rows = row < depth_ref[w]
-        pick_ref[0, w] = jnp.where(rows & (east_ref[w] == zone), 1.0, 0.0)
-        pick_ref[1, w] = jnp.where(rows & (east_ref[zone] == w), 1.0, 0.0)
+    lax.fori_loop(0, last, backward, 0)
 
 
 def by_place(mine_refs, other_refs, run):
@@ -246,39 +262,55 @@
     put(ends_ref, value, 1)
 
 
-def local_kernel(
-    live_ref, pick_ref, tiles_ref, cur_ref, above_ref, force_ref, diag_ref, inv_ref,
-    e_ref, f_ref,
-    s_ref, ends_ref, y_ref,
-):
+def source_kernel(
+    tiles_ref, live_ref, cur_ref, force_ref, diag_ref, inv_ref, e_ref, f_ref, s_ref
+):
+    del tiles_ref
     planes = cur_ref.shape[0]
-    ghosts = ghosts_of(pick_ref, tiles_ref)
     before, here = None, masked(live_ref, cell(cur_ref, 0))
     for j in range(planes):
-        after = cell(cur_ref, j + 1) if j < planes - 1 else has_above(cell(above_ref))
-        after = masked(live_ref, after)
         own = matvec(block(diag_ref, j), here)
-        res = []
-        for v in range(5):
-            sides = neighbours(here[v]) + ghost_at(ghosts, j, v)
-            res.append(force_ref[j, v] - own[v] + COUPLE * sides)
-        linked = matvec(block(f_ref, j), after)
-        if before is not None:
-            linked = add(linked, matvec(block(e_ref, j), before))
-        linked = [x * (1.0 / OMEGA) for x in linked]
-        put(s_ref, add(matvec(block(inv_ref, j), masked(live_ref, res)), linked), j)
-        before, here = here, after
-    sweeps(s_ref, e_ref, f_ref, y_ref, ends_ref, masked(live_ref, cell(cur_ref, planes - 1)))
-
-
-def second_kernel(
-    half_ref, live_ref, pick_ref, tiles_ref, cur_ref, above_ref, force_ref, diag_ref, low_ref, up_ref,
+        res = [force_ref[j, v] - own[v] + COUPLE * neighbours(here[v]) for v in range(5)]
+        out = matvec(block(inv_ref, j), masked(live_ref, res))
+        if j > 0:
+            linked = matvec(block(e_ref, j), before)
+            out = add(out, [x * (1.0 / OMEGA) for x in linked])
+        if j < planes - 1:
+            after = masked(live_ref, cell(cur_ref, j + 1))
+            linked = matvec(block(f_ref, j), after)
+            out = add(out, [x * (1.0 / OMEGA) for x in linked])
+            before, here = here, after
+        put(s_ref, out, j)
+
+
+def add_ghosts(live_ref, ghosts, s0_ref, inv_ref, s_ref, res0_ref=None, res_ref=None):
+    ghosts = jnp.where(live_ref[...] > 0.0, COUPLE * ghosts, 0.0)
+    for j in range(s_ref.shape[0]):
+        extra = [ghost_at(ghosts, j, v) for v in range(5)]
+        if res_ref is not None:
+            put(res_ref, add(cell(res0_ref, j), extra), j)
+        put(s_ref, add(cell(s0_ref, j), matvec(block(inv_ref, j), extra)), j)
+
+
+def local_kernel(
+    half_ref, live_ref, pick_ref, own_ref, got_ref, cur_ref, above_ref, s0_ref,
     inv_ref, e_ref, f_ref,
-    res_ref, s_ref, ends_ref, low0_ref, y_ref,
+    s_ref, ends_ref, y_ref,
 ):
     del half_ref
+    last = cur_ref.shape[0] - 1
+    add_ghosts(live_ref, ghosts_of(pick_ref, own_ref, got_ref), s0_ref, inv_ref, s_ref)
+    above = masked(live_ref, has_above(cell(above_ref)))
+    linked = matvec(block(f_ref, last), above)
+    put(s_ref, add(cell(s_ref, last), [x * (1.0 / OMEGA) for x in linked]), last)
+    sweeps(s_ref, e_ref, f_ref, y_ref, ends_ref, masked(live_ref, cell(cur_ref, last)))
+
+
+def residual_kernel(
+    live_ref, cur_ref, above_ref, force_ref, diag_ref, low_ref, up_ref, inv_ref,
+    res_ref, s_ref, low0_ref,
+):
     planes = cur_ref.shape[0]
-    ghosts = ghosts_of(pick_ref, tiles_ref)
     for r in range(5):
         put(low0_ref, cell(low_ref, 0, r), r)
     for j in range(planes):
@@ -291,13 +323,22 @@
         upper = matvec(block(up_ref, j), above)
         res = []
         for v in range(5):
-            sides = neighbours(here[v]) + ghost_at(ghosts, j, v)
-            all_of = applied[v] - upper[v] - COUPLE * sides
+            all_of = applied[v] - upper[v] - COUPLE * neighbours(here[v])
             res.append(force_ref[j, v] - all_of)
         res = masked(live_ref, res)
         put(res_ref, res, j)
         put(s_ref, matvec(block(inv_ref, j), res), j)
-    last = cell(cur_ref, planes - 1)
+
+
+def second_kernel(
+    half_ref, live_ref, pick_ref, own_ref, got_ref, cur_ref, res0_ref, s0_ref,
+    inv_ref, e_ref, f_ref,
+    res_ref, s_ref, ends_ref, y_ref,
+):
+    del half_ref
+    ghosts = ghosts_of(pick_ref, own_ref, got_ref)
+    add_ghosts(live_ref, ghosts, s0_ref, inv_ref, s_ref, res0_ref, res_ref)
+    last = cell(cur_ref, cur_ref.shape[0] - 1)
     sweeps(s_ref, e_ref, f_ref, y_ref, ends_ref, last)
     put(ends_ref, last, 2)
 
@@ -444,40 +485,61 @@
     flow_state, forcing, diag_block, lower_jac, upper_jac, block_inv, east_zone, zone_depth
 ):
     zones, parts = lax.axis_size("zone"), lax.axis_size("ja")
-    assert parts == 4 and ITERS == 2
+    assert parts == 4 and ITERS == 2 and zones > 4 and zones & (zones - 1) == 0
     current, force, diag, low, up, inv = (
         x[0] for x in (flow_state, forcing, diag_block, lower_jac, upper_jac, block_inv)
     )
     state = current.shape
-    planes, plane, blocks, tiles = state[0], state[1:], diag.shape, (zones, *state[2:])
+    planes, plane, blocks = state[0], state[1:], diag.shape
     matrix = blocks[1:]
     work = [buffer(*state)]
 
     def swap(x, bit):
         return lax.ppermute(x, "ja", [(p, p ^ bit) for p in range(parts)])
 
-    def faces(x):
-        return lax.all_to_all(x, "zone", 0, 0, tiled=True)
-
-    tile = call(pack_kernel, [tiles], flops=2 * 10**10)(current)[0]
-    got = faces(tile)
-    first = call(first_kernel, [plane], flops=10**5)(got, current)[0]
+    def doubled(tiles, works):
+        stride = 1
+        while True:
+            pairs = [(z, z ^ stride) for z in range(zones)]
+            got = lax.ppermute(tiles, "zone", pairs)
+            stride *= 2
+            if stride == zones:
+                return tiles, got
+            after = works.pop(0)(tiles) if works else tiles
+            both = [(stride, *tiles.shape[1:])]
+            tiles = call(merge_kernel, both, flops=10**5)(tiles, got, after)[0]
+
+    small = {}
+
+    def block_products(tiles):
+        small["products"] = call(
+            product_kernel,
+            [blocks, blocks, state[2:], (2, zones, *state[2:])],
+            [pltpu.SMEM((zones,), jnp.int32)] * 2 + [pltpu.SemaphoreType.DMA((2,))],
+            flops=2 * 10**9,
+            far=(0, 1),
+        )(zone_depth, east_zone, tiles, inv, low, up)
+        return small["products"][0]
+
+    def matrices(tiles):
+        e, f = small["products"][:2]
+        small["mats"] = call(
+            matrix_kernel, [(3, *matrix)], [buffer(*blocks)], flops=2 * 10**9
+        )(tiles, e, f)[0]
+        return small["mats"]
+
+    tile, first = call(pack_kernel, [(1, *state[2:]), plane], flops=10**10)(current)
     above = lax.ppermute(first, "ja", [((p + 1) % parts, p) for p in range(parts)])
-    e, f, mats, live, pick = call(
-        matrix_kernel,
-        [blocks, blocks, (3, *matrix), state[2:], (2, *tiles)],
-        [buffer(*blocks)]
-        + [pltpu.SMEM((zones,), jnp.int32)] * 2
-        + [pltpu.SemaphoreType.DMA((2,))],
-        flops=5 * 10**9,
-        far=(0, 1),
-    )(zone_depth, east_zone, got, inv, low, up)
+    tiles, got = doubled(tile, [block_products, matrices])
+    e, f, live, pick = small["products"]
+    mats = small["mats"]
     mats_other = swap(mats, 1)
-    s, ends = call(local_kernel, [state, (2, *plane)], work, flops=2 * 10**10)(
-        live, pick, got, current, above, force, diag, inv, e, f
+    s0 = call(source_kernel, [state])(tiles, live, current, force, diag, inv, e, f)[0]
+    half = call(beta_kernel, [(*matrix[:2], 8, matrix[3])], flops=10**5)(mats, mats_other)[0]
+    s, ends = call(local_kernel, [state, (2, *plane)], work)(
+        half, live, pick, tiles, got, current, above, s0, inv, e, f
     )
     ends_other = swap(ends, 1)
-    half = call(beta_kernel, [(*matrix[:2], 8, matrix[3])], flops=10**5)(mats, mats_other)[0]
     half = swap(half, 2)
     pair = call(mid_kernel, [(1, *plane)], flops=10**5)(ends, ends_other, mats, mats_other)[0]
     pair_other = swap(pair, 2)
@@ -485,16 +547,17 @@
     raised_other = swap(raised, 1)
     half_other = swap(half, 1)
     flows = [buffer(2, *plane)]
-    current, above, tile = call(final_kernel, [state, plane, tiles], work + flows)(
+    current, above, tile = call(final_kernel, [state, plane, tile.shape], work + flows)(
         live, current, above, s, e, f,
         ends, ends_other, mats, mats_other, pair, pair_other, raised, raised_other,
     )
 
-    got = faces(tile)
-    residual, s, ends, low0 = call(
-        second_kernel, [state, state, (3, *plane), matrix], work
-    )(
-        half_other, live, pick, got, current, above, force, diag, low, up, inv, e, f
+    residual, s0, low0 = call(residual_kernel, [state, state, matrix])(
+        live, current, above, force, diag, low, up, inv
+    )
+    tiles, got = doubled(tile, [])
+    residual, s, ends = call(second_kernel, [state, state, (3, *plane)], work)(
+        half_other, live, pick, tiles, got, current, residual, s0, inv, e, f
     )
     ends_other = swap(ends, 1)
     pair = call(mid_kernel, [(2, *plane)])(ends, ends_other, mats, mats_other)[0]

time: 59.1 us -> 45.5 us (0.77)
  blocking collectives: 14.2 us -> 0 us
  starting transfers between devices: 8.07 us -> 21.3 us
  local copies, waits for them, and re-layouts: 11.7 us -> 0.99 us
  waiting for transfers between devices: 15.9 us -> 14.7 us
    ppermute x0 -> x6, starting transfers between devices: none -> 14.8 us  [doubled(): got = lax.ppermute(tiles, 'zone', pairs)]
    all_to_all x1 -> x0, blocking collectives: 14.2 us -> none  [faces(): return lax.all_to_all(x, 'zone', 0, 0, tiled=True)]
    unnamed x44 -> x14, local copies, waits for them, and re-layouts: 11.7 us -> 0.99 us
    ppermute x0 -> x6, waiting for transfers between devices: none -> 7.09 us  [doubled(): got = lax.ppermute(tiles, 'zone', pairs)]
    all_to_all x1 -> x0, waiting for transfers between devices: 5.47 us -> none  [faces(): return lax.all_to_all(x, 'zone', 0, 0, tiled=True)]
    all_to_all x1 -> x0, starting transfers between devices: 3.35 us -> none  [faces(): return lax.all_to_all(x, 'zone', 0, 0, tiled=True)]
    ppermute x8, waiting for transfers between devices: 10.4 us -> 7.57 us  [swap(): return lax.ppermute(x, 'ja', [(p, p ^ bit) for p in range(parts)])]
    ppermute x1, starting transfers between devices: 0.01 us -> 1.26 us  [per_device(): lax.ppermute(first, 'ja', [((p + 1) % parts, p) for p in range(parts)])]
  transfers between devices with their start and end apart: 10 -> 15, of which waited for: 7 -> 11; matrix products, arithmetic and copies ran while one was open for 0% -> 0% of each run, Pallas kernels for 8% -> 7%
where the time goes in v8:
time: 45.5 us; the launch traced here: 45.4 us
  starting transfers between devices  21.3 us (47%)
  waiting for transfers between devices  14.7 us (32%)
  Pallas kernels  7.68 us (17%)
  local copies, waits for them, and re-layouts  0.99 us (2%)
  between operations  0.79 us (2%)
    ppermute x6, starting transfers between devices, doubled(): got = lax.ppermute(tiles, 'zone', pairs)  14.8 us
    pallas_call x18, Pallas kernels, run(): pl.pallas_call(kernel, out_shape=[jax.ShapeDtypeStruct(s, jnp.float32) fo...  7.68 us
    ppermute x8, waiting for transfers between devices, swap(): return lax.ppermute(x, 'ja', [(p, p ^ bit) for p in range(parts)])  7.57 us
    ppermute x6, waiting for transfers between devices, doubled(): got = lax.ppermute(tiles, 'zone', pairs)  7.09 us
    ppermute x8, starting transfers between devices, swap(): return lax.ppermute(x, 'ja', [(p, p ^ bit) for p in range(parts)])  5.24 us
    ppermute x1, starting transfers between devices, per_device(): lax.ppermute(first, 'ja', [((p + 1) % parts, p) for p in range(parts)])  1.26 us
    unnamed x14, local copies, waits for them, and re-layouts  0.99 us
  transfers between devices with their start and end apart: 15, of which 11 were waited for; matrix products, arithmetic and copies ran while one was open for 0% of the time, Pallas kernels for 7%

profile of v8, /device:TPU:0, one launch (start us, length us, event | category | flops | bytes accessed | tf_op | source)
XLA Modules:
  0.0 45.4 jit_solution(10034399964982233096)
XLA Ops:
  0.6 0.0 copy-start.2
  0.6 1.0 %copy-done.2 = f32[1,8,5,16,128]{4,3,2,1,0:T(8,128)S(1)} copy-done((f32[1,8,5,16,128]{4,3,2,1,0:T(8,128)S(1)}, f32[1,8,5,16,128]{4,3,2,1,0:T(8,128)}, u32[]{:S(2)}) %copy-start.2) | copy-done | bytes 327704
  1.6 0.0 copy-start
  1.6 0.0 copy-start.4
  1.6 0.0 copy-start.5
  1.6 0.1 shard_map.95
  1.8 3.0 %collective-permute-start.1 = (f32[1,16,128]{2,1,0:T(8,128)S(1)}, f32[1,16,128]{2,1,0:T(8,128)S(1)}, u32[]{:S(2)}, u32[]{:S(2)}) collective-permute-start(f32[1,16,128]{2,1,0:T(8,128)S(1)} %get-tuple-element.21.tile_ref.own_ref), channel_id=1, source_target_pairs={{0,4},{4,0},{8,12},{12,8},{16,20},{20,16},{24,28},{28,24},{1,5},{5... | collective-permute-start | bytes 24584 | tf_op jit(solution)/shard_map/ppermute | solution.py:504
  4.8 0.0 copy-done
  4.8 0.0 copy-done.4
  4.8 0.0 copy-done.5
  4.8 1.2 %shard_map.96 = (f32[8,5,5,16,128]{4,3,2,1,0:T(8,128)S(1)}, f32[8,5,5,16,128]{4,3,2,1,0:T(8,128)S(1)}, f32[16,128]{1,0:T(8,128)S(1)}, f32[2,8,16,128]{3,2,1,0:T(8,128)S(1)}) custom-call(s32[8]{0:T(128)} %depth_hbm.1, s32[8]{0:T(128)} %east_hbm.1, f32[1,16,128]{2,1,0:T(8,128)S(1)} %get-tuple-element.21.tile_ref.own_ref, f32[8,5,5,16,128]{4,3,2,1,0:T(8,128)S(1)} %bitcast.8, ...), custom_call_target="tpu_custom_call" | custom-call | flops 2000000000 | bytes 2000000 | tf_op jit(solution)/shard_map/pallas_call | solution.py:25
  6.0 0.4 collective-permute-done.1.got_ref
  6.4 0.0 copy-start.1
  6.4 0.0 copy-start.3
  6.4 0.0 copy-start.6
  6.4 1.7 %shard_map.98.mine_ref.after_ref.mats_ref = f32[3,5,5,16,128]{4,3,2,1,0:T(8,128)S(1)} custom-call(f32[2,16,128]{2,1,0:T(8,128)S(1)} %shard_map.97.tiles_ref.own_ref, f32[8,5,5,16,128]{4,3,2,1,0:T(8,128)S(1)} %get-tuple-element.24.after_ref.e_ref, f32[8,5,5,16,128]{4,3,2,1,0:T(8,128)S(1)} %get-tuple-element.25.f_ref), custom_call_target="tpu_custom_call" | custom-call | flops 2000000000 | bytes 2000000 | tf_op jit(solution)/shard_map/pallas_call | solution.py:25
  8.2 0.1 collective-permute-start.2
  8.3 2.1 %collective-permute-start.3 = (f32[2,16,128]{2,1,0:T(8,128)S(1)}, f32[2,16,128]{2,1,0:T(8,128)S(1)}, u32[]{:S(2)}, u32[]{:S(2)}) collective-permute-start(f32[2,16,128]{2,1,0:T(8,128)S(1)} %shard_map.97.tiles_ref.own_ref), channel_id=1, source_target_pairs={{0,8},{4,12},{8,0},{12,4},{16,24},{20,28},{24,16},{28,20},{1,9},{5... | collective-permute-start | bytes 49160 | tf_op jit(solution)/shard_map/ppermute | solution.py:504
  10.4 1.3 %collective-permute-start = (f32[5,16,128]{2,1,0:T(8,128)S(1)}, f32[5,16,128]{2,1,0:T(8,128)S(1)}, u32[]{:S(2)}, u32[]{:S(2)}) collective-permute-start(f32[5,16,128]{2,1,0:T(8,128)S(1)} %get-tuple-element.23), channel_id=1, source_target_pairs={{1,0},{2,1},{3,2},{0,3},{5,4},{6,5},{7,6},{4,7},{9,8},{10,9},{11,1... | collective-permute-start | bytes 122888 | tf_op jit(solution)/shard_map/ppermute | solution.py:532
  11.7 0.5 %collective-permute-done.3.got_ref = f32[2,16,128]{2,1,0:T(8,128)S(1)} collective-permute-done((f32[2,16,128]{2,1,0:T(8,128)S(1)}, f32[2,16,128]{2,1,0:T(8,128)S(1)}, u32[]{:S(2)}, u32[]{:S(2)}) %collective-permute-start.3) | collective-permute-done | bytes 16416 | tf_op jit(solution)/shard_map/ppermute | solution.py:504
  12.1 3.0 %collective-permute-start.4 = (f32[4,16,128]{2,1,0:T(8,128)S(1)}, f32[4,16,128]{2,1,0:T(8,128)S(1)}, u32[]{:S(2)}, u32[]{:S(2)}) collective-permute-start(f32[4,16,128]{2,1,0:T(8,128)S(1)} %shard_map.100.tiles_ref.own_ref), channel_id=1, source_target_pairs={{0,16},{4,20},{8,24},{12,28},{16,0},{20,4},{24,8},{28,12},{1,17},{... | collective-permute-start | bytes 98312 | tf_op jit(solution)/shard_map/ppermute | solution.py:504
  15.2 0.0 copy-done.1
  15.2 0.0 copy-done.3
  15.2 0.0 copy-done.6
  15.2 0.6 %shard_map.101.s0_ref = f32[8,5,16,128]{3,2,1,0:T(8,128)S(1)} custom-call(f32[4,16,128]{2,1,0:T(8,128)S(1)} %shard_map.100.tiles_ref.own_ref, f32[16,128]{1,0:T(8,128)S(1)} %get-tuple-element.22.live_ref, f32[8,5,16,128]{3,2,1,0:T(8,128)S(1)} %bitcast.16, f32[8,5,16,128]{3,2,1,0:T(8,128)S(1)} %bitcast.23, f32[8,5,5,16,128]{4,3,2,1,0:T(8,128)S(1)} %bitcast.13, ...), custom_call_target="tpu_custom_call" | custom-call | flops 1000000000 | bytes 1000000 | tf_op jit(solution)/shard_map/pallas_call | solution.py:25
  15.8 0.0 collective-permute-done.2.other_ref.mats_other_ref
  15.8 0.1 shard_map.99.half_ref
  15.9 0.0 collective-permute-done.above_ref
  15.9 1.2 %collective-permute-done.4.got_ref = f32[4,16,128]{2,1,0:T(8,128)S(1)} collective-permute-done((f32[4,16,128]{2,1,0:T(8,128)S(1)}, f32[4,16,128]{2,1,0:T(8,128)S(1)}, u32[]{:S(2)}, u32[]{:S(2)}) %collective-permute-start.4) | collective-permute-done | bytes 32800 | tf_op jit(solution)/shard_map/ppermute | solution.py:504
  17.1 0.5 %shard_map.102 = (f32[8,5,16,128]{3,2,1,0:T(8,128)S(1)}, f32[2,5,16,128]{3,2,1,0:T(8,128)S(1)}) custom-call(f32[5,5,8,128]{3,2,1,0:T(8,128)S(1)} %shard_map.99.half_ref, f32[16,128]{1,0:T(8,128)S(1)} %get-tuple-element.22.live_ref, f32[2,8,16,128]{3,2,1,0:T(8,128)S(1)} %get-tuple-element.26.pick_ref, f32[4,16,128]{2,1,0:T(8,128)S(1)} %shard_map.100.tiles_ref.own_ref, ...), custom_call_target="tpu_custom_call" | custom-call | flops 1000000000 | bytes 1000000 | tf_op jit(solution)/shard_map/pallas_call | solution.py:25
  17.6 0.1 collective-permute-start.5
  17.6 1.9 %collective-permute-start.7 = (f32[5,5,8,128]{3,2,1,0:T(8,128)S(1)}, f32[5,5,8,128]{3,2,1,0:T(8,128)S(1)}, u32[]{:S(2)}, u32[]{:S(2)}) collective-permute-start(f32[5,5,8,128]{3,2,1,0:T(8,128)S(1)} %shard_map.99.half_ref), channel_id=1, source_target_pairs={{0,2},{1,3},{2,0},{3,1},{4,6},{5,7},{6,4},{7,5},{8,10},{9,11},{10,... | collective-permute-start | bytes 307208 | tf_op jit(solution)/shard_map/ppermute | solution.py:498
  19.5 0.0 collective-permute-done.5.ends_other_ref
  19.6 1.3 %collective-permute-start.6 = (f32[1,5,16,128]{3,2,1,0:T(8,128)S(1)}, f32[1,5,16,128]{3,2,1,0:T(8,128)S(1)}, u32[]{:S(2)}, u32[]{:S(2)}) collective-permute-start(f32[1,5,16,128]{3,2,1,0:T(8,128)S(1)} %shard_map.103.pair_ref), channel_id=1, source_target_pairs={{0,2},{1,3},{2,0},{3,1},{4,6},{5,7},{6,4},{7,5},{8,10},{9,11},{10,... | collective-permute-start | bytes 122888 | tf_op jit(solution)/shard_map/ppermute | solution.py:498
  20.8 2.6 %collective-permute-done.7.half_ref = f32[5,5,8,128]{3,2,1,0:T(8,128)S(1)} collective-permute-done((f32[5,5,8,128]{3,2,1,0:T(8,128)S(1)}, f32[5,5,8,128]{3,2,1,0:T(8,128)S(1)}, u32[]{:S(2)}, u32[]{:S(2)}) %collective-permute-start.7) | collective-permute-done | bytes 102432 | tf_op jit(solution)/shard_map/ppermute | solution.py:498
  23.4 0.5 %collective-permute-done.6.pair_other_ref = f32[1,5,16,128]{3,2,1,0:T(8,128)S(1)} collective-permute-done((f32[1,5,16,128]{3,2,1,0:T(8,128)S(1)}, f32[1,5,16,128]{3,2,1,0:T(8,128)S(1)}, u32[]{:S(2)}, u32[]{:S(2)}) %collective-permute-start.6) | collective-permute-done | bytes 40992 | tf_op jit(solution)/shard_map/ppermute | solution.py:498
  23.9 0.1 collective-permute-start.8
  24.0 1.2 %collective-permute-done.8.raised_other_ref = f32[5,8,128]{2,1,0:T(8,128)S(1)} collective-permute-done((f32[5,8,128]{2,1,0:T(8,128)S(1)}, f32[5,8,128]{2,1,0:T(8,128)S(1)}, u32[]{:S(2)}, u32[]{:S(2)}) %collective-permute-start.8) | collective-permute-done | bytes 20512 | tf_op jit(solution)/shard_map/ppermute | solution.py:498
  25.1 0.4 shard_map.105
  25.6 1.9 %collective-permute-start.10 = (f32[1,16,128]{2,1,0:T(8,128)S(1)}, f32[1,16,128]{2,1,0:T(8,128)S(1)}, u32[]{:S(2)}, u32[]{:S(2)}) collective-permute-start(f32[1,16,128]{2,1,0:T(8,128)S(1)} %get-tuple-element.32.own_ref.after_ref), channel_id=1, source_target_pairs={{0,4},{4,0},{8,12},{12,8},{16,20},{20,16},{24,28},{28,24},{1,5},{5... | collective-permute-start | bytes 24584 | tf_op jit(solution)/shard_map/ppermute | solution.py:504
  27.4 1.9 %collective-permute-done.10.got_ref = f32[1,16,128]{2,1,0:T(8,128)S(1)} collective-permute-done((f32[1,16,128]{2,1,0:T(8,128)S(1)}, f32[1,16,128]{2,1,0:T(8,128)S(1)}, u32[]{:S(2)}, u32[]{:S(2)}) %collective-permute-start.10) | collective-permute-done | bytes 8224 | tf_op jit(solution)/shard_map/ppermute | solution.py:504
  29.3 1.8 %collective-permute-start.11 = (f32[2,16,128]{2,1,0:T(8,128)S(1)}, f32[2,16,128]{2,1,0:T(8,128)S(1)}, u32[]{:S(2)}, u32[]{:S(2)}) collective-permute-start(f32[2,16,128]{2,1,0:T(8,128)S(1)} %shard_map.107.own_ref.after_ref), channel_id=1, source_target_pairs={{0,8},{4,12},{8,0},{12,4},{16,24},{20,28},{24,16},{28,20},{1,9},{5... | collective-permute-start | bytes 49160 | tf_op jit(solution)/shard_map/ppermute | solution.py:504
  31.1 0.0 collective-permute-start.9
  31.1 1.9 %collective-permute-done.11.got_ref = f32[2,16,128]{2,1,0:T(8,128)S(1)} collective-permute-done((f32[2,16,128]{2,1,0:T(8,128)S(1)}, f32[2,16,128]{2,1,0:T(8,128)S(1)}, u32[]{:S(2)}, u32[]{:S(2)}) %collective-permute-start.11) | collective-permute-done | bytes 16416 | tf_op jit(solution)/shard_map/ppermute | solution.py:504
  33.0 2.9 %collective-permute-start.12 = (f32[4,16,128]{2,1,0:T(8,128)S(1)}, f32[4,16,128]{2,1,0:T(8,128)S(1)}, u32[]{:S(2)}, u32[]{:S(2)}) collective-permute-start(f32[4,16,128]{2,1,0:T(8,128)S(1)} %shard_map.108.own_ref), channel_id=1, source_target_pairs={{0,16},{4,20},{8,24},{12,28},{16,0},{20,4},{24,8},{28,12},{1,17},{... | collective-permute-start | bytes 98312 | tf_op jit(solution)/shard_map/ppermute | solution.py:504
  35.9 0.6 %shard_map.106 = (f32[8,5,16,128]{3,2,1,0:T(8,128)S(1)}, f32[8,5,16,128]{3,2,1,0:T(8,128)S(1)}, f32[5,5,16,128]{3,2,1,0:T(8,128)S(1)}) custom-call(f32[16,128]{1,0:T(8,128)S(1)} %get-tuple-element.22.live_ref, f32[8,5,16,128]{3,2,1,0:T(8,128)S(1)} %get-tuple-element.29.cur_ref, f32[5,16,128]{2,1,0:T(8,128)S(1)} %get-tuple-element.30.above_ref, ...), custom_call_target="tpu_custom_call" | custom-call | flops 1000000000 | bytes 1000000 | tf_op jit(solution)/shard_map/pallas_call | solution.py:25
  36.6 1.3 %collective-permute-done.12.got_ref = f32[4,16,128]{2,1,0:T(8,128)S(1)} collective-permute-done((f32[4,16,128]{2,1,0:T(8,128)S(1)}, f32[4,16,128]{2,1,0:T(8,128)S(1)}, u32[]{:S(2)}, u32[]{:S(2)}) %collective-permute-start.12) | collective-permute-done | bytes 32800 | tf_op jit(solution)/shard_map/ppermute | solution.py:504
  37.8 0.0 collective-permute-done.9.half_ref.half_other_ref
  37.8 0.5 %shard_map.109 = (f32[8,5,16,128]{3,2,1,0:T(8,128)S(1)}, f32[8,5,16,128]{3,2,1,0:T(8,128)S(1)}, f32[3,5,16,128]{3,2,1,0:T(8,128)S(1)}) custom-call(f32[5,5,8,128]{3,2,1,0:T(8,128)S(1)} %collective-permute-done.9.half_ref.half_other_ref, f32[16,128]{1,0:T(8,128)S(1)} %get-tuple-element.22.live_ref, f32[2,8,16,128]{3,2,1,0:T(8,128)S(1)} %get-tuple-element.26.pick_ref, ...), custom_call_target="tpu_custom_call" | custom-call | flops 1000000000 | bytes 1000000 | tf_op jit(solution)/shard_map/pallas_call | solution.py:25
  38.3 0.1 collective-permute-start.13
  38.4 1.3 %collective-permute-done.13.ends_other_ref = f32[3,5,16,128]{3,2,1,0:T(8,128)S(1)} collective-permute-done((f32[3,5,16,128]{3,2,1,0:T(8,128)S(1)}, f32[3,5,16,128]{3,2,1,0:T(8,128)S(1)}, u32[]{:S(2)}, u32[]{:S(2)}) %collective-permute-start.13) | collective-permute-done | bytes 122912 | tf_op jit(solution)/shard_map/ppermute | solution.py:498
  39.8 1.8 %collective-permute-start.14 = (f32[2,5,16,128]{3,2,1,0:T(8,128)S(1)}, f32[2,5,16,128]{3,2,1,0:T(8,128)S(1)}, u32[]{:S(2)}, u32[]{:S(2)}) collective-permute-start(f32[2,5,16,128]{3,2,1,0:T(8,128)S(1)} %shard_map.110.pair_ref), channel_id=1, source_target_pairs={{0,2},{1,3},{2,0},{3,1},{4,6},{5,7},{6,4},{7,5},{8,10},{9,11},{10,... | collective-permute-start | bytes 245768 | tf_op jit(solution)/shard_map/ppermute | solution.py:498
  41.6 0.7 %shard_map.111.res_in_hbm = f32[8,5,16,128]{3,2,1,0:T(8,128)} custom-call(f32[8,5,16,128]{3,2,1,0:T(8,128)S(1)} %get-tuple-element.35.res_ref), custom_call_target="tpu_custom_call" | custom-call | flops 1000000000 | bytes 1000000 | tf_op jit(solution)/shard_map/pallas_call | solution.py:25
  42.3 2.0 %collective-permute-done.14.pair_other_ref = f32[2,5,16,128]{3,2,1,0:T(8,128)S(1)} collective-permute-done((f32[2,5,16,128]{3,2,1,0:T(8,128)S(1)}, f32[2,5,16,128]{3,2,1,0:T(8,128)S(1)}, u32[]{:S(2)}, u32[]{:S(2)}) %collective-permute-start.14) | collective-permute-done | bytes 81952 | tf_op jit(solution)/shard_map/ppermute | solution.py:498
  44.3 1.1 %shard_map.112 = (f32[8,5,16,128]{3,2,1,0:T(8,128)}, f32[8,5,16,128]{3,2,1,0:T(8,128)}) custom-call(f32[16,128]{1,0:T(8,128)S(1)} %get-tuple-element.22.live_ref, f32[5,5,16,128]{3,2,1,0:T(8,128)S(1)} %get-tuple-element.31.low0_ref, f32[8,5,16,128]{3,2,1,0:T(8,128)S(1)} %get-tuple-element.29.cur_ref, ...), custom_call_target="tpu_custom_call", output_to_operand_aliasing={{1}: (15, {})} | custom-call | flops 1000000000 | bytes 1000000 | tf_op jit(solution)/shard_map/pallas_call | solution.py:25
  (7 shorter events, 0.1 us)
Async XLA Ops:
  0.6 1.0 %copy-start.2 = (f32[1,8,5,16,128]{4,3,2,1,0:T(8,128)S(1)}, f32[1,8,5,16,128]{4,3,2,1,0:T(8,128)}, u32[]{:S(2)}) copy-start(f32[1,8,5,16,128]{4,3,2,1,0:T(8,128)} %param.8) | copy-start | bytes 983044
  1.6 3.2 %copy-start = (f32[1,8,5,5,16,128]{5,4,3,2,1,0:T(8,128)S(1)}, f32[1,8,5,5,16,128]{5,4,3,2,1,0:T(8,128)}, u32[]{:S(2)}) copy-start(f32[1,8,5,5,16,128]{5,4,3,2,1,0:T(8,128)} %param.13) | copy-start | bytes 4915204
  1.6 3.2 %copy-start.4 = (f32[1,8,5,5,16,128]{5,4,3,2,1,0:T(8,128)S(1)}, f32[1,8,5,5,16,128]{5,4,3,2,1,0:T(8,128)}, u32[]{:S(2)}) copy-start(f32[1,8,5,5,16,128]{5,4,3,2,1,0:T(8,128)} %param.11) | copy-start | bytes 4915204
  1.6 3.2 %copy-start.5 = (f32[1,8,5,5,16,128]{5,4,3,2,1,0:T(8,128)S(1)}, f32[1,8,5,5,16,128]{5,4,3,2,1,0:T(8,128)}, u32[]{:S(2)}) copy-start(f32[1,8,5,5,16,128]{5,4,3,2,1,0:T(8,128)} %param.12) | copy-start | bytes 4915204
  1.8 4.7 %collective-permute-start.1 = (f32[1,16,128]{2,1,0:T(8,128)S(1)}, f32[1,16,128]{2,1,0:T(8,128)S(1)}, u32[]{:S(2)}, u32[]{:S(2)}) collective-permute-start(f32[1,16,128]{2,1,0:T(8,128)S(1)} %get-tuple-element.21.tile_ref.own_ref), channel_id=1, source_target_pairs={{0,4},{4,0},{8,12},{12,8},{16,20},{20,16},{24,28},{28,24},{1,5},{5... | collective-permute-start | bytes 24584 | tf_op jit(solution)/shard_map/ppermute | solution.py:504
  6.4 8.7 %copy-start.1 = (f32[1,8,5,5,16,128]{5,4,3,2,1,0:T(8,128)S(1)}, f32[1,8,5,5,16,128]{5,4,3,2,1,0:T(8,128)}, u32[]{:S(2)}) copy-start(f32[1,8,5,5,16,128]{5,4,3,2,1,0:T(8,128)} %param.10) | copy-start | bytes 4915204
  6.4 8.7 %copy-start.3 = (f32[1,8,5,16,128]{4,3,2,1,0:T(8,128)S(1)}, f32[1,8,5,16,128]{4,3,2,1,0:T(8,128)}, u32[]{:S(2)}) copy-start(f32[1,8,5,16,128]{4,3,2,1,0:T(8,128)} %param.8) | copy-start | bytes 983044
  6.4 8.7 %copy-start.6 = (f32[1,8,5,16,128]{4,3,2,1,0:T(8,128)S(1)}, f32[1,8,5,16,128]{4,3,2,1,0:T(8,128)}, u32[]{:S(2)}) copy-start(f32[1,8,5,16,128]{4,3,2,1,0:T(8,128)} %param.9) | copy-start | bytes 983044
  8.2 7.6 %collective-permute-start.2 = (f32[3,5,5,16,128]{4,3,2,1,0:T(8,128)S(1)}, f32[3,5,5,16,128]{4,3,2,1,0:T(8,128)S(1)}, u32[]{:S(2)}, u32[]{:S(2)}) collective-permute-start(f32[3,5,5,16,128]{4,3,2,1,0:T(8,128)S(1)} %shard_map.98.mine_ref.after_ref.mats_ref), channel_id=1, source_target_pairs={{0,1},{1,0},{2,3},{3,2},{4,5},{5,4},{6,7},{7,6},{8,9},{9,8},{10,11... | collective-permute-start | bytes 1843208 | tf_op jit(solution)/shard_map/ppermute | solution.py:498
  8.3 3.9 %collective-permute-start.3 = (f32[2,16,128]{2,1,0:T(8,128)S(1)}, f32[2,16,128]{2,1,0:T(8,128)S(1)}, u32[]{:S(2)}, u32[]{:S(2)}) collective-permute-start(f32[2,16,128]{2,1,0:T(8,128)S(1)} %shard_map.97.tiles_ref.own_ref), channel_id=1, source_target_pairs={{0,8},{4,12},{8,0},{12,4},{16,24},{20,28},{24,16},{28,20},{1,9},{5... | collective-permute-start | bytes 49160 | tf_op jit(solution)/shard_map/ppermute | solution.py:504
  10.4 5.5 %collective-permute-start = (f32[5,16,128]{2,1,0:T(8,128)S(1)}, f32[5,16,128]{2,1,0:T(8,128)S(1)}, u32[]{:S(2)}, u32[]{:S(2)}) collective-permute-start(f32[5,16,128]{2,1,0:T(8,128)S(1)} %get-tuple-element.23), channel_id=1, source_target_pairs={{1,0},{2,1},{3,2},{0,3},{5,4},{6,5},{7,6},{4,7},{9,8},{10,9},{11,1... | collective-permute-start | bytes 122888 | tf_op jit(solution)/shard_map/ppermute | solution.py:532
  12.1 4.9 %collective-permute-start.4 = (f32[4,16,128]{2,1,0:T(8,128)S(1)}, f32[4,16,128]{2,1,0:T(8,128)S(1)}, u32[]{:S(2)}, u32[]{:S(2)}) collective-permute-start(f32[4,16,128]{2,1,0:T(8,128)S(1)} %shard_map.100.tiles_ref.own_ref), channel_id=1, source_target_pairs={{0,16},{4,20},{8,24},{12,28},{16,0},{20,4},{24,8},{28,12},{1,17},{... | collective-permute-start | bytes 98312 | tf_op jit(solution)/shard_map/ppermute | solution.py:504
  17.6 1.9 %collective-permute-start.5 = (f32[2,5,16,128]{3,2,1,0:T(8,128)S(1)}, f32[2,5,16,128]{3,2,1,0:T(8,128)S(1)}, u32[]{:S(2)}, u32[]{:S(2)}) collective-permute-start(f32[2,5,16,128]{3,2,1,0:T(8,128)S(1)} %get-tuple-element.28.ends_ref), channel_id=1, source_target_pairs={{0,1},{1,0},{2,3},{3,2},{4,5},{5,4},{6,7},{7,6},{8,9},{9,8},{10,11... | collective-permute-start | bytes 245768 | tf_op jit(solution)/shard_map/ppermute | solution.py:498
  17.6 5.7 %collective-permute-start.7 = (f32[5,5,8,128]{3,2,1,0:T(8,128)S(1)}, f32[5,5,8,128]{3,2,1,0:T(8,128)S(1)}, u32[]{:S(2)}, u32[]{:S(2)}) collective-permute-start(f32[5,5,8,128]{3,2,1,0:T(8,128)S(1)} %shard_map.99.half_ref), channel_id=1, source_target_pairs={{0,2},{1,3},{2,0},{3,1},{4,6},{5,7},{6,4},{7,5},{8,10},{9,11},{10,... | collective-permute-start | bytes 307208 | tf_op jit(solution)/shard_map/ppermute | solution.py:498
  19.6 4.3 %collective-permute-start.6 = (f32[1,5,16,128]{3,2,1,0:T(8,128)S(1)}, f32[1,5,16,128]{3,2,1,0:T(8,128)S(1)}, u32[]{:S(2)}, u32[]{:S(2)}) collective-permute-start(f32[1,5,16,128]{3,2,1,0:T(8,128)S(1)} %shard_map.103.pair_ref), channel_id=1, source_target_pairs={{0,2},{1,3},{2,0},{3,1},{4,6},{5,7},{6,4},{7,5},{8,10},{9,11},{10,... | collective-permute-start | bytes 122888 | tf_op jit(solution)/shard_map/ppermute | solution.py:498
  23.9 1.3 %collective-permute-start.8 = (f32[5,8,128]{2,1,0:T(8,128)S(1)}, f32[5,8,128]{2,1,0:T(8,128)S(1)}, u32[]{:S(2)}, u32[]{:S(2)}) collective-permute-start(f32[5,8,128]{2,1,0:T(8,128)S(1)} %shard_map.104.raised_ref), channel_id=1, source_target_pairs={{0,1},{1,0},{2,3},{3,2},{4,5},{5,4},{6,7},{7,6},{8,9},{9,8},{10,11... | collective-permute-start | bytes 61448 | tf_op jit(solution)/shard_map/ppermute | solution.py:498
  25.6 3.7 %collective-permute-start.10 = (f32[1,16,128]{2,1,0:T(8,128)S(1)}, f32[1,16,128]{2,1,0:T(8,128)S(1)}, u32[]{:S(2)}, u32[]{:S(2)}) collective-permute-start(f32[1,16,128]{2,1,0:T(8,128)S(1)} %get-tuple-element.32.own_ref.after_ref), channel_id=1, source_target_pairs={{0,4},{4,0},{8,12},{12,8},{16,20},{20,16},{24,28},{28,24},{1,5},{5... | collective-permute-start | bytes 24584 | tf_op jit(solution)/shard_map/ppermute | solution.py:504
  29.3 3.7 %collective-permute-start.11 = (f32[2,16,128]{2,1,0:T(8,128)S(1)}, f32[2,16,128]{2,1,0:T(8,128)S(1)}, u32[]{:S(2)}, u32[]{:S(2)}) collective-permute-start(f32[2,16,128]{2,1,0:T(8,128)S(1)} %shard_map.107.own_ref.after_ref), channel_id=1, source_target_pairs={{0,8},{4,12},{8,0},{12,4},{16,24},{20,28},{24,16},{28,20},{1,9},{5... | collective-permute-start | bytes 49160 | tf_op jit(solution)/shard_map/ppermute | solution.py:504
  31.1 6.7 %collective-permute-start.9 = (f32[5,5,8,128]{3,2,1,0:T(8,128)S(1)}, f32[5,5,8,128]{3,2,1,0:T(8,128)S(1)}, u32[]{:S(2)}, u32[]{:S(2)}) collective-permute-start(f32[5,5,8,128]{3,2,1,0:T(8,128)S(1)} %collective-permute-done.7.half_ref), channel_id=1, source_target_pairs={{0,1},{1,0},{2,3},{3,2},{4,5},{5,4},{6,7},{7,6},{8,9},{9,8},{10,11... | collective-permute-start | bytes 307208 | tf_op jit(solution)/shard_map/ppermute | solution.py:498
  33.0 4.8 %collective-permute-start.12 = (f32[4,16,128]{2,1,0:T(8,128)S(1)}, f32[4,16,128]{2,1,0:T(8,128)S(1)}, u32[]{:S(2)}, u32[]{:S(2)}) collective-permute-start(f32[4,16,128]{2,1,0:T(8,128)S(1)} %shard_map.108.own_ref), channel_id=1, source_target_pairs={{0,16},{4,20},{8,24},{12,28},{16,0},{20,4},{24,8},{28,12},{1,17},{... | collective-permute-start | bytes 98312 | tf_op jit(solution)/shard_map/ppermute | solution.py:504
  38.3 1.4 %collective-permute-start.13 = (f32[3,5,16,128]{3,2,1,0:T(8,128)S(1)}, f32[3,5,16,128]{3,2,1,0:T(8,128)S(1)}, u32[]{:S(2)}, u32[]{:S(2)}) collective-permute-start(f32[3,5,16,128]{3,2,1,0:T(8,128)S(1)} %get-tuple-element.37.ends_ref), channel_id=1, source_target_pairs={{0,1},{1,0},{2,3},{3,2},{4,5},{5,4},{6,7},{7,6},{8,9},{9,8},{10,11... | collective-permute-start | bytes 368648 | tf_op jit(solution)/shard_map/ppermute | solution.py:498
  39.8 4.6 %collective-permute-start.14 = (f32[2,5,16,128]{3,2,1,0:T(8,128)S(1)}, f32[2,5,16,128]{3,2,1,0:T(8,128)S(1)}, u32[]{:S(2)}, u32[]{:S(2)}) collective-permute-start(f32[2,5,16,128]{3,2,1,0:T(8,128)S(1)} %shard_map.110.pair_ref), channel_id=1, source_target_pairs={{0,2},{1,3},{2,0},{3,1},{4,6},{5,7},{6,4},{7,5},{8,10},{9,11},{10,... | collective-permute-start | bytes 245768 | tf_op jit(solution)/shard_map/ppermute | solution.py:498

commit v9 on v7

--- a/solution.py
+++ b/solution.py
@@ -97,13 +97,27 @@
     return [jnp.where(inner, x, 0.0) for x in values]
 
 
-def first_kernel(tiles_ref, flow_ref, first_ref):
-    del tiles_ref
+def pack_kernel(flow_hbm, tile_ref, first_ref, flow_ref, sem):
+    copy = pltpu.make_async_copy(flow_hbm, flow_ref, sem)
+    copy.start()
+    copy.wait()
     put(first_ref, cell(flow_ref, 0))
-
-
-def pack_kernel(flow_ref, tile_ref):
     pack_faces(lambda j, v: flow_ref[j, v], flow_ref.shape[0], tile_ref)
+
+
+def merge_kernel(own_ref, got_ref, *refs):
+    out_ref = refs[-1]
+    count = own_ref.shape[0]
+    for w in range(count):
+        out_ref[w] = own_ref[w]
+        out_ref[count + w] = got_ref[w]
+
+
+def relay_kernel(own_ref, got_ref, mats_ref, mats_out_ref, out_ref):
+    merge_kernel(own_ref, got_ref, out_ref)
+    for i in range(3):
+        for r in range(5):
+            put(mats_out_ref, cell(mats_ref, i, r), i, r)
 
 
 def neighbours(x):
@@ -114,11 +128,11 @@
     return total + jnp.where(row == 15, 0.0, pltpu.roll(x, 15, 0))
 
 
-def ghosts_of(pick_ref, tiles_ref):
+def ghosts_of(pick_ref, tile_at):
     low = high = jnp.zeros((16, 128), jnp.float32)
-    for w in range(tiles_ref.shape[0]):
-        low = jnp.where(pick_ref[0, w] > 0.0, tiles_ref[w], low)
-        high = jnp.where(pick_ref[1, w] > 0.0, tiles_ref[w], high)
+    for i in range(pick_ref.shape[1]):
+        low = jnp.where(pick_ref[0, i] > 0.0, tile_at(i), low)
+        high = jnp.where(pick_ref[1, i] > 0.0, tile_at(i), high)
     return jnp.where(iota(1) % 2 == 0, pltpu.roll(low, 1, 1), pltpu.roll(high, 127, 1))
 
 
@@ -129,31 +143,35 @@
     return jnp.where((lane == 0) | (lane == 127), turned, 0.0)
 
 
+HALVES = [pl.ds(0, 8), pl.ds(8, 8)]
+
+
+def col(ref, q, j, rows):
+    return [ref[j, r, q, rows] for r in range(5)]
+
+
+def put_col(ref, values, q, j, rows):
+    for r in range(5):
+        ref[j, r, q, rows] = values[r]
+
+
+def mat(ref, j, rows):
+    return [[ref[j, r, c, rows] for c in range(5)] for r in range(5)]
+
+
 def matrix_kernel(
-    depth_hbm, east_hbm, tiles_ref, inv_ref, low_ref, up_ref,
+    depth_hbm, east_hbm, tile_ref, inv_ref, low_ref, up_ref,
     e_ref, f_ref, mats_ref, live_ref, pick_ref,
     y_ref, depth_ref, east_ref, sems,
 ):
-    del tiles_ref
-    planes = inv_ref.shape[0]
+    del tile_ref
+    last = inv_ref.shape[0] - 1
     scalars = [
         pltpu.make_async_copy(depth_hbm, depth_ref, sems.at[0]),
         pltpu.make_async_copy(east_hbm, east_ref, sems.at[1]),
     ]
     for copy in scalars:
         copy.start()
-    last = planes - 1
-    halves = [pl.ds(0, 8), pl.ds(8, 8)]
-
-    def col(ref, q, j, rows):
-        return [ref[j, r, q, rows] for r in range(5)]
-
-    def put_col(ref, values, q, j, rows):
-        for r in range(5):
-            ref[j, r, q, rows] = values[r]
-
-    def mat(ref, j, rows):
-        return [[ref[j, r, c, rows] for c in range(5)] for r in range(5)]
 
     def products(j, rows):
         inv = mat(inv_ref, j, rows)
@@ -163,27 +181,16 @@
                 put_col(out_ref, [OMEGA * x for x in product], q, j, rows)
 
     def forward(j, carry):
-        for rows in halves:
+        for rows in HALVES:
             products(j, rows)
             e = mat(e_ref, j, rows)
             for q in range(5):
                 put_col(y_ref, matvec(e, col(y_ref, q, j - 1, rows)), q, j, rows)
         return carry
 
-    for rows in halves:
-        products(0, rows)
-        for q in range(5):
-            put_col(y_ref, col(e_ref, q, 0, rows), q, 0, rows)
-    lax.fori_loop(1, planes, forward, 0)
-    for rows in halves:
-        for q in range(5):
-            put_col(mats_ref, col(y_ref, q, last, rows), q, 0, rows)
-            put_col(mats_ref, col(y_ref, q, last, rows), q, 1, rows)
-            put_col(mats_ref, col(f_ref, q, last, rows), q, 2, rows)
-
     def backward(step, carry):
-        j = planes - 2 - step
-        for rows in halves:
+        j = last - 1 - step
+        for rows in HALVES:
             f = mat(f_ref, j, rows)
             for q in range(5):
                 turned = matvec(f, col(mats_ref, q, 1, rows))
@@ -191,16 +198,27 @@
                 put_col(mats_ref, matvec(f, col(mats_ref, q, 2, rows)), q, 2, rows)
         return carry
 
-    lax.fori_loop(0, planes - 1, backward, 0)
+    for rows in HALVES:
+        products(0, rows)
+        for q in range(5):
+            put_col(y_ref, col(e_ref, q, 0, rows), q, 0, rows)
+    lax.fori_loop(1, last + 1, forward, 0)
+    for rows in HALVES:
+        for q in range(5):
+            put_col(mats_ref, col(y_ref, q, last, rows), q, 0, rows)
+            put_col(mats_ref, col(y_ref, q, last, rows), q, 1, rows)
+            put_col(mats_ref, col(f_ref, q, last, rows), q, 2, rows)
+    lax.fori_loop(0, last, backward, 0)
     for copy in scalars:
         copy.wait()
     zone = lax.axis_index("zone")
     row = iota(0)
     live_ref[...] = jnp.where(row < depth_ref[zone], 1.0, 0.0)
-    for w in range(pick_ref.shape[1]):
+    for i in range(pick_ref.shape[1]):
+        w = zone ^ i
         rows = row < depth_ref[w]
-        pick_ref[0, w] = jnp.where(rows & (east_ref[w] == zone), 1.0, 0.0)
-        pick_ref[1, w] = jnp.where(rows & (east_ref[zone] == w), 1.0, 0.0)
+        pick_ref[0, i] = jnp.where(rows & (east_ref[w] == zone), 1.0, 0.0)
+        pick_ref[1, i] = jnp.where(rows & (east_ref[zone] == w), 1.0, 0.0)
 
 
 def by_place(mine_refs, other_refs, run):
@@ -246,39 +264,55 @@
     put(ends_ref, value, 1)
 
 
-def local_kernel(
-    live_ref, pick_ref, tiles_ref, cur_ref, above_ref, force_ref, diag_ref, inv_ref,
-    e_ref, f_ref,
-    s_ref, ends_ref, y_ref,
-):
+def source_kernel(
+    tiles_ref, live_ref, cur_ref, force_ref, diag_ref, inv_ref, e_ref, f_ref, s_ref
+):
+    del tiles_ref
     planes = cur_ref.shape[0]
-    ghosts = ghosts_of(pick_ref, tiles_ref)
     before, here = None, masked(live_ref, cell(cur_ref, 0))
     for j in range(planes):
-        after = cell(cur_ref, j + 1) if j < planes - 1 else has_above(cell(above_ref))
-        after = masked(live_ref, after)
         own = matvec(block(diag_ref, j), here)
-        res = []
-        for v in range(5):
-            sides = neighbours(here[v]) + ghost_at(ghosts, j, v)
-            res.append(force_ref[j, v] - own[v] + COUPLE * sides)
-        linked = matvec(block(f_ref, j), after)
-        if before is not None:
-            linked = add(linked, matvec(block(e_ref, j), before))
-        linked = [x * (1.0 / OMEGA) for x in linked]
-        put(s_ref, add(matvec(block(inv_ref, j), masked(live_ref, res)), linked), j)
-        before, here = here, after
-    sweeps(s_ref, e_ref, f_ref, y_ref, ends_ref, masked(live_ref, cell(cur_ref, planes - 1)))
+        res = [force_ref[j, v] - own[v] + COUPLE * neighbours(here[v]) for v in range(5)]
+        out = matvec(block(inv_ref, j), masked(live_ref, res))
+        if j > 0:
+            linked = matvec(block(e_ref, j), before)
+            out = add(out, [x * (1.0 / OMEGA) for x in linked])
+        if j < planes - 1:
+            after = masked(live_ref, cell(cur_ref, j + 1))
+            linked = matvec(block(f_ref, j), after)
+            out = add(out, [x * (1.0 / OMEGA) for x in linked])
+            before, here = here, after
+        put(s_ref, out, j)
+
+
+def local_kernel(
+    half_ref, live_ref, pick_ref, own_ref, got_ref, cur_ref, above_ref, s0_ref,
+    inv_ref, e_ref, f_ref,
+    s_ref, ends_ref, half_out_ref, y_ref,
+):
+    for r in range(5):
+        put(half_out_ref, cell(half_ref, r), r)
+    last = cur_ref.shape[0] - 1
+    count = own_ref.shape[0]
+    ghosts = ghosts_of(pick_ref, lambda i: own_ref[i] if i < count else got_ref[i - count])
+    ghosts = jnp.where(live_ref[...] > 0.0, COUPLE * ghosts, 0.0)
+    for j in range(last + 1):
+        extra = [ghost_at(ghosts, j, v) for v in range(5)]
+        put(s_ref, add(cell(s0_ref, j), matvec(block(inv_ref, j), extra)), j)
+    above = masked(live_ref, has_above(cell(above_ref)))
+    linked = matvec(block(f_ref, last), above)
+    put(s_ref, add(cell(s_ref, last), [x * (1.0 / OMEGA) for x in linked]), last)
+    sweeps(s_ref, e_ref, f_ref, y_ref, ends_ref, masked(live_ref, cell(cur_ref, last)))
 
 
 def second_kernel(
-    half_ref, live_ref, pick_ref, tiles_ref, cur_ref, above_ref, force_ref, diag_ref, low_ref, up_ref,
+    live_ref, pick_ref, tiles_ref, cur_ref, above_ref, force_ref, diag_ref, low_ref, up_ref,
     inv_ref, e_ref, f_ref,
     res_ref, s_ref, ends_ref, low0_ref, y_ref,
 ):
-    del half_ref
     planes = cur_ref.shape[0]
-    ghosts = ghosts_of(pick_ref, tiles_ref)
+    zone = lax.axis_index("zone")
+    ghosts = ghosts_of(pick_ref, lambda i: tiles_ref[zone ^ i])
     for r in range(5):
         put(low0_ref, cell(low_ref, 0, r), r)
     for j in range(planes):
@@ -327,18 +361,6 @@
     by_place([ends_ref, mats_ref], [ends_other_ref, mats_other_ref], run)
 
 
-def raise_kernel(pair_ref, pair_other_ref, half_ref, raised_ref):
-    odd = lax.axis_index("ja") % 2
-    for side in range(2):
-        rows = pl.ds(8 * side, 8)
-
-        @pl.when(odd == side)
-        def _():
-            inflow = [pair_ref[0, v, rows] for v in range(5)]
-            alpha = [pair_other_ref[0, v, rows] for v in range(5)]
-            put(raised_ref, add(alpha, matvec(block(half_ref), inflow)))
-
-
 def join(mine_ref, other_ref, *at):
     mine, other = mine_ref[at], other_ref[at]
     odd = lax.axis_index("ja") % 2 == 1
@@ -346,10 +368,15 @@
 
 
 def inflows(
-    ends_ref, ends_other_ref, mats_ref, mats_other_ref, pair_ref, pair_other_ref, far, inflow_ref
+    ends_ref, ends_other_ref, mats_ref, mats_other_ref, pair_ref, pair_other_ref,
+    half_ref, half_other_ref, inflow_ref,
 ):
     ja = lax.axis_index("ja")
     zeros = [jnp.zeros((16, 128), jnp.float32)] * 5
+
+    def far():
+        beta = [[join(half_ref, half_other_ref, r, c) for c in range(5)] for r in range(5)]
+        return add(cell(pair_other_ref, 0), matvec(beta, cell(pair_ref, 0)))
 
     @pl.when(ja == 0)
     def _():
@@ -381,13 +408,13 @@
 def final_kernel(
     live_ref, cur_ref, above_ref, s_ref, e_ref, f_ref,
     ends_ref, ends_other_ref, mats_ref, mats_other_ref, pair_ref, pair_other_ref,
-    raised_ref, raised_other_ref,
+    half_ref, half_other_ref,
     new_ref, above_new_ref, tile_ref, y_ref, inflow_ref,
 ):
     planes = cur_ref.shape[0]
     inflows(
         ends_ref, ends_other_ref, mats_ref, mats_other_ref, pair_ref, pair_other_ref,
-        lambda: [join(raised_ref, raised_other_ref, v) for v in range(5)], inflow_ref,
+        half_ref, half_other_ref, inflow_ref,
     )
     value = cell(inflow_ref, 0)
     for j in range(planes):
@@ -417,14 +444,9 @@
     put(res0_ref, add(cell(res_ref, 0), masked(live_ref, matvec(block(low0_ref), before))))
     copies = [pltpu.make_async_copy(res0_ref, res_hbm.at[0], sems.at[planes])]
     copies[0].start()
-
-    def far():
-        beta = [[join(half_ref, half_other_ref, r, c) for c in range(5)] for r in range(5)]
-        return add(cell(pair_other_ref, 0), matvec(beta, cell(pair_ref, 0)))
-
     inflows(
         ends_ref, ends_other_ref, mats_ref, mats_other_ref, pair_ref, pair_other_ref,
-        far, inflow_ref,
+        half_ref, half_other_ref, inflow_ref,
     )
     value = cell(inflow_ref, 0)
     for j in range(planes):
@@ -444,57 +466,68 @@
     flow_state, forcing, diag_block, lower_jac, upper_jac, block_inv, east_zone, zone_depth
 ):
     zones, parts = lax.axis_size("zone"), lax.axis_size("ja")
-    assert parts == 4 and ITERS == 2
+    assert parts == 4 and ITERS == 2 and zones > 4 and zones & (zones - 1) == 0
     current, force, diag, low, up, inv = (
         x[0] for x in (flow_state, forcing, diag_block, lower_jac, upper_jac, block_inv)
     )
     state = current.shape
-    planes, plane, blocks, tiles = state[0], state[1:], diag.shape, (zones, *state[2:])
+    planes, plane, blocks = state[0], state[1:], diag.shape
     matrix = blocks[1:]
     work = [buffer(*state)]
 
     def swap(x, bit):
         return lax.ppermute(x, "ja", [(p, p ^ bit) for p in range(parts)])
 
-    def faces(x):
-        return lax.all_to_all(x, "zone", 0, 0, tiled=True)
-
-    tile = call(pack_kernel, [tiles], flops=2 * 10**10)(current)[0]
-    got = faces(tile)
-    first = call(first_kernel, [plane], flops=10**5)(got, current)[0]
+    tile, first = call(
+        pack_kernel,
+        [(1, *state[2:]), plane],
+        work + [pltpu.SemaphoreType.DMA],
+        flops=10**10,
+        far=(0,),
+    )(current)
     above = lax.ppermute(first, "ja", [((p + 1) % parts, p) for p in range(parts)])
     e, f, mats, live, pick = call(
         matrix_kernel,
-        [blocks, blocks, (3, *matrix), state[2:], (2, *tiles)],
+        [blocks, blocks, (3, *matrix), state[2:], (2, zones, *state[2:])],
         [buffer(*blocks)]
         + [pltpu.SMEM((zones,), jnp.int32)] * 2
         + [pltpu.SemaphoreType.DMA((2,))],
         flops=5 * 10**9,
         far=(0, 1),
-    )(zone_depth, east_zone, got, inv, low, up)
-    mats_other = swap(mats, 1)
-    s, ends = call(local_kernel, [state, (2, *plane)], work, flops=2 * 10**10)(
-        live, pick, got, current, above, force, diag, inv, e, f
+    )(zone_depth, east_zone, tile, inv, low, up)
+    tiles, stride = tile, 1
+    while True:
+        got = lax.ppermute(tiles, "zone", [(z, z ^ stride) for z in range(zones)])
+        stride *= 2
+        if stride == zones:
+            break
+        both = (stride, *state[2:])
+        if stride == 2:
+            mats, tiles = call(relay_kernel, [mats.shape, both], flops=10**5)(tiles, got, mats)
+            mats_other = swap(mats, 1)
+            half = call(beta_kernel, [(*matrix[:2], 8, matrix[3])], flops=10**5)(mats, mats_other)[0]
+        else:
+            tiles = call(merge_kernel, [both], flops=10**5)(tiles, got, half)[0]
+    half = swap(half, 2)
+    s0 = call(source_kernel, [state])(tiles, live, current, force, diag, inv, e, f)[0]
+    s, ends, half = call(local_kernel, [state, (2, *plane), half.shape], work)(
+        half, live, pick, tiles, got, current, above, s0, inv, e, f
     )
     ends_other = swap(ends, 1)
-    half = call(beta_kernel, [(*matrix[:2], 8, matrix[3])], flops=10**5)(mats, mats_other)[0]
-    half = swap(half, 2)
+    half_other = swap(half, 1)
     pair = call(mid_kernel, [(1, *plane)], flops=10**5)(ends, ends_other, mats, mats_other)[0]
     pair_other = swap(pair, 2)
-    raised = call(raise_kernel, [(plane[0], 8, plane[2])], flops=10**5)(pair, pair_other, half)[0]
-    raised_other = swap(raised, 1)
-    half_other = swap(half, 1)
     flows = [buffer(2, *plane)]
-    current, above, tile = call(final_kernel, [state, plane, tiles], work + flows)(
+    current, above, tile = call(
+        final_kernel, [state, plane, (zones, *state[2:])], work + flows
+    )(
         live, current, above, s, e, f,
-        ends, ends_other, mats, mats_other, pair, pair_other, raised, raised_other,
-    )
-
-    got = faces(tile)
-    residual, s, ends, low0 = call(
-        second_kernel, [state, state, (3, *plane), matrix], work
-    )(
-        half_other, live, pick, got, current, above, force, diag, low, up, inv, e, f
+        ends, ends_other, mats, mats_other, pair, pair_other, half, half_other,
+    )
+
+    got = lax.all_to_all(tile, "zone", 0, 0, tiled=True)
+    residual, s, ends, low0 = call(second_kernel, [state, state, (3, *plane), matrix], work)(
+        live, pick, got, current, above, force, diag, low, up, inv, e, f
     )
     ends_other = swap(ends, 1)
     pair = call(mid_kernel, [(2, *plane)])(ends, ends_other, mats, mats_other)[0]

time: 59.1 us -> 43.8 us (0.74)
  local copies, waits for them, and re-layouts: 11.7 us -> 0.03 us
  waiting for transfers between devices: 15.9 us -> 9.1 us
  starting transfers between devices: 8.07 us -> 12.5 us
  blocking collectives: 14.2 us -> 12.5 us
  Pallas kernels: 7.84 us -> 8.69 us
    unnamed x44 -> x12, local copies, waits for them, and re-layouts: 11.7 us -> 0.03 us
    ppermute x0 -> x3, starting transfers between devices: none -> 7.26 us  [per_device(): got = lax.ppermute(tiles, 'zone', [(z, z ^ stride) for z in range(zones)])]
    all_to_all x1 -> x0, waiting for transfers between devices: 5.47 us -> none  [faces(): return lax.all_to_all(x, 'zone', 0, 0, tiled=True)]
    all_to_all x1 -> x0, starting transfers between devices: 3.35 us -> none  [faces(): return lax.all_to_all(x, 'zone', 0, 0, tiled=True)]
    ppermute x8 -> x7, waiting for transfers between devices: 10.4 us -> 7.41 us  [swap(): return lax.ppermute(x, 'ja', [(p, p ^ bit) for p in range(parts)])]
    all_to_all x1, blocking collectives: 14.2 us -> 12.5 us  [per_device(): got = lax.all_to_all(tile, 'zone', 0, 0, tiled=True)]
    ppermute x0 -> x3, waiting for transfers between devices: none -> 1.68 us  [per_device(): got = lax.ppermute(tiles, 'zone', [(z, z ^ stride) for z in range(zones)])]
    pallas_call x12 -> x13, Pallas kernels: 7.84 us -> 8.69 us  [run(): pl.pallas_call(kernel, out_shape=[jax.ShapeDtypeStruct(s, jnp.float32) fo...]
  transfers between devices with their start and end apart: 10 -> 11, of which waited for: 7 -> 7; matrix products, arithmetic and copies ran while one was open for 0% -> 0% of each run, Pallas kernels for 8% -> 10%
where the time goes in v9:
time: 43.8 us; the launch traced here: 43.7 us
  starting transfers between devices  12.5 us (29%)
  blocking collectives  12.5 us (29%)
  waiting for transfers between devices  9.1 us (21%)
  Pallas kernels  8.69 us (20%)
  between operations  0.81 us (2%)
    all_to_all x1, blocking collectives, per_device(): got = lax.all_to_all(tile, 'zone', 0, 0, tiled=True)  12.5 us
    pallas_call x13, Pallas kernels, run(): pl.pallas_call(kernel, out_shape=[jax.ShapeDtypeStruct(s, jnp.float32) fo...  8.69 us
    ppermute x7, waiting for transfers between devices, swap(): return lax.ppermute(x, 'ja', [(p, p ^ bit) for p in range(parts)])  7.41 us
    ppermute x3, starting transfers between devices, per_device(): got = lax.ppermute(tiles, 'zone', [(z, z ^ stride) for z in range(zones)])  7.26 us
    ppermute x7, starting transfers between devices, swap(): return lax.ppermute(x, 'ja', [(p, p ^ bit) for p in range(parts)])  5.24 us
    ppermute x3, waiting for transfers between devices, per_device(): got = lax.ppermute(tiles, 'zone', [(z, z ^ stride) for z in range(zones)])  1.68 us
  transfers between devices with their start and end apart: 11, of which 7 were waited for; matrix products, arithmetic and copies ran while one was open for 0% of the time, Pallas kernels for 10%

profile of v9, /device:TPU:0, one launch (start us, length us, event | category | flops | bytes accessed | tf_op | source)
XLA Modules:
  0.0 43.7 jit_solution(5216580108480255894)
XLA Ops:
  0.6 0.0 copy-start
  0.6 0.0 copy-start.3
  0.7 0.0 copy-start.4
  0.7 1.3 %shard_map.95 = (f32[1,16,128]{2,1,0:T(8,128)S(1)}, f32[5,16,128]{2,1,0:T(8,128)S(1)}) custom-call(f32[8,5,16,128]{3,2,1,0:T(8,128)} %bitcast.14), custom_call_target="tpu_custom_call" | custom-call | flops 10000000000 | bytes 10000000 | tf_op jit(solution)/shard_map/pallas_call | solution.py:25
  2.0 3.0 %collective-permute-start.1 = (f32[1,16,128]{2,1,0:T(8,128)S(1)}, f32[1,16,128]{2,1,0:T(8,128)S(1)}, u32[]{:S(2)}, u32[]{:S(2)}) collective-permute-start(f32[1,16,128]{2,1,0:T(8,128)S(1)} %get-tuple-element.23.tile_ref.own_ref), channel_id=1, source_target_pairs={{0,4},{4,0},{8,12},{12,8},{16,20},{20,16},{24,28},{28,24},{1,5},{5... | collective-permute-start | bytes 24584 | tf_op jit(solution)/shard_map/ppermute | solution.py:500
  5.0 0.0 copy-done
  5.0 0.0 copy-done.3
  5.0 0.0 copy-done.4
  5.0 0.0 copy-start.5
  5.0 2.9 %shard_map.96 = (f32[8,5,5,16,128]{4,3,2,1,0:T(8,128)S(1)}, f32[8,5,5,16,128]{4,3,2,1,0:T(8,128)S(1)}, f32[3,5,5,16,128]{4,3,2,1,0:T(8,128)S(1)}, f32[16,128]{1,0:T(8,128)S(1)}, f32[2,8,16,128]{3,2,1,0:T(8,128)S(1)}) custom-call(s32[8]{0:T(128)} %depth_hbm.1, s32[8]{0:T(128)} %east_hbm.1, f32[1,16,128]{2,1,0:T(8,128)S(1)} %get-tuple-element.23.tile_ref.own_ref, ...), custom_call_target="tpu_custom_call" | custom-call | flops 5000000000 | bytes 5000000 | tf_op jit(solution)/shard_map/pallas_call | solution.py:25
  7.9 0.0 copy-start.1
  7.9 0.0 copy-start.2
  7.9 0.0 collective-permute-done.1.got_ref
  8.0 0.1 collective-permute-start.2
  8.0 1.6 %collective-permute-start.4 = (f32[2,16,128]{2,1,0:T(8,128)S(1)}, f32[2,16,128]{2,1,0:T(8,128)S(1)}, u32[]{:S(2)}, u32[]{:S(2)}) collective-permute-start(f32[2,16,128]{2,1,0:T(8,128)S(1)} %get-tuple-element.29.own_ref), channel_id=1, source_target_pairs={{0,8},{4,12},{8,0},{12,4},{16,24},{20,28},{24,16},{28,20},{1,9},{5... | collective-permute-start | bytes 49160 | tf_op jit(solution)/shard_map/ppermute | solution.py:500
  9.7 0.4 collective-permute-done.2.other_ref.mats_other_ref
  10.1 0.1 shard_map.98.refs_0_
  10.1 1.6 %collective-permute-start.3 = (f32[5,5,8,128]{3,2,1,0:T(8,128)S(1)}, f32[5,5,8,128]{3,2,1,0:T(8,128)S(1)}, u32[]{:S(2)}, u32[]{:S(2)}) collective-permute-start(f32[5,5,8,128]{3,2,1,0:T(8,128)S(1)} %shard_map.98.refs_0_), channel_id=1, source_target_pairs={{0,2},{1,3},{2,0},{3,1},{4,6},{5,7},{6,4},{7,5},{8,10},{9,11},{10,... | collective-permute-start | bytes 307208 | tf_op jit(solution)/shard_map/ppermute | solution.py:479
  11.7 0.0 collective-permute-start
  11.7 0.1 collective-permute-done.4.got_ref
  11.8 2.6 %collective-permute-start.5 = (f32[4,16,128]{2,1,0:T(8,128)S(1)}, f32[4,16,128]{2,1,0:T(8,128)S(1)}, u32[]{:S(2)}, u32[]{:S(2)}) collective-permute-start(f32[4,16,128]{2,1,0:T(8,128)S(1)} %shard_map.99.tiles_ref.own_ref), channel_id=1, source_target_pairs={{0,16},{4,20},{8,24},{12,28},{16,0},{20,4},{24,8},{28,12},{1,17},{... | collective-permute-start | bytes 98312 | tf_op jit(solution)/shard_map/ppermute | solution.py:500
  14.4 0.0 copy-done.5
  14.4 0.0 copy-done.1
  14.4 0.0 copy-done.2
  14.4 0.6 %shard_map.100.s0_ref = f32[8,5,16,128]{3,2,1,0:T(8,128)S(1)} custom-call(f32[4,16,128]{2,1,0:T(8,128)S(1)} %shard_map.99.tiles_ref.own_ref, f32[16,128]{1,0:T(8,128)S(1)} %get-tuple-element.24.live_ref, f32[8,5,16,128]{3,2,1,0:T(8,128)S(1)} %bitcast.15, f32[8,5,16,128]{3,2,1,0:T(8,128)S(1)} %bitcast.22, f32[8,5,5,16,128]{4,3,2,1,0:T(8,128)S(1)} %bitcast.12, ...), custom_call_target="tpu_custom_call" | custom-call | flops 1000000000 | bytes 1000000 | tf_op jit(solution)/shard_map/pallas_call | solution.py:25
  15.1 0.0 collective-permute-done.above_ref
  15.1 1.6 %collective-permute-done.5.got_ref = f32[4,16,128]{2,1,0:T(8,128)S(1)} collective-permute-done((f32[4,16,128]{2,1,0:T(8,128)S(1)}, f32[4,16,128]{2,1,0:T(8,128)S(1)}, u32[]{:S(2)}, u32[]{:S(2)}) %collective-permute-start.5) | collective-permute-done | bytes 32800 | tf_op jit(solution)/shard_map/ppermute | solution.py:500
  16.7 0.0 collective-permute-done.3.half_ref
  16.7 0.5 %shard_map.101 = (f32[8,5,16,128]{3,2,1,0:T(8,128)S(1)}, f32[2,5,16,128]{3,2,1,0:T(8,128)S(1)}, f32[5,5,8,128]{3,2,1,0:T(8,128)S(1)}) custom-call(f32[5,5,8,128]{3,2,1,0:T(8,128)S(1)} %collective-permute-done.3.half_ref, f32[16,128]{1,0:T(8,128)S(1)} %get-tuple-element.24.live_ref, f32[2,8,16,128]{3,2,1,0:T(8,128)S(1)} %get-tuple-element.25.pick_ref, ...), custom_call_target="tpu_custom_call" | custom-call | flops 1000000000 | bytes 1000000 | tf_op jit(solution)/shard_map/pallas_call | solution.py:25
  17.2 0.1 collective-permute-start.6
  17.3 0.5 %collective-permute-start.8 = (f32[5,5,8,128]{3,2,1,0:T(8,128)S(1)}, f32[5,5,8,128]{3,2,1,0:T(8,128)S(1)}, u32[]{:S(2)}, u32[]{:S(2)}) collective-permute-start(f32[5,5,8,128]{3,2,1,0:T(8,128)S(1)} %get-tuple-element.34.half_ref), channel_id=1, source_target_pairs={{0,1},{1,0},{2,3},{3,2},{4,5},{5,4},{6,7},{7,6},{8,9},{9,8},{10,11... | collective-permute-start | bytes 307208 | tf_op jit(solution)/shard_map/ppermute | solution.py:479
  17.7 0.8 %collective-permute-done.6.ends_other_ref = f32[2,5,16,128]{3,2,1,0:T(8,128)S(1)} collective-permute-done((f32[2,5,16,128]{3,2,1,0:T(8,128)S(1)}, f32[2,5,16,128]{3,2,1,0:T(8,128)S(1)}, u32[]{:S(2)}, u32[]{:S(2)}) %collective-permute-start.6) | collective-permute-done | bytes 81952 | tf_op jit(solution)/shard_map/ppermute | solution.py:479
  18.6 1.6 %collective-permute-start.7 = (f32[1,5,16,128]{3,2,1,0:T(8,128)S(1)}, f32[1,5,16,128]{3,2,1,0:T(8,128)S(1)}, u32[]{:S(2)}, u32[]{:S(2)}) collective-permute-start(f32[1,5,16,128]{3,2,1,0:T(8,128)S(1)} %shard_map.102.pair_ref), channel_id=1, source_target_pairs={{0,2},{1,3},{2,0},{3,1},{4,6},{5,7},{6,4},{7,5},{8,10},{9,11},{10,... | collective-permute-start | bytes 122888 | tf_op jit(solution)/shard_map/ppermute | solution.py:479
  20.1 0.0 collective-permute-done.8.half_other_ref
  20.1 2.5 %collective-permute-done.7.pair_other_ref = f32[1,5,16,128]{3,2,1,0:T(8,128)S(1)} collective-permute-done((f32[1,5,16,128]{3,2,1,0:T(8,128)S(1)}, f32[1,5,16,128]{3,2,1,0:T(8,128)S(1)}, u32[]{:S(2)}, u32[]{:S(2)}) %collective-permute-start.7) | collective-permute-done | bytes 40992 | tf_op jit(solution)/shard_map/ppermute | solution.py:479
  22.6 0.4 %shard_map.103 = (f32[8,5,16,128]{3,2,1,0:T(8,128)S(1)}, f32[5,16,128]{2,1,0:T(8,128)S(1)}, f32[8,16,128]{2,1,0:T(8,128)S(1)}) custom-call(f32[16,128]{1,0:T(8,128)S(1)} %get-tuple-element.24.live_ref, f32[8,5,16,128]{3,2,1,0:T(8,128)S(1)} %bitcast.17, f32[5,16,128]{2,1,0:T(8,128)S(1)} %collective-permute-done.above_ref, ...), custom_call_target="tpu_custom_call" | custom-call | flops 1000000000 | bytes 1000000 | tf_op jit(solution)/shard_map/pallas_call | solution.py:25
  23.1 12.5 %all_to_all.5.tiles_ref = f32[8,16,128]{2,1,0:T(8,128)S(1)} all-to-all(f32[8,16,128]{2,1,0:T(8,128)S(1)} %get-tuple-element.35), channel_id=1, replica_groups=mesh['zone'=8,'ja'=4] {'zone'}, dimensions={0} | all-to-all | bytes 131072 | tf_op jit(solution)/shard_map/all_to_all | solution.py:528
  35.6 1.0 %shard_map.104 = (f32[8,5,16,128]{3,2,1,0:T(8,128)S(1)}, f32[8,5,16,128]{3,2,1,0:T(8,128)S(1)}, f32[3,5,16,128]{3,2,1,0:T(8,128)S(1)}, f32[5,5,16,128]{3,2,1,0:T(8,128)S(1)}) custom-call(f32[16,128]{1,0:T(8,128)S(1)} %get-tuple-element.24.live_ref, f32[2,8,16,128]{3,2,1,0:T(8,128)S(1)} %get-tuple-element.25.pick_ref, f32[8,16,128]{2,1,0:T(8,128)S(1)} %all_to_all.5.tiles_ref, ...), custom_call_target="tpu_custom_call" | custom-call | flops 1000000000 | bytes 1000000 | tf_op jit(solution)/shard_map/pallas_call | solution.py:25
  36.6 0.1 collective-permute-start.9
  36.7 1.3 %collective-permute-done.9.ends_other_ref = f32[3,5,16,128]{3,2,1,0:T(8,128)S(1)} collective-permute-done((f32[3,5,16,128]{3,2,1,0:T(8,128)S(1)}, f32[3,5,16,128]{3,2,1,0:T(8,128)S(1)}, u32[]{:S(2)}, u32[]{:S(2)}) %collective-permute-start.9) | collective-permute-done | bytes 122912 | tf_op jit(solution)/shard_map/ppermute | solution.py:479
  38.0 1.4 %collective-permute-start.10 = (f32[2,5,16,128]{3,2,1,0:T(8,128)S(1)}, f32[2,5,16,128]{3,2,1,0:T(8,128)S(1)}, u32[]{:S(2)}, u32[]{:S(2)}) collective-permute-start(f32[2,5,16,128]{3,2,1,0:T(8,128)S(1)} %shard_map.105.pair_ref), channel_id=1, source_target_pairs={{0,2},{1,3},{2,0},{3,1},{4,6},{5,7},{6,4},{7,5},{8,10},{9,11},{10,... | collective-permute-start | bytes 245768 | tf_op jit(solution)/shard_map/ppermute | solution.py:479
  39.4 0.7 %shard_map.106.res_in_hbm = f32[8,5,16,128]{3,2,1,0:T(8,128)} custom-call(f32[8,5,16,128]{3,2,1,0:T(8,128)S(1)} %get-tuple-element.39.res_ref), custom_call_target="tpu_custom_call" | custom-call | flops 1000000000 | bytes 1000000 | tf_op jit(solution)/shard_map/pallas_call | solution.py:25
  40.1 2.4 %collective-permute-done.10.pair_other_ref = f32[2,5,16,128]{3,2,1,0:T(8,128)S(1)} collective-permute-done((f32[2,5,16,128]{3,2,1,0:T(8,128)S(1)}, f32[2,5,16,128]{3,2,1,0:T(8,128)S(1)}, u32[]{:S(2)}, u32[]{:S(2)}) %collective-permute-start.10) | collective-permute-done | bytes 81952 | tf_op jit(solution)/shard_map/ppermute | solution.py:479
  42.6 1.1 %shard_map.107 = (f32[8,5,16,128]{3,2,1,0:T(8,128)}, f32[8,5,16,128]{3,2,1,0:T(8,128)}) custom-call(f32[16,128]{1,0:T(8,128)S(1)} %get-tuple-element.24.live_ref, f32[5,5,16,128]{3,2,1,0:T(8,128)S(1)} %get-tuple-element.38.low0_ref, f32[8,5,16,128]{3,2,1,0:T(8,128)S(1)} %get-tuple-element.36.cur_ref, ...), custom_call_target="tpu_custom_call", output_to_operand_aliasing={{1}: (15, {})} | custom-call | flops 1000000000 | bytes 1000000 | tf_op jit(solution)/shard_map/pallas_call | solution.py:25
  (4 shorter events, 0.1 us)
Async XLA Ops:
  0.6 4.4 %copy-start = (f32[1,8,5,5,16,128]{5,4,3,2,1,0:T(8,128)S(1)}, f32[1,8,5,5,16,128]{5,4,3,2,1,0:T(8,128)}, u32[]{:S(2)}) copy-start(f32[1,8,5,5,16,128]{5,4,3,2,1,0:T(8,128)} %param.13) | copy-start | bytes 4915204
  0.6 4.3 %copy-start.3 = (f32[1,8,5,5,16,128]{5,4,3,2,1,0:T(8,128)S(1)}, f32[1,8,5,5,16,128]{5,4,3,2,1,0:T(8,128)}, u32[]{:S(2)}) copy-start(f32[1,8,5,5,16,128]{5,4,3,2,1,0:T(8,128)} %param.11) | copy-start | bytes 4915204
  0.7 4.3 %copy-start.4 = (f32[1,8,5,5,16,128]{5,4,3,2,1,0:T(8,128)S(1)}, f32[1,8,5,5,16,128]{5,4,3,2,1,0:T(8,128)}, u32[]{:S(2)}) copy-start(f32[1,8,5,5,16,128]{5,4,3,2,1,0:T(8,128)} %param.12) | copy-start | bytes 4915204
  2.0 5.9 %collective-permute-start.1 = (f32[1,16,128]{2,1,0:T(8,128)S(1)}, f32[1,16,128]{2,1,0:T(8,128)S(1)}, u32[]{:S(2)}, u32[]{:S(2)}) collective-permute-start(f32[1,16,128]{2,1,0:T(8,128)S(1)} %get-tuple-element.23.tile_ref.own_ref), channel_id=1, source_target_pairs={{0,4},{4,0},{8,12},{12,8},{16,20},{20,16},{24,28},{28,24},{1,5},{5... | collective-permute-start | bytes 24584 | tf_op jit(solution)/shard_map/ppermute | solution.py:500
  5.0 9.4 %copy-start.5 = (f32[1,8,5,16,128]{4,3,2,1,0:T(8,128)S(1)}, f32[1,8,5,16,128]{4,3,2,1,0:T(8,128)}, u32[]{:S(2)}) copy-start(f32[1,8,5,16,128]{4,3,2,1,0:T(8,128)} %param.9) | copy-start | bytes 983044
  7.9 6.6 %copy-start.1 = (f32[1,8,5,5,16,128]{5,4,3,2,1,0:T(8,128)S(1)}, f32[1,8,5,5,16,128]{5,4,3,2,1,0:T(8,128)}, u32[]{:S(2)}) copy-start(f32[1,8,5,5,16,128]{5,4,3,2,1,0:T(8,128)} %param.10) | copy-start | bytes 4915204
  7.9 6.6 %copy-start.2 = (f32[1,8,5,16,128]{4,3,2,1,0:T(8,128)S(1)}, f32[1,8,5,16,128]{4,3,2,1,0:T(8,128)}, u32[]{:S(2)}) copy-start(f32[1,8,5,16,128]{4,3,2,1,0:T(8,128)} %param.8) | copy-start | bytes 983044
  8.0 2.1 %collective-permute-start.2 = (f32[3,5,5,16,128]{4,3,2,1,0:T(8,128)S(1)}, f32[3,5,5,16,128]{4,3,2,1,0:T(8,128)S(1)}, u32[]{:S(2)}, u32[]{:S(2)}) collective-permute-start(f32[3,5,5,16,128]{4,3,2,1,0:T(8,128)S(1)} %get-tuple-element.28.mine_ref.mats_ref), channel_id=1, source_target_pairs={{0,1},{1,0},{2,3},{3,2},{4,5},{5,4},{6,7},{7,6},{8,9},{9,8},{10,11... | collective-permute-start | bytes 1843208 | tf_op jit(solution)/shard_map/ppermute | solution.py:479
  8.0 3.8 %collective-permute-start.4 = (f32[2,16,128]{2,1,0:T(8,128)S(1)}, f32[2,16,128]{2,1,0:T(8,128)S(1)}, u32[]{:S(2)}, u32[]{:S(2)}) collective-permute-start(f32[2,16,128]{2,1,0:T(8,128)S(1)} %get-tuple-element.29.own_ref), channel_id=1, source_target_pairs={{0,8},{4,12},{8,0},{12,4},{16,24},{20,28},{24,16},{28,20},{1,9},{5... | collective-permute-start | bytes 49160 | tf_op jit(solution)/shard_map/ppermute | solution.py:500
  10.1 6.5 %collective-permute-start.3 = (f32[5,5,8,128]{3,2,1,0:T(8,128)S(1)}, f32[5,5,8,128]{3,2,1,0:T(8,128)S(1)}, u32[]{:S(2)}, u32[]{:S(2)}) collective-permute-start(f32[5,5,8,128]{3,2,1,0:T(8,128)S(1)} %shard_map.98.refs_0_), channel_id=1, source_target_pairs={{0,2},{1,3},{2,0},{3,1},{4,6},{5,7},{6,4},{7,5},{8,10},{9,11},{10,... | collective-permute-start | bytes 307208 | tf_op jit(solution)/shard_map/ppermute | solution.py:479
  11.7 3.4 %collective-permute-start = (f32[5,16,128]{2,1,0:T(8,128)S(1)}, f32[5,16,128]{2,1,0:T(8,128)S(1)}, u32[]{:S(2)}, u32[]{:S(2)}) collective-permute-start(f32[5,16,128]{2,1,0:T(8,128)S(1)} %get-tuple-element.26), channel_id=1, source_target_pairs={{1,0},{2,1},{3,2},{0,3},{5,4},{6,5},{7,6},{4,7},{9,8},{10,9},{11,1... | collective-permute-start | bytes 122888 | tf_op jit(solution)/shard_map/ppermute | solution.py:488
  11.8 4.8 %collective-permute-start.5 = (f32[4,16,128]{2,1,0:T(8,128)S(1)}, f32[4,16,128]{2,1,0:T(8,128)S(1)}, u32[]{:S(2)}, u32[]{:S(2)}) collective-permute-start(f32[4,16,128]{2,1,0:T(8,128)S(1)} %shard_map.99.tiles_ref.own_ref), channel_id=1, source_target_pairs={{0,16},{4,20},{8,24},{12,28},{16,0},{20,4},{24,8},{28,12},{1,17},{... | collective-permute-start | bytes 98312 | tf_op jit(solution)/shard_map/ppermute | solution.py:500
  17.2 1.3 %collective-permute-start.6 = (f32[2,5,16,128]{3,2,1,0:T(8,128)S(1)}, f32[2,5,16,128]{3,2,1,0:T(8,128)S(1)}, u32[]{:S(2)}, u32[]{:S(2)}) collective-permute-start(f32[2,5,16,128]{3,2,1,0:T(8,128)S(1)} %get-tuple-element.33.ends_ref), channel_id=1, source_target_pairs={{0,1},{1,0},{2,3},{3,2},{4,5},{5,4},{6,7},{7,6},{8,9},{9,8},{10,11... | collective-permute-start | bytes 245768 | tf_op jit(solution)/shard_map/ppermute | solution.py:479
  17.3 2.9 %collective-permute-start.8 = (f32[5,5,8,128]{3,2,1,0:T(8,128)S(1)}, f32[5,5,8,128]{3,2,1,0:T(8,128)S(1)}, u32[]{:S(2)}, u32[]{:S(2)}) collective-permute-start(f32[5,5,8,128]{3,2,1,0:T(8,128)S(1)} %get-tuple-element.34.half_ref), channel_id=1, source_target_pairs={{0,1},{1,0},{2,3},{3,2},{4,5},{5,4},{6,7},{7,6},{8,9},{9,8},{10,11... | collective-permute-start | bytes 307208 | tf_op jit(solution)/shard_map/ppermute | solution.py:479
  18.6 4.1 %collective-permute-start.7 = (f32[1,5,16,128]{3,2,1,0:T(8,128)S(1)}, f32[1,5,16,128]{3,2,1,0:T(8,128)S(1)}, u32[]{:S(2)}, u32[]{:S(2)}) collective-permute-start(f32[1,5,16,128]{3,2,1,0:T(8,128)S(1)} %shard_map.102.pair_ref), channel_id=1, source_target_pairs={{0,2},{1,3},{2,0},{3,1},{4,6},{5,7},{6,4},{7,5},{8,10},{9,11},{10,... | collective-permute-start | bytes 122888 | tf_op jit(solution)/shard_map/ppermute | solution.py:479
  36.6 1.4 %collective-permute-start.9 = (f32[3,5,16,128]{3,2,1,0:T(8,128)S(1)}, f32[3,5,16,128]{3,2,1,0:T(8,128)S(1)}, u32[]{:S(2)}, u32[]{:S(2)}) collective-permute-start(f32[3,5,16,128]{3,2,1,0:T(8,128)S(1)} %get-tuple-element.41.ends_ref), channel_id=1, source_target_pairs={{0,1},{1,0},{2,3},{3,2},{4,5},{5,4},{6,7},{7,6},{8,9},{9,8},{10,11... | collective-permute-start | bytes 368648 | tf_op jit(solution)/shard_map/ppermute | solution.py:479
  38.0 4.6 %collective-permute-start.10 = (f32[2,5,16,128]{3,2,1,0:T(8,128)S(1)}, f32[2,5,16,128]{3,2,1,0:T(8,128)S(1)}, u32[]{:S(2)}, u32[]{:S(2)}) collective-permute-start(f32[2,5,16,128]{3,2,1,0:T(8,128)S(1)} %shard_map.105.pair_ref), channel_id=1, source_target_pairs={{0,2},{1,3},{2,0},{3,1},{4,6},{5,7},{6,4},{7,5},{8,10},{9,11},{10,... | collective-permute-start | bytes 245768 | tf_op jit(solution)/shard_map/ppermute | solution.py:479

commit v10 on v9

--- a/solution.py
+++ b/solution.py
@@ -61,6 +61,10 @@
     return [[ref[(*lead, r, c)] for c in range(5)] for r in range(5)]
 
 
+def matrix_of(ref, i):
+    return [cell(ref, 5 * i + r) for r in range(5)]
+
+
 def cell(ref, *lead):
     return [ref[(*lead, v)] for v in range(5)]
 
@@ -92,11 +96,6 @@
     return [jnp.where(live, x, 0.0) for x in values]
 
 
-def has_above(values):
-    inner = lax.axis_index("ja") < lax.axis_size("ja") - 1
-    return [jnp.where(inner, x, 0.0) for x in values]
-
-
 def pack_kernel(flow_hbm, tile_ref, first_ref, flow_ref, sem):
     copy = pltpu.make_async_copy(flow_hbm, flow_ref, sem)
     copy.start()
@@ -113,11 +112,11 @@
         out_ref[count + w] = got_ref[w]
 
 
-def relay_kernel(own_ref, got_ref, mats_ref, mats_out_ref, out_ref):
+def relay_kernel(own_ref, got_ref, mats_ref, first_ref, mats_out_ref, out_ref):
     merge_kernel(own_ref, got_ref, out_ref)
-    for i in range(3):
-        for r in range(5):
-            put(mats_out_ref, cell(mats_ref, i, r), i, r)
+    for i in range(15):
+        put(mats_out_ref, cell(mats_ref, i), i)
+    put(mats_out_ref, cell(first_ref), 15)
 
 
 def neighbours(x):
@@ -153,6 +152,15 @@
 def put_col(ref, values, q, j, rows):
     for r in range(5):
         ref[j, r, q, rows] = values[r]
+
+
+def put_mat_col(ref, values, q, i, rows):
+    for r in range(5):
+        ref[5 * i + r, q, rows] = values[r]
+
+
+def mat_col(ref, q, i, rows):
+    return [ref[5 * i + r, q, rows] for r in range(5)]
 
 
 def mat(ref, j, rows):
@@ -193,9 +201,9 @@
         for rows in HALVES:
             f = mat(f_ref, j, rows)
             for q in range(5):
-                turned = matvec(f, col(mats_ref, q, 1, rows))
-                put_col(mats_ref, add(col(y_ref, q, j, rows), turned), q, 1, rows)
-                put_col(mats_ref, matvec(f, col(mats_ref, q, 2, rows)), q, 2, rows)
+                turned = matvec(f, mat_col(mats_ref, q, 1, rows))
+                put_mat_col(mats_ref, add(col(y_ref, q, j, rows), turned), q, 1, rows)
+                put_mat_col(mats_ref, matvec(f, mat_col(mats_ref, q, 2, rows)), q, 2, rows)
         return carry
 
     for rows in HALVES:
@@ -205,9 +213,9 @@
     lax.fori_loop(1, last + 1, forward, 0)
     for rows in HALVES:
         for q in range(5):
-            put_col(mats_ref, col(y_ref, q, last, rows), q, 0, rows)
-            put_col(mats_ref, col(y_ref, q, last, rows), q, 1, rows)
-            put_col(mats_ref, col(f_ref, q, last, rows), q, 2, rows)
+            put_mat_col(mats_ref, col(y_ref, q, last, rows), q, 0, rows)
+            put_mat_col(mats_ref, col(y_ref, q, last, rows), q, 1, rows)
+            put_mat_col(mats_ref, col(f_ref, q, last, rows), q, 2, rows)
     lax.fori_loop(0, last, backward, 0)
     for copy in scalars:
         copy.wait()
@@ -234,19 +242,20 @@
 
 
 def beta_kernel(mine_ref, other_ref, half_ref):
+    for side in range(2):
+        put(half_ref, [mine_ref[15, v, HALVES[side]] for v in range(5)], 5 + side)
     odd = lax.axis_index("ja") % 2
     for side in range(2):
         lo, hi = (mine_ref, other_ref) if side == 0 else (other_ref, mine_ref)
-        rows = pl.ds(8 * side, 8)
+        rows = HALVES[side]
 
         @pl.when(odd == side)
         def _():
-            d_hi = [[hi[1, r, c, rows] for c in range(5)] for r in range(5)]
-            n_lo = [[lo[2, r, c, rows] for c in range(5)] for r in range(5)]
+            d_hi = [[hi[5 + r, c, rows] for c in range(5)] for r in range(5)]
+            n_lo = [[lo[10 + r, c, rows] for c in range(5)] for r in range(5)]
             for q in range(5):
-                m_col = [lo[0, r, q, rows] for r in range(5)]
-                d_col = [lo[1, r, q, rows] for r in range(5)]
-                out = add(d_col, matvec(n_lo, matvec(d_hi, m_col)))
+                out = matvec(n_lo, matvec(d_hi, mat_col(lo, q, 0, rows)))
+                out = add(mat_col(lo, q, 1, rows), out)
                 for r in range(5):
                     half_ref[r, q] = out[r]
 
@@ -286,9 +295,9 @@
 
 
 def local_kernel(
-    half_ref, live_ref, pick_ref, own_ref, got_ref, cur_ref, above_ref, s0_ref,
+    half_ref, mats_other_ref, live_ref, pick_ref, own_ref, got_ref, cur_ref, s0_ref,
     inv_ref, e_ref, f_ref,
-    s_ref, ends_ref, half_out_ref, y_ref,
+    s_ref, ends_ref, above_ref, half_out_ref, y_ref,
 ):
     for r in range(5):
         put(half_out_ref, cell(half_ref, r), r)
@@ -299,7 +308,14 @@
     for j in range(last + 1):
         extra = [ghost_at(ghosts, j, v) for v in range(5)]
         put(s_ref, add(cell(s0_ref, j), matvec(block(inv_ref, j), extra)), j)
-    above = masked(live_ref, has_above(cell(above_ref)))
+    ja = lax.axis_index("ja")
+    above = []
+    for v in range(5):
+        beyond = jnp.concatenate([half_ref[5, v], half_ref[6, v]], axis=0)
+        beyond = jnp.where(ja == 1, beyond, 0.0)
+        above.append(jnp.where(ja % 2 == 0, mats_other_ref[15, v], beyond))
+    above = masked(live_ref, above)
+    put(above_ref, above)
     linked = matvec(block(f_ref, last), above)
     put(s_ref, add(cell(s_ref, last), [x * (1.0 / OMEGA) for x in linked]), last)
     sweeps(s_ref, e_ref, f_ref, y_ref, ends_ref, masked(live_ref, cell(cur_ref, last)))
@@ -348,12 +364,12 @@
 
         @pl.when(lax.axis_index("ja") < 2)
         def _():
-            put(out_ref, add(cell(ends_hi, 0), matvec(block(mats_hi, 0), c_lo)), 0)
+            put(out_ref, add(cell(ends_hi, 0), matvec(matrix_of(mats_hi, 0), c_lo)), 0)
 
         @pl.when(lax.axis_index("ja") >= 2)
         def _():
-            turned = add(cell(ends_hi, 1), matvec(block(mats_hi, 1), c_lo))
-            put(out_ref, add(cell(ends_lo, 1), matvec(block(mats_lo, 2), turned)), 0)
+            turned = add(cell(ends_hi, 1), matvec(matrix_of(mats_hi, 1), c_lo))
+            put(out_ref, add(cell(ends_lo, 1), matvec(matrix_of(mats_lo, 2), turned)), 0)
 
         if out_ref.shape[0] > 1:
             put(out_ref, cell(ends_hi, 2), 1)
@@ -364,7 +380,7 @@
 def join(mine_ref, other_ref, *at):
     mine, other = mine_ref[at], other_ref[at]
     odd = lax.axis_index("ja") % 2 == 1
-    return jnp.concatenate([jnp.where(odd, other, mine), jnp.where(odd, mine, other)], axis=0)
+    return jnp.concatenate([jnp.where(odd, mine, other), jnp.where(odd, other, mine)], axis=0)
 
 
 def inflows(
@@ -381,8 +397,8 @@
     @pl.when(ja == 0)
     def _():
         put(inflow_ref, zeros, 0)
-        b = add(cell(ends_other_ref, 1), matvec(block(mats_other_ref, 1), cell(ends_ref, 0)))
-        b = add(b, matvec(block(mats_other_ref, 2), far()))
+        b = add(cell(ends_other_ref, 1), matvec(matrix_of(mats_other_ref, 1), cell(ends_ref, 0)))
+        b = add(b, matvec(matrix_of(mats_other_ref, 2), far()))
         put(inflow_ref, b, 1)
 
     @pl.when(ja == 1)
@@ -394,13 +410,13 @@
     def _():
         a = cell(pair_other_ref, 0)
         put(inflow_ref, a, 0)
-        a = add(cell(ends_ref, 0), matvec(block(mats_ref, 0), a))
-        b = add(cell(ends_other_ref, 1), matvec(block(mats_other_ref, 1), a))
+        a = add(cell(ends_ref, 0), matvec(matrix_of(mats_ref, 0), a))
+        b = add(cell(ends_other_ref, 1), matvec(matrix_of(mats_other_ref, 1), a))
         put(inflow_ref, b, 1)
 
     @pl.when(ja == 3)
     def _():
-        a = add(cell(ends_other_ref, 0), matvec(block(mats_other_ref, 0), cell(pair_other_ref, 0)))
+        a = add(cell(ends_other_ref, 0), matvec(matrix_of(mats_other_ref, 0), cell(pair_other_ref, 0)))
         put(inflow_ref, a, 0)
         put(inflow_ref, zeros, 1)
 
@@ -421,7 +437,7 @@
         value = add(cell(s_ref, j), matvec(block(e_ref, j), value))
         put(y_ref, value, j)
     value = cell(inflow_ref, 1)
-    put(above_new_ref, add(masked(live_ref, has_above(cell(above_ref))), value))
+    put(above_new_ref, add(cell(above_ref), value))
     for j in range(planes - 1, -1, -1):
         value = add(cell(y_ref, j), matvec(block(f_ref, j), value))
         put(new_ref, add(masked(live_ref, cell(cur_ref, j)), value), j)
@@ -485,10 +501,9 @@
         flops=10**10,
         far=(0,),
     )(current)
-    above = lax.ppermute(first, "ja", [((p + 1) % parts, p) for p in range(parts)])
     e, f, mats, live, pick = call(
         matrix_kernel,
-        [blocks, blocks, (3, *matrix), state[2:], (2, zones, *state[2:])],
+        [blocks, blocks, (15, *plane), state[2:], (2, zones, *state[2:])],
         [buffer(*blocks)]
         + [pltpu.SMEM((zones,), jnp.int32)] * 2
         + [pltpu.SemaphoreType.DMA((2,))],
@@ -503,20 +518,24 @@
             break
         both = (stride, *state[2:])
         if stride == 2:
-            mats, tiles = call(relay_kernel, [mats.shape, both], flops=10**5)(tiles, got, mats)
+            mats, tiles = call(relay_kernel, [(16, *plane), both], flops=10**5)(
+                tiles, got, mats, first
+            )
             mats_other = swap(mats, 1)
-            half = call(beta_kernel, [(*matrix[:2], 8, matrix[3])], flops=10**5)(mats, mats_other)[0]
+            half = call(beta_kernel, [(7, plane[0], 8, plane[2])], flops=10**5)(mats, mats_other)[0]
         else:
             tiles = call(merge_kernel, [both], flops=10**5)(tiles, got, half)[0]
-    half = swap(half, 2)
-    s0 = call(source_kernel, [state])(tiles, live, current, force, diag, inv, e, f)[0]
-    s, ends, half = call(local_kernel, [state, (2, *plane), half.shape], work)(
-        half, live, pick, tiles, got, current, above, s0, inv, e, f
+    half = swap(half, 3)
+    s0 = call(source_kernel, [state], flops=2 * 10**9)(tiles, live, current, force, diag, inv, e, f)[0]
+    s, ends, above, half = call(
+        local_kernel, [state, (2, *plane), plane, (5, *half.shape[1:])], work
+    )(
+        half, mats_other, live, pick, tiles, got, current, s0, inv, e, f
     )
     ends_other = swap(ends, 1)
     half_other = swap(half, 1)
     pair = call(mid_kernel, [(1, *plane)], flops=10**5)(ends, ends_other, mats, mats_other)[0]
-    pair_other = swap(pair, 2)
+    pair_other = swap(pair, 3)
     flows = [buffer(2, *plane)]
     current, above, tile = call(
         final_kernel, [state, plane, (zones, *state[2:])], work + flows
@@ -531,7 +550,7 @@
     )
     ends_other = swap(ends, 1)
     pair = call(mid_kernel, [(2, *plane)])(ends, ends_other, mats, mats_other)[0]
-    pair_other = swap(pair, 2)
+    pair_other = swap(pair, 3)
     written = call(write_kernel, [state], [pltpu.SemaphoreType.DMA], out_specs=[HBM])(residual)[0]
     current, residual = call(
         last_kernel,

time: 43.8 us -> 43.1 us (0.984)
  starting transfers between devices: 12.5 us -> 11.5 us
  waiting for transfers between devices: 9.1 us -> 9.92 us
  blocking collectives: 12.5 us -> 12 us
    ppermute x7, starting transfers between devices: 5.24 us -> 4.26 us  [swap(): return lax.ppermute(x, 'ja', [(p, p ^ bit) for p in range(parts)])]
    ppermute x3, waiting for transfers between devices: 1.68 us -> 2.3 us  [per_device(): got = lax.ppermute(tiles, 'zone', [(z, z ^ stride) for z in range(zones)])]
    all_to_all x1, blocking collectives: 12.5 us -> 12 us  [per_device(): got = lax.all_to_all(tile, 'zone', 0, 0, tiled=True)]
  transfers between devices with their start and end apart: 11 -> 10, of which waited for: 7 -> 7; matrix products, arithmetic and copies ran while one was open for 0% -> 0% of each run, Pallas kernels for 10% -> 10%
where the time goes in v10:
time: 43.1 us; the launch traced here: 42.9 us
  blocking collectives  12 us (28%)
  starting transfers between devices  11.5 us (27%)
  waiting for transfers between devices  9.92 us (23%)
  Pallas kernels  8.6 us (20%)
  between operations  0.8 us (2%)
    all_to_all x1, blocking collectives, per_device(): got = lax.all_to_all(tile, 'zone', 0, 0, tiled=True)  12 us
    pallas_call x13, Pallas kernels, run(): pl.pallas_call(kernel, out_shape=[jax.ShapeDtypeStruct(s, jnp.float32) fo...  8.6 us
    ppermute x7, waiting for transfers between devices, swap(): return lax.ppermute(x, 'ja', [(p, p ^ bit) for p in range(parts)])  7.63 us
    ppermute x3, starting transfers between devices, per_device(): got = lax.ppermute(tiles, 'zone', [(z, z ^ stride) for z in range(zones)])  7.26 us
    ppermute x7, starting transfers between devices, swap(): return lax.ppermute(x, 'ja', [(p, p ^ bit) for p in range(parts)])  4.26 us
    ppermute x3, waiting for transfers between devices, per_device(): got = lax.ppermute(tiles, 'zone', [(z, z ^ stride) for z in range(zones)])  2.3 us
  transfers between devices with their start and end apart: 10, of which 7 were waited for; matrix products, arithmetic and copies ran while one was open for 0% of the time, Pallas kernels for 10%

profile of v10, /device:TPU:0, one launch (start us, length us, event | category | flops | bytes accessed | tf_op | source)
XLA Modules:
  0.0 42.9 jit_solution(1564809771856511210)
XLA Ops:
  0.6 0.0 copy-start
  0.6 0.0 copy-start.3
  0.7 0.0 copy-start.4
  0.7 1.3 %shard_map.95 = (f32[1,16,128]{2,1,0:T(8,128)S(1)}, f32[5,16,128]{2,1,0:T(8,128)S(1)}) custom-call(f32[8,5,16,128]{3,2,1,0:T(8,128)} %bitcast.14), custom_call_target="tpu_custom_call" | custom-call | flops 10000000000 | bytes 10000000 | tf_op jit(solution)/shard_map/pallas_call | solution.py:25
  2.0 3.0 %collective-permute-start = (f32[1,16,128]{2,1,0:T(8,128)S(1)}, f32[1,16,128]{2,1,0:T(8,128)S(1)}, u32[]{:S(2)}, u32[]{:S(2)}) collective-permute-start(f32[1,16,128]{2,1,0:T(8,128)S(1)} %get-tuple-element.24.tile_ref.own_ref), channel_id=1, source_target_pairs={{0,4},{4,0},{8,12},{12,8},{16,20},{20,16},{24,28},{28,24},{1,5},{5... | collective-permute-start | bytes 24584 | tf_op jit(solution)/shard_map/ppermute | solution.py:515
  5.0 0.0 copy-done
  5.0 0.0 copy-done.3
  5.0 0.0 copy-done.4
  5.0 2.8 %shard_map.96 = (f32[8,5,5,16,128]{4,3,2,1,0:T(8,128)S(1)}, f32[8,5,5,16,128]{4,3,2,1,0:T(8,128)S(1)}, f32[15,5,16,128]{3,2,1,0:T(8,128)S(1)}, f32[16,128]{1,0:T(8,128)S(1)}, f32[2,8,16,128]{3,2,1,0:T(8,128)S(1)}) custom-call(s32[8]{0:T(128)} %depth_hbm.1, s32[8]{0:T(128)} %east_hbm.1, f32[1,16,128]{2,1,0:T(8,128)S(1)} %get-tuple-element.24.tile_ref.own_ref, ...), custom_call_target="tpu_custom_call" | custom-call | flops 5000000000 | bytes 5000000 | tf_op jit(solution)/shard_map/pallas_call | solution.py:25
  7.8 0.0 copy-start.1
  7.8 0.0 copy-start.2
  7.9 0.0 copy-start.5
  7.9 0.0 collective-permute-done.got_ref
  7.9 0.1 collective-permute-start.1
  8.0 1.6 %collective-permute-start.3 = (f32[2,16,128]{2,1,0:T(8,128)S(1)}, f32[2,16,128]{2,1,0:T(8,128)S(1)}, u32[]{:S(2)}, u32[]{:S(2)}) collective-permute-start(f32[2,16,128]{2,1,0:T(8,128)S(1)} %get-tuple-element.30.own_ref), channel_id=1, source_target_pairs={{0,8},{4,12},{8,0},{12,4},{16,24},{20,28},{24,16},{28,20},{1,9},{5... | collective-permute-start | bytes 49160 | tf_op jit(solution)/shard_map/ppermute | solution.py:515
  9.7 0.4 %collective-permute-done.1.other_ref.mats_other_ref = f32[16,5,16,128]{3,2,1,0:T(8,128)S(1)} collective-permute-done((f32[16,5,16,128]{3,2,1,0:T(8,128)S(1)}, f32[16,5,16,128]{3,2,1,0:T(8,128)S(1)}, u32[]{:S(2)}, u32[]{:S(2)}) %collective-permute-start.1) | collective-permute-done | bytes 655392 | tf_op jit(solution)/shard_map/ppermute | solution.py:495
  10.1 0.1 shard_map.98.refs_0_
  10.2 1.3 %collective-permute-start.2 = (f32[7,5,8,128]{3,2,1,0:T(8,128)S(1)}, f32[7,5,8,128]{3,2,1,0:T(8,128)S(1)}, u32[]{:S(2)}, u32[]{:S(2)}) collective-permute-start(f32[7,5,8,128]{3,2,1,0:T(8,128)S(1)} %shard_map.98.refs_0_), channel_id=1, source_target_pairs={{0,3},{1,2},{2,1},{3,0},{4,7},{5,6},{6,5},{7,4},{8,11},{9,10},{10,... | collective-permute-start | bytes 430088 | tf_op jit(solution)/shard_map/ppermute | solution.py:495
  11.5 0.3 collective-permute-done.3.got_ref
  11.8 2.6 %collective-permute-start.4 = (f32[4,16,128]{2,1,0:T(8,128)S(1)}, f32[4,16,128]{2,1,0:T(8,128)S(1)}, u32[]{:S(2)}, u32[]{:S(2)}) collective-permute-start(f32[4,16,128]{2,1,0:T(8,128)S(1)} %shard_map.99.tiles_ref.own_ref), channel_id=1, source_target_pairs={{0,16},{4,20},{8,24},{12,28},{16,0},{20,4},{24,8},{28,12},{1,17},{... | collective-permute-start | bytes 98312 | tf_op jit(solution)/shard_map/ppermute | solution.py:515
  14.4 0.0 copy-done.1
  14.4 0.0 copy-done.2
  14.4 0.0 copy-done.5
  14.4 0.6 %shard_map.100.s0_ref = f32[8,5,16,128]{3,2,1,0:T(8,128)S(1)} custom-call(f32[4,16,128]{2,1,0:T(8,128)S(1)} %shard_map.99.tiles_ref.own_ref, f32[16,128]{1,0:T(8,128)S(1)} %get-tuple-element.25.live_ref, f32[8,5,16,128]{3,2,1,0:T(8,128)S(1)} %bitcast.15, f32[8,5,16,128]{3,2,1,0:T(8,128)S(1)} %bitcast.22, f32[8,5,5,16,128]{4,3,2,1,0:T(8,128)S(1)} %bitcast.12, ...), custom_call_target="tpu_custom_call" | custom-call | flops 2000000000 | bytes 2000000 | tf_op jit(solution)/shard_map/pallas_call | solution.py:25
  15.0 2.0 %collective-permute-done.4.got_ref = f32[4,16,128]{2,1,0:T(8,128)S(1)} collective-permute-done((f32[4,16,128]{2,1,0:T(8,128)S(1)}, f32[4,16,128]{2,1,0:T(8,128)S(1)}, u32[]{:S(2)}, u32[]{:S(2)}) %collective-permute-start.4) | collective-permute-done | bytes 32800 | tf_op jit(solution)/shard_map/ppermute | solution.py:515
  17.0 0.0 collective-permute-done.2.half_ref
  17.0 0.5 %shard_map.101 = (f32[8,5,16,128]{3,2,1,0:T(8,128)S(1)}, f32[2,5,16,128]{3,2,1,0:T(8,128)S(1)}, f32[5,16,128]{2,1,0:T(8,128)S(1)}, f32[5,5,8,128]{3,2,1,0:T(8,128)S(1)}) custom-call(f32[7,5,8,128]{3,2,1,0:T(8,128)S(1)} %collective-permute-done.2.half_ref, f32[16,5,16,128]{3,2,1,0:T(8,128)S(1)} %collective-permute-done.1.other_ref.mats_other_ref, ...), custom_call_target="tpu_custom_call" | custom-call | flops 1000000000 | bytes 1000000 | tf_op jit(solution)/shard_map/pallas_call | solution.py:25
  17.5 0.1 collective-permute-start.5
  17.6 0.5 %collective-permute-start.7 = (f32[5,5,8,128]{3,2,1,0:T(8,128)S(1)}, f32[5,5,8,128]{3,2,1,0:T(8,128)S(1)}, u32[]{:S(2)}, u32[]{:S(2)}) collective-permute-start(f32[5,5,8,128]{3,2,1,0:T(8,128)S(1)} %get-tuple-element.36.half_ref), channel_id=1, source_target_pairs={{0,1},{1,0},{2,3},{3,2},{4,5},{5,4},{6,7},{7,6},{8,9},{9,8},{10,11... | collective-permute-start | bytes 307208 | tf_op jit(solution)/shard_map/ppermute | solution.py:495
  18.1 0.8 %collective-permute-done.5.ends_other_ref = f32[2,5,16,128]{3,2,1,0:T(8,128)S(1)} collective-permute-done((f32[2,5,16,128]{3,2,1,0:T(8,128)S(1)}, f32[2,5,16,128]{3,2,1,0:T(8,128)S(1)}, u32[]{:S(2)}, u32[]{:S(2)}) %collective-permute-start.5) | collective-permute-done | bytes 81952 | tf_op jit(solution)/shard_map/ppermute | solution.py:495
  18.9 1.0 %collective-permute-start.6 = (f32[1,5,16,128]{3,2,1,0:T(8,128)S(1)}, f32[1,5,16,128]{3,2,1,0:T(8,128)S(1)}, u32[]{:S(2)}, u32[]{:S(2)}) collective-permute-start(f32[1,5,16,128]{3,2,1,0:T(8,128)S(1)} %shard_map.102.pair_ref), channel_id=1, source_target_pairs={{0,3},{1,2},{2,1},{3,0},{4,7},{5,6},{6,5},{7,4},{8,11},{9,10},{10,... | collective-permute-start | bytes 122888 | tf_op jit(solution)/shard_map/ppermute | solution.py:495
  19.8 0.0 collective-permute-done.7.half_other_ref
  19.9 2.6 %collective-permute-done.6.pair_other_ref = f32[1,5,16,128]{3,2,1,0:T(8,128)S(1)} collective-permute-done((f32[1,5,16,128]{3,2,1,0:T(8,128)S(1)}, f32[1,5,16,128]{3,2,1,0:T(8,128)S(1)}, u32[]{:S(2)}, u32[]{:S(2)}) %collective-permute-start.6) | collective-permute-done | bytes 40992 | tf_op jit(solution)/shard_map/ppermute | solution.py:495
  22.5 0.4 shard_map.103
  22.9 12.0 %all_to_all.5.tiles_ref = f32[8,16,128]{2,1,0:T(8,128)S(1)} all-to-all(f32[8,16,128]{2,1,0:T(8,128)S(1)} %get-tuple-element.37), channel_id=1, replica_groups=mesh['zone'=8,'ja'=4] {'zone'}, dimensions={0} | all-to-all | bytes 131072 | tf_op jit(solution)/shard_map/all_to_all | solution.py:547
  34.9 1.0 %shard_map.104 = (f32[8,5,16,128]{3,2,1,0:T(8,128)S(1)}, f32[8,5,16,128]{3,2,1,0:T(8,128)S(1)}, f32[3,5,16,128]{3,2,1,0:T(8,128)S(1)}, f32[5,5,16,128]{3,2,1,0:T(8,128)S(1)}) custom-call(f32[16,128]{1,0:T(8,128)S(1)} %get-tuple-element.25.live_ref, f32[2,8,16,128]{3,2,1,0:T(8,128)S(1)} %get-tuple-element.26.pick_ref, f32[8,16,128]{2,1,0:T(8,128)S(1)} %all_to_all.5.tiles_ref, ...), custom_call_target="tpu_custom_call" | custom-call | flops 1000000000 | bytes 1000000 | tf_op jit(solution)/shard_map/pallas_call | solution.py:25
  35.9 0.1 collective-permute-start.8
  36.0 1.3 %collective-permute-done.8.ends_other_ref = f32[3,5,16,128]{3,2,1,0:T(8,128)S(1)} collective-permute-done((f32[3,5,16,128]{3,2,1,0:T(8,128)S(1)}, f32[3,5,16,128]{3,2,1,0:T(8,128)S(1)}, u32[]{:S(2)}, u32[]{:S(2)}) %collective-permute-start.8) | collective-permute-done | bytes 122912 | tf_op jit(solution)/shard_map/ppermute | solution.py:495
  37.4 1.3 %collective-permute-start.9 = (f32[2,5,16,128]{3,2,1,0:T(8,128)S(1)}, f32[2,5,16,128]{3,2,1,0:T(8,128)S(1)}, u32[]{:S(2)}, u32[]{:S(2)}) collective-permute-start(f32[2,5,16,128]{3,2,1,0:T(8,128)S(1)} %shard_map.105.pair_ref), channel_id=1, source_target_pairs={{0,3},{1,2},{2,1},{3,0},{4,7},{5,6},{6,5},{7,4},{8,11},{9,10},{10,... | collective-permute-start | bytes 245768 | tf_op jit(solution)/shard_map/ppermute | solution.py:495
  38.7 0.7 %shard_map.106.res_in_hbm = f32[8,5,16,128]{3,2,1,0:T(8,128)} custom-call(f32[8,5,16,128]{3,2,1,0:T(8,128)S(1)} %get-tuple-element.41.res_ref), custom_call_target="tpu_custom_call" | custom-call | flops 1000000000 | bytes 1000000 | tf_op jit(solution)/shard_map/pallas_call | solution.py:25
  39.4 2.5 %collective-permute-done.9.pair_other_ref = f32[2,5,16,128]{3,2,1,0:T(8,128)S(1)} collective-permute-done((f32[2,5,16,128]{3,2,1,0:T(8,128)S(1)}, f32[2,5,16,128]{3,2,1,0:T(8,128)S(1)}, u32[]{:S(2)}, u32[]{:S(2)}) %collective-permute-start.9) | collective-permute-done | bytes 81952 | tf_op jit(solution)/shard_map/ppermute | solution.py:495
  41.9 1.1 %shard_map.107 = (f32[8,5,16,128]{3,2,1,0:T(8,128)}, f32[8,5,16,128]{3,2,1,0:T(8,128)}) custom-call(f32[16,128]{1,0:T(8,128)S(1)} %get-tuple-element.25.live_ref, f32[5,5,16,128]{3,2,1,0:T(8,128)S(1)} %get-tuple-element.40.low0_ref, f32[8,5,16,128]{3,2,1,0:T(8,128)S(1)} %get-tuple-element.38.cur_ref, ...), custom_call_target="tpu_custom_call", output_to_operand_aliasing={{1}: (15, {})} | custom-call | flops 1000000000 | bytes 1000000 | tf_op jit(solution)/shard_map/pallas_call | solution.py:25
  (4 shorter events, 0.1 us)
Async XLA Ops:
  0.6 4.4 %copy-start = (f32[1,8,5,5,16,128]{5,4,3,2,1,0:T(8,128)S(1)}, f32[1,8,5,5,16,128]{5,4,3,2,1,0:T(8,128)}, u32[]{:S(2)}) copy-start(f32[1,8,5,5,16,128]{5,4,3,2,1,0:T(8,128)} %param.13) | copy-start | bytes 4915204
  0.6 4.3 %copy-start.3 = (f32[1,8,5,5,16,128]{5,4,3,2,1,0:T(8,128)S(1)}, f32[1,8,5,5,16,128]{5,4,3,2,1,0:T(8,128)}, u32[]{:S(2)}) copy-start(f32[1,8,5,5,16,128]{5,4,3,2,1,0:T(8,128)} %param.11) | copy-start | bytes 4915204
  0.7 4.3 %copy-start.4 = (f32[1,8,5,5,16,128]{5,4,3,2,1,0:T(8,128)S(1)}, f32[1,8,5,5,16,128]{5,4,3,2,1,0:T(8,128)}, u32[]{:S(2)}) copy-start(f32[1,8,5,5,16,128]{5,4,3,2,1,0:T(8,128)} %param.12) | copy-start | bytes 4915204
  2.0 5.9 %collective-permute-start = (f32[1,16,128]{2,1,0:T(8,128)S(1)}, f32[1,16,128]{2,1,0:T(8,128)S(1)}, u32[]{:S(2)}, u32[]{:S(2)}) collective-permute-start(f32[1,16,128]{2,1,0:T(8,128)S(1)} %get-tuple-element.24.tile_ref.own_ref), channel_id=1, source_target_pairs={{0,4},{4,0},{8,12},{12,8},{16,20},{20,16},{24,28},{28,24},{1,5},{5... | collective-permute-start | bytes 24584 | tf_op jit(solution)/shard_map/ppermute | solution.py:515
  7.8 6.6 %copy-start.1 = (f32[1,8,5,5,16,128]{5,4,3,2,1,0:T(8,128)S(1)}, f32[1,8,5,5,16,128]{5,4,3,2,1,0:T(8,128)}, u32[]{:S(2)}) copy-start(f32[1,8,5,5,16,128]{5,4,3,2,1,0:T(8,128)} %param.10) | copy-start | bytes 4915204
  7.8 6.6 %copy-start.2 = (f32[1,8,5,16,128]{4,3,2,1,0:T(8,128)S(1)}, f32[1,8,5,16,128]{4,3,2,1,0:T(8,128)}, u32[]{:S(2)}) copy-start(f32[1,8,5,16,128]{4,3,2,1,0:T(8,128)} %param.8) | copy-start | bytes 983044
  7.9 6.6 %copy-start.5 = (f32[1,8,5,16,128]{4,3,2,1,0:T(8,128)S(1)}, f32[1,8,5,16,128]{4,3,2,1,0:T(8,128)}, u32[]{:S(2)}) copy-start(f32[1,8,5,16,128]{4,3,2,1,0:T(8,128)} %param.9) | copy-start | bytes 983044
  7.9 2.2 %collective-permute-start.1 = (f32[16,5,16,128]{3,2,1,0:T(8,128)S(1)}, f32[16,5,16,128]{3,2,1,0:T(8,128)S(1)}, u32[]{:S(2)}, u32[]{:S(2)}) collective-permute-start(f32[16,5,16,128]{3,2,1,0:T(8,128)S(1)} %get-tuple-element.29.mine_ref.mats_ref), channel_id=1, source_target_pairs={{0,1},{1,0},{2,3},{3,2},{4,5},{5,4},{6,7},{7,6},{8,9},{9,8},{10,11... | collective-permute-start | bytes 1966088 | tf_op jit(solution)/shard_map/ppermute | solution.py:495
  8.0 3.8 %collective-permute-start.3 = (f32[2,16,128]{2,1,0:T(8,128)S(1)}, f32[2,16,128]{2,1,0:T(8,128)S(1)}, u32[]{:S(2)}, u32[]{:S(2)}) collective-permute-start(f32[2,16,128]{2,1,0:T(8,128)S(1)} %get-tuple-element.30.own_ref), channel_id=1, source_target_pairs={{0,8},{4,12},{8,0},{12,4},{16,24},{20,28},{24,16},{28,20},{1,9},{5... | collective-permute-start | bytes 49160 | tf_op jit(solution)/shard_map/ppermute | solution.py:515
  10.2 6.8 %collective-permute-start.2 = (f32[7,5,8,128]{3,2,1,0:T(8,128)S(1)}, f32[7,5,8,128]{3,2,1,0:T(8,128)S(1)}, u32[]{:S(2)}, u32[]{:S(2)}) collective-permute-start(f32[7,5,8,128]{3,2,1,0:T(8,128)S(1)} %shard_map.98.refs_0_), channel_id=1, source_target_pairs={{0,3},{1,2},{2,1},{3,0},{4,7},{5,6},{6,5},{7,4},{8,11},{9,10},{10,... | collective-permute-start | bytes 430088 | tf_op jit(solution)/shard_map/ppermute | solution.py:495
  11.8 5.2 %collective-permute-start.4 = (f32[4,16,128]{2,1,0:T(8,128)S(1)}, f32[4,16,128]{2,1,0:T(8,128)S(1)}, u32[]{:S(2)}, u32[]{:S(2)}) collective-permute-start(f32[4,16,128]{2,1,0:T(8,128)S(1)} %shard_map.99.tiles_ref.own_ref), channel_id=1, source_target_pairs={{0,16},{4,20},{8,24},{12,28},{16,0},{20,4},{24,8},{28,12},{1,17},{... | collective-permute-start | bytes 98312 | tf_op jit(solution)/shard_map/ppermute | solution.py:515
  17.5 1.3 %collective-permute-start.5 = (f32[2,5,16,128]{3,2,1,0:T(8,128)S(1)}, f32[2,5,16,128]{3,2,1,0:T(8,128)S(1)}, u32[]{:S(2)}, u32[]{:S(2)}) collective-permute-start(f32[2,5,16,128]{3,2,1,0:T(8,128)S(1)} %get-tuple-element.35.ends_ref), channel_id=1, source_target_pairs={{0,1},{1,0},{2,3},{3,2},{4,5},{5,4},{6,7},{7,6},{8,9},{9,8},{10,11... | collective-permute-start | bytes 245768 | tf_op jit(solution)/shard_map/ppermute | solution.py:495
  17.6 2.3 %collective-permute-start.7 = (f32[5,5,8,128]{3,2,1,0:T(8,128)S(1)}, f32[5,5,8,128]{3,2,1,0:T(8,128)S(1)}, u32[]{:S(2)}, u32[]{:S(2)}) collective-permute-start(f32[5,5,8,128]{3,2,1,0:T(8,128)S(1)} %get-tuple-element.36.half_ref), channel_id=1, source_target_pairs={{0,1},{1,0},{2,3},{3,2},{4,5},{5,4},{6,7},{7,6},{8,9},{9,8},{10,11... | collective-permute-start | bytes 307208 | tf_op jit(solution)/shard_map/ppermute | solution.py:495
  18.9 3.6 %collective-permute-start.6 = (f32[1,5,16,128]{3,2,1,0:T(8,128)S(1)}, f32[1,5,16,128]{3,2,1,0:T(8,128)S(1)}, u32[]{:S(2)}, u32[]{:S(2)}) collective-permute-start(f32[1,5,16,128]{3,2,1,0:T(8,128)S(1)} %shard_map.102.pair_ref), channel_id=1, source_target_pairs={{0,3},{1,2},{2,1},{3,0},{4,7},{5,6},{6,5},{7,4},{8,11},{9,10},{10,... | collective-permute-start | bytes 122888 | tf_op jit(solution)/shard_map/ppermute | solution.py:495
  35.9 1.4 %collective-permute-start.8 = (f32[3,5,16,128]{3,2,1,0:T(8,128)S(1)}, f32[3,5,16,128]{3,2,1,0:T(8,128)S(1)}, u32[]{:S(2)}, u32[]{:S(2)}) collective-permute-start(f32[3,5,16,128]{3,2,1,0:T(8,128)S(1)} %get-tuple-element.43.ends_ref), channel_id=1, source_target_pairs={{0,1},{1,0},{2,3},{3,2},{4,5},{5,4},{6,7},{7,6},{8,9},{9,8},{10,11... | collective-permute-start | bytes 368648 | tf_op jit(solution)/shard_map/ppermute | solution.py:495
  37.4 4.5 %collective-permute-start.9 = (f32[2,5,16,128]{3,2,1,0:T(8,128)S(1)}, f32[2,5,16,128]{3,2,1,0:T(8,128)S(1)}, u32[]{:S(2)}, u32[]{:S(2)}) collective-permute-start(f32[2,5,16,128]{3,2,1,0:T(8,128)S(1)} %shard_map.105.pair_ref), channel_id=1, source_target_pairs={{0,3},{1,2},{2,1},{3,0},{4,7},{5,6},{6,5},{7,4},{8,11},{9,10},{10,... | collective-permute-start | bytes 245768 | tf_op jit(solution)/shard_map/ppermute | solution.py:495

commit v11 on v10

--- a/solution.py
+++ b/solution.py
@@ -96,11 +96,12 @@
     return [jnp.where(live, x, 0.0) for x in values]
 
 
-def pack_kernel(flow_hbm, tile_ref, first_ref, flow_ref, sem):
+def pack_kernel(flow_hbm, tile_ref, first_ref, last_ref, flow_ref, sem):
     copy = pltpu.make_async_copy(flow_hbm, flow_ref, sem)
     copy.start()
     copy.wait()
     put(first_ref, cell(flow_ref, 0))
+    put(last_ref, cell(flow_ref, flow_ref.shape[0] - 1))
     pack_faces(lambda j, v: flow_ref[j, v], flow_ref.shape[0], tile_ref)
 
 
@@ -114,9 +115,9 @@
 
 def relay_kernel(own_ref, got_ref, mats_ref, first_ref, mats_out_ref, out_ref):
     merge_kernel(own_ref, got_ref, out_ref)
-    for i in range(15):
+    for i in range(20):
         put(mats_out_ref, cell(mats_ref, i), i)
-    put(mats_out_ref, cell(first_ref), 15)
+    put(mats_out_ref, cell(first_ref), 20)
 
 
 def neighbours(x):
@@ -125,6 +126,13 @@
     total = total + jnp.where(lane == 127, 0.0, pltpu.roll(x, 127, 1))
     total = total + jnp.where(row == 0, 0.0, pltpu.roll(x, 1, 0))
     return total + jnp.where(row == 15, 0.0, pltpu.roll(x, 15, 0))
+
+
+def offset_of(place, zones):
+    offset, stride = 0, zones // 2
+    while stride:
+        offset, place, stride = offset + stride * (place % 2), place // 2, stride // 2
+    return offset
 
 
 def ghosts_of(pick_ref, tile_at):
@@ -216,6 +224,7 @@
             put_mat_col(mats_ref, col(y_ref, q, last, rows), q, 0, rows)
             put_mat_col(mats_ref, col(y_ref, q, last, rows), q, 1, rows)
             put_mat_col(mats_ref, col(f_ref, q, last, rows), q, 2, rows)
+            put_mat_col(mats_ref, col(f_ref, q, last, rows), q, 3, rows)
     lax.fori_loop(0, last, backward, 0)
     for copy in scalars:
         copy.wait()
@@ -223,7 +232,7 @@
     row = iota(0)
     live_ref[...] = jnp.where(row < depth_ref[zone], 1.0, 0.0)
     for i in range(pick_ref.shape[1]):
-        w = zone ^ i
+        w = zone ^ offset_of(i, pick_ref.shape[1])
         rows = row < depth_ref[w]
         pick_ref[0, i] = jnp.where(rows & (east_ref[w] == zone), 1.0, 0.0)
         pick_ref[1, i] = jnp.where(rows & (east_ref[zone] == w), 1.0, 0.0)
@@ -241,15 +250,22 @@
         run(*other_refs, *mine_refs)
 
 
-def beta_kernel(mine_ref, other_ref, half_ref):
+def half_kernel(mine_ref, other_ref, last_ref, half_ref):
+    ja = lax.axis_index("ja")
+    low_pair = ja < 2
     for side in range(2):
-        put(half_ref, [mine_ref[15, v, HALVES[side]] for v in range(5)], 5 + side)
-    odd = lax.axis_index("ja") % 2
+        edge = [jnp.where(low_pair, last_ref[v], mine_ref[20, v]) for v in range(5)]
+        put(half_ref, [x[8 * side : 8 * side + 8] for x in edge], 5 + side)
     for side in range(2):
         lo, hi = (mine_ref, other_ref) if side == 0 else (other_ref, mine_ref)
         rows = HALVES[side]
 
-        @pl.when(odd == side)
+        @pl.when((ja % 2 == side) & low_pair)
+        def _():
+            for r in range(5):
+                put(half_ref, [hi[15 + r, c, rows] for c in range(5)], r)
+
+        @pl.when((ja % 2 == side) & (ja >= 2))
         def _():
             d_hi = [[hi[5 + r, c, rows] for c in range(5)] for r in range(5)]
             n_lo = [[lo[10 + r, c, rows] for c in range(5)] for r in range(5)]
@@ -297,7 +313,7 @@
 def local_kernel(
     half_ref, mats_other_ref, live_ref, pick_ref, own_ref, got_ref, cur_ref, s0_ref,
     inv_ref, e_ref, f_ref,
-    s_ref, ends_ref, above_ref, half_out_ref, y_ref,
+    s_ref, ends_ref, above_ref, beyond_ref, half_out_ref, y_ref,
 ):
     for r in range(5):
         put(half_out_ref, cell(half_ref, r), r)
@@ -308,13 +324,14 @@
     for j in range(last + 1):
         extra = [ghost_at(ghosts, j, v) for v in range(5)]
         put(s_ref, add(cell(s0_ref, j), matvec(block(inv_ref, j), extra)), j)
+    beyond = [jnp.concatenate([half_ref[5, v], half_ref[6, v]], axis=0) for v in range(5)]
+    beyond = masked(live_ref, beyond)
+    put(beyond_ref, beyond)
     ja = lax.axis_index("ja")
-    above = []
-    for v in range(5):
-        beyond = jnp.concatenate([half_ref[5, v], half_ref[6, v]], axis=0)
-        beyond = jnp.where(ja == 1, beyond, 0.0)
-        above.append(jnp.where(ja % 2 == 0, mats_other_ref[15, v], beyond))
-    above = masked(live_ref, above)
+    above = masked(live_ref, cell(mats_other_ref, 20))
+    above = [
+        jnp.where(ja % 2 == 0, x, jnp.where(ja == 1, z, 0.0)) for x, z in zip(above, beyond)
+    ]
     put(above_ref, above)
     linked = matvec(block(f_ref, last), above)
     put(s_ref, add(cell(s_ref, last), [x * (1.0 / OMEGA) for x in linked]), last)
@@ -328,7 +345,7 @@
 ):
     planes = cur_ref.shape[0]
     zone = lax.axis_index("zone")
-    ghosts = ghosts_of(pick_ref, lambda i: tiles_ref[zone ^ i])
+    ghosts = ghosts_of(pick_ref, lambda i: tiles_ref[zone ^ offset_of(i, tiles_ref.shape[0])])
     for r in range(5):
         put(low0_ref, cell(low_ref, 0, r), r)
     for j in range(planes):
@@ -371,8 +388,6 @@
             turned = add(cell(ends_hi, 1), matvec(matrix_of(mats_hi, 1), c_lo))
             put(out_ref, add(cell(ends_lo, 1), matvec(matrix_of(mats_lo, 2), turned)), 0)
 
-        if out_ref.shape[0] > 1:
-            put(out_ref, cell(ends_hi, 2), 1)
 
     by_place([ends_ref, mats_ref], [ends_other_ref, mats_other_ref], run)
 
@@ -422,10 +437,10 @@
 
 
 def final_kernel(
-    live_ref, cur_ref, above_ref, s_ref, e_ref, f_ref,
+    live_ref, cur_ref, above_ref, beyond_ref, s_ref, e_ref, f_ref,
     ends_ref, ends_other_ref, mats_ref, mats_other_ref, pair_ref, pair_other_ref,
     half_ref, half_other_ref,
-    new_ref, above_new_ref, tile_ref, y_ref, inflow_ref,
+    new_ref, above_new_ref, below_new_ref, tile_ref, y_ref, inflow_ref,
 ):
     planes = cur_ref.shape[0]
     inflows(
@@ -441,11 +456,15 @@
     for j in range(planes - 1, -1, -1):
         value = add(cell(y_ref, j), matvec(block(f_ref, j), value))
         put(new_ref, add(masked(live_ref, cell(cur_ref, j)), value), j)
+    coupling = [[join(half_ref, half_other_ref, r, c) for c in range(5)] for r in range(5)]
+    raised = add(cell(inflow_ref, 0), matvec(coupling, value))
+    kept = [x * (1.0 - 1.0 / OMEGA) for x in cell(beyond_ref)]
+    put(below_new_ref, add(raised, kept))
     pack_faces(lambda j, v: new_ref[j, v], planes, tile_ref)
 
 
 def last_kernel(
-    live_ref, low0_ref, cur_ref, res_ref, s_ref, e_ref, f_ref,
+    live_ref, low0_ref, below_ref, cur_ref, res_ref, s_ref, e_ref, f_ref,
     ends_ref, ends_other_ref, mats_ref, mats_other_ref, pair_ref, pair_other_ref,
     half_ref, half_other_ref, res_in_hbm,
     new_hbm, res_hbm, y_ref, inflow_ref, new_ref, res0_ref, sems,
@@ -454,7 +473,7 @@
     planes = cur_ref.shape[0]
     ja = lax.axis_index("ja")
     before = [
-        jnp.where(ja == 0, 0.0, jnp.where(ja == 2, pair_other_ref[1, v], ends_other_ref[2, v]))
+        jnp.where(ja == 0, 0.0, jnp.where(ja == 2, below_ref[v], ends_other_ref[2, v]))
         for v in range(5)
     ]
     put(res0_ref, add(cell(res_ref, 0), masked(live_ref, matvec(block(low0_ref), before))))
@@ -494,41 +513,43 @@
     def swap(x, bit):
         return lax.ppermute(x, "ja", [(p, p ^ bit) for p in range(parts)])
 
-    tile, first = call(
+    tile, first, final = call(
         pack_kernel,
-        [(1, *state[2:]), plane],
+        [(1, *state[2:]), plane, plane],
         work + [pltpu.SemaphoreType.DMA],
         flops=10**10,
         far=(0,),
     )(current)
     e, f, mats, live, pick = call(
         matrix_kernel,
-        [blocks, blocks, (15, *plane), state[2:], (2, zones, *state[2:])],
+        [blocks, blocks, (20, *plane), state[2:], (2, zones, *state[2:])],
         [buffer(*blocks)]
         + [pltpu.SMEM((zones,), jnp.int32)] * 2
         + [pltpu.SemaphoreType.DMA((2,))],
         flops=5 * 10**9,
         far=(0, 1),
     )(zone_depth, east_zone, tile, inv, low, up)
-    tiles, stride = tile, 1
+    tiles, stride = tile, zones // 2
     while True:
         got = lax.ppermute(tiles, "zone", [(z, z ^ stride) for z in range(zones)])
-        stride *= 2
-        if stride == zones:
+        if stride == 1:
             break
-        both = (stride, *state[2:])
-        if stride == 2:
-            mats, tiles = call(relay_kernel, [(16, *plane), both], flops=10**5)(
+        both = (2 * tiles.shape[0], *state[2:])
+        if stride == zones // 2:
+            mats, tiles = call(relay_kernel, [(21, *plane), both], flops=10**5)(
                 tiles, got, mats, first
             )
             mats_other = swap(mats, 1)
-            half = call(beta_kernel, [(7, plane[0], 8, plane[2])], flops=10**5)(mats, mats_other)[0]
+            half = call(half_kernel, [(7, plane[0], 8, plane[2])], flops=10**5)(
+                mats, mats_other, final
+            )[0]
         else:
             tiles = call(merge_kernel, [both], flops=10**5)(tiles, got, half)[0]
+        stride //= 2
     half = swap(half, 3)
     s0 = call(source_kernel, [state], flops=2 * 10**9)(tiles, live, current, force, diag, inv, e, f)[0]
-    s, ends, above, half = call(
-        local_kernel, [state, (2, *plane), plane, (5, *half.shape[1:])], work
+    s, ends, above, beyond, half = call(
+        local_kernel, [state, (2, *plane), plane, plane, (5, *half.shape[1:])], work
     )(
         half, mats_other, live, pick, tiles, got, current, s0, inv, e, f
     )
@@ -537,10 +558,10 @@
     pair = call(mid_kernel, [(1, *plane)], flops=10**5)(ends, ends_other, mats, mats_other)[0]
     pair_other = swap(pair, 3)
     flows = [buffer(2, *plane)]
-    current, above, tile = call(
-        final_kernel, [state, plane, (zones, *state[2:])], work + flows
+    current, above, below, tile = call(
+        final_kernel, [state, plane, plane, (zones, *state[2:])], work + flows
     )(
-        live, current, above, s, e, f,
+        live, current, above, beyond, s, e, f,
         ends, ends_other, mats, mats_other, pair, pair_other, half, half_other,
     )
 
@@ -549,7 +570,7 @@
         live, pick, got, current, above, force, diag, low, up, inv, e, f
     )
     ends_other = swap(ends, 1)
-    pair = call(mid_kernel, [(2, *plane)])(ends, ends_other, mats, mats_other)[0]
+    pair = call(mid_kernel, [(1, *plane)])(ends, ends_other, mats, mats_other)[0]
     pair_other = swap(pair, 3)
     written = call(write_kernel, [state], [pltpu.SemaphoreType.DMA], out_specs=[HBM])(residual)[0]
     current, residual = call(
@@ -557,9 +578,9 @@
         [state, state],
         work + flows + work + [buffer(*plane), pltpu.SemaphoreType.DMA((planes + 1,))],
         out_specs=[HBM, HBM],
-        alias={15: 1},
+        alias={16: 1},
     )(
-        live, low0, current, residual, s, e, f,
+        live, low0, below, current, residual, s, e, f,
         ends, ends_other, mats, mats_other, pair, pair_other, half, half_other, written,
     )
     return (current[None], residual[None])

time: 43.1 us -> 42.1 us (0.977)
  waiting for transfers between devices: 9.92 us -> 8.83 us
  starting transfers between devices: 11.5 us -> 12.1 us
    ppermute x7, waiting for transfers between devices: 7.63 us -> 7.06 us  [swap(): return lax.ppermute(x, 'ja', [(p, p ^ bit) for p in range(parts)])]
    ppermute x7, starting transfers between devices: 4.26 us -> 4.8 us  [swap(): return lax.ppermute(x, 'ja', [(p, p ^ bit) for p in range(parts)])]
    ppermute x3, waiting for transfers between devices: 2.3 us -> 1.77 us  [per_device(): got = lax.ppermute(tiles, 'zone', [(z, z ^ stride) for z in range(zones)])]
    all_to_all x1, blocking collectives: 12 us -> 11.6 us  [per_device(): got = lax.all_to_all(tile, 'zone', 0, 0, tiled=True)]
where the time goes in v11:
time: 42.1 us; the launch traced here: 41.9 us
  starting transfers between devices  12.1 us (29%)
  blocking collectives  11.6 us (28%)
  waiting for transfers between devices  8.83 us (21%)
  Pallas kernels  8.66 us (21%)
  between operations  0.8 us (2%)
    all_to_all x1, blocking collectives, per_device(): got = lax.all_to_all(tile, 'zone', 0, 0, tiled=True)  11.6 us
    pallas_call x13, Pallas kernels, run(): pl.pallas_call(kernel, out_shape=[jax.ShapeDtypeStruct(s, jnp.float32) fo...  8.66 us
    ppermute x3, starting transfers between devices, per_device(): got = lax.ppermute(tiles, 'zone', [(z, z ^ stride) for z in range(zones)])  7.26 us
    ppermute x7, waiting for transfers between devices, swap(): return lax.ppermute(x, 'ja', [(p, p ^ bit) for p in range(parts)])  7.06 us
    ppermute x7, starting transfers between devices, swap(): return lax.ppermute(x, 'ja', [(p, p ^ bit) for p in range(parts)])  4.8 us
    ppermute x3, waiting for transfers between devices, per_device(): got = lax.ppermute(tiles, 'zone', [(z, z ^ stride) for z in range(zones)])  1.77 us
  transfers between devices with their start and end apart: 10, of which 7 were waited for; matrix products, arithmetic and copies ran while one was open for 0% of the time, Pallas kernels for 10%

profile of v11, /device:TPU:0, one launch (start us, length us, event | category | flops | bytes accessed | tf_op | source)
XLA Modules:
  0.0 41.9 jit_solution(15184201785327727091)
XLA Ops:
  0.6 0.0 copy-start
  0.6 0.0 copy-start.3
  0.7 0.0 copy-start.4
  0.7 1.3 %shard_map.95 = (f32[1,16,128]{2,1,0:T(8,128)S(1)}, f32[5,16,128]{2,1,0:T(8,128)S(1)}, f32[5,16,128]{2,1,0:T(8,128)S(1)}) custom-call(f32[8,5,16,128]{3,2,1,0:T(8,128)} %bitcast.14), custom_call_target="tpu_custom_call" | custom-call | flops 10000000000 | bytes 10000000 | tf_op jit(solution)/shard_map/pallas_call | solution.py:25
  2.0 4.1 %collective-permute-start = (f32[1,16,128]{2,1,0:T(8,128)S(1)}, f32[1,16,128]{2,1,0:T(8,128)S(1)}, u32[]{:S(2)}, u32[]{:S(2)}) collective-permute-start(f32[1,16,128]{2,1,0:T(8,128)S(1)} %get-tuple-element.27.tile_ref.own_ref), channel_id=1, source_target_pairs={{0,16},{4,20},{8,24},{12,28},{16,0},{20,4},{24,8},{28,12},{1,17},{... | collective-permute-start | bytes 24584 | tf_op jit(solution)/shard_map/ppermute | solution.py:534
  6.1 0.0 copy-done
  6.1 0.0 copy-done.3
  6.1 0.0 copy-done.4
  6.1 2.9 %shard_map.96 = (f32[8,5,5,16,128]{4,3,2,1,0:T(8,128)S(1)}, f32[8,5,5,16,128]{4,3,2,1,0:T(8,128)S(1)}, f32[20,5,16,128]{3,2,1,0:T(8,128)S(1)}, f32[16,128]{1,0:T(8,128)S(1)}, f32[2,8,16,128]{3,2,1,0:T(8,128)S(1)}) custom-call(s32[8]{0:T(128)} %depth_hbm.1, s32[8]{0:T(128)} %east_hbm.1, f32[1,16,128]{2,1,0:T(8,128)S(1)} %get-tuple-element.27.tile_ref.own_ref, ...), custom_call_target="tpu_custom_call" | custom-call | flops 5000000000 | bytes 5000000 | tf_op jit(solution)/shard_map/pallas_call | solution.py:25
  8.9 0.0 copy-start.1
  9.0 0.0 copy-start.2
  9.0 0.0 copy-start.5
  9.0 0.0 collective-permute-done.got_ref
  9.0 0.1 shard_map.97
  9.1 0.1 collective-permute-start.1
  9.1 1.6 %collective-permute-start.3 = (f32[2,16,128]{2,1,0:T(8,128)S(1)}, f32[2,16,128]{2,1,0:T(8,128)S(1)}, u32[]{:S(2)}, u32[]{:S(2)}) collective-permute-start(f32[2,16,128]{2,1,0:T(8,128)S(1)} %get-tuple-element.34.own_ref), channel_id=1, source_target_pairs={{0,8},{4,12},{8,0},{12,4},{16,24},{20,28},{24,16},{28,20},{1,9},{5... | collective-permute-start | bytes 49160 | tf_op jit(solution)/shard_map/ppermute | solution.py:534
  10.8 0.7 %collective-permute-done.1.other_ref.mats_other_ref = f32[21,5,16,128]{3,2,1,0:T(8,128)S(1)} collective-permute-done((f32[21,5,16,128]{3,2,1,0:T(8,128)S(1)}, f32[21,5,16,128]{3,2,1,0:T(8,128)S(1)}, u32[]{:S(2)}, u32[]{:S(2)}) %collective-permute-start.1) | collective-permute-done | bytes 860192 | tf_op jit(solution)/shard_map/ppermute | solution.py:514
  11.5 1.4 %collective-permute-start.2 = (f32[7,5,8,128]{3,2,1,0:T(8,128)S(1)}, f32[7,5,8,128]{3,2,1,0:T(8,128)S(1)}, u32[]{:S(2)}, u32[]{:S(2)}) collective-permute-start(f32[7,5,8,128]{3,2,1,0:T(8,128)S(1)} %shard_map.98.refs_0_), channel_id=1, source_target_pairs={{0,3},{1,2},{2,1},{3,0},{4,7},{5,6},{6,5},{7,4},{8,11},{9,10},{10,... | collective-permute-start | bytes 430088 | tf_op jit(solution)/shard_map/ppermute | solution.py:514
  12.9 0.0 collective-permute-done.3.got_ref
  12.9 1.5 %collective-permute-start.4 = (f32[4,16,128]{2,1,0:T(8,128)S(1)}, f32[4,16,128]{2,1,0:T(8,128)S(1)}, u32[]{:S(2)}, u32[]{:S(2)}) collective-permute-start(f32[4,16,128]{2,1,0:T(8,128)S(1)} %shard_map.99.tiles_ref.own_ref), channel_id=1, source_target_pairs={{0,4},{4,0},{8,12},{12,8},{16,20},{20,16},{24,28},{28,24},{1,5},{5... | collective-permute-start | bytes 98312 | tf_op jit(solution)/shard_map/ppermute | solution.py:534
  14.5 0.0 copy-done.1
  14.5 0.0 copy-done.2
  14.5 0.0 copy-done.5
  14.5 0.6 %shard_map.100.s0_ref = f32[8,5,16,128]{3,2,1,0:T(8,128)S(1)} custom-call(f32[4,16,128]{2,1,0:T(8,128)S(1)} %shard_map.99.tiles_ref.own_ref, f32[16,128]{1,0:T(8,128)S(1)} %get-tuple-element.28.live_ref, f32[8,5,16,128]{3,2,1,0:T(8,128)S(1)} %bitcast.15, f32[8,5,16,128]{3,2,1,0:T(8,128)S(1)} %bitcast.22, f32[8,5,5,16,128]{4,3,2,1,0:T(8,128)S(1)} %bitcast.12, ...), custom_call_target="tpu_custom_call" | custom-call | flops 2000000000 | bytes 2000000 | tf_op jit(solution)/shard_map/pallas_call | solution.py:25
  15.1 1.7 %collective-permute-done.4.got_ref = f32[4,16,128]{2,1,0:T(8,128)S(1)} collective-permute-done((f32[4,16,128]{2,1,0:T(8,128)S(1)}, f32[4,16,128]{2,1,0:T(8,128)S(1)}, u32[]{:S(2)}, u32[]{:S(2)}) %collective-permute-start.4) | collective-permute-done | bytes 32800 | tf_op jit(solution)/shard_map/ppermute | solution.py:534
  16.9 0.5 %collective-permute-done.2.half_ref = f32[7,5,8,128]{3,2,1,0:T(8,128)S(1)} collective-permute-done((f32[7,5,8,128]{3,2,1,0:T(8,128)S(1)}, f32[7,5,8,128]{3,2,1,0:T(8,128)S(1)}, u32[]{:S(2)}, u32[]{:S(2)}) %collective-permute-start.2) | collective-permute-done | bytes 143392 | tf_op jit(solution)/shard_map/ppermute | solution.py:514
  17.4 0.5 %shard_map.101 = (f32[8,5,16,128]{3,2,1,0:T(8,128)S(1)}, f32[2,5,16,128]{3,2,1,0:T(8,128)S(1)}, f32[5,16,128]{2,1,0:T(8,128)S(1)}, f32[5,16,128]{2,1,0:T(8,128)S(1)}, f32[5,5,8,128]{3,2,1,0:T(8,128)S(1)}) custom-call(f32[7,5,8,128]{3,2,1,0:T(8,128)S(1)} %collective-permute-done.2.half_ref, ...), custom_call_target="tpu_custom_call" | custom-call | flops 1000000000 | bytes 1000000 | tf_op jit(solution)/shard_map/pallas_call | solution.py:25
  17.9 0.2 collective-permute-start.5
  18.1 0.4 collective-permute-start.7
  18.4 0.8 %collective-permute-done.5.ends_other_ref = f32[2,5,16,128]{3,2,1,0:T(8,128)S(1)} collective-permute-done((f32[2,5,16,128]{3,2,1,0:T(8,128)S(1)}, f32[2,5,16,128]{3,2,1,0:T(8,128)S(1)}, u32[]{:S(2)}, u32[]{:S(2)}) %collective-permute-start.5) | collective-permute-done | bytes 81952 | tf_op jit(solution)/shard_map/ppermute | solution.py:514
  19.2 1.4 %collective-permute-start.6 = (f32[1,5,16,128]{3,2,1,0:T(8,128)S(1)}, f32[1,5,16,128]{3,2,1,0:T(8,128)S(1)}, u32[]{:S(2)}, u32[]{:S(2)}) collective-permute-start(f32[1,5,16,128]{3,2,1,0:T(8,128)S(1)} %shard_map.102.pair_ref), channel_id=1, source_target_pairs={{0,3},{1,2},{2,1},{3,0},{4,7},{5,6},{6,5},{7,4},{8,11},{9,10},{10,... | collective-permute-start | bytes 122888 | tf_op jit(solution)/shard_map/ppermute | solution.py:514
  20.6 0.0 collective-permute-done.7.half_other_ref
  20.6 2.2 %collective-permute-done.6.pair_other_ref = f32[1,5,16,128]{3,2,1,0:T(8,128)S(1)} collective-permute-done((f32[1,5,16,128]{3,2,1,0:T(8,128)S(1)}, f32[1,5,16,128]{3,2,1,0:T(8,128)S(1)}, u32[]{:S(2)}, u32[]{:S(2)}) %collective-permute-start.6) | collective-permute-done | bytes 40992 | tf_op jit(solution)/shard_map/ppermute | solution.py:514
  22.8 0.5 %shard_map.103 = (f32[8,5,16,128]{3,2,1,0:T(8,128)S(1)}, f32[5,16,128]{2,1,0:T(8,128)S(1)}, f32[5,16,128]{2,1,0:T(8,128)S(1)}, f32[8,16,128]{2,1,0:T(8,128)S(1)}) custom-call(f32[16,128]{1,0:T(8,128)S(1)} %get-tuple-element.28.live_ref, f32[8,5,16,128]{3,2,1,0:T(8,128)S(1)} %bitcast.17, f32[5,16,128]{2,1,0:T(8,128)S(1)} %get-tuple-element.37.above_ref, ...), custom_call_target="tpu_custom_call" | custom-call | flops 1000000000 | bytes 1000000 | tf_op jit(solution)/shard_map/pallas_call | solution.py:25
  23.3 11.6 %all_to_all.5.tiles_ref = f32[8,16,128]{2,1,0:T(8,128)S(1)} all-to-all(f32[8,16,128]{2,1,0:T(8,128)S(1)} %get-tuple-element.42), channel_id=1, replica_groups=mesh['zone'=8,'ja'=4] {'zone'}, dimensions={0} | all-to-all | bytes 131072 | tf_op jit(solution)/shard_map/all_to_all | solution.py:568
  34.9 0.9 %shard_map.104 = (f32[8,5,16,128]{3,2,1,0:T(8,128)S(1)}, f32[8,5,16,128]{3,2,1,0:T(8,128)S(1)}, f32[3,5,16,128]{3,2,1,0:T(8,128)S(1)}, f32[5,5,16,128]{3,2,1,0:T(8,128)S(1)}) custom-call(f32[16,128]{1,0:T(8,128)S(1)} %get-tuple-element.28.live_ref, f32[2,8,16,128]{3,2,1,0:T(8,128)S(1)} %get-tuple-element.29.pick_ref, f32[8,16,128]{2,1,0:T(8,128)S(1)} %all_to_all.5.tiles_ref, ...), custom_call_target="tpu_custom_call" | custom-call | flops 1000000000 | bytes 1000000 | tf_op jit(solution)/shard_map/pallas_call | solution.py:25
  35.8 0.1 collective-permute-start.8
  35.9 1.3 %collective-permute-done.8.ends_other_ref = f32[3,5,16,128]{3,2,1,0:T(8,128)S(1)} collective-permute-done((f32[3,5,16,128]{3,2,1,0:T(8,128)S(1)}, f32[3,5,16,128]{3,2,1,0:T(8,128)S(1)}, u32[]{:S(2)}, u32[]{:S(2)}) %collective-permute-start.8) | collective-permute-done | bytes 122912 | tf_op jit(solution)/shard_map/ppermute | solution.py:514
  37.2 1.3 %collective-permute-start.9 = (f32[1,5,16,128]{3,2,1,0:T(8,128)S(1)}, f32[1,5,16,128]{3,2,1,0:T(8,128)S(1)}, u32[]{:S(2)}, u32[]{:S(2)}) collective-permute-start(f32[1,5,16,128]{3,2,1,0:T(8,128)S(1)} %shard_map.105.pair_ref), channel_id=1, source_target_pairs={{0,3},{1,2},{2,1},{3,0},{4,7},{5,6},{6,5},{7,4},{8,11},{9,10},{10,... | collective-permute-start | bytes 122888 | tf_op jit(solution)/shard_map/ppermute | solution.py:514
  38.6 0.7 %shard_map.106.res_in_hbm = f32[8,5,16,128]{3,2,1,0:T(8,128)} custom-call(f32[8,5,16,128]{3,2,1,0:T(8,128)S(1)} %get-tuple-element.47.res_ref), custom_call_target="tpu_custom_call" | custom-call | flops 1000000000 | bytes 1000000 | tf_op jit(solution)/shard_map/pallas_call | solution.py:25
  39.3 1.5 %collective-permute-done.9.pair_other_ref = f32[1,5,16,128]{3,2,1,0:T(8,128)S(1)} collective-permute-done((f32[1,5,16,128]{3,2,1,0:T(8,128)S(1)}, f32[1,5,16,128]{3,2,1,0:T(8,128)S(1)}, u32[]{:S(2)}, u32[]{:S(2)}) %collective-permute-start.9) | collective-permute-done | bytes 40992 | tf_op jit(solution)/shard_map/ppermute | solution.py:514
  40.9 1.1 %shard_map.107 = (f32[8,5,16,128]{3,2,1,0:T(8,128)}, f32[8,5,16,128]{3,2,1,0:T(8,128)}) custom-call(f32[16,128]{1,0:T(8,128)S(1)} %get-tuple-element.28.live_ref, f32[5,5,16,128]{3,2,1,0:T(8,128)S(1)} %get-tuple-element.45.low0_ref, f32[5,16,128]{2,1,0:T(8,128)S(1)} %get-tuple-element.46.below_ref, ...), custom_call_target="tpu_custom_call", output_to_operand_aliasing={{1}: (16, {})} | custom-call | flops 1000000000 | bytes 1000000 | tf_op jit(solution)/shard_map/pallas_call | solution.py:25
  (4 shorter events, 0.1 us)
Async XLA Ops:
  0.6 5.4 %copy-start = (f32[1,8,5,5,16,128]{5,4,3,2,1,0:T(8,128)S(1)}, f32[1,8,5,5,16,128]{5,4,3,2,1,0:T(8,128)}, u32[]{:S(2)}) copy-start(f32[1,8,5,5,16,128]{5,4,3,2,1,0:T(8,128)} %param.13) | copy-start | bytes 4915204
  0.6 5.4 %copy-start.3 = (f32[1,8,5,5,16,128]{5,4,3,2,1,0:T(8,128)S(1)}, f32[1,8,5,5,16,128]{5,4,3,2,1,0:T(8,128)}, u32[]{:S(2)}) copy-start(f32[1,8,5,5,16,128]{5,4,3,2,1,0:T(8,128)} %param.11) | copy-start | bytes 4915204
  0.7 5.4 %copy-start.4 = (f32[1,8,5,5,16,128]{5,4,3,2,1,0:T(8,128)S(1)}, f32[1,8,5,5,16,128]{5,4,3,2,1,0:T(8,128)}, u32[]{:S(2)}) copy-start(f32[1,8,5,5,16,128]{5,4,3,2,1,0:T(8,128)} %param.12) | copy-start | bytes 4915204
  2.0 7.0 %collective-permute-start = (f32[1,16,128]{2,1,0:T(8,128)S(1)}, f32[1,16,128]{2,1,0:T(8,128)S(1)}, u32[]{:S(2)}, u32[]{:S(2)}) collective-permute-start(f32[1,16,128]{2,1,0:T(8,128)S(1)} %get-tuple-element.27.tile_ref.own_ref), channel_id=1, source_target_pairs={{0,16},{4,20},{8,24},{12,28},{16,0},{20,4},{24,8},{28,12},{1,17},{... | collective-permute-start | bytes 24584 | tf_op jit(solution)/shard_map/ppermute | solution.py:534
  8.9 5.5 %copy-start.1 = (f32[1,8,5,5,16,128]{5,4,3,2,1,0:T(8,128)S(1)}, f32[1,8,5,5,16,128]{5,4,3,2,1,0:T(8,128)}, u32[]{:S(2)}) copy-start(f32[1,8,5,5,16,128]{5,4,3,2,1,0:T(8,128)} %param.10) | copy-start | bytes 4915204
  9.0 5.5 %copy-start.2 = (f32[1,8,5,16,128]{4,3,2,1,0:T(8,128)S(1)}, f32[1,8,5,16,128]{4,3,2,1,0:T(8,128)}, u32[]{:S(2)}) copy-start(f32[1,8,5,16,128]{4,3,2,1,0:T(8,128)} %param.8) | copy-start | bytes 983044
  9.0 5.5 %copy-start.5 = (f32[1,8,5,16,128]{4,3,2,1,0:T(8,128)S(1)}, f32[1,8,5,16,128]{4,3,2,1,0:T(8,128)}, u32[]{:S(2)}) copy-start(f32[1,8,5,16,128]{4,3,2,1,0:T(8,128)} %param.9) | copy-start | bytes 983044
  9.1 2.5 %collective-permute-start.1 = (f32[21,5,16,128]{3,2,1,0:T(8,128)S(1)}, f32[21,5,16,128]{3,2,1,0:T(8,128)S(1)}, u32[]{:S(2)}, u32[]{:S(2)}) collective-permute-start(f32[21,5,16,128]{3,2,1,0:T(8,128)S(1)} %get-tuple-element.32.mine_ref.mats_ref), channel_id=1, source_target_pairs={{0,1},{1,0},{2,3},{3,2},{4,5},{5,4},{6,7},{7,6},{8,9},{9,8},{10,11... | collective-permute-start | bytes 2580488 | tf_op jit(solution)/shard_map/ppermute | solution.py:514
  9.1 3.8 %collective-permute-start.3 = (f32[2,16,128]{2,1,0:T(8,128)S(1)}, f32[2,16,128]{2,1,0:T(8,128)S(1)}, u32[]{:S(2)}, u32[]{:S(2)}) collective-permute-start(f32[2,16,128]{2,1,0:T(8,128)S(1)} %get-tuple-element.34.own_ref), channel_id=1, source_target_pairs={{0,8},{4,12},{8,0},{12,4},{16,24},{20,28},{24,16},{28,20},{1,9},{5... | collective-permute-start | bytes 49160 | tf_op jit(solution)/shard_map/ppermute | solution.py:534
  11.5 5.8 %collective-permute-start.2 = (f32[7,5,8,128]{3,2,1,0:T(8,128)S(1)}, f32[7,5,8,128]{3,2,1,0:T(8,128)S(1)}, u32[]{:S(2)}, u32[]{:S(2)}) collective-permute-start(f32[7,5,8,128]{3,2,1,0:T(8,128)S(1)} %shard_map.98.refs_0_), channel_id=1, source_target_pairs={{0,3},{1,2},{2,1},{3,0},{4,7},{5,6},{6,5},{7,4},{8,11},{9,10},{10,... | collective-permute-start | bytes 430088 | tf_op jit(solution)/shard_map/ppermute | solution.py:514
  12.9 3.9 %collective-permute-start.4 = (f32[4,16,128]{2,1,0:T(8,128)S(1)}, f32[4,16,128]{2,1,0:T(8,128)S(1)}, u32[]{:S(2)}, u32[]{:S(2)}) collective-permute-start(f32[4,16,128]{2,1,0:T(8,128)S(1)} %shard_map.99.tiles_ref.own_ref), channel_id=1, source_target_pairs={{0,4},{4,0},{8,12},{12,8},{16,20},{20,16},{24,28},{28,24},{1,5},{5... | collective-permute-start | bytes 98312 | tf_op jit(solution)/shard_map/ppermute | solution.py:534
  17.9 1.3 %collective-permute-start.5 = (f32[2,5,16,128]{3,2,1,0:T(8,128)S(1)}, f32[2,5,16,128]{3,2,1,0:T(8,128)S(1)}, u32[]{:S(2)}, u32[]{:S(2)}) collective-permute-start(f32[2,5,16,128]{3,2,1,0:T(8,128)S(1)} %get-tuple-element.40.ends_ref), channel_id=1, source_target_pairs={{0,1},{1,0},{2,3},{3,2},{4,5},{5,4},{6,7},{7,6},{8,9},{9,8},{10,11... | collective-permute-start | bytes 245768 | tf_op jit(solution)/shard_map/ppermute | solution.py:514
  18.1 2.6 %collective-permute-start.7 = (f32[5,5,8,128]{3,2,1,0:T(8,128)S(1)}, f32[5,5,8,128]{3,2,1,0:T(8,128)S(1)}, u32[]{:S(2)}, u32[]{:S(2)}) collective-permute-start(f32[5,5,8,128]{3,2,1,0:T(8,128)S(1)} %get-tuple-element.41.half_ref), channel_id=1, source_target_pairs={{0,1},{1,0},{2,3},{3,2},{4,5},{5,4},{6,7},{7,6},{8,9},{9,8},{10,11... | collective-permute-start | bytes 307208 | tf_op jit(solution)/shard_map/ppermute | solution.py:514
  19.2 3.6 %collective-permute-start.6 = (f32[1,5,16,128]{3,2,1,0:T(8,128)S(1)}, f32[1,5,16,128]{3,2,1,0:T(8,128)S(1)}, u32[]{:S(2)}, u32[]{:S(2)}) collective-permute-start(f32[1,5,16,128]{3,2,1,0:T(8,128)S(1)} %shard_map.102.pair_ref), channel_id=1, source_target_pairs={{0,3},{1,2},{2,1},{3,0},{4,7},{5,6},{6,5},{7,4},{8,11},{9,10},{10,... | collective-permute-start | bytes 122888 | tf_op jit(solution)/shard_map/ppermute | solution.py:514
  35.8 1.4 %collective-permute-start.8 = (f32[3,5,16,128]{3,2,1,0:T(8,128)S(1)}, f32[3,5,16,128]{3,2,1,0:T(8,128)S(1)}, u32[]{:S(2)}, u32[]{:S(2)}) collective-permute-start(f32[3,5,16,128]{3,2,1,0:T(8,128)S(1)} %get-tuple-element.49.ends_ref), channel_id=1, source_target_pairs={{0,1},{1,0},{2,3},{3,2},{4,5},{5,4},{6,7},{7,6},{8,9},{9,8},{10,11... | collective-permute-start | bytes 368648 | tf_op jit(solution)/shard_map/ppermute | solution.py:514
  37.2 3.6 %collective-permute-start.9 = (f32[1,5,16,128]{3,2,1,0:T(8,128)S(1)}, f32[1,5,16,128]{3,2,1,0:T(8,128)S(1)}, u32[]{:S(2)}, u32[]{:S(2)}) collective-permute-start(f32[1,5,16,128]{3,2,1,0:T(8,128)S(1)} %shard_map.105.pair_ref), channel_id=1, source_target_pairs={{0,3},{1,2},{2,1},{3,0},{4,7},{5,6},{6,5},{7,4},{8,11},{9,10},{10,... | collective-permute-start | bytes 122888 | tf_op jit(solution)/shard_map/ppermute | solution.py:514

commit v12 on v11

--- a/solution.py
+++ b/solution.py
@@ -254,7 +254,8 @@
     ja = lax.axis_index("ja")
     low_pair = ja < 2
     for side in range(2):
-        edge = [jnp.where(low_pair, last_ref[v], mine_ref[20, v]) for v in range(5)]
+        first = [jnp.where(ja == 3, other_ref[20, v], mine_ref[20, v]) for v in range(5)]
+        edge = [jnp.where(low_pair, last_ref[v], first[v]) for v in range(5)]
         put(half_ref, [x[8 * side : 8 * side + 8] for x in edge], 5 + side)
     for side in range(2):
         lo, hi = (mine_ref, other_ref) if side == 0 else (other_ref, mine_ref)
@@ -311,12 +312,10 @@
 
 
 def local_kernel(
-    half_ref, mats_other_ref, live_ref, pick_ref, own_ref, got_ref, cur_ref, s0_ref,
+    mats_other_ref, live_ref, pick_ref, own_ref, got_ref, cur_ref, s0_ref,
     inv_ref, e_ref, f_ref,
-    s_ref, ends_ref, above_ref, beyond_ref, half_out_ref, y_ref,
-):
-    for r in range(5):
-        put(half_out_ref, cell(half_ref, r), r)
+    s_ref, ends_ref, above_ref, y_ref,
+):
     last = cur_ref.shape[0] - 1
     count = own_ref.shape[0]
     ghosts = ghosts_of(pick_ref, lambda i: own_ref[i] if i < count else got_ref[i - count])
@@ -324,14 +323,8 @@
     for j in range(last + 1):
         extra = [ghost_at(ghosts, j, v) for v in range(5)]
         put(s_ref, add(cell(s0_ref, j), matvec(block(inv_ref, j), extra)), j)
-    beyond = [jnp.concatenate([half_ref[5, v], half_ref[6, v]], axis=0) for v in range(5)]
-    beyond = masked(live_ref, beyond)
-    put(beyond_ref, beyond)
-    ja = lax.axis_index("ja")
-    above = masked(live_ref, cell(mats_other_ref, 20))
-    above = [
-        jnp.where(ja % 2 == 0, x, jnp.where(ja == 1, z, 0.0)) for x, z in zip(above, beyond)
-    ]
+    even = lax.axis_index("ja") % 2 == 0
+    above = [jnp.where(even, x, 0.0) for x in masked(live_ref, cell(mats_other_ref, 20))]
     put(above_ref, above)
     linked = matvec(block(f_ref, last), above)
     put(s_ref, add(cell(s_ref, last), [x * (1.0 / OMEGA) for x in linked]), last)
@@ -375,21 +368,44 @@
     copy.wait()
 
 
+def compose(ends_lo, mats_lo, ends_hi, mats_hi, out_ref, first=None):
+    c_lo = cell(ends_lo, 0)
+
+    @pl.when(lax.axis_index("ja") < 2)
+    def _():
+        put(out_ref, add(cell(ends_hi, 0), matvec(matrix_of(mats_hi, 0), c_lo)), 0)
+
+    @pl.when(lax.axis_index("ja") >= 2)
+    def _():
+        turned = add(cell(ends_hi, 1), matvec(matrix_of(mats_hi, 1), c_lo))
+        raised = add(cell(ends_lo, 1), matvec(matrix_of(mats_lo, 2), turned))
+        if first is not None:
+            raised = add(raised, first(mats_lo))
+        put(out_ref, raised, 0)
+
+
 def mid_kernel(ends_ref, ends_other_ref, mats_ref, mats_other_ref, out_ref):
     def run(ends_lo, mats_lo, ends_hi, mats_hi):
-        c_lo = cell(ends_lo, 0)
-
-        @pl.when(lax.axis_index("ja") < 2)
-        def _():
-            put(out_ref, add(cell(ends_hi, 0), matvec(matrix_of(mats_hi, 0), c_lo)), 0)
-
-        @pl.when(lax.axis_index("ja") >= 2)
-        def _():
-            turned = add(cell(ends_hi, 1), matvec(matrix_of(mats_hi, 1), c_lo))
-            put(out_ref, add(cell(ends_lo, 1), matvec(matrix_of(mats_lo, 2), turned)), 0)
-
+        compose(ends_lo, mats_lo, ends_hi, mats_hi, out_ref)
 
     by_place([ends_ref, mats_ref], [ends_other_ref, mats_other_ref], run)
+
+
+def first_mid_kernel(
+    live_ref, half_ref, ends_ref, ends_other_ref, mats_ref, mats_other_ref,
+    out_ref, beyond_ref, half_out_ref,
+):
+    def first(mats_lo):
+        return [x * (1.0 / OMEGA) for x in masked(live_ref, cell(mats_lo, 20))]
+
+    def run(ends_lo, mats_lo, ends_hi, mats_hi):
+        compose(ends_lo, mats_lo, ends_hi, mats_hi, out_ref, first)
+
+    by_place([ends_ref, mats_ref], [ends_other_ref, mats_other_ref], run)
+    for r in range(5):
+        put(half_out_ref, cell(half_ref, r), r)
+    beyond = [jnp.concatenate([half_ref[5, v], half_ref[6, v]], axis=0) for v in range(5)]
+    put(beyond_ref, masked(live_ref, beyond))
 
 
 def join(mine_ref, other_ref, *at):
@@ -400,30 +416,43 @@
 
 def inflows(
     ends_ref, ends_other_ref, mats_ref, mats_other_ref, pair_ref, pair_other_ref,
-    half_ref, half_other_ref, inflow_ref,
+    half_ref, half_other_ref, inflow_ref, live_ref=None, beyond_ref=None,
 ):
     ja = lax.axis_index("ja")
     zeros = [jnp.zeros((16, 128), jnp.float32)] * 5
 
-    def far():
-        beta = [[join(half_ref, half_other_ref, r, c) for c in range(5)] for r in range(5)]
-        return add(cell(pair_other_ref, 0), matvec(beta, cell(pair_ref, 0)))
+    def joined():
+        return [[join(half_ref, half_other_ref, r, c) for c in range(5)] for r in range(5)]
+
+    def passed(value, coupling, first):
+        if beyond_ref is None:
+            return value
+        return add(value, [x * (1.0 / OMEGA) for x in matvec(coupling, first)])
+
+    def far(mats_hi_ref):
+        first = None if beyond_ref is None else cell(beyond_ref)
+        a = passed(cell(pair_ref, 0), matrix_of(mats_hi_ref, 3), first)
+        return add(cell(pair_other_ref, 0), matvec(joined(), a))
+
+    def near(mats_lo_ref):
+        first = None if beyond_ref is None else masked(live_ref, cell(mats_lo_ref, 20))
+        return passed(cell(pair_other_ref, 0), joined(), first)
 
     @pl.when(ja == 0)
     def _():
         put(inflow_ref, zeros, 0)
         b = add(cell(ends_other_ref, 1), matvec(matrix_of(mats_other_ref, 1), cell(ends_ref, 0)))
-        b = add(b, matvec(matrix_of(mats_other_ref, 2), far()))
+        b = add(b, matvec(matrix_of(mats_other_ref, 2), far(mats_other_ref)))
         put(inflow_ref, b, 1)
 
     @pl.when(ja == 1)
     def _():
         put(inflow_ref, cell(ends_other_ref, 0), 0)
-        put(inflow_ref, far(), 1)
+        put(inflow_ref, far(mats_ref), 1)
 
     @pl.when(ja == 2)
     def _():
-        a = cell(pair_other_ref, 0)
+        a = near(mats_ref)
         put(inflow_ref, a, 0)
         a = add(cell(ends_ref, 0), matvec(matrix_of(mats_ref, 0), a))
         b = add(cell(ends_other_ref, 1), matvec(matrix_of(mats_other_ref, 1), a))
@@ -431,7 +460,8 @@
 
     @pl.when(ja == 3)
     def _():
-        a = add(cell(ends_other_ref, 0), matvec(matrix_of(mats_other_ref, 0), cell(pair_other_ref, 0)))
+        a = near(mats_other_ref)
+        a = add(cell(ends_other_ref, 0), matvec(matrix_of(mats_other_ref, 0), a))
         put(inflow_ref, a, 0)
         put(inflow_ref, zeros, 1)
 
@@ -445,20 +475,22 @@
     planes = cur_ref.shape[0]
     inflows(
         ends_ref, ends_other_ref, mats_ref, mats_other_ref, pair_ref, pair_other_ref,
-        half_ref, half_other_ref, inflow_ref,
+        half_ref, half_other_ref, inflow_ref, live_ref, beyond_ref,
     )
     value = cell(inflow_ref, 0)
     for j in range(planes):
         value = add(cell(s_ref, j), matvec(block(e_ref, j), value))
         put(y_ref, value, j)
     value = cell(inflow_ref, 1)
-    put(above_new_ref, add(cell(above_ref), value))
+    kept = [x * (1.0 - 1.0 / OMEGA) for x in cell(beyond_ref)]
+    inner = lax.axis_index("ja") == 1
+    above = add(cell(above_ref), [jnp.where(inner, x, 0.0) for x in kept])
+    put(above_new_ref, add(above, value))
     for j in range(planes - 1, -1, -1):
         value = add(cell(y_ref, j), matvec(block(f_ref, j), value))
         put(new_ref, add(masked(live_ref, cell(cur_ref, j)), value), j)
     coupling = [[join(half_ref, half_other_ref, r, c) for c in range(5)] for r in range(5)]
     raised = add(cell(inflow_ref, 0), matvec(coupling, value))
-    kept = [x * (1.0 - 1.0 / OMEGA) for x in cell(beyond_ref)]
     put(below_new_ref, add(raised, kept))
     pack_faces(lambda j, v: new_ref[j, v], planes, tile_ref)
 
@@ -548,14 +580,14 @@
         stride //= 2
     half = swap(half, 3)
     s0 = call(source_kernel, [state], flops=2 * 10**9)(tiles, live, current, force, diag, inv, e, f)[0]
-    s, ends, above, beyond, half = call(
-        local_kernel, [state, (2, *plane), plane, plane, (5, *half.shape[1:])], work
-    )(
-        half, mats_other, live, pick, tiles, got, current, s0, inv, e, f
+    s, ends, above = call(local_kernel, [state, (2, *plane), plane], work)(
+        mats_other, live, pick, tiles, got, current, s0, inv, e, f
     )
     ends_other = swap(ends, 1)
+    pair, beyond, half = call(
+        first_mid_kernel, [(1, *plane), plane, (5, *half.shape[1:])], flops=10**5
+    )(live, half, ends, ends_other, mats, mats_other)
     half_other = swap(half, 1)
-    pair = call(mid_kernel, [(1, *plane)], flops=10**5)(ends, ends_other, mats, mats_other)[0]
     pair_other = swap(pair, 3)
     flows = [buffer(2, *plane)]
     current, above, below, tile = call(

time: 42.1 us -> 41.7 us (level)
  transfers between devices with their start and end apart: 10 -> 10, of which waited for: 7 -> 6; matrix products, arithmetic and copies ran while one was open for 0% -> 0% of each run, Pallas kernels for 10% -> 11%
where the time goes in v12:
time: 41.7 us; the launch traced here: 41.5 us
  starting transfers between devices  11.8 us (28%)
  blocking collectives  11.6 us (28%)
  Pallas kernels  8.67 us (21%)
  waiting for transfers between devices  8.62 us (21%)
  between operations  0.8 us (2%)
    all_to_all x1, blocking collectives, per_device(): got = lax.all_to_all(tile, 'zone', 0, 0, tiled=True)  11.6 us
    pallas_call x13, Pallas kernels, run(): pl.pallas_call(kernel, out_shape=[jax.ShapeDtypeStruct(s, jnp.float32) fo...  8.67 us
    ppermute x3, starting transfers between devices, per_device(): got = lax.ppermute(tiles, 'zone', [(z, z ^ stride) for z in range(zones)])  7.26 us
    ppermute x7, waiting for transfers between devices, swap(): return lax.ppermute(x, 'ja', [(p, p ^ bit) for p in range(parts)])  6.85 us
    ppermute x7, starting transfers between devices, swap(): return lax.ppermute(x, 'ja', [(p, p ^ bit) for p in range(parts)])  4.58 us
    ppermute x3, waiting for transfers between devices, per_device(): got = lax.ppermute(tiles, 'zone', [(z, z ^ stride) for z in range(zones)])  1.76 us
  transfers between devices with their start and end apart: 10, of which 6 were waited for; matrix products, arithmetic and copies ran while one was open for 0% of the time, Pallas kernels for 11%

profile of v12, /device:TPU:0, one launch (start us, length us, event | category | flops | bytes accessed | tf_op | source)
XLA Modules:
  0.0 41.5 jit_solution(3104384263419576480)
XLA Ops:
  0.6 0.0 copy-start
  0.6 0.0 copy-start.3
  0.7 0.0 copy-start.4
  0.7 1.3 %shard_map.95 = (f32[1,16,128]{2,1,0:T(8,128)S(1)}, f32[5,16,128]{2,1,0:T(8,128)S(1)}, f32[5,16,128]{2,1,0:T(8,128)S(1)}) custom-call(f32[8,5,16,128]{3,2,1,0:T(8,128)} %bitcast.14), custom_call_target="tpu_custom_call" | custom-call | flops 10000000000 | bytes 10000000 | tf_op jit(solution)/shard_map/pallas_call | solution.py:25
  2.0 4.1 %collective-permute-start = (f32[1,16,128]{2,1,0:T(8,128)S(1)}, f32[1,16,128]{2,1,0:T(8,128)S(1)}, u32[]{:S(2)}, u32[]{:S(2)}) collective-permute-start(f32[1,16,128]{2,1,0:T(8,128)S(1)} %get-tuple-element.28.tile_ref.own_ref), channel_id=1, source_target_pairs={{0,16},{4,20},{8,24},{12,28},{16,0},{20,4},{24,8},{28,12},{1,17},{... | collective-permute-start | bytes 24584 | tf_op jit(solution)/shard_map/ppermute | solution.py:566
  6.1 0.0 copy-done
  6.1 0.0 copy-done.3
  6.1 0.0 copy-done.4
  6.1 2.9 %shard_map.96 = (f32[8,5,5,16,128]{4,3,2,1,0:T(8,128)S(1)}, f32[8,5,5,16,128]{4,3,2,1,0:T(8,128)S(1)}, f32[20,5,16,128]{3,2,1,0:T(8,128)S(1)}, f32[16,128]{1,0:T(8,128)S(1)}, f32[2,8,16,128]{3,2,1,0:T(8,128)S(1)}) custom-call(s32[8]{0:T(128)} %depth_hbm.1, s32[8]{0:T(128)} %east_hbm.1, f32[1,16,128]{2,1,0:T(8,128)S(1)} %get-tuple-element.28.tile_ref.own_ref, ...), custom_call_target="tpu_custom_call" | custom-call | flops 5000000000 | bytes 5000000 | tf_op jit(solution)/shard_map/pallas_call | solution.py:25
  8.9 0.0 copy-start.1
  9.0 0.0 copy-start.2
  9.0 0.0 copy-start.5
  9.0 0.0 collective-permute-done.got_ref
  9.0 0.1 shard_map.97
  9.1 0.1 collective-permute-start.1
  9.1 1.6 %collective-permute-start.2 = (f32[2,16,128]{2,1,0:T(8,128)S(1)}, f32[2,16,128]{2,1,0:T(8,128)S(1)}, u32[]{:S(2)}, u32[]{:S(2)}) collective-permute-start(f32[2,16,128]{2,1,0:T(8,128)S(1)} %get-tuple-element.34.own_ref), channel_id=1, source_target_pairs={{0,8},{4,12},{8,0},{12,4},{16,24},{20,28},{24,16},{28,20},{1,9},{5... | collective-permute-start | bytes 49160 | tf_op jit(solution)/shard_map/ppermute | solution.py:566
  10.8 0.7 %collective-permute-done.1.other_ref.mats_other_ref = f32[21,5,16,128]{3,2,1,0:T(8,128)S(1)} collective-permute-done((f32[21,5,16,128]{3,2,1,0:T(8,128)S(1)}, f32[21,5,16,128]{3,2,1,0:T(8,128)S(1)}, u32[]{:S(2)}, u32[]{:S(2)}) %collective-permute-start.1) | collective-permute-done | bytes 860192 | tf_op jit(solution)/shard_map/ppermute | solution.py:546
  11.6 1.4 %collective-permute-start.4 = (f32[7,5,8,128]{3,2,1,0:T(8,128)S(1)}, f32[7,5,8,128]{3,2,1,0:T(8,128)S(1)}, u32[]{:S(2)}, u32[]{:S(2)}) collective-permute-start(f32[7,5,8,128]{3,2,1,0:T(8,128)S(1)} %shard_map.98.refs_0_), channel_id=1, source_target_pairs={{0,3},{1,2},{2,1},{3,0},{4,7},{5,6},{6,5},{7,4},{8,11},{9,10},{10,... | collective-permute-start | bytes 430088 | tf_op jit(solution)/shard_map/ppermute | solution.py:546
  12.9 0.0 collective-permute-done.2.got_ref
  12.9 1.5 %collective-permute-start.3 = (f32[4,16,128]{2,1,0:T(8,128)S(1)}, f32[4,16,128]{2,1,0:T(8,128)S(1)}, u32[]{:S(2)}, u32[]{:S(2)}) collective-permute-start(f32[4,16,128]{2,1,0:T(8,128)S(1)} %shard_map.99.tiles_ref.own_ref), channel_id=1, source_target_pairs={{0,4},{4,0},{8,12},{12,8},{16,20},{20,16},{24,28},{28,24},{1,5},{5... | collective-permute-start | bytes 98312 | tf_op jit(solution)/shard_map/ppermute | solution.py:566
  14.5 0.0 copy-done.1
  14.5 0.0 copy-done.2
  14.5 0.0 copy-done.5
  14.5 0.6 %shard_map.100.s0_ref = f32[8,5,16,128]{3,2,1,0:T(8,128)S(1)} custom-call(f32[4,16,128]{2,1,0:T(8,128)S(1)} %shard_map.99.tiles_ref.own_ref, f32[16,128]{1,0:T(8,128)S(1)} %get-tuple-element.29.live_ref, f32[8,5,16,128]{3,2,1,0:T(8,128)S(1)} %bitcast.15, f32[8,5,16,128]{3,2,1,0:T(8,128)S(1)} %bitcast.22, f32[8,5,5,16,128]{4,3,2,1,0:T(8,128)S(1)} %bitcast.12, ...), custom_call_target="tpu_custom_call" | custom-call | flops 2000000000 | bytes 2000000 | tf_op jit(solution)/shard_map/pallas_call | solution.py:25
  15.1 1.7 %collective-permute-done.3.got_ref = f32[4,16,128]{2,1,0:T(8,128)S(1)} collective-permute-done((f32[4,16,128]{2,1,0:T(8,128)S(1)}, f32[4,16,128]{2,1,0:T(8,128)S(1)}, u32[]{:S(2)}, u32[]{:S(2)}) %collective-permute-start.3) | collective-permute-done | bytes 32800 | tf_op jit(solution)/shard_map/ppermute | solution.py:566
  16.9 0.5 %shard_map.101 = (f32[8,5,16,128]{3,2,1,0:T(8,128)S(1)}, f32[2,5,16,128]{3,2,1,0:T(8,128)S(1)}, f32[5,16,128]{2,1,0:T(8,128)S(1)}) custom-call(f32[21,5,16,128]{3,2,1,0:T(8,128)S(1)} %collective-permute-done.1.other_ref.mats_other_ref, f32[16,128]{1,0:T(8,128)S(1)} %get-tuple-element.29.live_ref, f32[2,8,16,128]{3,2,1,0:T(8,128)S(1)} %get-tuple-element.30.pick_ref, ...), custom_call_target="tpu_custom_call" | custom-call | flops 1000000000 | bytes 1000000 | tf_op jit(solution)/shard_map/pallas_call | solution.py:25
  17.4 0.1 collective-permute-start.5
  17.4 1.3 %collective-permute-done.5.ends_other_ref = f32[2,5,16,128]{3,2,1,0:T(8,128)S(1)} collective-permute-done((f32[2,5,16,128]{3,2,1,0:T(8,128)S(1)}, f32[2,5,16,128]{3,2,1,0:T(8,128)S(1)}, u32[]{:S(2)}, u32[]{:S(2)}) %collective-permute-start.5) | collective-permute-done | bytes 81952 | tf_op jit(solution)/shard_map/ppermute | solution.py:546
  18.7 0.0 collective-permute-done.4.half_ref
  18.7 0.2 collective-permute-start.7
  19.0 1.5 %collective-permute-start.6 = (f32[1,5,16,128]{3,2,1,0:T(8,128)S(1)}, f32[1,5,16,128]{3,2,1,0:T(8,128)S(1)}, u32[]{:S(2)}, u32[]{:S(2)}) collective-permute-start(f32[1,5,16,128]{3,2,1,0:T(8,128)S(1)} %get-tuple-element.42.pair_ref), channel_id=1, source_target_pairs={{0,3},{1,2},{2,1},{3,0},{4,7},{5,6},{6,5},{7,4},{8,11},{9,10},{10,... | collective-permute-start | bytes 122888 | tf_op jit(solution)/shard_map/ppermute | solution.py:546
  20.4 2.0 %collective-permute-done.6.pair_other_ref = f32[1,5,16,128]{3,2,1,0:T(8,128)S(1)} collective-permute-done((f32[1,5,16,128]{3,2,1,0:T(8,128)S(1)}, f32[1,5,16,128]{3,2,1,0:T(8,128)S(1)}, u32[]{:S(2)}, u32[]{:S(2)}) %collective-permute-start.6) | collective-permute-done | bytes 40992 | tf_op jit(solution)/shard_map/ppermute | solution.py:546
  22.4 0.0 collective-permute-done.7.half_other_ref
  22.4 0.5 %shard_map.103 = (f32[8,5,16,128]{3,2,1,0:T(8,128)S(1)}, f32[5,16,128]{2,1,0:T(8,128)S(1)}, f32[5,16,128]{2,1,0:T(8,128)S(1)}, f32[8,16,128]{2,1,0:T(8,128)S(1)}) custom-call(f32[16,128]{1,0:T(8,128)S(1)} %get-tuple-element.29.live_ref, f32[8,5,16,128]{3,2,1,0:T(8,128)S(1)} %bitcast.17, f32[5,16,128]{2,1,0:T(8,128)S(1)} %get-tuple-element.38.above_ref, ...), custom_call_target="tpu_custom_call" | custom-call | flops 1000000000 | bytes 1000000 | tf_op jit(solution)/shard_map/pallas_call | solution.py:25
  22.9 11.6 %all_to_all.5.tiles_ref = f32[8,16,128]{2,1,0:T(8,128)S(1)} all-to-all(f32[8,16,128]{2,1,0:T(8,128)S(1)} %get-tuple-element.44), channel_id=1, replica_groups=mesh['zone'=8,'ja'=4] {'zone'}, dimensions={0} | all-to-all | bytes 131072 | tf_op jit(solution)/shard_map/all_to_all | solution.py:600
  34.4 0.9 %shard_map.104 = (f32[8,5,16,128]{3,2,1,0:T(8,128)S(1)}, f32[8,5,16,128]{3,2,1,0:T(8,128)S(1)}, f32[3,5,16,128]{3,2,1,0:T(8,128)S(1)}, f32[5,5,16,128]{3,2,1,0:T(8,128)S(1)}) custom-call(f32[16,128]{1,0:T(8,128)S(1)} %get-tuple-element.29.live_ref, f32[2,8,16,128]{3,2,1,0:T(8,128)S(1)} %get-tuple-element.30.pick_ref, f32[8,16,128]{2,1,0:T(8,128)S(1)} %all_to_all.5.tiles_ref, ...), custom_call_target="tpu_custom_call" | custom-call | flops 1000000000 | bytes 1000000 | tf_op jit(solution)/shard_map/pallas_call | solution.py:25
  35.4 0.1 collective-permute-start.8
  35.5 1.3 %collective-permute-done.8.ends_other_ref = f32[3,5,16,128]{3,2,1,0:T(8,128)S(1)} collective-permute-done((f32[3,5,16,128]{3,2,1,0:T(8,128)S(1)}, f32[3,5,16,128]{3,2,1,0:T(8,128)S(1)}, u32[]{:S(2)}, u32[]{:S(2)}) %collective-permute-start.8) | collective-permute-done | bytes 122912 | tf_op jit(solution)/shard_map/ppermute | solution.py:546
  36.8 1.3 %collective-permute-start.9 = (f32[1,5,16,128]{3,2,1,0:T(8,128)S(1)}, f32[1,5,16,128]{3,2,1,0:T(8,128)S(1)}, u32[]{:S(2)}, u32[]{:S(2)}) collective-permute-start(f32[1,5,16,128]{3,2,1,0:T(8,128)S(1)} %shard_map.105.pair_ref), channel_id=1, source_target_pairs={{0,3},{1,2},{2,1},{3,0},{4,7},{5,6},{6,5},{7,4},{8,11},{9,10},{10,... | collective-permute-start | bytes 122888 | tf_op jit(solution)/shard_map/ppermute | solution.py:546
  38.2 0.7 %shard_map.106.res_in_hbm = f32[8,5,16,128]{3,2,1,0:T(8,128)} custom-call(f32[8,5,16,128]{3,2,1,0:T(8,128)S(1)} %get-tuple-element.49.res_ref), custom_call_target="tpu_custom_call" | custom-call | flops 1000000000 | bytes 1000000 | tf_op jit(solution)/shard_map/pallas_call | solution.py:25
  38.9 1.6 %collective-permute-done.9.pair_other_ref = f32[1,5,16,128]{3,2,1,0:T(8,128)S(1)} collective-permute-done((f32[1,5,16,128]{3,2,1,0:T(8,128)S(1)}, f32[1,5,16,128]{3,2,1,0:T(8,128)S(1)}, u32[]{:S(2)}, u32[]{:S(2)}) %collective-permute-start.9) | collective-permute-done | bytes 40992 | tf_op jit(solution)/shard_map/ppermute | solution.py:546
  40.4 1.1 %shard_map.107 = (f32[8,5,16,128]{3,2,1,0:T(8,128)}, f32[8,5,16,128]{3,2,1,0:T(8,128)}) custom-call(f32[16,128]{1,0:T(8,128)S(1)} %get-tuple-element.29.live_ref, f32[5,5,16,128]{3,2,1,0:T(8,128)S(1)} %get-tuple-element.47.low0_ref, f32[5,16,128]{2,1,0:T(8,128)S(1)} %get-tuple-element.48.below_ref, ...), custom_call_target="tpu_custom_call", output_to_operand_aliasing={{1}: (16, {})} | custom-call | flops 1000000000 | bytes 1000000 | tf_op jit(solution)/shard_map/pallas_call | solution.py:25
  (4 shorter events, 0.1 us)
Async XLA Ops:
  0.6 5.4 %copy-start = (f32[1,8,5,5,16,128]{5,4,3,2,1,0:T(8,128)S(1)}, f32[1,8,5,5,16,128]{5,4,3,2,1,0:T(8,128)}, u32[]{:S(2)}) copy-start(f32[1,8,5,5,16,128]{5,4,3,2,1,0:T(8,128)} %param.13) | copy-start | bytes 4915204
  0.6 5.4 %copy-start.3 = (f32[1,8,5,5,16,128]{5,4,3,2,1,0:T(8,128)S(1)}, f32[1,8,5,5,16,128]{5,4,3,2,1,0:T(8,128)}, u32[]{:S(2)}) copy-start(f32[1,8,5,5,16,128]{5,4,3,2,1,0:T(8,128)} %param.11) | copy-start | bytes 4915204
  0.7 5.4 %copy-start.4 = (f32[1,8,5,5,16,128]{5,4,3,2,1,0:T(8,128)S(1)}, f32[1,8,5,5,16,128]{5,4,3,2,1,0:T(8,128)}, u32[]{:S(2)}) copy-start(f32[1,8,5,5,16,128]{5,4,3,2,1,0:T(8,128)} %param.12) | copy-start | bytes 4915204
  2.0 7.0 %collective-permute-start = (f32[1,16,128]{2,1,0:T(8,128)S(1)}, f32[1,16,128]{2,1,0:T(8,128)S(1)}, u32[]{:S(2)}, u32[]{:S(2)}) collective-permute-start(f32[1,16,128]{2,1,0:T(8,128)S(1)} %get-tuple-element.28.tile_ref.own_ref), channel_id=1, source_target_pairs={{0,16},{4,20},{8,24},{12,28},{16,0},{20,4},{24,8},{28,12},{1,17},{... | collective-permute-start | bytes 24584 | tf_op jit(solution)/shard_map/ppermute | solution.py:566
  8.9 5.5 %copy-start.1 = (f32[1,8,5,5,16,128]{5,4,3,2,1,0:T(8,128)S(1)}, f32[1,8,5,5,16,128]{5,4,3,2,1,0:T(8,128)}, u32[]{:S(2)}) copy-start(f32[1,8,5,5,16,128]{5,4,3,2,1,0:T(8,128)} %param.10) | copy-start | bytes 4915204
  9.0 5.5 %copy-start.2 = (f32[1,8,5,16,128]{4,3,2,1,0:T(8,128)S(1)}, f32[1,8,5,16,128]{4,3,2,1,0:T(8,128)}, u32[]{:S(2)}) copy-start(f32[1,8,5,16,128]{4,3,2,1,0:T(8,128)} %param.8) | copy-start | bytes 983044
  9.0 5.5 %copy-start.5 = (f32[1,8,5,16,128]{4,3,2,1,0:T(8,128)S(1)}, f32[1,8,5,16,128]{4,3,2,1,0:T(8,128)}, u32[]{:S(2)}) copy-start(f32[1,8,5,16,128]{4,3,2,1,0:T(8,128)} %param.9) | copy-start | bytes 983044
  9.1 2.5 %collective-permute-start.1 = (f32[21,5,16,128]{3,2,1,0:T(8,128)S(1)}, f32[21,5,16,128]{3,2,1,0:T(8,128)S(1)}, u32[]{:S(2)}, u32[]{:S(2)}) collective-permute-start(f32[21,5,16,128]{3,2,1,0:T(8,128)S(1)} %get-tuple-element.33.mine_ref.mats_ref), channel_id=1, source_target_pairs={{0,1},{1,0},{2,3},{3,2},{4,5},{5,4},{6,7},{7,6},{8,9},{9,8},{10,11... | collective-permute-start | bytes 2580488 | tf_op jit(solution)/shard_map/ppermute | solution.py:546
  9.1 3.8 %collective-permute-start.2 = (f32[2,16,128]{2,1,0:T(8,128)S(1)}, f32[2,16,128]{2,1,0:T(8,128)S(1)}, u32[]{:S(2)}, u32[]{:S(2)}) collective-permute-start(f32[2,16,128]{2,1,0:T(8,128)S(1)} %get-tuple-element.34.own_ref), channel_id=1, source_target_pairs={{0,8},{4,12},{8,0},{12,4},{16,24},{20,28},{24,16},{28,20},{1,9},{5... | collective-permute-start | bytes 49160 | tf_op jit(solution)/shard_map/ppermute | solution.py:566
  11.6 7.1 %collective-permute-start.4 = (f32[7,5,8,128]{3,2,1,0:T(8,128)S(1)}, f32[7,5,8,128]{3,2,1,0:T(8,128)S(1)}, u32[]{:S(2)}, u32[]{:S(2)}) collective-permute-start(f32[7,5,8,128]{3,2,1,0:T(8,128)S(1)} %shard_map.98.refs_0_), channel_id=1, source_target_pairs={{0,3},{1,2},{2,1},{3,0},{4,7},{5,6},{6,5},{7,4},{8,11},{9,10},{10,... | collective-permute-start | bytes 430088 | tf_op jit(solution)/shard_map/ppermute | solution.py:546
  12.9 3.9 %collective-permute-start.3 = (f32[4,16,128]{2,1,0:T(8,128)S(1)}, f32[4,16,128]{2,1,0:T(8,128)S(1)}, u32[]{:S(2)}, u32[]{:S(2)}) collective-permute-start(f32[4,16,128]{2,1,0:T(8,128)S(1)} %shard_map.99.tiles_ref.own_ref), channel_id=1, source_target_pairs={{0,4},{4,0},{8,12},{12,8},{16,20},{20,16},{24,28},{28,24},{1,5},{5... | collective-permute-start | bytes 98312 | tf_op jit(solution)/shard_map/ppermute | solution.py:566
  17.4 1.3 %collective-permute-start.5 = (f32[2,5,16,128]{3,2,1,0:T(8,128)S(1)}, f32[2,5,16,128]{3,2,1,0:T(8,128)S(1)}, u32[]{:S(2)}, u32[]{:S(2)}) collective-permute-start(f32[2,5,16,128]{3,2,1,0:T(8,128)S(1)} %get-tuple-element.39.ends_ref), channel_id=1, source_target_pairs={{0,1},{1,0},{2,3},{3,2},{4,5},{5,4},{6,7},{7,6},{8,9},{9,8},{10,11... | collective-permute-start | bytes 245768 | tf_op jit(solution)/shard_map/ppermute | solution.py:546
  18.7 3.7 %collective-permute-start.7 = (f32[5,5,8,128]{3,2,1,0:T(8,128)S(1)}, f32[5,5,8,128]{3,2,1,0:T(8,128)S(1)}, u32[]{:S(2)}, u32[]{:S(2)}) collective-permute-start(f32[5,5,8,128]{3,2,1,0:T(8,128)S(1)} %get-tuple-element.43.half_ref), channel_id=1, source_target_pairs={{0,1},{1,0},{2,3},{3,2},{4,5},{5,4},{6,7},{7,6},{8,9},{9,8},{10,11... | collective-permute-start | bytes 307208 | tf_op jit(solution)/shard_map/ppermute | solution.py:546
  19.0 3.4 %collective-permute-start.6 = (f32[1,5,16,128]{3,2,1,0:T(8,128)S(1)}, f32[1,5,16,128]{3,2,1,0:T(8,128)S(1)}, u32[]{:S(2)}, u32[]{:S(2)}) collective-permute-start(f32[1,5,16,128]{3,2,1,0:T(8,128)S(1)} %get-tuple-element.42.pair_ref), channel_id=1, source_target_pairs={{0,3},{1,2},{2,1},{3,0},{4,7},{5,6},{6,5},{7,4},{8,11},{9,10},{10,... | collective-permute-start | bytes 122888 | tf_op jit(solution)/shard_map/ppermute | solution.py:546
  35.4 1.4 %collective-permute-start.8 = (f32[3,5,16,128]{3,2,1,0:T(8,128)S(1)}, f32[3,5,16,128]{3,2,1,0:T(8,128)S(1)}, u32[]{:S(2)}, u32[]{:S(2)}) collective-permute-start(f32[3,5,16,128]{3,2,1,0:T(8,128)S(1)} %get-tuple-element.51.ends_ref), channel_id=1, source_target_pairs={{0,1},{1,0},{2,3},{3,2},{4,5},{5,4},{6,7},{7,6},{8,9},{9,8},{10,11... | collective-permute-start | bytes 368648 | tf_op jit(solution)/shard_map/ppermute | solution.py:546
  36.8 3.6 %collective-permute-start.9 = (f32[1,5,16,128]{3,2,1,0:T(8,128)S(1)}, f32[1,5,16,128]{3,2,1,0:T(8,128)S(1)}, u32[]{:S(2)}, u32[]{:S(2)}) collective-permute-start(f32[1,5,16,128]{3,2,1,0:T(8,128)S(1)} %shard_map.105.pair_ref), channel_id=1, source_target_pairs={{0,3},{1,2},{2,1},{3,0},{4,7},{5,6},{6,5},{7,4},{8,11},{9,10},{10,... | collective-permute-start | bytes 122888 | tf_op jit(solution)/shard_map/ppermute | solution.py:546

commit v13 on v12

--- a/solution.py
+++ b/solution.py
@@ -113,6 +113,17 @@
         out_ref[count + w] = got_ref[w]
 
 
+def select_kernel(own_ref, got_ref, after_ref, pick_ref, partner_ref, mine_ref, theirs_ref):
+    del after_ref
+    count = own_ref.shape[0]
+
+    def tile_at(i):
+        return own_ref[i] if i < count else got_ref[i - count]
+
+    mine_ref[...] = ghosts_of(pick_ref, tile_at, 2 * count)
+    theirs_ref[...] = ghosts_of(partner_ref, tile_at, 2 * count)
+
+
 def relay_kernel(own_ref, got_ref, mats_ref, first_ref, mats_out_ref, out_ref):
     merge_kernel(own_ref, got_ref, out_ref)
     for i in range(20):
@@ -135,9 +146,9 @@
     return offset
 
 
-def ghosts_of(pick_ref, tile_at):
+def ghosts_of(pick_ref, tile_at, count):
     low = high = jnp.zeros((16, 128), jnp.float32)
-    for i in range(pick_ref.shape[1]):
+    for i in range(count):
         low = jnp.where(pick_ref[0, i] > 0.0, tile_at(i), low)
         high = jnp.where(pick_ref[1, i] > 0.0, tile_at(i), high)
     return jnp.where(iota(1) % 2 == 0, pltpu.roll(low, 1, 1), pltpu.roll(high, 127, 1))
@@ -177,7 +188,7 @@
 
 def matrix_kernel(
     depth_hbm, east_hbm, tile_ref, inv_ref, low_ref, up_ref,
-    e_ref, f_ref, mats_ref, live_ref, pick_ref,
+    e_ref, f_ref, mats_ref, live_ref, pick_ref, partner_ref,
     y_ref, depth_ref, east_ref, sems,
 ):
     del tile_ref
@@ -236,6 +247,9 @@
         rows = row < depth_ref[w]
         pick_ref[0, i] = jnp.where(rows & (east_ref[w] == zone), 1.0, 0.0)
         pick_ref[1, i] = jnp.where(rows & (east_ref[zone] == w), 1.0, 0.0)
+        if i < partner_ref.shape[1]:
+            partner_ref[0, i] = jnp.where(rows & (east_ref[w] == zone ^ 1), 1.0, 0.0)
+            partner_ref[1, i] = jnp.where(rows & (east_ref[zone ^ 1] == w), 1.0, 0.0)
 
 
 def by_place(mine_refs, other_refs, run):
@@ -312,14 +326,12 @@
 
 
 def local_kernel(
-    mats_other_ref, live_ref, pick_ref, own_ref, got_ref, cur_ref, s0_ref,
+    mats_other_ref, live_ref, mine_ref, got_ref, cur_ref, s0_ref,
     inv_ref, e_ref, f_ref,
     s_ref, ends_ref, above_ref, y_ref,
 ):
     last = cur_ref.shape[0] - 1
-    count = own_ref.shape[0]
-    ghosts = ghosts_of(pick_ref, lambda i: own_ref[i] if i < count else got_ref[i - count])
-    ghosts = jnp.where(live_ref[...] > 0.0, COUPLE * ghosts, 0.0)
+    ghosts = jnp.where(live_ref[...] > 0.0, COUPLE * (mine_ref[...] + got_ref[...]), 0.0)
     for j in range(last + 1):
         extra = [ghost_at(ghosts, j, v) for v in range(5)]
         put(s_ref, add(cell(s0_ref, j), matvec(block(inv_ref, j), extra)), j)
@@ -332,40 +344,58 @@
 
 
 def second_kernel(
-    live_ref, pick_ref, tiles_ref, cur_ref, above_ref, force_ref, diag_ref, low_ref, up_ref,
-    inv_ref, e_ref, f_ref,
-    res_ref, s_ref, ends_ref, low0_ref, y_ref,
+    live_ref, pick_ref, tiles_ref, cur_ref, above_ref, force_ref, diag_ref, inv_ref, e_ref, f_ref,
+    own_ref, s_ref, ends_ref, y_ref,
 ):
     planes = cur_ref.shape[0]
-    zone = lax.axis_index("zone")
-    ghosts = ghosts_of(pick_ref, lambda i: tiles_ref[zone ^ offset_of(i, tiles_ref.shape[0])])
-    for r in range(5):
-        put(low0_ref, cell(low_ref, 0, r), r)
+    zone, zones = lax.axis_index("zone"), tiles_ref.shape[0]
+    ghosts = ghosts_of(pick_ref, lambda i: tiles_ref[zone ^ offset_of(i, zones)], zones)
+    value = None
     for j in range(planes):
         here = cell(cur_ref, j)
         applied = matvec(block(diag_ref, j), here)
-        if j > 0:
-            lower = matvec(block(low_ref, j), cell(cur_ref, j - 1))
-            applied = [x - z for x, z in zip(applied, lower)]
-        above = cell(cur_ref, j + 1) if j < planes - 1 else cell(above_ref)
-        upper = matvec(block(up_ref, j), above)
         res = []
         for v in range(5):
             sides = neighbours(here[v]) + ghost_at(ghosts, j, v)
-            all_of = applied[v] - upper[v] - COUPLE * sides
-            res.append(force_ref[j, v] - all_of)
+            res.append(force_ref[j, v] - applied[v] + COUPLE * sides)
         res = masked(live_ref, res)
-        put(res_ref, res, j)
-        put(s_ref, matvec(block(inv_ref, j), res), j)
-    last = cell(cur_ref, planes - 1)
-    sweeps(s_ref, e_ref, f_ref, y_ref, ends_ref, last)
-    put(ends_ref, last, 2)
-
-
-def write_kernel(res_ref, res_hbm, sem):
-    copy = pltpu.make_async_copy(res_ref, res_hbm, sem)
-    copy.start()
-    copy.wait()
+        put(own_ref, res, j)
+        above = cell(cur_ref, j + 1) if j < planes - 1 else cell(above_ref)
+        linked = matvec(block(f_ref, j), [x * (1.0 / OMEGA) for x in above])
+        s = add(matvec(block(inv_ref, j), res), linked)
+        put(s_ref, s, j)
+        value = s if j == 0 else add(s, matvec(block(e_ref, j), value))
+        put(y_ref, value, j)
+        value = add(value, [x * (1.0 / OMEGA) for x in here])
+    put(ends_ref, value, 0)
+    put(ends_ref, here, 2)
+    value = cell(y_ref, planes - 1)
+    for j in range(planes - 2, -1, -1):
+        value = add(cell(y_ref, j), matvec(block(f_ref, j), value))
+    put(ends_ref, value, 1)
+
+
+def write_kernel(
+    live_ref, below_ref, ends_other_ref, cur_ref, above_ref, own_ref, low_ref, up_ref,
+    res_hbm, done_ref, res_ref, sems,
+):
+    planes = cur_ref.shape[0]
+    ja = lax.axis_index("ja")
+    before = [
+        jnp.where(ja == 0, 0.0, jnp.where(ja == 2, below_ref[v], ends_other_ref[2, v]))
+        for v in range(5)
+    ]
+    copies = []
+    for j in range(planes):
+        lower = matvec(block(low_ref, j), before if j == 0 else cell(cur_ref, j - 1))
+        above = cell(cur_ref, j + 1) if j < planes - 1 else cell(above_ref)
+        coupled = masked(live_ref, add(lower, matvec(block(up_ref, j), above)))
+        put(res_ref, add(cell(own_ref, j), coupled), j)
+        copies.append(pltpu.make_async_copy(res_ref.at[j], res_hbm.at[j], sems.at[j]))
+        copies[-1].start()
+    done_ref[...] = live_ref[...]
+    for copy in copies:
+        copy.wait()
 
 
 def compose(ends_lo, mats_lo, ends_hi, mats_hi, out_ref, first=None):
@@ -496,21 +526,14 @@
 
 
 def last_kernel(
-    live_ref, low0_ref, below_ref, cur_ref, res_ref, s_ref, e_ref, f_ref,
+    done_ref, cur_ref, s_ref, e_ref, f_ref,
     ends_ref, ends_other_ref, mats_ref, mats_other_ref, pair_ref, pair_other_ref,
-    half_ref, half_other_ref, res_in_hbm,
-    new_hbm, res_hbm, y_ref, inflow_ref, new_ref, res0_ref, sems,
-):
-    del res_in_hbm
+    half_ref, half_other_ref,
+    new_hbm, y_ref, inflow_ref, new_ref, sems,
+):
+    del done_ref
     planes = cur_ref.shape[0]
-    ja = lax.axis_index("ja")
-    before = [
-        jnp.where(ja == 0, 0.0, jnp.where(ja == 2, below_ref[v], ends_other_ref[2, v]))
-        for v in range(5)
-    ]
-    put(res0_ref, add(cell(res_ref, 0), masked(live_ref, matvec(block(low0_ref), before))))
-    copies = [pltpu.make_async_copy(res0_ref, res_hbm.at[0], sems.at[planes])]
-    copies[0].start()
+    copies = []
     inflows(
         ends_ref, ends_other_ref, mats_ref, mats_other_ref, pair_ref, pair_other_ref,
         half_ref, half_other_ref, inflow_ref,
@@ -519,6 +542,7 @@
     for j in range(planes):
         value = add(cell(s_ref, j), matvec(block(e_ref, j), value))
         put(y_ref, value, j)
+        value = add(value, [x * (1.0 / OMEGA) for x in cell(cur_ref, j)])
     value = cell(inflow_ref, 1)
     for j in range(planes - 1, -1, -1):
         value = add(cell(y_ref, j), matvec(block(f_ref, j), value))
@@ -552,9 +576,12 @@
         flops=10**10,
         far=(0,),
     )(current)
-    e, f, mats, live, pick = call(
+    e, f, mats, live, pick, partner = call(
         matrix_kernel,
-        [blocks, blocks, (20, *plane), state[2:], (2, zones, *state[2:])],
+        [
+            blocks, blocks, (20, *plane), state[2:],
+            (2, zones, *state[2:]), (2, zones // 2, *state[2:]),
+        ],
         [buffer(*blocks)]
         + [pltpu.SMEM((zones,), jnp.int32)] * 2
         + [pltpu.SemaphoreType.DMA((2,))],
@@ -562,10 +589,8 @@
         far=(0, 1),
     )(zone_depth, east_zone, tile, inv, low, up)
     tiles, stride = tile, zones // 2
-    while True:
+    while stride > 1:
         got = lax.ppermute(tiles, "zone", [(z, z ^ stride) for z in range(zones)])
-        if stride == 1:
-            break
         both = (2 * tiles.shape[0], *state[2:])
         if stride == zones // 2:
             mats, tiles = call(relay_kernel, [(21, *plane), both], flops=10**5)(
@@ -575,13 +600,18 @@
             half = call(half_kernel, [(7, plane[0], 8, plane[2])], flops=10**5)(
                 mats, mats_other, final
             )[0]
+        elif stride > 2:
+            tiles = call(merge_kernel, [both], flops=10**5)(tiles, got, half)[0]
         else:
-            tiles = call(merge_kernel, [both], flops=10**5)(tiles, got, half)[0]
+            tiles, theirs = call(select_kernel, [state[2:]] * 2, flops=10**5)(
+                tiles, got, half, pick, partner
+            )
         stride //= 2
+    got = lax.ppermute(theirs, "zone", [(z, z ^ 1) for z in range(zones)])
     half = swap(half, 3)
     s0 = call(source_kernel, [state], flops=2 * 10**9)(tiles, live, current, force, diag, inv, e, f)[0]
     s, ends, above = call(local_kernel, [state, (2, *plane), plane], work)(
-        mats_other, live, pick, tiles, got, current, s0, inv, e, f
+        mats_other, live, tiles, got, current, s0, inv, e, f
     )
     ends_other = swap(ends, 1)
     pair, beyond, half = call(
@@ -598,23 +628,27 @@
     )
 
     got = lax.all_to_all(tile, "zone", 0, 0, tiled=True)
-    residual, s, ends, low0 = call(second_kernel, [state, state, (3, *plane), matrix], work)(
-        live, pick, got, current, above, force, diag, low, up, inv, e, f
+    own, s, ends = call(second_kernel, [state, state, (3, *plane)], work)(
+        live, pick, got, current, above, force, diag, inv, e, f
     )
     ends_other = swap(ends, 1)
-    pair = call(mid_kernel, [(1, *plane)])(ends, ends_other, mats, mats_other)[0]
+    pair = call(mid_kernel, [(1, *plane)], flops=10**5)(ends, ends_other, mats, mats_other)[0]
     pair_other = swap(pair, 3)
-    written = call(write_kernel, [state], [pltpu.SemaphoreType.DMA], out_specs=[HBM])(residual)[0]
-    current, residual = call(
+    residual, done = call(
+        write_kernel,
+        [state, state[2:]],
+        work + [pltpu.SemaphoreType.DMA((planes,))],
+        out_specs=[HBM, VMEM],
+    )(live, below, ends_other, current, above, own, low, up)
+    current = call(
         last_kernel,
-        [state, state],
-        work + flows + work + [buffer(*plane), pltpu.SemaphoreType.DMA((planes + 1,))],
-        out_specs=[HBM, HBM],
-        alias={16: 1},
+        [state],
+        work + flows + work + [pltpu.SemaphoreType.DMA((planes,))],
+        out_specs=[HBM],
     )(
-        live, low0, below, current, residual, s, e, f,
-        ends, ends_other, mats, mats_other, pair, pair_other, half, half_other, written,
-    )
+        done, current, s, e, f,
+        ends, ends_other, mats, mats_other, pair, pair_other, half, half_other,
+    )[0]
     return (current[None], residual[None])
 
 

time: 41.7 us -> 41.4 us (level)
  waiting for transfers between devices: 8.62 us -> 8.13 us
    ppermute x3 -> x2, waiting for transfers between devices: 1.76 us -> 0.03 us  [per_device(): got = lax.ppermute(tiles, 'zone', [(z, z ^ stride) for z in range(zones)])]
    ppermute x0 -> x1, starting transfers between devices: none -> 1.53 us  [per_device(): got = lax.ppermute(theirs, 'zone', [(z, z ^ 1) for z in range(zones)])]
    ppermute x3 -> x2, starting transfers between devices: 7.26 us -> 5.74 us  [per_device(): got = lax.ppermute(tiles, 'zone', [(z, z ^ stride) for z in range(zones)])]
    ppermute x0 -> x1, waiting for transfers between devices: none -> 1.48 us  [per_device(): got = lax.ppermute(theirs, 'zone', [(z, z ^ 1) for z in range(zones)])]
  transfers between devices with their start and end apart: 10 -> 10, of which waited for: 6 -> 6; matrix products, arithmetic and copies ran while one was open for 0% -> 0% of each run, Pallas kernels for 11% -> 12%
where the time goes in v13:
time: 41.4 us; the launch traced here: 41.2 us
  starting transfers between devices  11.8 us (29%)
  blocking collectives  11.6 us (28%)
  Pallas kernels  8.8 us (21%)
  waiting for transfers between devices  8.13 us (20%)
  between operations  0.8 us (2%)
    all_to_all x1, blocking collectives, per_device(): got = lax.all_to_all(tile, 'zone', 0, 0, tiled=True)  11.6 us
    pallas_call x13, Pallas kernels, run(): pl.pallas_call(kernel, out_shape=[jax.ShapeDtypeStruct(s, jnp.float32) fo...  8.8 us
    ppermute x7, waiting for transfers between devices, swap(): return lax.ppermute(x, 'ja', [(p, p ^ bit) for p in range(parts)])  6.63 us
    ppermute x2, starting transfers between devices, per_device(): got = lax.ppermute(tiles, 'zone', [(z, z ^ stride) for z in range(zones)])  5.74 us
    ppermute x7, starting transfers between devices, swap(): return lax.ppermute(x, 'ja', [(p, p ^ bit) for p in range(parts)])  4.57 us
    ppermute x1, starting transfers between devices, per_device(): got = lax.ppermute(theirs, 'zone', [(z, z ^ 1) for z in range(zones)])  1.53 us
    ppermute x1, waiting for transfers between devices, per_device(): got = lax.ppermute(theirs, 'zone', [(z, z ^ 1) for z in range(zones)])  1.48 us
  transfers between devices with their start and end apart: 10, of which 6 were waited for; matrix products, arithmetic and copies ran while one was open for 0% of the time, Pallas kernels for 12%

profile of v13, /device:TPU:0, one launch (start us, length us, event | category | flops | bytes accessed | tf_op | source)
XLA Modules:
  0.0 41.2 jit_solution(8042794618634864476)
XLA Ops:
  0.6 0.0 copy-start
  0.6 0.0 copy-start.3
  0.7 0.0 copy-start.4
  0.7 1.3 %shard_map.95 = (f32[1,16,128]{2,1,0:T(8,128)S(1)}, f32[5,16,128]{2,1,0:T(8,128)S(1)}, f32[5,16,128]{2,1,0:T(8,128)S(1)}) custom-call(f32[8,5,16,128]{3,2,1,0:T(8,128)} %bitcast.14), custom_call_target="tpu_custom_call" | custom-call | flops 10000000000 | bytes 10000000 | tf_op jit(solution)/shard_map/pallas_call | solution.py:25
  2.0 4.1 %collective-permute-start = (f32[1,16,128]{2,1,0:T(8,128)S(1)}, f32[1,16,128]{2,1,0:T(8,128)S(1)}, u32[]{:S(2)}, u32[]{:S(2)}) collective-permute-start(f32[1,16,128]{2,1,0:T(8,128)S(1)} %get-tuple-element.30.tile_ref.own_ref), channel_id=1, source_target_pairs={{0,16},{4,20},{8,24},{12,28},{16,0},{20,4},{24,8},{28,12},{1,17},{... | collective-permute-start | bytes 24584 | tf_op jit(solution)/shard_map/ppermute | solution.py:593
  6.1 0.0 copy-done
  6.1 0.0 copy-done.3
  6.1 0.0 copy-done.4
  6.1 2.8 %shard_map.96 = (f32[8,5,5,16,128]{4,3,2,1,0:T(8,128)S(1)}, f32[8,5,5,16,128]{4,3,2,1,0:T(8,128)S(1)}, f32[20,5,16,128]{3,2,1,0:T(8,128)S(1)}, f32[16,128]{1,0:T...) custom-call(s32[8]{0:T(128)} %depth_hbm.1, s32[8]{0:T(128)} %east_hbm.1, ...), custom_call_target="tpu_custom_call" | custom-call | flops 5000000000 | bytes 5000000 | tf_op jit(solution)/shard_map/pallas_call | solution.py:25
  8.9 0.0 copy-start.1
  8.9 0.0 copy-start.2
  8.9 0.0 copy-start.5
  8.9 0.0 collective-permute-done.got_ref
  9.0 0.1 shard_map.97
  9.0 0.1 collective-permute-start.1
  9.1 1.6 %collective-permute-start.2 = (f32[2,16,128]{2,1,0:T(8,128)S(1)}, f32[2,16,128]{2,1,0:T(8,128)S(1)}, u32[]{:S(2)}, u32[]{:S(2)}) collective-permute-start(f32[2,16,128]{2,1,0:T(8,128)S(1)} %get-tuple-element.35.own_ref), channel_id=1, source_target_pairs={{0,8},{4,12},{8,0},{12,4},{16,24},{20,28},{24,16},{28,20},{1,9},{5... | collective-permute-start | bytes 49160 | tf_op jit(solution)/shard_map/ppermute | solution.py:593
  10.7 0.7 %collective-permute-done.1.other_ref.mats_other_ref = f32[21,5,16,128]{3,2,1,0:T(8,128)S(1)} collective-permute-done((f32[21,5,16,128]{3,2,1,0:T(8,128)S(1)}, f32[21,5,16,128]{3,2,1,0:T(8,128)S(1)}, u32[]{:S(2)}, u32[]{:S(2)}) %collective-permute-start.1) | collective-permute-done | bytes 860192 | tf_op jit(solution)/shard_map/ppermute | solution.py:570
  11.5 1.4 %collective-permute-start.4 = (f32[7,5,8,128]{3,2,1,0:T(8,128)S(1)}, f32[7,5,8,128]{3,2,1,0:T(8,128)S(1)}, u32[]{:S(2)}, u32[]{:S(2)}) collective-permute-start(f32[7,5,8,128]{3,2,1,0:T(8,128)S(1)} %shard_map.98.after_ref), channel_id=1, source_target_pairs={{0,3},{1,2},{2,1},{3,0},{4,7},{5,6},{6,5},{7,4},{8,11},{9,10},{10,... | collective-permute-start | bytes 430088 | tf_op jit(solution)/shard_map/ppermute | solution.py:570
  12.9 0.0 collective-permute-done.2.got_ref
  12.9 0.1 shard_map.99
  13.0 1.5 %collective-permute-start.3 = (f32[16,128]{1,0:T(8,128)S(1)}, f32[16,128]{1,0:T(8,128)S(1)}, u32[]{:S(2)}, u32[]{:S(2)}) collective-permute-start(f32[16,128]{1,0:T(8,128)S(1)} %get-tuple-element.40), channel_id=1, source_target_pairs={{0,4},{4,0},{8,12},{12,8},{16,20},{20,16},{24,28},{28,24},{1,5},{5... | collective-permute-start | bytes 24584 | tf_op jit(solution)/shard_map/ppermute | solution.py:610
  14.5 0.0 copy-done.1
  14.5 0.0 copy-done.2
  14.5 0.0 copy-done.5
  14.5 0.6 %shard_map.100.s0_ref = f32[8,5,16,128]{3,2,1,0:T(8,128)S(1)} custom-call(f32[16,128]{1,0:T(8,128)S(1)} %get-tuple-element.39.tiles_ref.mine_ref, f32[16,128]{1,0:T(8,128)S(1)} %get-tuple-element.31.live_ref, f32[8,5,16,128]{3,2,1,0:T(8,128)S(1)} %bitcast.15, f32[8,5,16,128]{3,2,1,0:T(8,128)S(1)} %bitcast.22, f32[8,5,5,16,128]{4,3,2,1,0:T(8,128)S(1)} %bitcast.12, ...), custom_call_target="tpu_custom_call" | custom-call | flops 2000000000 | bytes 2000000 | tf_op jit(solution)/shard_map/pallas_call | solution.py:25
  15.2 1.5 %collective-permute-done.3.got_ref = f32[16,128]{1,0:T(8,128)S(1)} collective-permute-done((f32[16,128]{1,0:T(8,128)S(1)}, f32[16,128]{1,0:T(8,128)S(1)}, u32[]{:S(2)}, u32[]{:S(2)}) %collective-permute-start.3) | collective-permute-done | bytes 8224 | tf_op jit(solution)/shard_map/ppermute | solution.py:610
  16.6 0.4 %shard_map.101 = (f32[8,5,16,128]{3,2,1,0:T(8,128)S(1)}, f32[2,5,16,128]{3,2,1,0:T(8,128)S(1)}, f32[5,16,128]{2,1,0:T(8,128)S(1)}) custom-call(f32[21,5,16,128]{3,2,1,0:T(8,128)S(1)} %collective-permute-done.1.other_ref.mats_other_ref, f32[16,128]{1,0:T(8,128)S(1)} %get-tuple-element.31.live_ref, f32[16,128]{1,0:T(8,128)S(1)} %get-tuple-element.39.tiles_ref.mine_ref, ...), custom_call_target="tpu_custom_call" | custom-call | flops 1000000000 | bytes 1000000 | tf_op jit(solution)/shard_map/pallas_call | solution.py:25
  17.1 0.1 collective-permute-start.5
  17.2 1.3 %collective-permute-done.5.ends_other_ref = f32[2,5,16,128]{3,2,1,0:T(8,128)S(1)} collective-permute-done((f32[2,5,16,128]{3,2,1,0:T(8,128)S(1)}, f32[2,5,16,128]{3,2,1,0:T(8,128)S(1)}, u32[]{:S(2)}, u32[]{:S(2)}) %collective-permute-start.5) | collective-permute-done | bytes 81952 | tf_op jit(solution)/shard_map/ppermute | solution.py:570
  18.4 0.0 collective-permute-done.4.half_ref
  18.5 0.2 collective-permute-start.7
  18.7 1.5 %collective-permute-start.6 = (f32[1,5,16,128]{3,2,1,0:T(8,128)S(1)}, f32[1,5,16,128]{3,2,1,0:T(8,128)S(1)}, u32[]{:S(2)}, u32[]{:S(2)}) collective-permute-start(f32[1,5,16,128]{3,2,1,0:T(8,128)S(1)} %get-tuple-element.47.pair_ref), channel_id=1, source_target_pairs={{0,3},{1,2},{2,1},{3,0},{4,7},{5,6},{6,5},{7,4},{8,11},{9,10},{10,... | collective-permute-start | bytes 122888 | tf_op jit(solution)/shard_map/ppermute | solution.py:570
  20.2 2.0 %collective-permute-done.6.pair_other_ref = f32[1,5,16,128]{3,2,1,0:T(8,128)S(1)} collective-permute-done((f32[1,5,16,128]{3,2,1,0:T(8,128)S(1)}, f32[1,5,16,128]{3,2,1,0:T(8,128)S(1)}, u32[]{:S(2)}, u32[]{:S(2)}) %collective-permute-start.6) | collective-permute-done | bytes 40992 | tf_op jit(solution)/shard_map/ppermute | solution.py:570
  22.1 0.0 collective-permute-done.7.half_other_ref
  22.1 0.5 %shard_map.103 = (f32[8,5,16,128]{3,2,1,0:T(8,128)S(1)}, f32[5,16,128]{2,1,0:T(8,128)S(1)}, f32[5,16,128]{2,1,0:T(8,128)S(1)}, f32[8,16,128]{2,1,0:T(8,128)S(1)}) custom-call(f32[16,128]{1,0:T(8,128)S(1)} %get-tuple-element.31.live_ref, f32[8,5,16,128]{3,2,1,0:T(8,128)S(1)} %bitcast.17, f32[5,16,128]{2,1,0:T(8,128)S(1)} %get-tuple-element.43.above_ref, ...), custom_call_target="tpu_custom_call" | custom-call | flops 1000000000 | bytes 1000000 | tf_op jit(solution)/shard_map/pallas_call | solution.py:25
  22.6 11.6 %all_to_all.5.tiles_ref = f32[8,16,128]{2,1,0:T(8,128)S(1)} all-to-all(f32[8,16,128]{2,1,0:T(8,128)S(1)} %get-tuple-element.50), channel_id=1, replica_groups=mesh['zone'=8,'ja'=4] {'zone'}, dimensions={0} | all-to-all | bytes 131072 | tf_op jit(solution)/shard_map/all_to_all | solution.py:630
  34.2 0.9 %shard_map.104 = (f32[8,5,16,128]{3,2,1,0:T(8,128)S(1)}, f32[8,5,16,128]{3,2,1,0:T(8,128)S(1)}, f32[3,5,16,128]{3,2,1,0:T(8,128)S(1)}) custom-call(f32[16,128]{1,0:T(8,128)S(1)} %get-tuple-element.31.live_ref, f32[2,8,16,128]{3,2,1,0:T(8,128)S(1)} %get-tuple-element.37.pick_ref, f32[8,16,128]{2,1,0:T(8,128)S(1)} %all_to_all.5.tiles_ref, ...), custom_call_target="tpu_custom_call" | custom-call | flops 1000000000 | bytes 1000000 | tf_op jit(solution)/shard_map/pallas_call | solution.py:25
  35.1 0.1 collective-permute-start.8
  35.2 1.3 %collective-permute-done.8.ends_other_ref = f32[3,5,16,128]{3,2,1,0:T(8,128)S(1)} collective-permute-done((f32[3,5,16,128]{3,2,1,0:T(8,128)S(1)}, f32[3,5,16,128]{3,2,1,0:T(8,128)S(1)}, u32[]{:S(2)}, u32[]{:S(2)}) %collective-permute-start.8) | collective-permute-done | bytes 122912 | tf_op jit(solution)/shard_map/ppermute | solution.py:570
  36.5 1.3 %collective-permute-start.9 = (f32[1,5,16,128]{3,2,1,0:T(8,128)S(1)}, f32[1,5,16,128]{3,2,1,0:T(8,128)S(1)}, u32[]{:S(2)}, u32[]{:S(2)}) collective-permute-start(f32[1,5,16,128]{3,2,1,0:T(8,128)S(1)} %shard_map.106.pair_ref), channel_id=1, source_target_pairs={{0,3},{1,2},{2,1},{3,0},{4,7},{5,6},{6,5},{7,4},{8,11},{9,10},{10,... | collective-permute-start | bytes 122888 | tf_op jit(solution)/shard_map/ppermute | solution.py:570
  37.8 1.0 %shard_map.105 = (f32[8,5,16,128]{3,2,1,0:T(8,128)}, f32[16,128]{1,0:T(8,128)S(1)}) custom-call(f32[16,128]{1,0:T(8,128)S(1)} %get-tuple-element.31.live_ref, f32[5,16,128]{2,1,0:T(8,128)S(1)} %get-tuple-element.49.below_ref, f32[3,5,16,128]{3,2,1,0:T(8,128)S(1)} %collective-permute-done.8.ends_other_ref, f32[8,5,16,128]{3,2,1,0:T(8,128)S(1)} %get-tuple-element.51.cur_ref, ...), custom_call_target="tpu_custom_call" | custom-call | flops 1000000000 | bytes 1000000 | tf_op jit(solution)/shard_map/pallas_call | solution.py:25
  38.8 1.3 %collective-permute-done.9.pair_other_ref = f32[1,5,16,128]{3,2,1,0:T(8,128)S(1)} collective-permute-done((f32[1,5,16,128]{3,2,1,0:T(8,128)S(1)}, f32[1,5,16,128]{3,2,1,0:T(8,128)S(1)}, u32[]{:S(2)}, u32[]{:S(2)}) %collective-permute-start.9) | collective-permute-done | bytes 40992 | tf_op jit(solution)/shard_map/ppermute | solution.py:570
  40.1 1.1 %shard_map.107 = f32[8,5,16,128]{3,2,1,0:T(8,128)} custom-call(f32[16,128]{1,0:T(8,128)S(1)} %get-tuple-element.55.done_ref, f32[8,5,16,128]{3,2,1,0:T(8,128)S(1)} %get-tuple-element.51.cur_ref, f32[8,5,16,128]{3,2,1,0:T(8,128)S(1)} %get-tuple-element.56.s_ref, f32[8,5,5,16,128]{4,3,2,1,0:T(8,128)S(1)} %get-tuple-element.41.e_ref, ...), custom_call_target="tpu_custom_call" | custom-call | flops 1000000000 | bytes 1000000 | tf_op jit(solution)/shard_map/pallas_call | solution.py:25
  (3 shorter events, 0.1 us)
Async XLA Ops:
  0.6 5.4 %copy-start = (f32[1,8,5,5,16,128]{5,4,3,2,1,0:T(8,128)S(1)}, f32[1,8,5,5,16,128]{5,4,3,2,1,0:T(8,128)}, u32[]{:S(2)}) copy-start(f32[1,8,5,5,16,128]{5,4,3,2,1,0:T(8,128)} %param.13) | copy-start | bytes 4915204
  0.6 5.4 %copy-start.3 = (f32[1,8,5,5,16,128]{5,4,3,2,1,0:T(8,128)S(1)}, f32[1,8,5,5,16,128]{5,4,3,2,1,0:T(8,128)}, u32[]{:S(2)}) copy-start(f32[1,8,5,5,16,128]{5,4,3,2,1,0:T(8,128)} %param.11) | copy-start | bytes 4915204
  0.7 5.4 %copy-start.4 = (f32[1,8,5,5,16,128]{5,4,3,2,1,0:T(8,128)S(1)}, f32[1,8,5,5,16,128]{5,4,3,2,1,0:T(8,128)}, u32[]{:S(2)}) copy-start(f32[1,8,5,5,16,128]{5,4,3,2,1,0:T(8,128)} %param.12) | copy-start | bytes 4915204
  2.0 7.0 %collective-permute-start = (f32[1,16,128]{2,1,0:T(8,128)S(1)}, f32[1,16,128]{2,1,0:T(8,128)S(1)}, u32[]{:S(2)}, u32[]{:S(2)}) collective-permute-start(f32[1,16,128]{2,1,0:T(8,128)S(1)} %get-tuple-element.30.tile_ref.own_ref), channel_id=1, source_target_pairs={{0,16},{4,20},{8,24},{12,28},{16,0},{20,4},{24,8},{28,12},{1,17},{... | collective-permute-start | bytes 24584 | tf_op jit(solution)/shard_map/ppermute | solution.py:593
  8.9 5.6 %copy-start.1 = (f32[1,8,5,5,16,128]{5,4,3,2,1,0:T(8,128)S(1)}, f32[1,8,5,5,16,128]{5,4,3,2,1,0:T(8,128)}, u32[]{:S(2)}) copy-start(f32[1,8,5,5,16,128]{5,4,3,2,1,0:T(8,128)} %param.10) | copy-start | bytes 4915204
  8.9 5.6 %copy-start.2 = (f32[1,8,5,16,128]{4,3,2,1,0:T(8,128)S(1)}, f32[1,8,5,16,128]{4,3,2,1,0:T(8,128)}, u32[]{:S(2)}) copy-start(f32[1,8,5,16,128]{4,3,2,1,0:T(8,128)} %param.8) | copy-start | bytes 983044
  8.9 5.6 %copy-start.5 = (f32[1,8,5,16,128]{4,3,2,1,0:T(8,128)S(1)}, f32[1,8,5,16,128]{4,3,2,1,0:T(8,128)}, u32[]{:S(2)}) copy-start(f32[1,8,5,16,128]{4,3,2,1,0:T(8,128)} %param.9) | copy-start | bytes 983044
  9.0 2.5 %collective-permute-start.1 = (f32[21,5,16,128]{3,2,1,0:T(8,128)S(1)}, f32[21,5,16,128]{3,2,1,0:T(8,128)S(1)}, u32[]{:S(2)}, u32[]{:S(2)}) collective-permute-start(f32[21,5,16,128]{3,2,1,0:T(8,128)S(1)} %get-tuple-element.34.mine_ref.mats_ref), channel_id=1, source_target_pairs={{0,1},{1,0},{2,3},{3,2},{4,5},{5,4},{6,7},{7,6},{8,9},{9,8},{10,11... | collective-permute-start | bytes 2580488 | tf_op jit(solution)/shard_map/ppermute | solution.py:570
  9.1 3.8 %collective-permute-start.2 = (f32[2,16,128]{2,1,0:T(8,128)S(1)}, f32[2,16,128]{2,1,0:T(8,128)S(1)}, u32[]{:S(2)}, u32[]{:S(2)}) collective-permute-start(f32[2,16,128]{2,1,0:T(8,128)S(1)} %get-tuple-element.35.own_ref), channel_id=1, source_target_pairs={{0,8},{4,12},{8,0},{12,4},{16,24},{20,28},{24,16},{28,20},{1,9},{5... | collective-permute-start | bytes 49160 | tf_op jit(solution)/shard_map/ppermute | solution.py:593
  11.5 6.9 %collective-permute-start.4 = (f32[7,5,8,128]{3,2,1,0:T(8,128)S(1)}, f32[7,5,8,128]{3,2,1,0:T(8,128)S(1)}, u32[]{:S(2)}, u32[]{:S(2)}) collective-permute-start(f32[7,5,8,128]{3,2,1,0:T(8,128)S(1)} %shard_map.98.after_ref), channel_id=1, source_target_pairs={{0,3},{1,2},{2,1},{3,0},{4,7},{5,6},{6,5},{7,4},{8,11},{9,10},{10,... | collective-permute-start | bytes 430088 | tf_op jit(solution)/shard_map/ppermute | solution.py:570
  13.0 3.7 %collective-permute-start.3 = (f32[16,128]{1,0:T(8,128)S(1)}, f32[16,128]{1,0:T(8,128)S(1)}, u32[]{:S(2)}, u32[]{:S(2)}) collective-permute-start(f32[16,128]{1,0:T(8,128)S(1)} %get-tuple-element.40), channel_id=1, source_target_pairs={{0,4},{4,0},{8,12},{12,8},{16,20},{20,16},{24,28},{28,24},{1,5},{5... | collective-permute-start | bytes 24584 | tf_op jit(solution)/shard_map/ppermute | solution.py:610
  17.1 1.3 %collective-permute-start.5 = (f32[2,5,16,128]{3,2,1,0:T(8,128)S(1)}, f32[2,5,16,128]{3,2,1,0:T(8,128)S(1)}, u32[]{:S(2)}, u32[]{:S(2)}) collective-permute-start(f32[2,5,16,128]{3,2,1,0:T(8,128)S(1)} %get-tuple-element.44.ends_ref), channel_id=1, source_target_pairs={{0,1},{1,0},{2,3},{3,2},{4,5},{5,4},{6,7},{7,6},{8,9},{9,8},{10,11... | collective-permute-start | bytes 245768 | tf_op jit(solution)/shard_map/ppermute | solution.py:570
  18.5 3.7 %collective-permute-start.7 = (f32[5,5,8,128]{3,2,1,0:T(8,128)S(1)}, f32[5,5,8,128]{3,2,1,0:T(8,128)S(1)}, u32[]{:S(2)}, u32[]{:S(2)}) collective-permute-start(f32[5,5,8,128]{3,2,1,0:T(8,128)S(1)} %get-tuple-element.48.half_ref), channel_id=1, source_target_pairs={{0,1},{1,0},{2,3},{3,2},{4,5},{5,4},{6,7},{7,6},{8,9},{9,8},{10,11... | collective-permute-start | bytes 307208 | tf_op jit(solution)/shard_map/ppermute | solution.py:570
  18.7 3.4 %collective-permute-start.6 = (f32[1,5,16,128]{3,2,1,0:T(8,128)S(1)}, f32[1,5,16,128]{3,2,1,0:T(8,128)S(1)}, u32[]{:S(2)}, u32[]{:S(2)}) collective-permute-start(f32[1,5,16,128]{3,2,1,0:T(8,128)S(1)} %get-tuple-element.47.pair_ref), channel_id=1, source_target_pairs={{0,3},{1,2},{2,1},{3,0},{4,7},{5,6},{6,5},{7,4},{8,11},{9,10},{10,... | collective-permute-start | bytes 122888 | tf_op jit(solution)/shard_map/ppermute | solution.py:570
  35.1 1.4 %collective-permute-start.8 = (f32[3,5,16,128]{3,2,1,0:T(8,128)S(1)}, f32[3,5,16,128]{3,2,1,0:T(8,128)S(1)}, u32[]{:S(2)}, u32[]{:S(2)}) collective-permute-start(f32[3,5,16,128]{3,2,1,0:T(8,128)S(1)} %get-tuple-element.53.ends_ref), channel_id=1, source_target_pairs={{0,1},{1,0},{2,3},{3,2},{4,5},{5,4},{6,7},{7,6},{8,9},{9,8},{10,11... | collective-permute-start | bytes 368648 | tf_op jit(solution)/shard_map/ppermute | solution.py:570
  36.5 3.6 %collective-permute-start.9 = (f32[1,5,16,128]{3,2,1,0:T(8,128)S(1)}, f32[1,5,16,128]{3,2,1,0:T(8,128)S(1)}, u32[]{:S(2)}, u32[]{:S(2)}) collective-permute-start(f32[1,5,16,128]{3,2,1,0:T(8,128)S(1)} %shard_map.106.pair_ref), channel_id=1, source_target_pairs={{0,3},{1,2},{2,1},{3,0},{4,7},{5,6},{6,5},{7,4},{8,11},{9,10},{10,... | collective-permute-start | bytes 122888 | tf_op jit(solution)/shard_map/ppermute | solution.py:570

commit v14 on v13

--- a/solution.py
+++ b/solution.py
@@ -7,6 +7,7 @@
 
 ITERS = 2
 OMEGA = 1.2
+PART = 7
 COUPLE = 0.25
 
 VMEM = pl.BlockSpec(memory_space=pltpu.VMEM)
@@ -96,10 +97,15 @@
     return [jnp.where(live, x, 0.0) for x in values]
 
 
-def pack_kernel(flow_hbm, tile_ref, first_ref, last_ref, flow_ref, sem):
-    copy = pltpu.make_async_copy(flow_hbm, flow_ref, sem)
-    copy.start()
-    copy.wait()
+def pack_kernel(flow_hbm, tile_ref, first_ref, last_ref, flow_ref, sems):
+    copies = [
+        pltpu.make_async_copy(flow_hbm.at[j], flow_ref.at[j], sems.at[j])
+        for j in range(flow_ref.shape[0])
+    ]
+    for copy in copies:
+        copy.start()
+    for copy in copies:
+        copy.wait()
     put(first_ref, cell(flow_ref, 0))
     put(last_ref, cell(flow_ref, flow_ref.shape[0] - 1))
     pack_faces(lambda j, v: flow_ref[j, v], flow_ref.shape[0], tile_ref)
@@ -423,7 +429,7 @@
 
 def first_mid_kernel(
     live_ref, half_ref, ends_ref, ends_other_ref, mats_ref, mats_other_ref,
-    out_ref, beyond_ref, half_out_ref,
+    out_ref, beyond_ref, half_out_ref, *part_refs,
 ):
     def first(mats_lo):
         return [x * (1.0 / OMEGA) for x in masked(live_ref, cell(mats_lo, 20))]
@@ -434,25 +440,29 @@
     by_place([ends_ref, mats_ref], [ends_other_ref, mats_other_ref], run)
     for r in range(5):
         put(half_out_ref, cell(half_ref, r), r)
+        for c in range(5):
+            part, place = divmod(5 * r + c, PART)
+            part_refs[part][place] = half_ref[r, c]
     beyond = [jnp.concatenate([half_ref[5, v], half_ref[6, v]], axis=0) for v in range(5)]
     put(beyond_ref, masked(live_ref, beyond))
 
 
-def join(mine_ref, other_ref, *at):
-    mine, other = mine_ref[at], other_ref[at]
+def join(mine_ref, other_refs, r, c):
+    part, place = divmod(5 * r + c, PART)
+    mine, other = mine_ref[r, c], other_refs[part][place]
     odd = lax.axis_index("ja") % 2 == 1
     return jnp.concatenate([jnp.where(odd, mine, other), jnp.where(odd, other, mine)], axis=0)
 
 
 def inflows(
     ends_ref, ends_other_ref, mats_ref, mats_other_ref, pair_ref, pair_other_ref,
-    half_ref, half_other_ref, inflow_ref, live_ref=None, beyond_ref=None,
+    half_ref, half_other_refs, inflow_ref, live_ref=None, beyond_ref=None,
 ):
     ja = lax.axis_index("ja")
     zeros = [jnp.zeros((16, 128), jnp.float32)] * 5
 
     def joined():
-        return [[join(half_ref, half_other_ref, r, c) for c in range(5)] for r in range(5)]
+        return [[join(half_ref, half_other_refs, r, c) for c in range(5)] for r in range(5)]
 
     def passed(value, coupling, first):
         if beyond_ref is None:
@@ -499,13 +509,14 @@
 def final_kernel(
     live_ref, cur_ref, above_ref, beyond_ref, s_ref, e_ref, f_ref,
     ends_ref, ends_other_ref, mats_ref, mats_other_ref, pair_ref, pair_other_ref,
-    half_ref, half_other_ref,
-    new_ref, above_new_ref, below_new_ref, tile_ref, y_ref, inflow_ref,
-):
+    half_ref, *rest,
+):
+    half_other_refs = rest[:4]
+    new_ref, above_new_ref, below_new_ref, tile_ref, y_ref, inflow_ref = rest[4:]
     planes = cur_ref.shape[0]
     inflows(
         ends_ref, ends_other_ref, mats_ref, mats_other_ref, pair_ref, pair_other_ref,
-        half_ref, half_other_ref, inflow_ref, live_ref, beyond_ref,
+        half_ref, half_other_refs, inflow_ref, live_ref, beyond_ref,
     )
     value = cell(inflow_ref, 0)
     for j in range(planes):
@@ -519,7 +530,7 @@
     for j in range(planes - 1, -1, -1):
         value = add(cell(y_ref, j), matvec(block(f_ref, j), value))
         put(new_ref, add(masked(live_ref, cell(cur_ref, j)), value), j)
-    coupling = [[join(half_ref, half_other_ref, r, c) for c in range(5)] for r in range(5)]
+    coupling = [[join(half_ref, half_other_refs, r, c) for c in range(5)] for r in range(5)]
     raised = add(cell(inflow_ref, 0), matvec(coupling, value))
     put(below_new_ref, add(raised, kept))
     pack_faces(lambda j, v: new_ref[j, v], planes, tile_ref)
@@ -528,15 +539,16 @@
 def last_kernel(
     done_ref, cur_ref, s_ref, e_ref, f_ref,
     ends_ref, ends_other_ref, mats_ref, mats_other_ref, pair_ref, pair_other_ref,
-    half_ref, half_other_ref,
-    new_hbm, y_ref, inflow_ref, new_ref, sems,
-):
+    half_ref, *rest,
+):
+    half_other_refs = rest[:4]
+    new_hbm, y_ref, inflow_ref, new_ref, sems = rest[4:]
     del done_ref
     planes = cur_ref.shape[0]
     copies = []
     inflows(
         ends_ref, ends_other_ref, mats_ref, mats_other_ref, pair_ref, pair_other_ref,
-        half_ref, half_other_ref, inflow_ref,
+        half_ref, half_other_refs, inflow_ref,
     )
     value = cell(inflow_ref, 0)
     for j in range(planes):
@@ -572,7 +584,7 @@
     tile, first, final = call(
         pack_kernel,
         [(1, *state[2:]), plane, plane],
-        work + [pltpu.SemaphoreType.DMA],
+        work + [pltpu.SemaphoreType.DMA((planes,))],
         flops=10**10,
         far=(0,),
     )(current)
@@ -614,17 +626,18 @@
         mats_other, live, tiles, got, current, s0, inv, e, f
     )
     ends_other = swap(ends, 1)
-    pair, beyond, half = call(
-        first_mid_kernel, [(1, *plane), plane, (5, *half.shape[1:])], flops=10**5
+    parts_of = [(min(PART, 25 - i), *half.shape[2:]) for i in range(0, 25, PART)]
+    pair, beyond, half, *sent = call(
+        first_mid_kernel, [(1, *plane), plane, (5, *half.shape[1:])] + parts_of, flops=10**5
     )(live, half, ends, ends_other, mats, mats_other)
-    half_other = swap(half, 1)
+    half_other = [swap(x, 1) for x in sent]
     pair_other = swap(pair, 3)
     flows = [buffer(2, *plane)]
     current, above, below, tile = call(
         final_kernel, [state, plane, plane, (zones, *state[2:])], work + flows
     )(
         live, current, above, beyond, s, e, f,
-        ends, ends_other, mats, mats_other, pair, pair_other, half, half_other,
+        ends, ends_other, mats, mats_other, pair, pair_other, half, *half_other,
     )
 
     got = lax.all_to_all(tile, "zone", 0, 0, tiled=True)
@@ -647,7 +660,7 @@
         out_specs=[HBM],
     )(
         done, current, s, e, f,
-        ends, ends_other, mats, mats_other, pair, pair_other, half, half_other,
+        ends, ends_other, mats, mats_other, pair, pair_other, half, *half_other,
     )[0]
     return (current[None], residual[None])
 

time: 41.4 us -> 41.3 us (level)
  waiting for transfers between devices: 8.13 us -> 7.4 us
  starting transfers between devices: 11.8 us -> 12.5 us
    ppermute x7 -> x10, waiting for transfers between devices: 6.63 us -> 5.9 us  [swap(): return lax.ppermute(x, 'ja', [(p, p ^ bit) for p in range(parts)])]
    ppermute x7 -> x10, starting transfers between devices: 4.57 us -> 5.23 us  [swap(): return lax.ppermute(x, 'ja', [(p, p ^ bit) for p in range(parts)])]
  transfers between devices with their start and end apart: 10 -> 13, of which waited for: 6 -> 7; matrix products, arithmetic and copies ran while one was open for 0% -> 0% of each run, Pallas kernels for 12% -> 12%
where the time goes in v14:
time: 41.3 us; the launch traced here: 41.2 us
  starting transfers between devices  12.5 us (30%)
  blocking collectives  11.6 us (28%)
  Pallas kernels  8.81 us (21%)
  waiting for transfers between devices  7.4 us (18%)
  between operations  0.81 us (2%)
    all_to_all x1, blocking collectives, per_device(): got = lax.all_to_all(tile, 'zone', 0, 0, tiled=True)  11.6 us
    pallas_call x13, Pallas kernels, run(): pl.pallas_call(kernel, out_shape=[jax.ShapeDtypeStruct(s, jnp.float32) fo...  8.81 us
    ppermute x10, waiting for transfers between devices, swap(): return lax.ppermute(x, 'ja', [(p, p ^ bit) for p in range(parts)])  5.9 us
    ppermute x2, starting transfers between devices, per_device(): got = lax.ppermute(tiles, 'zone', [(z, z ^ stride) for z in range(zones)])  5.74 us
    ppermute x10, starting transfers between devices, swap(): return lax.ppermute(x, 'ja', [(p, p ^ bit) for p in range(parts)])  5.23 us
    ppermute x1, starting transfers between devices, per_device(): got = lax.ppermute(theirs, 'zone', [(z, z ^ 1) for z in range(zones)])  1.53 us
    ppermute x1, waiting for transfers between devices, per_device(): got = lax.ppermute(theirs, 'zone', [(z, z ^ 1) for z in range(zones)])  1.48 us
  transfers between devices with their start and end apart: 13, of which 7 were waited for; matrix products, arithmetic and copies ran while one was open for 0% of the time, Pallas kernels for 12%

profile of v14, /device:TPU:0, one launch (start us, length us, event | category | flops | bytes accessed | tf_op | source)
XLA Modules:
  0.0 41.2 jit_solution(7732158251951738640)
XLA Ops:
  0.6 0.0 copy-start
  0.6 0.0 copy-start.3
  0.7 0.0 copy-start.4
  0.7 1.3 %shard_map.95 = (f32[1,16,128]{2,1,0:T(8,128)S(1)}, f32[5,16,128]{2,1,0:T(8,128)S(1)}, f32[5,16,128]{2,1,0:T(8,128)S(1)}) custom-call(f32[8,5,16,128]{3,2,1,0:T(8,128)} %bitcast.14), custom_call_target="tpu_custom_call" | custom-call | flops 10000000000 | bytes 10000000 | tf_op jit(solution)/shard_map/pallas_call | solution.py:26
  2.0 4.1 %collective-permute-start = (f32[1,16,128]{2,1,0:T(8,128)S(1)}, f32[1,16,128]{2,1,0:T(8,128)S(1)}, u32[]{:S(2)}, u32[]{:S(2)}) collective-permute-start(f32[1,16,128]{2,1,0:T(8,128)S(1)} %get-tuple-element.34.tile_ref.own_ref), channel_id=1, source_target_pairs={{0,16},{4,20},{8,24},{12,28},{16,0},{20,4},{24,8},{28,12},{1,17},{... | collective-permute-start | bytes 24584 | tf_op jit(solution)/shard_map/ppermute | solution.py:605
  6.1 0.0 copy-done
  6.1 0.0 copy-done.3
  6.1 0.0 copy-done.4
  6.1 2.8 %shard_map.96 = (f32[8,5,5,16,128]{4,3,2,1,0:T(8,128)S(1)}, f32[8,5,5,16,128]{4,3,2,1,0:T(8,128)S(1)}, f32[20,5,16,128]{3,2,1,0:T(8,128)S(1)}, f32[16,128]{1,0:T...) custom-call(s32[8]{0:T(128)} %depth_hbm.1, s32[8]{0:T(128)} %east_hbm.1, ...), custom_call_target="tpu_custom_call" | custom-call | flops 5000000000 | bytes 5000000 | tf_op jit(solution)/shard_map/pallas_call | solution.py:26
  8.9 0.0 copy-start.1
  8.9 0.0 copy-start.2
  8.9 0.0 copy-start.5
  8.9 0.0 collective-permute-done.got_ref
  9.0 0.1 shard_map.97
  9.0 0.1 collective-permute-start.1
  9.1 1.6 %collective-permute-start.2 = (f32[2,16,128]{2,1,0:T(8,128)S(1)}, f32[2,16,128]{2,1,0:T(8,128)S(1)}, u32[]{:S(2)}, u32[]{:S(2)}) collective-permute-start(f32[2,16,128]{2,1,0:T(8,128)S(1)} %get-tuple-element.39.own_ref), channel_id=1, source_target_pairs={{0,8},{4,12},{8,0},{12,4},{16,24},{20,28},{24,16},{28,20},{1,9},{5... | collective-permute-start | bytes 49160 | tf_op jit(solution)/shard_map/ppermute | solution.py:605
  10.7 0.7 %collective-permute-done.1.other_ref.mats_other_ref = f32[21,5,16,128]{3,2,1,0:T(8,128)S(1)} collective-permute-done((f32[21,5,16,128]{3,2,1,0:T(8,128)S(1)}, f32[21,5,16,128]{3,2,1,0:T(8,128)S(1)}, u32[]{:S(2)}, u32[]{:S(2)}) %collective-permute-start.1) | collective-permute-done | bytes 860192 | tf_op jit(solution)/shard_map/ppermute | solution.py:582
  11.5 1.4 %collective-permute-start.4 = (f32[7,5,8,128]{3,2,1,0:T(8,128)S(1)}, f32[7,5,8,128]{3,2,1,0:T(8,128)S(1)}, u32[]{:S(2)}, u32[]{:S(2)}) collective-permute-start(f32[7,5,8,128]{3,2,1,0:T(8,128)S(1)} %shard_map.98.after_ref), channel_id=1, source_target_pairs={{0,3},{1,2},{2,1},{3,0},{4,7},{5,6},{6,5},{7,4},{8,11},{9,10},{10,... | collective-permute-start | bytes 430088 | tf_op jit(solution)/shard_map/ppermute | solution.py:582
  12.9 0.0 collective-permute-done.2.got_ref
  12.9 0.1 shard_map.99
  13.0 1.5 %collective-permute-start.3 = (f32[16,128]{1,0:T(8,128)S(1)}, f32[16,128]{1,0:T(8,128)S(1)}, u32[]{:S(2)}, u32[]{:S(2)}) collective-permute-start(f32[16,128]{1,0:T(8,128)S(1)} %get-tuple-element.44), channel_id=1, source_target_pairs={{0,4},{4,0},{8,12},{12,8},{16,20},{20,16},{24,28},{28,24},{1,5},{5... | collective-permute-start | bytes 24584 | tf_op jit(solution)/shard_map/ppermute | solution.py:622
  14.5 0.0 copy-done.1
  14.5 0.0 copy-done.2
  14.5 0.0 copy-done.5
  14.5 0.6 %shard_map.100.s0_ref = f32[8,5,16,128]{3,2,1,0:T(8,128)S(1)} custom-call(f32[16,128]{1,0:T(8,128)S(1)} %get-tuple-element.43.tiles_ref.mine_ref, f32[16,128]{1,0:T(8,128)S(1)} %get-tuple-element.35.live_ref, f32[8,5,16,128]{3,2,1,0:T(8,128)S(1)} %bitcast.15, f32[8,5,16,128]{3,2,1,0:T(8,128)S(1)} %bitcast.22, f32[8,5,5,16,128]{4,3,2,1,0:T(8,128)S(1)} %bitcast.12, ...), custom_call_target="tpu_custom_call" | custom-call | flops 2000000000 | bytes 2000000 | tf_op jit(solution)/shard_map/pallas_call | solution.py:26
  15.2 1.5 %collective-permute-done.3.got_ref = f32[16,128]{1,0:T(8,128)S(1)} collective-permute-done((f32[16,128]{1,0:T(8,128)S(1)}, f32[16,128]{1,0:T(8,128)S(1)}, u32[]{:S(2)}, u32[]{:S(2)}) %collective-permute-start.3) | collective-permute-done | bytes 8224 | tf_op jit(solution)/shard_map/ppermute | solution.py:622
  16.7 0.4 %shard_map.101 = (f32[8,5,16,128]{3,2,1,0:T(8,128)S(1)}, f32[2,5,16,128]{3,2,1,0:T(8,128)S(1)}, f32[5,16,128]{2,1,0:T(8,128)S(1)}) custom-call(f32[21,5,16,128]{3,2,1,0:T(8,128)S(1)} %collective-permute-done.1.other_ref.mats_other_ref, f32[16,128]{1,0:T(8,128)S(1)} %get-tuple-element.35.live_ref, f32[16,128]{1,0:T(8,128)S(1)} %get-tuple-element.43.tiles_ref.mine_ref, ...), custom_call_target="tpu_custom_call" | custom-call | flops 1000000000 | bytes 1000000 | tf_op jit(solution)/shard_map/pallas_call | solution.py:26
  17.1 0.1 collective-permute-start.5
  17.2 1.3 %collective-permute-done.5.ends_other_ref = f32[2,5,16,128]{3,2,1,0:T(8,128)S(1)} collective-permute-done((f32[2,5,16,128]{3,2,1,0:T(8,128)S(1)}, f32[2,5,16,128]{3,2,1,0:T(8,128)S(1)}, u32[]{:S(2)}, u32[]{:S(2)}) %collective-permute-start.5) | collective-permute-done | bytes 81952 | tf_op jit(solution)/shard_map/ppermute | solution.py:582
  18.4 0.0 collective-permute-done.4.half_ref
  18.5 1.3 %collective-permute-start.6 = (f32[1,5,16,128]{3,2,1,0:T(8,128)S(1)}, f32[1,5,16,128]{3,2,1,0:T(8,128)S(1)}, u32[]{:S(2)}, u32[]{:S(2)}) collective-permute-start(f32[1,5,16,128]{3,2,1,0:T(8,128)S(1)} %get-tuple-element.51.pair_ref), channel_id=1, source_target_pairs={{0,3},{1,2},{2,1},{3,0},{4,7},{5,6},{6,5},{7,4},{8,11},{9,10},{10,... | collective-permute-start | bytes 122888 | tf_op jit(solution)/shard_map/ppermute | solution.py:582
  19.8 0.4 collective-permute-start.7
  20.2 0.1 collective-permute-start.8
  20.3 0.4 collective-permute-start.9
  20.7 0.1 collective-permute-start.10
  20.8 1.0 %collective-permute-done.10.rest_3_ = f32[4,8,128]{2,1,0:T(8,128)S(1)} collective-permute-done((f32[4,8,128]{2,1,0:T(8,128)S(1)}, f32[4,8,128]{2,1,0:T(8,128)S(1)}, u32[]{:S(2)}, u32[]{:S(2)}) %collective-permute-start.10) | collective-permute-done | bytes 16416 | tf_op jit(solution)/shard_map/ppermute | solution.py:582
  21.9 0.0 collective-permute-done.7.rest_0_
  21.9 0.0 collective-permute-done.8.rest_1_
  21.9 0.0 collective-permute-done.9.rest_2_
  21.9 0.2 collective-permute-done.6.pair_other_ref
  22.1 0.5 %shard_map.103 = (f32[8,5,16,128]{3,2,1,0:T(8,128)S(1)}, f32[5,16,128]{2,1,0:T(8,128)S(1)}, f32[5,16,128]{2,1,0:T(8,128)S(1)}, f32[8,16,128]{2,1,0:T(8,128)S(1)}) custom-call(f32[16,128]{1,0:T(8,128)S(1)} %get-tuple-element.35.live_ref, f32[8,5,16,128]{3,2,1,0:T(8,128)S(1)} %bitcast.17, f32[5,16,128]{2,1,0:T(8,128)S(1)} %get-tuple-element.47.above_ref, ...), custom_call_target="tpu_custom_call" | custom-call | flops 1000000000 | bytes 1000000 | tf_op jit(solution)/shard_map/pallas_call | solution.py:26
  22.6 11.6 %all_to_all.5.tiles_ref = f32[8,16,128]{2,1,0:T(8,128)S(1)} all-to-all(f32[8,16,128]{2,1,0:T(8,128)S(1)} %get-tuple-element.58), channel_id=1, replica_groups=mesh['zone'=8,'ja'=4] {'zone'}, dimensions={0} | all-to-all | bytes 131072 | tf_op jit(solution)/shard_map/all_to_all | solution.py:643
  34.2 0.9 %shard_map.104 = (f32[8,5,16,128]{3,2,1,0:T(8,128)S(1)}, f32[8,5,16,128]{3,2,1,0:T(8,128)S(1)}, f32[3,5,16,128]{3,2,1,0:T(8,128)S(1)}) custom-call(f32[16,128]{1,0:T(8,128)S(1)} %get-tuple-element.35.live_ref, f32[2,8,16,128]{3,2,1,0:T(8,128)S(1)} %get-tuple-element.41.pick_ref, f32[8,16,128]{2,1,0:T(8,128)S(1)} %all_to_all.5.tiles_ref, ...), custom_call_target="tpu_custom_call" | custom-call | flops 1000000000 | bytes 1000000 | tf_op jit(solution)/shard_map/pallas_call | solution.py:26
  35.1 0.1 collective-permute-start.11
  35.1 1.3 %collective-permute-done.11.ends_other_ref = f32[3,5,16,128]{3,2,1,0:T(8,128)S(1)} collective-permute-done((f32[3,5,16,128]{3,2,1,0:T(8,128)S(1)}, f32[3,5,16,128]{3,2,1,0:T(8,128)S(1)}, u32[]{:S(2)}, u32[]{:S(2)}) %collective-permute-start.11) | collective-permute-done | bytes 122912 | tf_op jit(solution)/shard_map/ppermute | solution.py:582
  36.5 1.3 %collective-permute-start.12 = (f32[1,5,16,128]{3,2,1,0:T(8,128)S(1)}, f32[1,5,16,128]{3,2,1,0:T(8,128)S(1)}, u32[]{:S(2)}, u32[]{:S(2)}) collective-permute-start(f32[1,5,16,128]{3,2,1,0:T(8,128)S(1)} %shard_map.106.pair_ref), channel_id=1, source_target_pairs={{0,3},{1,2},{2,1},{3,0},{4,7},{5,6},{6,5},{7,4},{8,11},{9,10},{10,... | collective-permute-start | bytes 122888 | tf_op jit(solution)/shard_map/ppermute | solution.py:582
  37.8 1.0 %shard_map.105 = (f32[8,5,16,128]{3,2,1,0:T(8,128)}, f32[16,128]{1,0:T(8,128)S(1)}) custom-call(f32[16,128]{1,0:T(8,128)S(1)} %get-tuple-element.35.live_ref, f32[5,16,128]{2,1,0:T(8,128)S(1)} %get-tuple-element.57.below_ref, f32[3,5,16,128]{3,2,1,0:T(8,128)S(1)} %collective-permute-done.11.ends_other_ref, f32[8,5,16,128]{3,2,1,0:T(8,128)S(1)} %get-tuple-element.59.cur_ref, ...), custom_call_target="tpu_custom_call" | custom-call | flops 1000000000 | bytes 1000000 | tf_op jit(solution)/shard_map/pallas_call | solution.py:26
  38.8 1.3 %collective-permute-done.12.pair_other_ref = f32[1,5,16,128]{3,2,1,0:T(8,128)S(1)} collective-permute-done((f32[1,5,16,128]{3,2,1,0:T(8,128)S(1)}, f32[1,5,16,128]{3,2,1,0:T(8,128)S(1)}, u32[]{:S(2)}, u32[]{:S(2)}) %collective-permute-start.12) | collective-permute-done | bytes 40992 | tf_op jit(solution)/shard_map/ppermute | solution.py:582
  40.1 1.1 %shard_map.107 = f32[8,5,16,128]{3,2,1,0:T(8,128)} custom-call(f32[16,128]{1,0:T(8,128)S(1)} %get-tuple-element.63.done_ref, f32[8,5,16,128]{3,2,1,0:T(8,128)S(1)} %get-tuple-element.59.cur_ref, f32[8,5,16,128]{3,2,1,0:T(8,128)S(1)} %get-tuple-element.64.s_ref, f32[8,5,5,16,128]{4,3,2,1,0:T(8,128)S(1)} %get-tuple-element.45.e_ref, ...), custom_call_target="tpu_custom_call" | custom-call | flops 1000000000 | bytes 1000000 | tf_op jit(solution)/shard_map/pallas_call | solution.py:26
  (3 shorter events, 0.1 us)
Async XLA Ops:
  0.6 5.4 %copy-start = (f32[1,8,5,5,16,128]{5,4,3,2,1,0:T(8,128)S(1)}, f32[1,8,5,5,16,128]{5,4,3,2,1,0:T(8,128)}, u32[]{:S(2)}) copy-start(f32[1,8,5,5,16,128]{5,4,3,2,1,0:T(8,128)} %param.13) | copy-start | bytes 4915204
  0.6 5.4 %copy-start.3 = (f32[1,8,5,5,16,128]{5,4,3,2,1,0:T(8,128)S(1)}, f32[1,8,5,5,16,128]{5,4,3,2,1,0:T(8,128)}, u32[]{:S(2)}) copy-start(f32[1,8,5,5,16,128]{5,4,3,2,1,0:T(8,128)} %param.11) | copy-start | bytes 4915204
  0.7 5.4 %copy-start.4 = (f32[1,8,5,5,16,128]{5,4,3,2,1,0:T(8,128)S(1)}, f32[1,8,5,5,16,128]{5,4,3,2,1,0:T(8,128)}, u32[]{:S(2)}) copy-start(f32[1,8,5,5,16,128]{5,4,3,2,1,0:T(8,128)} %param.12) | copy-start | bytes 4915204
  2.0 7.0 %collective-permute-start = (f32[1,16,128]{2,1,0:T(8,128)S(1)}, f32[1,16,128]{2,1,0:T(8,128)S(1)}, u32[]{:S(2)}, u32[]{:S(2)}) collective-permute-start(f32[1,16,128]{2,1,0:T(8,128)S(1)} %get-tuple-element.34.tile_ref.own_ref), channel_id=1, source_target_pairs={{0,16},{4,20},{8,24},{12,28},{16,0},{20,4},{24,8},{28,12},{1,17},{... | collective-permute-start | bytes 24584 | tf_op jit(solution)/shard_map/ppermute | solution.py:605
  8.9 5.6 %copy-start.1 = (f32[1,8,5,5,16,128]{5,4,3,2,1,0:T(8,128)S(1)}, f32[1,8,5,5,16,128]{5,4,3,2,1,0:T(8,128)}, u32[]{:S(2)}) copy-start(f32[1,8,5,5,16,128]{5,4,3,2,1,0:T(8,128)} %param.10) | copy-start | bytes 4915204
  8.9 5.6 %copy-start.2 = (f32[1,8,5,16,128]{4,3,2,1,0:T(8,128)S(1)}, f32[1,8,5,16,128]{4,3,2,1,0:T(8,128)}, u32[]{:S(2)}) copy-start(f32[1,8,5,16,128]{4,3,2,1,0:T(8,128)} %param.8) | copy-start | bytes 983044
  8.9 5.6 %copy-start.5 = (f32[1,8,5,16,128]{4,3,2,1,0:T(8,128)S(1)}, f32[1,8,5,16,128]{4,3,2,1,0:T(8,128)}, u32[]{:S(2)}) copy-start(f32[1,8,5,16,128]{4,3,2,1,0:T(8,128)} %param.9) | copy-start | bytes 983044
  9.0 2.5 %collective-permute-start.1 = (f32[21,5,16,128]{3,2,1,0:T(8,128)S(1)}, f32[21,5,16,128]{3,2,1,0:T(8,128)S(1)}, u32[]{:S(2)}, u32[]{:S(2)}) collective-permute-start(f32[21,5,16,128]{3,2,1,0:T(8,128)S(1)} %get-tuple-element.38.mine_ref.mats_ref), channel_id=1, source_target_pairs={{0,1},{1,0},{2,3},{3,2},{4,5},{5,4},{6,7},{7,6},{8,9},{9,8},{10,11... | collective-permute-start | bytes 2580488 | tf_op jit(solution)/shard_map/ppermute | solution.py:582
  9.1 3.8 %collective-permute-start.2 = (f32[2,16,128]{2,1,0:T(8,128)S(1)}, f32[2,16,128]{2,1,0:T(8,128)S(1)}, u32[]{:S(2)}, u32[]{:S(2)}) collective-permute-start(f32[2,16,128]{2,1,0:T(8,128)S(1)} %get-tuple-element.39.own_ref), channel_id=1, source_target_pairs={{0,8},{4,12},{8,0},{12,4},{16,24},{20,28},{24,16},{28,20},{1,9},{5... | collective-permute-start | bytes 49160 | tf_op jit(solution)/shard_map/ppermute | solution.py:605
  11.5 6.9 %collective-permute-start.4 = (f32[7,5,8,128]{3,2,1,0:T(8,128)S(1)}, f32[7,5,8,128]{3,2,1,0:T(8,128)S(1)}, u32[]{:S(2)}, u32[]{:S(2)}) collective-permute-start(f32[7,5,8,128]{3,2,1,0:T(8,128)S(1)} %shard_map.98.after_ref), channel_id=1, source_target_pairs={{0,3},{1,2},{2,1},{3,0},{4,7},{5,6},{6,5},{7,4},{8,11},{9,10},{10,... | collective-permute-start | bytes 430088 | tf_op jit(solution)/shard_map/ppermute | solution.py:582
  13.0 3.7 %collective-permute-start.3 = (f32[16,128]{1,0:T(8,128)S(1)}, f32[16,128]{1,0:T(8,128)S(1)}, u32[]{:S(2)}, u32[]{:S(2)}) collective-permute-start(f32[16,128]{1,0:T(8,128)S(1)} %get-tuple-element.44), channel_id=1, source_target_pairs={{0,4},{4,0},{8,12},{12,8},{16,20},{20,16},{24,28},{28,24},{1,5},{5... | collective-permute-start | bytes 24584 | tf_op jit(solution)/shard_map/ppermute | solution.py:622
  17.1 1.3 %collective-permute-start.5 = (f32[2,5,16,128]{3,2,1,0:T(8,128)S(1)}, f32[2,5,16,128]{3,2,1,0:T(8,128)S(1)}, u32[]{:S(2)}, u32[]{:S(2)}) collective-permute-start(f32[2,5,16,128]{3,2,1,0:T(8,128)S(1)} %get-tuple-element.48.ends_ref), channel_id=1, source_target_pairs={{0,1},{1,0},{2,3},{3,2},{4,5},{5,4},{6,7},{7,6},{8,9},{9,8},{10,11... | collective-permute-start | bytes 245768 | tf_op jit(solution)/shard_map/ppermute | solution.py:582
  18.5 3.6 %collective-permute-start.6 = (f32[1,5,16,128]{3,2,1,0:T(8,128)S(1)}, f32[1,5,16,128]{3,2,1,0:T(8,128)S(1)}, u32[]{:S(2)}, u32[]{:S(2)}) collective-permute-start(f32[1,5,16,128]{3,2,1,0:T(8,128)S(1)} %get-tuple-element.51.pair_ref), channel_id=1, source_target_pairs={{0,3},{1,2},{2,1},{3,0},{4,7},{5,6},{6,5},{7,4},{8,11},{9,10},{10,... | collective-permute-start | bytes 122888 | tf_op jit(solution)/shard_map/ppermute | solution.py:582
  19.8 2.1 %collective-permute-start.7 = (f32[7,8,128]{2,1,0:T(8,128)S(1)}, f32[7,8,128]{2,1,0:T(8,128)S(1)}, u32[]{:S(2)}, u32[]{:S(2)}) collective-permute-start(f32[7,8,128]{2,1,0:T(8,128)S(1)} %get-tuple-element.53), channel_id=1, source_target_pairs={{0,1},{1,0},{2,3},{3,2},{4,5},{5,4},{6,7},{7,6},{8,9},{9,8},{10,11... | collective-permute-start | bytes 86024 | tf_op jit(solution)/shard_map/ppermute | solution.py:582
  20.2 1.7 %collective-permute-start.8 = (f32[7,8,128]{2,1,0:T(8,128)S(1)}, f32[7,8,128]{2,1,0:T(8,128)S(1)}, u32[]{:S(2)}, u32[]{:S(2)}) collective-permute-start(f32[7,8,128]{2,1,0:T(8,128)S(1)} %get-tuple-element.54), channel_id=1, source_target_pairs={{0,1},{1,0},{2,3},{3,2},{4,5},{5,4},{6,7},{7,6},{8,9},{9,8},{10,11... | collective-permute-start | bytes 86024 | tf_op jit(solution)/shard_map/ppermute | solution.py:582
  20.3 1.6 %collective-permute-start.9 = (f32[7,8,128]{2,1,0:T(8,128)S(1)}, f32[7,8,128]{2,1,0:T(8,128)S(1)}, u32[]{:S(2)}, u32[]{:S(2)}) collective-permute-start(f32[7,8,128]{2,1,0:T(8,128)S(1)} %get-tuple-element.55), channel_id=1, source_target_pairs={{0,1},{1,0},{2,3},{3,2},{4,5},{5,4},{6,7},{7,6},{8,9},{9,8},{10,11... | collective-permute-start | bytes 86024 | tf_op jit(solution)/shard_map/ppermute | solution.py:582
  20.7 1.2 %collective-permute-start.10 = (f32[4,8,128]{2,1,0:T(8,128)S(1)}, f32[4,8,128]{2,1,0:T(8,128)S(1)}, u32[]{:S(2)}, u32[]{:S(2)}) collective-permute-start(f32[4,8,128]{2,1,0:T(8,128)S(1)} %get-tuple-element.56), channel_id=1, source_target_pairs={{0,1},{1,0},{2,3},{3,2},{4,5},{5,4},{6,7},{7,6},{8,9},{9,8},{10,11... | collective-permute-start | bytes 49160 | tf_op jit(solution)/shard_map/ppermute | solution.py:582
  35.1 1.4 %collective-permute-start.11 = (f32[3,5,16,128]{3,2,1,0:T(8,128)S(1)}, f32[3,5,16,128]{3,2,1,0:T(8,128)S(1)}, u32[]{:S(2)}, u32[]{:S(2)}) collective-permute-start(f32[3,5,16,128]{3,2,1,0:T(8,128)S(1)} %get-tuple-element.61.ends_ref), channel_id=1, source_target_pairs={{0,1},{1,0},{2,3},{3,2},{4,5},{5,4},{6,7},{7,6},{8,9},{9,8},{10,11... | collective-permute-start | bytes 368648 | tf_op jit(solution)/shard_map/ppermute | solution.py:582
  36.5 3.6 %collective-permute-start.12 = (f32[1,5,16,128]{3,2,1,0:T(8,128)S(1)}, f32[1,5,16,128]{3,2,1,0:T(8,128)S(1)}, u32[]{:S(2)}, u32[]{:S(2)}) collective-permute-start(f32[1,5,16,128]{3,2,1,0:T(8,128)S(1)} %shard_map.106.pair_ref), channel_id=1, source_target_pairs={{0,3},{1,2},{2,1},{3,0},{4,7},{5,6},{6,5},{7,4},{8,11},{9,10},{10,... | collective-permute-start | bytes 122888 | tf_op jit(solution)/shard_map/ppermute | solution.py:582

commit v15 on v14

--- a/solution.py
+++ b/solution.py
@@ -47,14 +47,16 @@
     return lax.broadcasted_iota(jnp.int32, (16, 128), dim)
 
 
-def matvec(matrix, vector):
-    n = len(vector)
+def matvec(matrix, vector, base=None):
     out = []
-    for r in range(n):
-        acc = matrix[r][0] * vector[0]
-        for c in range(1, n):
-            acc = acc + matrix[r][c] * vector[c]
-        out.append(acc)
+    for r, row in enumerate(matrix):
+        terms = [m * x for m, x in zip(row, vector)]
+        if base is not None:
+            terms.insert(0, base[r])
+        while len(terms) > 1:
+            pairs = [x + z for x, z in zip(terms[::2], terms[1::2])]
+            terms = pairs + terms[2 * len(pairs) :]
+        out.append(terms[0])
     return out
 
 
@@ -302,11 +304,11 @@
     value = cell(s_ref, 0)
     put(y_ref, value, 0)
     for j in range(1, planes):
-        value = add(cell(s_ref, j), matvec(block(e_ref, j), value))
+        value = matvec(block(e_ref, j), value, cell(s_ref, j))
         put(y_ref, value, j)
     put(ends_ref, [x + z * (1.0 / OMEGA) for x, z in zip(value, last)], 0)
     for j in range(planes - 2, -1, -1):
-        value = add(cell(y_ref, j), matvec(block(f_ref, j), value))
+        value = matvec(block(f_ref, j), value, cell(y_ref, j))
     put(ends_ref, value, 1)
 
 
@@ -340,7 +342,7 @@
     ghosts = jnp.where(live_ref[...] > 0.0, COUPLE * (mine_ref[...] + got_ref[...]), 0.0)
     for j in range(last + 1):
         extra = [ghost_at(ghosts, j, v) for v in range(5)]
-        put(s_ref, add(cell(s0_ref, j), matvec(block(inv_ref, j), extra)), j)
+        put(s_ref, matvec(block(inv_ref, j), extra, cell(s0_ref, j)), j)
     even = lax.axis_index("ja") % 2 == 0
     above = [jnp.where(even, x, 0.0) for x in masked(live_ref, cell(mats_other_ref, 20))]
     put(above_ref, above)
@@ -370,14 +372,14 @@
         linked = matvec(block(f_ref, j), [x * (1.0 / OMEGA) for x in above])
         s = add(matvec(block(inv_ref, j), res), linked)
         put(s_ref, s, j)
-        value = s if j == 0 else add(s, matvec(block(e_ref, j), value))
+        value = s if j == 0 else matvec(block(e_ref, j), value, s)
         put(y_ref, value, j)
         value = add(value, [x * (1.0 / OMEGA) for x in here])
     put(ends_ref, value, 0)
     put(ends_ref, here, 2)
     value = cell(y_ref, planes - 1)
     for j in range(planes - 2, -1, -1):
-        value = add(cell(y_ref, j), matvec(block(f_ref, j), value))
+        value = matvec(block(f_ref, j), value, cell(y_ref, j))
     put(ends_ref, value, 1)
 
 
@@ -409,12 +411,12 @@
 
     @pl.when(lax.axis_index("ja") < 2)
     def _():
-        put(out_ref, add(cell(ends_hi, 0), matvec(matrix_of(mats_hi, 0), c_lo)), 0)
+        put(out_ref, matvec(matrix_of(mats_hi, 0), c_lo, cell(ends_hi, 0)), 0)
 
     @pl.when(lax.axis_index("ja") >= 2)
     def _():
-        turned = add(cell(ends_hi, 1), matvec(matrix_of(mats_hi, 1), c_lo))
-        raised = add(cell(ends_lo, 1), matvec(matrix_of(mats_lo, 2), turned))
+        turned = matvec(matrix_of(mats_hi, 1), c_lo, cell(ends_hi, 1))
+        raised = matvec(matrix_of(mats_lo, 2), turned, cell(ends_lo, 1))
         if first is not None:
             raised = add(raised, first(mats_lo))
         put(out_ref, raised, 0)
@@ -481,8 +483,8 @@
     @pl.when(ja == 0)
     def _():
         put(inflow_ref, zeros, 0)
-        b = add(cell(ends_other_ref, 1), matvec(matrix_of(mats_other_ref, 1), cell(ends_ref, 0)))
-        b = add(b, matvec(matrix_of(mats_other_ref, 2), far(mats_other_ref)))
+        b = matvec(matrix_of(mats_other_ref, 1), cell(ends_ref, 0), cell(ends_other_ref, 1))
+        b = matvec(matrix_of(mats_other_ref, 2), far(mats_other_ref), b)
         put(inflow_ref, b, 1)
 
     @pl.when(ja == 1)
@@ -494,14 +496,14 @@
     def _():
         a = near(mats_ref)
         put(inflow_ref, a, 0)
-        a = add(cell(ends_ref, 0), matvec(matrix_of(mats_ref, 0), a))
-        b = add(cell(ends_other_ref, 1), matvec(matrix_of(mats_other_ref, 1), a))
+        a = matvec(matrix_of(mats_ref, 0), a, cell(ends_ref, 0))
+        b = matvec(matrix_of(mats_other_ref, 1), a, cell(ends_other_ref, 1))
         put(inflow_ref, b, 1)
 
     @pl.when(ja == 3)
     def _():
         a = near(mats_other_ref)
-        a = add(cell(ends_other_ref, 0), matvec(matrix_of(mats_other_ref, 0), a))
+        a = matvec(matrix_of(mats_other_ref, 0), a, cell(ends_other_ref, 0))
         put(inflow_ref, a, 0)
         put(inflow_ref, zeros, 1)
 
@@ -520,7 +522,7 @@
     )
     value = cell(inflow_ref, 0)
     for j in range(planes):
-        value = add(cell(s_ref, j), matvec(block(e_ref, j), value))
+        value = matvec(block(e_ref, j), value, cell(s_ref, j))
         put(y_ref, value, j)
     value = cell(inflow_ref, 1)
     kept = [x * (1.0 - 1.0 / OMEGA) for x in cell(beyond_ref)]
@@ -528,7 +530,7 @@
     above = add(cell(above_ref), [jnp.where(inner, x, 0.0) for x in kept])
     put(above_new_ref, add(above, value))
     for j in range(planes - 1, -1, -1):
-        value = add(cell(y_ref, j), matvec(block(f_ref, j), value))
+        value = matvec(block(f_ref, j), value, cell(y_ref, j))
         put(new_ref, add(masked(live_ref, cell(cur_ref, j)), value), j)
     coupling = [[join(half_ref, half_other_refs, r, c) for c in range(5)] for r in range(5)]
     raised = add(cell(inflow_ref, 0), matvec(coupling, value))
@@ -552,12 +554,12 @@
     )
     value = cell(inflow_ref, 0)
     for j in range(planes):
-        value = add(cell(s_ref, j), matvec(block(e_ref, j), value))
+        value = matvec(block(e_ref, j), value, cell(s_ref, j))
         put(y_ref, value, j)
         value = add(value, [x * (1.0 / OMEGA) for x in cell(cur_ref, j)])
     value = cell(inflow_ref, 1)
     for j in range(planes - 1, -1, -1):
-        value = add(cell(y_ref, j), matvec(block(f_ref, j), value))
+        value = matvec(block(f_ref, j), value, cell(y_ref, j))
         put(new_ref, add(cell(cur_ref, j), value), j)
         copies.append(pltpu.make_async_copy(new_ref.at[j], new_hbm.at[j], sems.at[j]))
         copies[-1].start()

time: 41.3 us -> 41.3 us (level)
  no operation moved by 1% of the time
where the time goes in v15:
time: 41.3 us; the launch traced here: 41.1 us
  starting transfers between devices  12.5 us (30%)
  blocking collectives  11.6 us (28%)
  Pallas kernels  8.78 us (21%)
  waiting for transfers between devices  7.4 us (18%)
  between operations  0.8 us (2%)
    all_to_all x1, blocking collectives, per_device(): got = lax.all_to_all(tile, 'zone', 0, 0, tiled=True)  11.6 us
    pallas_call x13, Pallas kernels, run(): pl.pallas_call(kernel, out_shape=[jax.ShapeDtypeStruct(s, jnp.float32) fo...  8.78 us
    ppermute x10, waiting for transfers between devices, swap(): return lax.ppermute(x, 'ja', [(p, p ^ bit) for p in range(parts)])  5.88 us
    ppermute x2, starting transfers between devices, per_device(): got = lax.ppermute(tiles, 'zone', [(z, z ^ stride) for z in range(zones)])  5.74 us
    ppermute x10, starting transfers between devices, swap(): return lax.ppermute(x, 'ja', [(p, p ^ bit) for p in range(parts)])  5.25 us
    ppermute x1, starting transfers between devices, per_device(): got = lax.ppermute(theirs, 'zone', [(z, z ^ 1) for z in range(zones)])  1.53 us
    ppermute x1, waiting for transfers between devices, per_device(): got = lax.ppermute(theirs, 'zone', [(z, z ^ 1) for z in range(zones)])  1.49 us
  transfers between devices with their start and end apart: 13, of which 7 were waited for; matrix products, arithmetic and copies ran while one was open for 0% of the time, Pallas kernels for 12%

profile of v15, /device:TPU:0, one launch (start us, length us, event | category | flops | bytes accessed | tf_op | source)
XLA Modules:
  0.0 41.1 jit_solution(17849631759148039133)
XLA Ops:
  0.6 0.0 copy-start
  0.6 0.0 copy-start.3
  0.7 0.0 copy-start.4
  0.7 1.3 %shard_map.95 = (f32[1,16,128]{2,1,0:T(8,128)S(1)}, f32[5,16,128]{2,1,0:T(8,128)S(1)}, f32[5,16,128]{2,1,0:T(8,128)S(1)}) custom-call(f32[8,5,16,128]{3,2,1,0:T(8,128)} %bitcast.14), custom_call_target="tpu_custom_call" | custom-call | flops 10000000000 | bytes 10000000 | tf_op jit(solution)/shard_map/pallas_call | solution.py:26
  2.0 4.1 %collective-permute-start = (f32[1,16,128]{2,1,0:T(8,128)S(1)}, f32[1,16,128]{2,1,0:T(8,128)S(1)}, u32[]{:S(2)}, u32[]{:S(2)}) collective-permute-start(f32[1,16,128]{2,1,0:T(8,128)S(1)} %get-tuple-element.34.tile_ref.own_ref), channel_id=1, source_target_pairs={{0,16},{4,20},{8,24},{12,28},{16,0},{20,4},{24,8},{28,12},{1,17},{... | collective-permute-start | bytes 24584 | tf_op jit(solution)/shard_map/ppermute | solution.py:607
  6.1 0.0 copy-done
  6.1 0.0 copy-done.3
  6.1 0.0 copy-done.4
  6.1 2.8 %shard_map.96 = (f32[8,5,5,16,128]{4,3,2,1,0:T(8,128)S(1)}, f32[8,5,5,16,128]{4,3,2,1,0:T(8,128)S(1)}, f32[20,5,16,128]{3,2,1,0:T(8,128)S(1)}, f32[16,128]{1,0:T...) custom-call(s32[8]{0:T(128)} %depth_hbm.1, s32[8]{0:T(128)} %east_hbm.1, ...), custom_call_target="tpu_custom_call" | custom-call | flops 5000000000 | bytes 5000000 | tf_op jit(solution)/shard_map/pallas_call | solution.py:26
  8.9 0.0 copy-start.1
  8.9 0.0 copy-start.2
  8.9 0.0 copy-start.5
  8.9 0.0 collective-permute-done.got_ref
  9.0 0.1 shard_map.97
  9.0 0.1 collective-permute-start.1
  9.1 1.6 %collective-permute-start.2 = (f32[2,16,128]{2,1,0:T(8,128)S(1)}, f32[2,16,128]{2,1,0:T(8,128)S(1)}, u32[]{:S(2)}, u32[]{:S(2)}) collective-permute-start(f32[2,16,128]{2,1,0:T(8,128)S(1)} %get-tuple-element.39.own_ref), channel_id=1, source_target_pairs={{0,8},{4,12},{8,0},{12,4},{16,24},{20,28},{24,16},{28,20},{1,9},{5... | collective-permute-start | bytes 49160 | tf_op jit(solution)/shard_map/ppermute | solution.py:607
  10.7 0.7 %collective-permute-done.1.other_ref.mats_other_ref = f32[21,5,16,128]{3,2,1,0:T(8,128)S(1)} collective-permute-done((f32[21,5,16,128]{3,2,1,0:T(8,128)S(1)}, f32[21,5,16,128]{3,2,1,0:T(8,128)S(1)}, u32[]{:S(2)}, u32[]{:S(2)}) %collective-permute-start.1) | collective-permute-done | bytes 860192 | tf_op jit(solution)/shard_map/ppermute | solution.py:584
  11.5 1.4 %collective-permute-start.4 = (f32[7,5,8,128]{3,2,1,0:T(8,128)S(1)}, f32[7,5,8,128]{3,2,1,0:T(8,128)S(1)}, u32[]{:S(2)}, u32[]{:S(2)}) collective-permute-start(f32[7,5,8,128]{3,2,1,0:T(8,128)S(1)} %shard_map.98.after_ref), channel_id=1, source_target_pairs={{0,3},{1,2},{2,1},{3,0},{4,7},{5,6},{6,5},{7,4},{8,11},{9,10},{10,... | collective-permute-start | bytes 430088 | tf_op jit(solution)/shard_map/ppermute | solution.py:584
  12.9 0.0 collective-permute-done.2.got_ref
  12.9 0.1 shard_map.99
  13.0 1.5 %collective-permute-start.3 = (f32[16,128]{1,0:T(8,128)S(1)}, f32[16,128]{1,0:T(8,128)S(1)}, u32[]{:S(2)}, u32[]{:S(2)}) collective-permute-start(f32[16,128]{1,0:T(8,128)S(1)} %get-tuple-element.44), channel_id=1, source_target_pairs={{0,4},{4,0},{8,12},{12,8},{16,20},{20,16},{24,28},{28,24},{1,5},{5... | collective-permute-start | bytes 24584 | tf_op jit(solution)/shard_map/ppermute | solution.py:624
  14.5 0.0 copy-done.1
  14.5 0.0 copy-done.2
  14.5 0.0 copy-done.5
  14.5 0.6 %shard_map.100.s0_ref = f32[8,5,16,128]{3,2,1,0:T(8,128)S(1)} custom-call(f32[16,128]{1,0:T(8,128)S(1)} %get-tuple-element.43.tiles_ref.mine_ref, f32[16,128]{1,0:T(8,128)S(1)} %get-tuple-element.35.live_ref, f32[8,5,16,128]{3,2,1,0:T(8,128)S(1)} %bitcast.15, f32[8,5,16,128]{3,2,1,0:T(8,128)S(1)} %bitcast.22, f32[8,5,5,16,128]{4,3,2,1,0:T(8,128)S(1)} %bitcast.12, ...), custom_call_target="tpu_custom_call" | custom-call | flops 2000000000 | bytes 2000000 | tf_op jit(solution)/shard_map/pallas_call | solution.py:26
  15.2 1.5 %collective-permute-done.3.got_ref = f32[16,128]{1,0:T(8,128)S(1)} collective-permute-done((f32[16,128]{1,0:T(8,128)S(1)}, f32[16,128]{1,0:T(8,128)S(1)}, u32[]{:S(2)}, u32[]{:S(2)}) %collective-permute-start.3) | collective-permute-done | bytes 8224 | tf_op jit(solution)/shard_map/ppermute | solution.py:624
  16.7 0.4 %shard_map.101 = (f32[8,5,16,128]{3,2,1,0:T(8,128)S(1)}, f32[2,5,16,128]{3,2,1,0:T(8,128)S(1)}, f32[5,16,128]{2,1,0:T(8,128)S(1)}) custom-call(f32[21,5,16,128]{3,2,1,0:T(8,128)S(1)} %collective-permute-done.1.other_ref.mats_other_ref, f32[16,128]{1,0:T(8,128)S(1)} %get-tuple-element.35.live_ref, f32[16,128]{1,0:T(8,128)S(1)} %get-tuple-element.43.tiles_ref.mine_ref, ...), custom_call_target="tpu_custom_call" | custom-call | flops 1000000000 | bytes 1000000 | tf_op jit(solution)/shard_map/pallas_call | solution.py:26
  17.1 0.1 collective-permute-start.5
  17.1 1.3 %collective-permute-done.5.ends_other_ref = f32[2,5,16,128]{3,2,1,0:T(8,128)S(1)} collective-permute-done((f32[2,5,16,128]{3,2,1,0:T(8,128)S(1)}, f32[2,5,16,128]{3,2,1,0:T(8,128)S(1)}, u32[]{:S(2)}, u32[]{:S(2)}) %collective-permute-start.5) | collective-permute-done | bytes 81952 | tf_op jit(solution)/shard_map/ppermute | solution.py:584
  18.4 0.0 collective-permute-done.4.half_ref
  18.5 1.3 %collective-permute-start.6 = (f32[1,5,16,128]{3,2,1,0:T(8,128)S(1)}, f32[1,5,16,128]{3,2,1,0:T(8,128)S(1)}, u32[]{:S(2)}, u32[]{:S(2)}) collective-permute-start(f32[1,5,16,128]{3,2,1,0:T(8,128)S(1)} %get-tuple-element.51.pair_ref), channel_id=1, source_target_pairs={{0,3},{1,2},{2,1},{3,0},{4,7},{5,6},{6,5},{7,4},{8,11},{9,10},{10,... | collective-permute-start | bytes 122888 | tf_op jit(solution)/shard_map/ppermute | solution.py:584
  19.8 0.4 collective-permute-start.7
  20.2 0.1 collective-permute-start.8
  20.3 0.4 collective-permute-start.9
  20.7 0.1 collective-permute-start.10
  20.8 1.0 %collective-permute-done.10.rest_3_ = f32[4,8,128]{2,1,0:T(8,128)S(1)} collective-permute-done((f32[4,8,128]{2,1,0:T(8,128)S(1)}, f32[4,8,128]{2,1,0:T(8,128)S(1)}, u32[]{:S(2)}, u32[]{:S(2)}) %collective-permute-start.10) | collective-permute-done | bytes 16416 | tf_op jit(solution)/shard_map/ppermute | solution.py:584
  21.9 0.0 collective-permute-done.7.rest_0_
  21.9 0.0 collective-permute-done.8.rest_1_
  21.9 0.0 collective-permute-done.9.rest_2_
  21.9 0.2 collective-permute-done.6.pair_other_ref
  22.1 0.5 %shard_map.103 = (f32[8,5,16,128]{3,2,1,0:T(8,128)S(1)}, f32[5,16,128]{2,1,0:T(8,128)S(1)}, f32[5,16,128]{2,1,0:T(8,128)S(1)}, f32[8,16,128]{2,1,0:T(8,128)S(1)}) custom-call(f32[16,128]{1,0:T(8,128)S(1)} %get-tuple-element.35.live_ref, f32[8,5,16,128]{3,2,1,0:T(8,128)S(1)} %bitcast.17, f32[5,16,128]{2,1,0:T(8,128)S(1)} %get-tuple-element.47.above_ref, ...), custom_call_target="tpu_custom_call" | custom-call | flops 1000000000 | bytes 1000000 | tf_op jit(solution)/shard_map/pallas_call | solution.py:26
  22.6 11.6 %all_to_all.5.tiles_ref = f32[8,16,128]{2,1,0:T(8,128)S(1)} all-to-all(f32[8,16,128]{2,1,0:T(8,128)S(1)} %get-tuple-element.58), channel_id=1, replica_groups=mesh['zone'=8,'ja'=4] {'zone'}, dimensions={0} | all-to-all | bytes 131072 | tf_op jit(solution)/shard_map/all_to_all | solution.py:645
  34.1 0.9 %shard_map.104 = (f32[8,5,16,128]{3,2,1,0:T(8,128)S(1)}, f32[8,5,16,128]{3,2,1,0:T(8,128)S(1)}, f32[3,5,16,128]{3,2,1,0:T(8,128)S(1)}) custom-call(f32[16,128]{1,0:T(8,128)S(1)} %get-tuple-element.35.live_ref, f32[2,8,16,128]{3,2,1,0:T(8,128)S(1)} %get-tuple-element.41.pick_ref, f32[8,16,128]{2,1,0:T(8,128)S(1)} %all_to_all.5.tiles_ref, ...), custom_call_target="tpu_custom_call" | custom-call | flops 1000000000 | bytes 1000000 | tf_op jit(solution)/shard_map/pallas_call | solution.py:26
  35.0 0.1 collective-permute-start.11
  35.1 1.3 %collective-permute-done.11.ends_other_ref = f32[3,5,16,128]{3,2,1,0:T(8,128)S(1)} collective-permute-done((f32[3,5,16,128]{3,2,1,0:T(8,128)S(1)}, f32[3,5,16,128]{3,2,1,0:T(8,128)S(1)}, u32[]{:S(2)}, u32[]{:S(2)}) %collective-permute-start.11) | collective-permute-done | bytes 122912 | tf_op jit(solution)/shard_map/ppermute | solution.py:584
  36.5 1.3 %collective-permute-start.12 = (f32[1,5,16,128]{3,2,1,0:T(8,128)S(1)}, f32[1,5,16,128]{3,2,1,0:T(8,128)S(1)}, u32[]{:S(2)}, u32[]{:S(2)}) collective-permute-start(f32[1,5,16,128]{3,2,1,0:T(8,128)S(1)} %shard_map.106.pair_ref), channel_id=1, source_target_pairs={{0,3},{1,2},{2,1},{3,0},{4,7},{5,6},{6,5},{7,4},{8,11},{9,10},{10,... | collective-permute-start | bytes 122888 | tf_op jit(solution)/shard_map/ppermute | solution.py:584
  37.8 0.9 %shard_map.105 = (f32[8,5,16,128]{3,2,1,0:T(8,128)}, f32[16,128]{1,0:T(8,128)S(1)}) custom-call(f32[16,128]{1,0:T(8,128)S(1)} %get-tuple-element.35.live_ref, f32[5,16,128]{2,1,0:T(8,128)S(1)} %get-tuple-element.57.below_ref, f32[3,5,16,128]{3,2,1,0:T(8,128)S(1)} %collective-permute-done.11.ends_other_ref, f32[8,5,16,128]{3,2,1,0:T(8,128)S(1)} %get-tuple-element.59.cur_ref, ...), custom_call_target="tpu_custom_call" | custom-call | flops 1000000000 | bytes 1000000 | tf_op jit(solution)/shard_map/pallas_call | solution.py:26
  38.7 1.3 %collective-permute-done.12.pair_other_ref = f32[1,5,16,128]{3,2,1,0:T(8,128)S(1)} collective-permute-done((f32[1,5,16,128]{3,2,1,0:T(8,128)S(1)}, f32[1,5,16,128]{3,2,1,0:T(8,128)S(1)}, u32[]{:S(2)}, u32[]{:S(2)}) %collective-permute-start.12) | collective-permute-done | bytes 40992 | tf_op jit(solution)/shard_map/ppermute | solution.py:584
  40.1 1.1 %shard_map.107 = f32[8,5,16,128]{3,2,1,0:T(8,128)} custom-call(f32[16,128]{1,0:T(8,128)S(1)} %get-tuple-element.63.done_ref, f32[8,5,16,128]{3,2,1,0:T(8,128)S(1)} %get-tuple-element.59.cur_ref, f32[8,5,16,128]{3,2,1,0:T(8,128)S(1)} %get-tuple-element.64.s_ref, f32[8,5,5,16,128]{4,3,2,1,0:T(8,128)S(1)} %get-tuple-element.45.e_ref, ...), custom_call_target="tpu_custom_call" | custom-call | flops 1000000000 | bytes 1000000 | tf_op jit(solution)/shard_map/pallas_call | solution.py:26
  (3 shorter events, 0.1 us)
Async XLA Ops:
  0.6 5.4 %copy-start = (f32[1,8,5,5,16,128]{5,4,3,2,1,0:T(8,128)S(1)}, f32[1,8,5,5,16,128]{5,4,3,2,1,0:T(8,128)}, u32[]{:S(2)}) copy-start(f32[1,8,5,5,16,128]{5,4,3,2,1,0:T(8,128)} %param.13) | copy-start | bytes 4915204
  0.6 5.4 %copy-start.3 = (f32[1,8,5,5,16,128]{5,4,3,2,1,0:T(8,128)S(1)}, f32[1,8,5,5,16,128]{5,4,3,2,1,0:T(8,128)}, u32[]{:S(2)}) copy-start(f32[1,8,5,5,16,128]{5,4,3,2,1,0:T(8,128)} %param.11) | copy-start | bytes 4915204
  0.7 5.4 %copy-start.4 = (f32[1,8,5,5,16,128]{5,4,3,2,1,0:T(8,128)S(1)}, f32[1,8,5,5,16,128]{5,4,3,2,1,0:T(8,128)}, u32[]{:S(2)}) copy-start(f32[1,8,5,5,16,128]{5,4,3,2,1,0:T(8,128)} %param.12) | copy-start | bytes 4915204
  2.0 7.0 %collective-permute-start = (f32[1,16,128]{2,1,0:T(8,128)S(1)}, f32[1,16,128]{2,1,0:T(8,128)S(1)}, u32[]{:S(2)}, u32[]{:S(2)}) collective-permute-start(f32[1,16,128]{2,1,0:T(8,128)S(1)} %get-tuple-element.34.tile_ref.own_ref), channel_id=1, source_target_pairs={{0,16},{4,20},{8,24},{12,28},{16,0},{20,4},{24,8},{28,12},{1,17},{... | collective-permute-start | bytes 24584 | tf_op jit(solution)/shard_map/ppermute | solution.py:607
  8.9 5.6 %copy-start.1 = (f32[1,8,5,5,16,128]{5,4,3,2,1,0:T(8,128)S(1)}, f32[1,8,5,5,16,128]{5,4,3,2,1,0:T(8,128)}, u32[]{:S(2)}) copy-start(f32[1,8,5,5,16,128]{5,4,3,2,1,0:T(8,128)} %param.10) | copy-start | bytes 4915204
  8.9 5.6 %copy-start.2 = (f32[1,8,5,16,128]{4,3,2,1,0:T(8,128)S(1)}, f32[1,8,5,16,128]{4,3,2,1,0:T(8,128)}, u32[]{:S(2)}) copy-start(f32[1,8,5,16,128]{4,3,2,1,0:T(8,128)} %param.8) | copy-start | bytes 983044
  8.9 5.6 %copy-start.5 = (f32[1,8,5,16,128]{4,3,2,1,0:T(8,128)S(1)}, f32[1,8,5,16,128]{4,3,2,1,0:T(8,128)}, u32[]{:S(2)}) copy-start(f32[1,8,5,16,128]{4,3,2,1,0:T(8,128)} %param.9) | copy-start | bytes 983044
  9.0 2.5 %collective-permute-start.1 = (f32[21,5,16,128]{3,2,1,0:T(8,128)S(1)}, f32[21,5,16,128]{3,2,1,0:T(8,128)S(1)}, u32[]{:S(2)}, u32[]{:S(2)}) collective-permute-start(f32[21,5,16,128]{3,2,1,0:T(8,128)S(1)} %get-tuple-element.38.mine_ref.mats_ref), channel_id=1, source_target_pairs={{0,1},{1,0},{2,3},{3,2},{4,5},{5,4},{6,7},{7,6},{8,9},{9,8},{10,11... | collective-permute-start | bytes 2580488 | tf_op jit(solution)/shard_map/ppermute | solution.py:584
  9.1 3.8 %collective-permute-start.2 = (f32[2,16,128]{2,1,0:T(8,128)S(1)}, f32[2,16,128]{2,1,0:T(8,128)S(1)}, u32[]{:S(2)}, u32[]{:S(2)}) collective-permute-start(f32[2,16,128]{2,1,0:T(8,128)S(1)} %get-tuple-element.39.own_ref), channel_id=1, source_target_pairs={{0,8},{4,12},{8,0},{12,4},{16,24},{20,28},{24,16},{28,20},{1,9},{5... | collective-permute-start | bytes 49160 | tf_op jit(solution)/shard_map/ppermute | solution.py:607
  11.5 6.9 %collective-permute-start.4 = (f32[7,5,8,128]{3,2,1,0:T(8,128)S(1)}, f32[7,5,8,128]{3,2,1,0:T(8,128)S(1)}, u32[]{:S(2)}, u32[]{:S(2)}) collective-permute-start(f32[7,5,8,128]{3,2,1,0:T(8,128)S(1)} %shard_map.98.after_ref), channel_id=1, source_target_pairs={{0,3},{1,2},{2,1},{3,0},{4,7},{5,6},{6,5},{7,4},{8,11},{9,10},{10,... | collective-permute-start | bytes 430088 | tf_op jit(solution)/shard_map/ppermute | solution.py:584
  13.0 3.7 %collective-permute-start.3 = (f32[16,128]{1,0:T(8,128)S(1)}, f32[16,128]{1,0:T(8,128)S(1)}, u32[]{:S(2)}, u32[]{:S(2)}) collective-permute-start(f32[16,128]{1,0:T(8,128)S(1)} %get-tuple-element.44), channel_id=1, source_target_pairs={{0,4},{4,0},{8,12},{12,8},{16,20},{20,16},{24,28},{28,24},{1,5},{5... | collective-permute-start | bytes 24584 | tf_op jit(solution)/shard_map/ppermute | solution.py:624
  17.1 1.3 %collective-permute-start.5 = (f32[2,5,16,128]{3,2,1,0:T(8,128)S(1)}, f32[2,5,16,128]{3,2,1,0:T(8,128)S(1)}, u32[]{:S(2)}, u32[]{:S(2)}) collective-permute-start(f32[2,5,16,128]{3,2,1,0:T(8,128)S(1)} %get-tuple-element.48.ends_ref), channel_id=1, source_target_pairs={{0,1},{1,0},{2,3},{3,2},{4,5},{5,4},{6,7},{7,6},{8,9},{9,8},{10,11... | collective-permute-start | bytes 245768 | tf_op jit(solution)/shard_map/ppermute | solution.py:584
  18.5 3.6 %collective-permute-start.6 = (f32[1,5,16,128]{3,2,1,0:T(8,128)S(1)}, f32[1,5,16,128]{3,2,1,0:T(8,128)S(1)}, u32[]{:S(2)}, u32[]{:S(2)}) collective-permute-start(f32[1,5,16,128]{3,2,1,0:T(8,128)S(1)} %get-tuple-element.51.pair_ref), channel_id=1, source_target_pairs={{0,3},{1,2},{2,1},{3,0},{4,7},{5,6},{6,5},{7,4},{8,11},{9,10},{10,... | collective-permute-start | bytes 122888 | tf_op jit(solution)/shard_map/ppermute | solution.py:584
  19.8 2.1 %collective-permute-start.7 = (f32[7,8,128]{2,1,0:T(8,128)S(1)}, f32[7,8,128]{2,1,0:T(8,128)S(1)}, u32[]{:S(2)}, u32[]{:S(2)}) collective-permute-start(f32[7,8,128]{2,1,0:T(8,128)S(1)} %get-tuple-element.53), channel_id=1, source_target_pairs={{0,1},{1,0},{2,3},{3,2},{4,5},{5,4},{6,7},{7,6},{8,9},{9,8},{10,11... | collective-permute-start | bytes 86024 | tf_op jit(solution)/shard_map/ppermute | solution.py:584
  20.2 1.7 %collective-permute-start.8 = (f32[7,8,128]{2,1,0:T(8,128)S(1)}, f32[7,8,128]{2,1,0:T(8,128)S(1)}, u32[]{:S(2)}, u32[]{:S(2)}) collective-permute-start(f32[7,8,128]{2,1,0:T(8,128)S(1)} %get-tuple-element.54), channel_id=1, source_target_pairs={{0,1},{1,0},{2,3},{3,2},{4,5},{5,4},{6,7},{7,6},{8,9},{9,8},{10,11... | collective-permute-start | bytes 86024 | tf_op jit(solution)/shard_map/ppermute | solution.py:584
  20.3 1.6 %collective-permute-start.9 = (f32[7,8,128]{2,1,0:T(8,128)S(1)}, f32[7,8,128]{2,1,0:T(8,128)S(1)}, u32[]{:S(2)}, u32[]{:S(2)}) collective-permute-start(f32[7,8,128]{2,1,0:T(8,128)S(1)} %get-tuple-element.55), channel_id=1, source_target_pairs={{0,1},{1,0},{2,3},{3,2},{4,5},{5,4},{6,7},{7,6},{8,9},{9,8},{10,11... | collective-permute-start | bytes 86024 | tf_op jit(solution)/shard_map/ppermute | solution.py:584
  20.7 1.2 %collective-permute-start.10 = (f32[4,8,128]{2,1,0:T(8,128)S(1)}, f32[4,8,128]{2,1,0:T(8,128)S(1)}, u32[]{:S(2)}, u32[]{:S(2)}) collective-permute-start(f32[4,8,128]{2,1,0:T(8,128)S(1)} %get-tuple-element.56), channel_id=1, source_target_pairs={{0,1},{1,0},{2,3},{3,2},{4,5},{5,4},{6,7},{7,6},{8,9},{9,8},{10,11... | collective-permute-start | bytes 49160 | tf_op jit(solution)/shard_map/ppermute | solution.py:584
  35.0 1.4 %collective-permute-start.11 = (f32[3,5,16,128]{3,2,1,0:T(8,128)S(1)}, f32[3,5,16,128]{3,2,1,0:T(8,128)S(1)}, u32[]{:S(2)}, u32[]{:S(2)}) collective-permute-start(f32[3,5,16,128]{3,2,1,0:T(8,128)S(1)} %get-tuple-element.61.ends_ref), channel_id=1, source_target_pairs={{0,1},{1,0},{2,3},{3,2},{4,5},{5,4},{6,7},{7,6},{8,9},{9,8},{10,11... | collective-permute-start | bytes 368648 | tf_op jit(solution)/shard_map/ppermute | solution.py:584
  36.5 3.6 %collective-permute-start.12 = (f32[1,5,16,128]{3,2,1,0:T(8,128)S(1)}, f32[1,5,16,128]{3,2,1,0:T(8,128)S(1)}, u32[]{:S(2)}, u32[]{:S(2)}) collective-permute-start(f32[1,5,16,128]{3,2,1,0:T(8,128)S(1)} %shard_map.106.pair_ref), channel_id=1, source_target_pairs={{0,3},{1,2},{2,1},{3,0},{4,7},{5,6},{6,5},{7,4},{8,11},{9,10},{10,... | collective-permute-start | bytes 122888 | tf_op jit(solution)/shard_map/ppermute | solution.py:584

commit v16 on v15

--- a/solution.py
+++ b/solution.py
@@ -121,19 +121,19 @@
         out_ref[count + w] = got_ref[w]
 
 
-def select_kernel(own_ref, got_ref, after_ref, pick_ref, partner_ref, mine_ref, theirs_ref):
-    del after_ref
-    count = own_ref.shape[0]
-
+def select_kernel(tiles_ref, pick_ref, partner_ref, mine_ref, theirs_ref):
     def tile_at(i):
-        return own_ref[i] if i < count else got_ref[i - count]
-
-    mine_ref[...] = ghosts_of(pick_ref, tile_at, 2 * count)
-    theirs_ref[...] = ghosts_of(partner_ref, tile_at, 2 * count)
-
-
-def relay_kernel(own_ref, got_ref, mats_ref, first_ref, mats_out_ref, out_ref):
-    merge_kernel(own_ref, got_ref, out_ref)
+        return tiles_ref[i]
+
+    mine_ref[...] = ghosts_of(pick_ref, tile_at, tiles_ref.shape[0])
+    theirs_ref[...] = ghosts_of(partner_ref, tile_at, tiles_ref.shape[0])
+
+
+def relay_kernel(
+    own_ref, half_ref, quarter_ref, both_ref, mats_ref, first_ref, mats_out_ref, out_ref
+):
+    for i, ref in enumerate((own_ref, half_ref, quarter_ref, both_ref)):
+        out_ref[i] = ref[0]
     for i in range(20):
         put(mats_out_ref, cell(mats_ref, i), i)
     put(mats_out_ref, cell(first_ref), 20)
@@ -334,10 +334,11 @@
 
 
 def local_kernel(
-    mats_other_ref, live_ref, mine_ref, got_ref, cur_ref, s0_ref,
+    half_ref, mats_other_ref, live_ref, mine_ref, got_ref, cur_ref, s0_ref,
     inv_ref, e_ref, f_ref,
     s_ref, ends_ref, above_ref, y_ref,
 ):
+    del half_ref
     last = cur_ref.shape[0] - 1
     ghosts = jnp.where(live_ref[...] > 0.0, COUPLE * (mine_ref[...] + got_ref[...]), 0.0)
     for j in range(last + 1):
@@ -429,10 +430,7 @@
     by_place([ends_ref, mats_ref], [ends_other_ref, mats_other_ref], run)
 
 
-def first_mid_kernel(
-    live_ref, half_ref, ends_ref, ends_other_ref, mats_ref, mats_other_ref,
-    out_ref, beyond_ref, half_out_ref, *part_refs,
-):
+def first_mid_kernel(live_ref, ends_ref, ends_other_ref, mats_ref, mats_other_ref, out_ref):
     def first(mats_lo):
         return [x * (1.0 / OMEGA) for x in masked(live_ref, cell(mats_lo, 20))]
 
@@ -440,6 +438,10 @@
         compose(ends_lo, mats_lo, ends_hi, mats_hi, out_ref, first)
 
     by_place([ends_ref, mats_ref], [ends_other_ref, mats_other_ref], run)
+
+
+def parts_kernel(live_ref, half_ref, pair_ref, beyond_ref, half_out_ref, *part_refs):
+    del pair_ref
     for r in range(5):
         put(half_out_ref, cell(half_ref, r), r)
         for c in range(5):
@@ -602,36 +604,36 @@
         flops=5 * 10**9,
         far=(0, 1),
     )(zone_depth, east_zone, tile, inv, low, up)
-    tiles, stride = tile, zones // 2
+    def exchange(x, stride):
+        return lax.ppermute(x, "zone", [(z, z ^ stride) for z in range(zones)])
+
+    far, near = zones // 2, zones // 4
+    gots = [exchange(tile, stride) for stride in (far, near, far + near)]
+    mats, tiles = call(relay_kernel, [(21, *plane), (4, *state[2:])], flops=10**5)(
+        tile, *gots, mats, first
+    )
+    stride = zones // 8
     while stride > 1:
-        got = lax.ppermute(tiles, "zone", [(z, z ^ stride) for z in range(zones)])
         both = (2 * tiles.shape[0], *state[2:])
-        if stride == zones // 2:
-            mats, tiles = call(relay_kernel, [(21, *plane), both], flops=10**5)(
-                tiles, got, mats, first
-            )
-            mats_other = swap(mats, 1)
-            half = call(half_kernel, [(7, plane[0], 8, plane[2])], flops=10**5)(
-                mats, mats_other, final
-            )[0]
-        elif stride > 2:
-            tiles = call(merge_kernel, [both], flops=10**5)(tiles, got, half)[0]
-        else:
-            tiles, theirs = call(select_kernel, [state[2:]] * 2, flops=10**5)(
-                tiles, got, half, pick, partner
-            )
+        tiles = call(merge_kernel, [both], flops=10**5)(tiles, exchange(tiles, stride))[0]
         stride //= 2
-    got = lax.ppermute(theirs, "zone", [(z, z ^ 1) for z in range(zones)])
-    half = swap(half, 3)
+    tiles, theirs = call(select_kernel, [state[2:]] * 2, flops=10**5)(tiles, pick, partner)
+    got = exchange(theirs, 1)
+    mats_other = swap(mats, 1)
+    half = call(half_kernel, [(7, plane[0], 8, plane[2])], flops=10**5)(mats, mats_other, final)[0]
     s0 = call(source_kernel, [state], flops=2 * 10**9)(tiles, live, current, force, diag, inv, e, f)[0]
     s, ends, above = call(local_kernel, [state, (2, *plane), plane], work)(
-        mats_other, live, tiles, got, current, s0, inv, e, f
-    )
+        half, mats_other, live, tiles, got, current, s0, inv, e, f
+    )
+    half = swap(half, 3)
     ends_other = swap(ends, 1)
+    pair = call(first_mid_kernel, [(1, *plane)], flops=10**5)(
+        live, ends, ends_other, mats, mats_other
+    )[0]
     parts_of = [(min(PART, 25 - i), *half.shape[2:]) for i in range(0, 25, PART)]
-    pair, beyond, half, *sent = call(
-        first_mid_kernel, [(1, *plane), plane, (5, *half.shape[1:])] + parts_of, flops=10**5
-    )(live, half, ends, ends_other, mats, mats_other)
+    beyond, half, *sent = call(
+        parts_kernel, [plane, (5, *half.shape[1:])] + parts_of, flops=10**5
+    )(live, half, pair)
     half_other = [swap(x, 1) for x in sent]
     pair_other = swap(pair, 3)
     flows = [buffer(2, *plane)]

time: 41.3 us -> 41.3 us (level)
  waiting for transfers between devices: 7.4 us -> 6.82 us
  starting transfers between devices: 12.5 us -> 13 us
    ppermute x3 -> x4, waiting for transfers between devices: 1.52 us -> 1.02 us  [exchange(): return lax.ppermute(x, 'zone', [(z, z ^ stride) for z in range(zones)])]
    ppermute x10, starting transfers between devices: 5.25 us -> 5.68 us  [swap(): return lax.ppermute(x, 'ja', [(p, p ^ bit) for p in range(parts)])]
    ppermute x3 -> x4, starting transfers between devices: 7.27 us -> 7.29 us  [exchange(): return lax.ppermute(x, 'zone', [(z, z ^ stride) for z in range(zones)])]
    pallas_call x13 -> x14, Pallas kernels: 8.78 us -> 8.78 us  [run(): pl.pallas_call(kernel, out_shape=[jax.ShapeDtypeStruct(s, jnp.float32) fo...]
  transfers between devices with their start and end apart: 13 -> 14, of which waited for: 7 -> 8; matrix products, arithmetic and copies ran while one was open for 0% -> 0% of each run, Pallas kernels for 12% -> 12%
where the time goes in v16:
time: 41.3 us; the launch traced here: 41.1 us
  starting transfers between devices  13 us (31%)
  blocking collectives  11.7 us (28%)
  Pallas kernels  8.78 us (21%)
  waiting for transfers between devices  6.82 us (17%)
  between operations  0.8 us (2%)
    all_to_all x1, blocking collectives, per_device(): got = lax.all_to_all(tile, 'zone', 0, 0, tiled=True)  11.7 us
    pallas_call x14, Pallas kernels, run(): pl.pallas_call(kernel, out_shape=[jax.ShapeDtypeStruct(s, jnp.float32) fo...  8.78 us
    ppermute x4, starting transfers between devices, exchange(): return lax.ppermute(x, 'zone', [(z, z ^ stride) for z in range(zones)])  7.29 us
    ppermute x10, waiting for transfers between devices, swap(): return lax.ppermute(x, 'ja', [(p, p ^ bit) for p in range(parts)])  5.8 us
    ppermute x10, starting transfers between devices, swap(): return lax.ppermute(x, 'ja', [(p, p ^ bit) for p in range(parts)])  5.68 us
    ppermute x4, waiting for transfers between devices, exchange(): return lax.ppermute(x, 'zone', [(z, z ^ stride) for z in range(zones)])  1.02 us
  transfers between devices with their start and end apart: 14, of which 8 were waited for; matrix products, arithmetic and copies ran while one was open for 0% of the time, Pallas kernels for 12%

profile of v16, /device:TPU:0, one launch (start us, length us, event | category | flops | bytes accessed | tf_op | source)
XLA Modules:
  0.0 41.1 jit_solution(11994430260577232777)
XLA Ops:
  0.6 0.0 copy-start
  0.6 0.0 copy-start.3
  0.7 0.0 copy-start.4
  0.7 1.3 %shard_map.95 = (f32[1,16,128]{2,1,0:T(8,128)S(1)}, f32[5,16,128]{2,1,0:T(8,128)S(1)}, f32[5,16,128]{2,1,0:T(8,128)S(1)}) custom-call(f32[8,5,16,128]{3,2,1,0:T(8,128)} %bitcast.14), custom_call_target="tpu_custom_call" | custom-call | flops 10000000000 | bytes 10000000 | tf_op jit(solution)/shard_map/pallas_call | solution.py:26
  2.0 5.1 %collective-permute-start.2 = (f32[1,16,128]{2,1,0:T(8,128)S(1)}, f32[1,16,128]{2,1,0:T(8,128)S(1)}, u32[]{:S(2)}, u32[]{:S(2)}) collective-permute-start(f32[1,16,128]{2,1,0:T(8,128)S(1)} %get-tuple-element.33.tile_ref.own_ref), channel_id=1, source_target_pairs={{0,24},{4,28},{8,16},{12,20},{16,8},{20,12},{24,0},{28,4},{1,25},{... | collective-permute-start | bytes 24584 | tf_op jit(solution)/shard_map/ppermute | solution.py:608
  7.1 0.0 collective-permute-start.1
  7.1 0.6 %collective-permute-start = (f32[1,16,128]{2,1,0:T(8,128)S(1)}, f32[1,16,128]{2,1,0:T(8,128)S(1)}, u32[]{:S(2)}, u32[]{:S(2)}) collective-permute-start(f32[1,16,128]{2,1,0:T(8,128)S(1)} %get-tuple-element.33.tile_ref.own_ref), channel_id=1, source_target_pairs={{0,16},{4,20},{8,24},{12,28},{16,0},{20,4},{24,8},{28,12},{1,17},{... | collective-permute-start | bytes 24584 | tf_op jit(solution)/shard_map/ppermute | solution.py:608
  7.7 0.0 copy-done
  7.7 0.0 copy-done.3
  7.7 0.0 copy-done.4
  7.7 0.0 copy-start.1
  7.7 0.0 copy-start.2
  7.7 0.0 copy-start.5
  7.8 2.8 %shard_map.96 = (f32[8,5,5,16,128]{4,3,2,1,0:T(8,128)S(1)}, f32[8,5,5,16,128]{4,3,2,1,0:T(8,128)S(1)}, f32[20,5,16,128]{3,2,1,0:T(8,128)S(1)}, f32[16,128]{1,0:T...) custom-call(s32[8]{0:T(128)} %depth_hbm.1, s32[8]{0:T(128)} %east_hbm.1, ...), custom_call_target="tpu_custom_call" | custom-call | flops 5000000000 | bytes 5000000 | tf_op jit(solution)/shard_map/pallas_call | solution.py:26
  10.6 0.0 collective-permute-done.2.both_ref
  10.6 0.1 collective-permute-done.1.quarter_ref
  10.7 0.9 %collective-permute-done.half_ref = f32[1,16,128]{2,1,0:T(8,128)S(1)} collective-permute-done((f32[1,16,128]{2,1,0:T(8,128)S(1)}, f32[1,16,128]{2,1,0:T(8,128)S(1)}, u32[]{:S(2)}, u32[]{:S(2)}) %collective-permute-start) | collective-permute-done | bytes 8224 | tf_op jit(solution)/shard_map/ppermute | solution.py:608
  11.6 0.1 shard_map.97
  11.7 0.1 collective-permute-start.3
  11.8 0.1 shard_map.99
  11.8 1.5 %collective-permute-start.4 = (f32[16,128]{1,0:T(8,128)S(1)}, f32[16,128]{1,0:T(8,128)S(1)}, u32[]{:S(2)}, u32[]{:S(2)}) collective-permute-start(f32[16,128]{1,0:T(8,128)S(1)} %get-tuple-element.43), channel_id=1, source_target_pairs={{0,4},{4,0},{8,12},{12,8},{16,20},{20,16},{24,28},{28,24},{1,5},{5... | collective-permute-start | bytes 24584 | tf_op jit(solution)/shard_map/ppermute | solution.py:608
  13.4 0.0 copy-done.1
  13.4 0.0 copy-done.2
  13.4 0.0 copy-done.5
  13.4 0.6 %shard_map.100.s0_ref = f32[8,5,16,128]{3,2,1,0:T(8,128)S(1)} custom-call(f32[16,128]{1,0:T(8,128)S(1)} %get-tuple-element.42.tiles_ref.mine_ref, f32[16,128]{1,0:T(8,128)S(1)} %get-tuple-element.34.live_ref, f32[8,5,16,128]{3,2,1,0:T(8,128)S(1)} %bitcast.15, f32[8,5,16,128]{3,2,1,0:T(8,128)S(1)} %bitcast.22, f32[8,5,5,16,128]{4,3,2,1,0:T(8,128)S(1)} %bitcast.12, ...), custom_call_target="tpu_custom_call" | custom-call | flops 2000000000 | bytes 2000000 | tf_op jit(solution)/shard_map/pallas_call | solution.py:26
  14.0 0.1 collective-permute-done.3.other_ref.mats_other_ref
  14.2 1.4 %collective-permute-start.5 = (f32[7,5,8,128]{3,2,1,0:T(8,128)S(1)}, f32[7,5,8,128]{3,2,1,0:T(8,128)S(1)}, u32[]{:S(2)}, u32[]{:S(2)}) collective-permute-start(f32[7,5,8,128]{3,2,1,0:T(8,128)S(1)} %shard_map.98.half_ref), channel_id=1, source_target_pairs={{0,3},{1,2},{2,1},{3,0},{4,7},{5,6},{6,5},{7,4},{8,11},{9,10},{10,... | collective-permute-start | bytes 430088 | tf_op jit(solution)/shard_map/ppermute | solution.py:586
  15.5 0.0 collective-permute-done.4.got_ref
  15.6 0.4 %shard_map.101 = (f32[8,5,16,128]{3,2,1,0:T(8,128)S(1)}, f32[2,5,16,128]{3,2,1,0:T(8,128)S(1)}, f32[5,16,128]{2,1,0:T(8,128)S(1)}) custom-call(f32[7,5,8,128]{3,2,1,0:T(8,128)S(1)} %shard_map.98.half_ref, f32[21,5,16,128]{3,2,1,0:T(8,128)S(1)} %collective-permute-done.3.other_ref.mats_other_ref, f32[16,128]{1,0:T(8,128)S(1)} %get-tuple-element.34.live_ref, ...), custom_call_target="tpu_custom_call" | custom-call | flops 1000000000 | bytes 1000000 | tf_op jit(solution)/shard_map/pallas_call | solution.py:26
  16.0 0.4 %collective-permute-start.6 = (f32[2,5,16,128]{3,2,1,0:T(8,128)S(1)}, f32[2,5,16,128]{3,2,1,0:T(8,128)S(1)}, u32[]{:S(2)}, u32[]{:S(2)}) collective-permute-start(f32[2,5,16,128]{3,2,1,0:T(8,128)S(1)} %get-tuple-element.47.ends_ref), channel_id=1, source_target_pairs={{0,1},{1,0},{2,3},{3,2},{4,5},{5,4},{6,7},{7,6},{8,9},{9,8},{10,11... | collective-permute-start | bytes 245768 | tf_op jit(solution)/shard_map/ppermute | solution.py:586
  16.4 0.9 %collective-permute-done.6.ends_other_ref = f32[2,5,16,128]{3,2,1,0:T(8,128)S(1)} collective-permute-done((f32[2,5,16,128]{3,2,1,0:T(8,128)S(1)}, f32[2,5,16,128]{3,2,1,0:T(8,128)S(1)}, u32[]{:S(2)}, u32[]{:S(2)}) %collective-permute-start.6) | collective-permute-done | bytes 81952 | tf_op jit(solution)/shard_map/ppermute | solution.py:586
  17.4 1.3 %collective-permute-start.7 = (f32[1,5,16,128]{3,2,1,0:T(8,128)S(1)}, f32[1,5,16,128]{3,2,1,0:T(8,128)S(1)}, u32[]{:S(2)}, u32[]{:S(2)}) collective-permute-start(f32[1,5,16,128]{3,2,1,0:T(8,128)S(1)} %shard_map.102.pair_ref), channel_id=1, source_target_pairs={{0,3},{1,2},{2,1},{3,0},{4,7},{5,6},{6,5},{7,4},{8,11},{9,10},{10,... | collective-permute-start | bytes 122888 | tf_op jit(solution)/shard_map/ppermute | solution.py:586
  18.7 1.3 %collective-permute-done.5.half_ref = f32[7,5,8,128]{3,2,1,0:T(8,128)S(1)} collective-permute-done((f32[7,5,8,128]{3,2,1,0:T(8,128)S(1)}, f32[7,5,8,128]{3,2,1,0:T(8,128)S(1)}, u32[]{:S(2)}, u32[]{:S(2)}) %collective-permute-start.5) | collective-permute-done | bytes 143392 | tf_op jit(solution)/shard_map/ppermute | solution.py:586
  20.0 0.2 collective-permute-start.8
  20.2 0.4 collective-permute-start.9
  20.6 0.1 collective-permute-start.10
  20.7 0.4 collective-permute-start.11
  21.1 0.0 collective-permute-done.7.pair_other_ref
  21.1 0.8 %collective-permute-done.11.rest_3_ = f32[4,8,128]{2,1,0:T(8,128)S(1)} collective-permute-done((f32[4,8,128]{2,1,0:T(8,128)S(1)}, f32[4,8,128]{2,1,0:T(8,128)S(1)}, u32[]{:S(2)}, u32[]{:S(2)}) %collective-permute-start.11) | collective-permute-done | bytes 16416 | tf_op jit(solution)/shard_map/ppermute | solution.py:586
  21.9 0.0 collective-permute-done.8.rest_0_
  21.9 0.0 collective-permute-done.9.rest_1_
  21.9 0.0 collective-permute-done.10.rest_2_
  22.0 0.5 %shard_map.104 = (f32[8,5,16,128]{3,2,1,0:T(8,128)S(1)}, f32[5,16,128]{2,1,0:T(8,128)S(1)}, f32[5,16,128]{2,1,0:T(8,128)S(1)}, f32[8,16,128]{2,1,0:T(8,128)S(1)}) custom-call(f32[16,128]{1,0:T(8,128)S(1)} %get-tuple-element.34.live_ref, f32[8,5,16,128]{3,2,1,0:T(8,128)S(1)} %bitcast.17, f32[5,16,128]{2,1,0:T(8,128)S(1)} %get-tuple-element.46.above_ref, ...), custom_call_target="tpu_custom_call" | custom-call | flops 1000000000 | bytes 1000000 | tf_op jit(solution)/shard_map/pallas_call | solution.py:26
  22.4 11.7 %all_to_all.5.tiles_ref = f32[8,16,128]{2,1,0:T(8,128)S(1)} all-to-all(f32[8,16,128]{2,1,0:T(8,128)S(1)} %get-tuple-element.56), channel_id=1, replica_groups=mesh['zone'=8,'ja'=4] {'zone'}, dimensions={0} | all-to-all | bytes 131072 | tf_op jit(solution)/shard_map/all_to_all | solution.py:647
  34.1 0.9 %shard_map.105 = (f32[8,5,16,128]{3,2,1,0:T(8,128)S(1)}, f32[8,5,16,128]{3,2,1,0:T(8,128)S(1)}, f32[3,5,16,128]{3,2,1,0:T(8,128)S(1)}) custom-call(f32[16,128]{1,0:T(8,128)S(1)} %get-tuple-element.34.live_ref, f32[2,8,16,128]{3,2,1,0:T(8,128)S(1)} %get-tuple-element.40.pick_ref, f32[8,16,128]{2,1,0:T(8,128)S(1)} %all_to_all.5.tiles_ref, ...), custom_call_target="tpu_custom_call" | custom-call | flops 1000000000 | bytes 1000000 | tf_op jit(solution)/shard_map/pallas_call | solution.py:26
  35.0 0.1 collective-permute-start.12
  35.1 1.3 %collective-permute-done.12.ends_other_ref = f32[3,5,16,128]{3,2,1,0:T(8,128)S(1)} collective-permute-done((f32[3,5,16,128]{3,2,1,0:T(8,128)S(1)}, f32[3,5,16,128]{3,2,1,0:T(8,128)S(1)}, u32[]{:S(2)}, u32[]{:S(2)}) %collective-permute-start.12) | collective-permute-done | bytes 122912 | tf_op jit(solution)/shard_map/ppermute | solution.py:586
  36.4 1.4 %collective-permute-start.13 = (f32[1,5,16,128]{3,2,1,0:T(8,128)S(1)}, f32[1,5,16,128]{3,2,1,0:T(8,128)S(1)}, u32[]{:S(2)}, u32[]{:S(2)}) collective-permute-start(f32[1,5,16,128]{3,2,1,0:T(8,128)S(1)} %shard_map.107.pair_ref), channel_id=1, source_target_pairs={{0,3},{1,2},{2,1},{3,0},{4,7},{5,6},{6,5},{7,4},{8,11},{9,10},{10,... | collective-permute-start | bytes 122888 | tf_op jit(solution)/shard_map/ppermute | solution.py:586
  37.8 1.0 %shard_map.106 = (f32[8,5,16,128]{3,2,1,0:T(8,128)}, f32[16,128]{1,0:T(8,128)S(1)}) custom-call(f32[16,128]{1,0:T(8,128)S(1)} %get-tuple-element.34.live_ref, f32[5,16,128]{2,1,0:T(8,128)S(1)} %get-tuple-element.55.below_ref, f32[3,5,16,128]{3,2,1,0:T(8,128)S(1)} %collective-permute-done.12.ends_other_ref, f32[8,5,16,128]{3,2,1,0:T(8,128)S(1)} %get-tuple-element.57.cur_ref, ...), custom_call_target="tpu_custom_call" | custom-call | flops 1000000000 | bytes 1000000 | tf_op jit(solution)/shard_map/pallas_call | solution.py:26
  38.8 1.2 %collective-permute-done.13.pair_other_ref = f32[1,5,16,128]{3,2,1,0:T(8,128)S(1)} collective-permute-done((f32[1,5,16,128]{3,2,1,0:T(8,128)S(1)}, f32[1,5,16,128]{3,2,1,0:T(8,128)S(1)}, u32[]{:S(2)}, u32[]{:S(2)}) %collective-permute-start.13) | collective-permute-done | bytes 40992 | tf_op jit(solution)/shard_map/ppermute | solution.py:586
  40.0 1.0 %shard_map.108 = f32[8,5,16,128]{3,2,1,0:T(8,128)} custom-call(f32[16,128]{1,0:T(8,128)S(1)} %get-tuple-element.61.done_ref, f32[8,5,16,128]{3,2,1,0:T(8,128)S(1)} %get-tuple-element.57.cur_ref, f32[8,5,16,128]{3,2,1,0:T(8,128)S(1)} %get-tuple-element.62.s_ref, f32[8,5,5,16,128]{4,3,2,1,0:T(8,128)S(1)} %get-tuple-element.44.e_ref, ...), custom_call_target="tpu_custom_call" | custom-call | flops 1000000000 | bytes 1000000 | tf_op jit(solution)/shard_map/pallas_call | solution.py:26
  (4 shorter events, 0.1 us)
Async XLA Ops:
  0.6 7.1 %copy-start = (f32[1,8,5,5,16,128]{5,4,3,2,1,0:T(8,128)S(1)}, f32[1,8,5,5,16,128]{5,4,3,2,1,0:T(8,128)}, u32[]{:S(2)}) copy-start(f32[1,8,5,5,16,128]{5,4,3,2,1,0:T(8,128)} %param.13) | copy-start | bytes 4915204
  0.6 7.1 %copy-start.3 = (f32[1,8,5,5,16,128]{5,4,3,2,1,0:T(8,128)S(1)}, f32[1,8,5,5,16,128]{5,4,3,2,1,0:T(8,128)}, u32[]{:S(2)}) copy-start(f32[1,8,5,5,16,128]{5,4,3,2,1,0:T(8,128)} %param.11) | copy-start | bytes 4915204
  0.7 7.1 %copy-start.4 = (f32[1,8,5,5,16,128]{5,4,3,2,1,0:T(8,128)S(1)}, f32[1,8,5,5,16,128]{5,4,3,2,1,0:T(8,128)}, u32[]{:S(2)}) copy-start(f32[1,8,5,5,16,128]{5,4,3,2,1,0:T(8,128)} %param.12) | copy-start | bytes 4915204
  2.0 8.6 %collective-permute-start.2 = (f32[1,16,128]{2,1,0:T(8,128)S(1)}, f32[1,16,128]{2,1,0:T(8,128)S(1)}, u32[]{:S(2)}, u32[]{:S(2)}) collective-permute-start(f32[1,16,128]{2,1,0:T(8,128)S(1)} %get-tuple-element.33.tile_ref.own_ref), channel_id=1, source_target_pairs={{0,24},{4,28},{8,16},{12,20},{16,8},{20,12},{24,0},{28,4},{1,25},{... | collective-permute-start | bytes 24584 | tf_op jit(solution)/shard_map/ppermute | solution.py:608
  7.1 3.7 %collective-permute-start.1 = (f32[1,16,128]{2,1,0:T(8,128)S(1)}, f32[1,16,128]{2,1,0:T(8,128)S(1)}, u32[]{:S(2)}, u32[]{:S(2)}) collective-permute-start(f32[1,16,128]{2,1,0:T(8,128)S(1)} %get-tuple-element.33.tile_ref.own_ref), channel_id=1, source_target_pairs={{0,8},{4,12},{8,0},{12,4},{16,24},{20,28},{24,16},{28,20},{1,9},{5... | collective-permute-start | bytes 24584 | tf_op jit(solution)/shard_map/ppermute | solution.py:608
  7.1 4.5 %collective-permute-start = (f32[1,16,128]{2,1,0:T(8,128)S(1)}, f32[1,16,128]{2,1,0:T(8,128)S(1)}, u32[]{:S(2)}, u32[]{:S(2)}) collective-permute-start(f32[1,16,128]{2,1,0:T(8,128)S(1)} %get-tuple-element.33.tile_ref.own_ref), channel_id=1, source_target_pairs={{0,16},{4,20},{8,24},{12,28},{16,0},{20,4},{24,8},{28,12},{1,17},{... | collective-permute-start | bytes 24584 | tf_op jit(solution)/shard_map/ppermute | solution.py:608
  7.7 5.7 %copy-start.1 = (f32[1,8,5,5,16,128]{5,4,3,2,1,0:T(8,128)S(1)}, f32[1,8,5,5,16,128]{5,4,3,2,1,0:T(8,128)}, u32[]{:S(2)}) copy-start(f32[1,8,5,5,16,128]{5,4,3,2,1,0:T(8,128)} %param.10) | copy-start | bytes 4915204
  7.7 5.7 %copy-start.2 = (f32[1,8,5,16,128]{4,3,2,1,0:T(8,128)S(1)}, f32[1,8,5,16,128]{4,3,2,1,0:T(8,128)}, u32[]{:S(2)}) copy-start(f32[1,8,5,16,128]{4,3,2,1,0:T(8,128)} %param.8) | copy-start | bytes 983044
  7.7 5.6 %copy-start.5 = (f32[1,8,5,16,128]{4,3,2,1,0:T(8,128)S(1)}, f32[1,8,5,16,128]{4,3,2,1,0:T(8,128)}, u32[]{:S(2)}) copy-start(f32[1,8,5,16,128]{4,3,2,1,0:T(8,128)} %param.9) | copy-start | bytes 983044
  11.7 2.5 %collective-permute-start.3 = (f32[21,5,16,128]{3,2,1,0:T(8,128)S(1)}, f32[21,5,16,128]{3,2,1,0:T(8,128)S(1)}, u32[]{:S(2)}, u32[]{:S(2)}) collective-permute-start(f32[21,5,16,128]{3,2,1,0:T(8,128)S(1)} %get-tuple-element.37.mine_ref.mats_ref), channel_id=1, source_target_pairs={{0,1},{1,0},{2,3},{3,2},{4,5},{5,4},{6,7},{7,6},{8,9},{9,8},{10,11... | collective-permute-start | bytes 2580488 | tf_op jit(solution)/shard_map/ppermute | solution.py:586
  11.8 3.7 %collective-permute-start.4 = (f32[16,128]{1,0:T(8,128)S(1)}, f32[16,128]{1,0:T(8,128)S(1)}, u32[]{:S(2)}, u32[]{:S(2)}) collective-permute-start(f32[16,128]{1,0:T(8,128)S(1)} %get-tuple-element.43), channel_id=1, source_target_pairs={{0,4},{4,0},{8,12},{12,8},{16,20},{20,16},{24,28},{28,24},{1,5},{5... | collective-permute-start | bytes 24584 | tf_op jit(solution)/shard_map/ppermute | solution.py:608
  14.2 5.8 %collective-permute-start.5 = (f32[7,5,8,128]{3,2,1,0:T(8,128)S(1)}, f32[7,5,8,128]{3,2,1,0:T(8,128)S(1)}, u32[]{:S(2)}, u32[]{:S(2)}) collective-permute-start(f32[7,5,8,128]{3,2,1,0:T(8,128)S(1)} %shard_map.98.half_ref), channel_id=1, source_target_pairs={{0,3},{1,2},{2,1},{3,0},{4,7},{5,6},{6,5},{7,4},{8,11},{9,10},{10,... | collective-permute-start | bytes 430088 | tf_op jit(solution)/shard_map/ppermute | solution.py:586
  16.0 1.4 %collective-permute-start.6 = (f32[2,5,16,128]{3,2,1,0:T(8,128)S(1)}, f32[2,5,16,128]{3,2,1,0:T(8,128)S(1)}, u32[]{:S(2)}, u32[]{:S(2)}) collective-permute-start(f32[2,5,16,128]{3,2,1,0:T(8,128)S(1)} %get-tuple-element.47.ends_ref), channel_id=1, source_target_pairs={{0,1},{1,0},{2,3},{3,2},{4,5},{5,4},{6,7},{7,6},{8,9},{9,8},{10,11... | collective-permute-start | bytes 245768 | tf_op jit(solution)/shard_map/ppermute | solution.py:586
  17.4 3.7 %collective-permute-start.7 = (f32[1,5,16,128]{3,2,1,0:T(8,128)S(1)}, f32[1,5,16,128]{3,2,1,0:T(8,128)S(1)}, u32[]{:S(2)}, u32[]{:S(2)}) collective-permute-start(f32[1,5,16,128]{3,2,1,0:T(8,128)S(1)} %shard_map.102.pair_ref), channel_id=1, source_target_pairs={{0,3},{1,2},{2,1},{3,0},{4,7},{5,6},{6,5},{7,4},{8,11},{9,10},{10,... | collective-permute-start | bytes 122888 | tf_op jit(solution)/shard_map/ppermute | solution.py:586
  20.0 1.9 %collective-permute-start.8 = (f32[7,8,128]{2,1,0:T(8,128)S(1)}, f32[7,8,128]{2,1,0:T(8,128)S(1)}, u32[]{:S(2)}, u32[]{:S(2)}) collective-permute-start(f32[7,8,128]{2,1,0:T(8,128)S(1)} %get-tuple-element.51), channel_id=1, source_target_pairs={{0,1},{1,0},{2,3},{3,2},{4,5},{5,4},{6,7},{7,6},{8,9},{9,8},{10,11... | collective-permute-start | bytes 86024 | tf_op jit(solution)/shard_map/ppermute | solution.py:586
  20.2 1.7 %collective-permute-start.9 = (f32[7,8,128]{2,1,0:T(8,128)S(1)}, f32[7,8,128]{2,1,0:T(8,128)S(1)}, u32[]{:S(2)}, u32[]{:S(2)}) collective-permute-start(f32[7,8,128]{2,1,0:T(8,128)S(1)} %get-tuple-element.52), channel_id=1, source_target_pairs={{0,1},{1,0},{2,3},{3,2},{4,5},{5,4},{6,7},{7,6},{8,9},{9,8},{10,11... | collective-permute-start | bytes 86024 | tf_op jit(solution)/shard_map/ppermute | solution.py:586
  20.6 1.4 %collective-permute-start.10 = (f32[7,8,128]{2,1,0:T(8,128)S(1)}, f32[7,8,128]{2,1,0:T(8,128)S(1)}, u32[]{:S(2)}, u32[]{:S(2)}) collective-permute-start(f32[7,8,128]{2,1,0:T(8,128)S(1)} %get-tuple-element.53), channel_id=1, source_target_pairs={{0,1},{1,0},{2,3},{3,2},{4,5},{5,4},{6,7},{7,6},{8,9},{9,8},{10,11... | collective-permute-start | bytes 86024 | tf_op jit(solution)/shard_map/ppermute | solution.py:586
  20.7 1.2 %collective-permute-start.11 = (f32[4,8,128]{2,1,0:T(8,128)S(1)}, f32[4,8,128]{2,1,0:T(8,128)S(1)}, u32[]{:S(2)}, u32[]{:S(2)}) collective-permute-start(f32[4,8,128]{2,1,0:T(8,128)S(1)} %get-tuple-element.54), channel_id=1, source_target_pairs={{0,1},{1,0},{2,3},{3,2},{4,5},{5,4},{6,7},{7,6},{8,9},{9,8},{10,11... | collective-permute-start | bytes 49160 | tf_op jit(solution)/shard_map/ppermute | solution.py:586
  35.0 1.4 %collective-permute-start.12 = (f32[3,5,16,128]{3,2,1,0:T(8,128)S(1)}, f32[3,5,16,128]{3,2,1,0:T(8,128)S(1)}, u32[]{:S(2)}, u32[]{:S(2)}) collective-permute-start(f32[3,5,16,128]{3,2,1,0:T(8,128)S(1)} %get-tuple-element.59.ends_ref), channel_id=1, source_target_pairs={{0,1},{1,0},{2,3},{3,2},{4,5},{5,4},{6,7},{7,6},{8,9},{9,8},{10,11... | collective-permute-start | bytes 368648 | tf_op jit(solution)/shard_map/ppermute | solution.py:586
  36.4 3.6 %collective-permute-start.13 = (f32[1,5,16,128]{3,2,1,0:T(8,128)S(1)}, f32[1,5,16,128]{3,2,1,0:T(8,128)S(1)}, u32[]{:S(2)}, u32[]{:S(2)}) collective-permute-start(f32[1,5,16,128]{3,2,1,0:T(8,128)S(1)} %shard_map.107.pair_ref), channel_id=1, source_target_pairs={{0,3},{1,2},{2,1},{3,0},{4,7},{5,6},{6,5},{7,4},{8,11},{9,10},{10,... | collective-permute-start | bytes 122888 | tf_op jit(solution)/shard_map/ppermute | solution.py:586

commit v17 on v16

--- a/solution.py
+++ b/solution.py
@@ -7,7 +7,7 @@
 
 ITERS = 2
 OMEGA = 1.2
-PART = 7
+PART = 10
 COUPLE = 0.25
 
 VMEM = pl.BlockSpec(memory_space=pltpu.VMEM)
@@ -130,13 +130,15 @@
 
 
 def relay_kernel(
-    own_ref, half_ref, quarter_ref, both_ref, mats_ref, first_ref, mats_out_ref, out_ref
+    own_ref, half_ref, quarter_ref, both_ref, mats_ref, first_ref, last_ref,
+    mats_out_ref, out_ref,
 ):
     for i, ref in enumerate((own_ref, half_ref, quarter_ref, both_ref)):
         out_ref[i] = ref[0]
     for i in range(20):
         put(mats_out_ref, cell(mats_ref, i), i)
     put(mats_out_ref, cell(first_ref), 20)
+    put(mats_out_ref, cell(last_ref), 21)
 
 
 def neighbours(x):
@@ -272,21 +274,17 @@
         run(*other_refs, *mine_refs)
 
 
-def half_kernel(mine_ref, other_ref, last_ref, half_ref):
+def half_kernel(mine_ref, other_ref, half_ref):
     ja = lax.axis_index("ja")
-    low_pair = ja < 2
-    for side in range(2):
-        first = [jnp.where(ja == 3, other_ref[20, v], mine_ref[20, v]) for v in range(5)]
-        edge = [jnp.where(low_pair, last_ref[v], first[v]) for v in range(5)]
-        put(half_ref, [x[8 * side : 8 * side + 8] for x in edge], 5 + side)
     for side in range(2):
         lo, hi = (mine_ref, other_ref) if side == 0 else (other_ref, mine_ref)
         rows = HALVES[side]
 
-        @pl.when((ja % 2 == side) & low_pair)
+        @pl.when((ja % 2 == side) & (ja < 2))
         def _():
             for r in range(5):
                 put(half_ref, [hi[15 + r, c, rows] for c in range(5)], r)
+            put(half_ref, [hi[21, v, rows] for v in range(5)], 5)
 
         @pl.when((ja % 2 == side) & (ja >= 2))
         def _():
@@ -297,6 +295,7 @@
                 out = add(mat_col(lo, q, 1, rows), out)
                 for r in range(5):
                     half_ref[r, q] = out[r]
+            put(half_ref, [lo[20, v, rows] for v in range(5)], 5)
 
 
 def sweeps(s_ref, e_ref, f_ref, y_ref, ends_ref, last):
@@ -440,15 +439,13 @@
     by_place([ends_ref, mats_ref], [ends_other_ref, mats_other_ref], run)
 
 
-def parts_kernel(live_ref, half_ref, pair_ref, beyond_ref, half_out_ref, *part_refs):
+def parts_kernel(half_ref, pair_ref, half_out_ref, *part_refs):
     del pair_ref
-    for r in range(5):
+    for r in range(6):
         put(half_out_ref, cell(half_ref, r), r)
         for c in range(5):
             part, place = divmod(5 * r + c, PART)
             part_refs[part][place] = half_ref[r, c]
-    beyond = [jnp.concatenate([half_ref[5, v], half_ref[6, v]], axis=0) for v in range(5)]
-    put(beyond_ref, masked(live_ref, beyond))
 
 
 def join(mine_ref, other_refs, r, c):
@@ -460,7 +457,7 @@
 
 def inflows(
     ends_ref, ends_other_ref, mats_ref, mats_other_ref, pair_ref, pair_other_ref,
-    half_ref, half_other_refs, inflow_ref, live_ref=None, beyond_ref=None,
+    half_ref, half_other_refs, inflow_ref, live_ref=None, beyond=None,
 ):
     ja = lax.axis_index("ja")
     zeros = [jnp.zeros((16, 128), jnp.float32)] * 5
@@ -469,17 +466,17 @@
         return [[join(half_ref, half_other_refs, r, c) for c in range(5)] for r in range(5)]
 
     def passed(value, coupling, first):
-        if beyond_ref is None:
+        if beyond is None:
             return value
         return add(value, [x * (1.0 / OMEGA) for x in matvec(coupling, first)])
 
     def far(mats_hi_ref):
-        first = None if beyond_ref is None else cell(beyond_ref)
+        first = beyond
         a = passed(cell(pair_ref, 0), matrix_of(mats_hi_ref, 3), first)
         return add(cell(pair_other_ref, 0), matvec(joined(), a))
 
     def near(mats_lo_ref):
-        first = None if beyond_ref is None else masked(live_ref, cell(mats_lo_ref, 20))
+        first = None if beyond is None else masked(live_ref, cell(mats_lo_ref, 20))
         return passed(cell(pair_other_ref, 0), joined(), first)
 
     @pl.when(ja == 0)
@@ -511,23 +508,24 @@
 
 
 def final_kernel(
-    live_ref, cur_ref, above_ref, beyond_ref, s_ref, e_ref, f_ref,
+    live_ref, cur_ref, above_ref, s_ref, e_ref, f_ref,
     ends_ref, ends_other_ref, mats_ref, mats_other_ref, pair_ref, pair_other_ref,
     half_ref, *rest,
 ):
-    half_other_refs = rest[:4]
-    new_ref, above_new_ref, below_new_ref, tile_ref, y_ref, inflow_ref = rest[4:]
+    half_other_refs = rest[:3]
+    new_ref, above_new_ref, below_new_ref, tile_ref, y_ref, inflow_ref = rest[3:]
     planes = cur_ref.shape[0]
+    beyond = masked(live_ref, [join(half_ref, half_other_refs, 5, v) for v in range(5)])
     inflows(
         ends_ref, ends_other_ref, mats_ref, mats_other_ref, pair_ref, pair_other_ref,
-        half_ref, half_other_refs, inflow_ref, live_ref, beyond_ref,
+        half_ref, half_other_refs, inflow_ref, live_ref, beyond,
     )
     value = cell(inflow_ref, 0)
     for j in range(planes):
         value = matvec(block(e_ref, j), value, cell(s_ref, j))
         put(y_ref, value, j)
     value = cell(inflow_ref, 1)
-    kept = [x * (1.0 - 1.0 / OMEGA) for x in cell(beyond_ref)]
+    kept = [x * (1.0 - 1.0 / OMEGA) for x in beyond]
     inner = lax.axis_index("ja") == 1
     above = add(cell(above_ref), [jnp.where(inner, x, 0.0) for x in kept])
     put(above_new_ref, add(above, value))
@@ -545,8 +543,8 @@
     ends_ref, ends_other_ref, mats_ref, mats_other_ref, pair_ref, pair_other_ref,
     half_ref, *rest,
 ):
-    half_other_refs = rest[:4]
-    new_hbm, y_ref, inflow_ref, new_ref, sems = rest[4:]
+    half_other_refs = rest[:3]
+    new_hbm, y_ref, inflow_ref, new_ref, sems = rest[3:]
     del done_ref
     planes = cur_ref.shape[0]
     copies = []
@@ -609,8 +607,8 @@
 
     far, near = zones // 2, zones // 4
     gots = [exchange(tile, stride) for stride in (far, near, far + near)]
-    mats, tiles = call(relay_kernel, [(21, *plane), (4, *state[2:])], flops=10**5)(
-        tile, *gots, mats, first
+    mats, tiles = call(relay_kernel, [(22, *plane), (4, *state[2:])], flops=10**5)(
+        tile, *gots, mats, first, final
     )
     stride = zones // 8
     while stride > 1:
@@ -620,7 +618,7 @@
     tiles, theirs = call(select_kernel, [state[2:]] * 2, flops=10**5)(tiles, pick, partner)
     got = exchange(theirs, 1)
     mats_other = swap(mats, 1)
-    half = call(half_kernel, [(7, plane[0], 8, plane[2])], flops=10**5)(mats, mats_other, final)[0]
+    half = call(half_kernel, [(6, plane[0], 8, plane[2])], flops=10**5)(mats, mats_other)[0]
     s0 = call(source_kernel, [state], flops=2 * 10**9)(tiles, live, current, force, diag, inv, e, f)[0]
     s, ends, above = call(local_kernel, [state, (2, *plane), plane], work)(
         half, mats_other, live, tiles, got, current, s0, inv, e, f
@@ -630,17 +628,15 @@
     pair = call(first_mid_kernel, [(1, *plane)], flops=10**5)(
         live, ends, ends_other, mats, mats_other
     )[0]
-    parts_of = [(min(PART, 25 - i), *half.shape[2:]) for i in range(0, 25, PART)]
-    beyond, half, *sent = call(
-        parts_kernel, [plane, (5, *half.shape[1:])] + parts_of, flops=10**5
-    )(live, half, pair)
+    parts_of = [(PART, *half.shape[2:])] * (30 // PART)
+    half, *sent = call(parts_kernel, [half.shape] + parts_of, flops=10**5)(half, pair)
     half_other = [swap(x, 1) for x in sent]
     pair_other = swap(pair, 3)
     flows = [buffer(2, *plane)]
     current, above, below, tile = call(
         final_kernel, [state, plane, plane, (zones, *state[2:])], work + flows
     )(
-        live, current, above, beyond, s, e, f,
+        live, current, above, s, e, f,
         ends, ends_other, mats, mats_other, pair, pair_other, half, *half_other,
     )
 

time: 41.3 us -> 40.7 us (0.985)
  starting transfers between devices: 13 us -> 12.5 us
    ppermute x10 -> x9, starting transfers between devices: 5.68 us -> 5.23 us  [swap(): return lax.ppermute(x, 'ja', [(p, p ^ bit) for p in range(parts)])]
    ppermute x10 -> x9, waiting for transfers between devices: 5.8 us -> 5.8 us  [swap(): return lax.ppermute(x, 'ja', [(p, p ^ bit) for p in range(parts)])]
  transfers between devices with their start and end apart: 14 -> 13, of which waited for: 8 -> 10; matrix products, arithmetic and copies ran while one was open for 0% -> 0% of each run, Pallas kernels for 12% -> 12%
where the time goes in v17:
time: 40.7 us; the launch traced here: 40.5 us
  starting transfers between devices  12.5 us (31%)
  blocking collectives  11.7 us (29%)
  Pallas kernels  8.68 us (21%)
  waiting for transfers between devices  6.8 us (17%)
  between operations  0.79 us (2%)
    all_to_all x1, blocking collectives, per_device(): got = lax.all_to_all(tile, 'zone', 0, 0, tiled=True)  11.7 us
    pallas_call x14, Pallas kernels, run(): pl.pallas_call(kernel, out_shape=[jax.ShapeDtypeStruct(s, jnp.float32) fo...  8.68 us
    ppermute x4, starting transfers between devices, exchange(): return lax.ppermute(x, 'zone', [(z, z ^ stride) for z in range(zones)])  7.29 us
    ppermute x9, waiting for transfers between devices, swap(): return lax.ppermute(x, 'ja', [(p, p ^ bit) for p in range(parts)])  5.8 us
    ppermute x9, starting transfers between devices, swap(): return lax.ppermute(x, 'ja', [(p, p ^ bit) for p in range(parts)])  5.23 us
    ppermute x4, waiting for transfers between devices, exchange(): return lax.ppermute(x, 'zone', [(z, z ^ stride) for z in range(zones)])  1.01 us
  transfers between devices with their start and end apart: 13, of which 10 were waited for; matrix products, arithmetic and copies ran while one was open for 0% of the time, Pallas kernels for 12%

profile of v17, /device:TPU:0, one launch (start us, length us, event | category | flops | bytes accessed | tf_op | source)
XLA Modules:
  0.0 40.5 jit_solution(8525139358557680732)
XLA Ops:
  0.6 0.0 copy-start
  0.6 0.0 copy-start.3
  0.7 0.0 copy-start.4
  0.7 1.3 %shard_map.95 = (f32[1,16,128]{2,1,0:T(8,128)S(1)}, f32[5,16,128]{2,1,0:T(8,128)S(1)}, f32[5,16,128]{2,1,0:T(8,128)S(1)}) custom-call(f32[8,5,16,128]{3,2,1,0:T(8,128)} %bitcast.14), custom_call_target="tpu_custom_call" | custom-call | flops 10000000000 | bytes 10000000 | tf_op jit(solution)/shard_map/pallas_call | solution.py:26
  2.0 5.1 %collective-permute-start.2 = (f32[1,16,128]{2,1,0:T(8,128)S(1)}, f32[1,16,128]{2,1,0:T(8,128)S(1)}, u32[]{:S(2)}, u32[]{:S(2)}) collective-permute-start(f32[1,16,128]{2,1,0:T(8,128)S(1)} %get-tuple-element.31.tile_ref.own_ref), channel_id=1, source_target_pairs={{0,24},{4,28},{8,16},{12,20},{16,8},{20,12},{24,0},{28,4},{1,25},{... | collective-permute-start | bytes 24584 | tf_op jit(solution)/shard_map/ppermute | solution.py:606
  7.1 0.0 collective-permute-start.1
  7.1 0.6 %collective-permute-start = (f32[1,16,128]{2,1,0:T(8,128)S(1)}, f32[1,16,128]{2,1,0:T(8,128)S(1)}, u32[]{:S(2)}, u32[]{:S(2)}) collective-permute-start(f32[1,16,128]{2,1,0:T(8,128)S(1)} %get-tuple-element.31.tile_ref.own_ref), channel_id=1, source_target_pairs={{0,16},{4,20},{8,24},{12,28},{16,0},{20,4},{24,8},{28,12},{1,17},{... | collective-permute-start | bytes 24584 | tf_op jit(solution)/shard_map/ppermute | solution.py:606
  7.7 0.0 copy-done
  7.7 0.0 copy-done.3
  7.7 0.0 copy-done.4
  7.7 0.0 copy-start.1
  7.7 0.0 copy-start.2
  7.7 0.0 copy-start.5
  7.8 2.9 %shard_map.96 = (f32[8,5,5,16,128]{4,3,2,1,0:T(8,128)S(1)}, f32[8,5,5,16,128]{4,3,2,1,0:T(8,128)S(1)}, f32[20,5,16,128]{3,2,1,0:T(8,128)S(1)}, f32[16,128]{1,0:T...) custom-call(s32[8]{0:T(128)} %depth_hbm.1, s32[8]{0:T(128)} %east_hbm.1, ...), custom_call_target="tpu_custom_call" | custom-call | flops 5000000000 | bytes 5000000 | tf_op jit(solution)/shard_map/pallas_call | solution.py:26
  10.6 0.0 collective-permute-done.2.both_ref
  10.6 0.1 collective-permute-done.1.quarter_ref
  10.7 0.9 %collective-permute-done.half_ref = f32[1,16,128]{2,1,0:T(8,128)S(1)} collective-permute-done((f32[1,16,128]{2,1,0:T(8,128)S(1)}, f32[1,16,128]{2,1,0:T(8,128)S(1)}, u32[]{:S(2)}, u32[]{:S(2)}) %collective-permute-start) | collective-permute-done | bytes 8224 | tf_op jit(solution)/shard_map/ppermute | solution.py:606
  11.6 0.1 shard_map.97
  11.7 0.1 collective-permute-start.3
  11.8 0.1 shard_map.99
  11.8 1.5 %collective-permute-start.4 = (f32[16,128]{1,0:T(8,128)S(1)}, f32[16,128]{1,0:T(8,128)S(1)}, u32[]{:S(2)}, u32[]{:S(2)}) collective-permute-start(f32[16,128]{1,0:T(8,128)S(1)} %get-tuple-element.41), channel_id=1, source_target_pairs={{0,4},{4,0},{8,12},{12,8},{16,20},{20,16},{24,28},{28,24},{1,5},{5... | collective-permute-start | bytes 24584 | tf_op jit(solution)/shard_map/ppermute | solution.py:606
  13.4 0.0 copy-done.1
  13.4 0.0 copy-done.2
  13.4 0.0 copy-done.5
  13.4 0.6 %shard_map.100.s0_ref = f32[8,5,16,128]{3,2,1,0:T(8,128)S(1)} custom-call(f32[16,128]{1,0:T(8,128)S(1)} %get-tuple-element.40.tiles_ref.mine_ref, f32[16,128]{1,0:T(8,128)S(1)} %get-tuple-element.32.live_ref, f32[8,5,16,128]{3,2,1,0:T(8,128)S(1)} %bitcast.15, f32[8,5,16,128]{3,2,1,0:T(8,128)S(1)} %bitcast.22, f32[8,5,5,16,128]{4,3,2,1,0:T(8,128)S(1)} %bitcast.12, ...), custom_call_target="tpu_custom_call" | custom-call | flops 2000000000 | bytes 2000000 | tf_op jit(solution)/shard_map/pallas_call | solution.py:26
  14.0 0.2 collective-permute-done.3.other_ref.mats_other_ref
  14.2 1.3 %collective-permute-start.7 = (f32[6,5,8,128]{3,2,1,0:T(8,128)S(1)}, f32[6,5,8,128]{3,2,1,0:T(8,128)S(1)}, u32[]{:S(2)}, u32[]{:S(2)}) collective-permute-start(f32[6,5,8,128]{3,2,1,0:T(8,128)S(1)} %shard_map.98.half_ref), channel_id=1, source_target_pairs={{0,3},{1,2},{2,1},{3,0},{4,7},{5,6},{6,5},{7,4},{8,11},{9,10},{10,... | collective-permute-start | bytes 368648 | tf_op jit(solution)/shard_map/ppermute | solution.py:584
  15.6 0.0 collective-permute-done.4.got_ref
  15.6 0.4 %shard_map.101 = (f32[8,5,16,128]{3,2,1,0:T(8,128)S(1)}, f32[2,5,16,128]{3,2,1,0:T(8,128)S(1)}, f32[5,16,128]{2,1,0:T(8,128)S(1)}) custom-call(f32[6,5,8,128]{3,2,1,0:T(8,128)S(1)} %shard_map.98.half_ref, f32[22,5,16,128]{3,2,1,0:T(8,128)S(1)} %collective-permute-done.3.other_ref.mats_other_ref, f32[16,128]{1,0:T(8,128)S(1)} %get-tuple-element.32.live_ref, ...), custom_call_target="tpu_custom_call" | custom-call | flops 1000000000 | bytes 1000000 | tf_op jit(solution)/shard_map/pallas_call | solution.py:26
  16.0 0.4 %collective-permute-start.5 = (f32[2,5,16,128]{3,2,1,0:T(8,128)S(1)}, f32[2,5,16,128]{3,2,1,0:T(8,128)S(1)}, u32[]{:S(2)}, u32[]{:S(2)}) collective-permute-start(f32[2,5,16,128]{3,2,1,0:T(8,128)S(1)} %get-tuple-element.46.ends_ref), channel_id=1, source_target_pairs={{0,1},{1,0},{2,3},{3,2},{4,5},{5,4},{6,7},{7,6},{8,9},{9,8},{10,11... | collective-permute-start | bytes 245768 | tf_op jit(solution)/shard_map/ppermute | solution.py:584
  16.5 0.9 %collective-permute-done.5.ends_other_ref = f32[2,5,16,128]{3,2,1,0:T(8,128)S(1)} collective-permute-done((f32[2,5,16,128]{3,2,1,0:T(8,128)S(1)}, f32[2,5,16,128]{3,2,1,0:T(8,128)S(1)}, u32[]{:S(2)}, u32[]{:S(2)}) %collective-permute-start.5) | collective-permute-done | bytes 81952 | tf_op jit(solution)/shard_map/ppermute | solution.py:584
  17.4 1.2 %collective-permute-start.6 = (f32[1,5,16,128]{3,2,1,0:T(8,128)S(1)}, f32[1,5,16,128]{3,2,1,0:T(8,128)S(1)}, u32[]{:S(2)}, u32[]{:S(2)}) collective-permute-start(f32[1,5,16,128]{3,2,1,0:T(8,128)S(1)} %shard_map.102.pair_ref), channel_id=1, source_target_pairs={{0,3},{1,2},{2,1},{3,0},{4,7},{5,6},{6,5},{7,4},{8,11},{9,10},{10,... | collective-permute-start | bytes 122888 | tf_op jit(solution)/shard_map/ppermute | solution.py:584
  18.6 1.0 %collective-permute-done.7.half_ref = f32[6,5,8,128]{3,2,1,0:T(8,128)S(1)} collective-permute-done((f32[6,5,8,128]{3,2,1,0:T(8,128)S(1)}, f32[6,5,8,128]{3,2,1,0:T(8,128)S(1)}, u32[]{:S(2)}, u32[]{:S(2)}) %collective-permute-start.7) | collective-permute-done | bytes 122912 | tf_op jit(solution)/shard_map/ppermute | solution.py:584
  19.6 0.2 collective-permute-start.8
  19.8 0.4 collective-permute-start.9
  20.2 0.1 collective-permute-start.10
  20.3 0.6 %collective-permute-done.6.pair_other_ref = f32[1,5,16,128]{3,2,1,0:T(8,128)S(1)} collective-permute-done((f32[1,5,16,128]{3,2,1,0:T(8,128)S(1)}, f32[1,5,16,128]{3,2,1,0:T(8,128)S(1)}, u32[]{:S(2)}, u32[]{:S(2)}) %collective-permute-start.6) | collective-permute-done | bytes 40992 | tf_op jit(solution)/shard_map/ppermute | solution.py:584
  20.9 0.0 collective-permute-done.8.rest_0_
  20.9 0.2 collective-permute-done.9.rest_1_
  21.1 0.3 collective-permute-done.10.rest_2_
  21.4 0.5 %shard_map.104 = (f32[8,5,16,128]{3,2,1,0:T(8,128)S(1)}, f32[5,16,128]{2,1,0:T(8,128)S(1)}, f32[5,16,128]{2,1,0:T(8,128)S(1)}, f32[8,16,128]{2,1,0:T(8,128)S(1)}) custom-call(f32[16,128]{1,0:T(8,128)S(1)} %get-tuple-element.32.live_ref, f32[8,5,16,128]{3,2,1,0:T(8,128)S(1)} %bitcast.17, f32[5,16,128]{2,1,0:T(8,128)S(1)} %get-tuple-element.44.above_ref, ...), custom_call_target="tpu_custom_call" | custom-call | flops 1000000000 | bytes 1000000 | tf_op jit(solution)/shard_map/pallas_call | solution.py:26
  21.9 11.7 %all_to_all.5.tiles_ref = f32[8,16,128]{2,1,0:T(8,128)S(1)} all-to-all(f32[8,16,128]{2,1,0:T(8,128)S(1)} %get-tuple-element.52), channel_id=1, replica_groups=mesh['zone'=8,'ja'=4] {'zone'}, dimensions={0} | all-to-all | bytes 131072 | tf_op jit(solution)/shard_map/all_to_all | solution.py:643
  33.6 0.8 %shard_map.105 = (f32[8,5,16,128]{3,2,1,0:T(8,128)S(1)}, f32[8,5,16,128]{3,2,1,0:T(8,128)S(1)}, f32[3,5,16,128]{3,2,1,0:T(8,128)S(1)}) custom-call(f32[16,128]{1,0:T(8,128)S(1)} %get-tuple-element.32.live_ref, f32[2,8,16,128]{3,2,1,0:T(8,128)S(1)} %get-tuple-element.38.pick_ref, f32[8,16,128]{2,1,0:T(8,128)S(1)} %all_to_all.5.tiles_ref, ...), custom_call_target="tpu_custom_call" | custom-call | flops 1000000000 | bytes 1000000 | tf_op jit(solution)/shard_map/pallas_call | solution.py:26
  34.4 0.1 collective-permute-start.11
  34.5 1.3 %collective-permute-done.11.ends_other_ref = f32[3,5,16,128]{3,2,1,0:T(8,128)S(1)} collective-permute-done((f32[3,5,16,128]{3,2,1,0:T(8,128)S(1)}, f32[3,5,16,128]{3,2,1,0:T(8,128)S(1)}, u32[]{:S(2)}, u32[]{:S(2)}) %collective-permute-start.11) | collective-permute-done | bytes 122912 | tf_op jit(solution)/shard_map/ppermute | solution.py:584
  35.8 1.3 %collective-permute-start.12 = (f32[1,5,16,128]{3,2,1,0:T(8,128)S(1)}, f32[1,5,16,128]{3,2,1,0:T(8,128)S(1)}, u32[]{:S(2)}, u32[]{:S(2)}) collective-permute-start(f32[1,5,16,128]{3,2,1,0:T(8,128)S(1)} %shard_map.107.pair_ref), channel_id=1, source_target_pairs={{0,3},{1,2},{2,1},{3,0},{4,7},{5,6},{6,5},{7,4},{8,11},{9,10},{10,... | collective-permute-start | bytes 122888 | tf_op jit(solution)/shard_map/ppermute | solution.py:584
  37.2 1.0 %shard_map.106 = (f32[8,5,16,128]{3,2,1,0:T(8,128)}, f32[16,128]{1,0:T(8,128)S(1)}) custom-call(f32[16,128]{1,0:T(8,128)S(1)} %get-tuple-element.32.live_ref, f32[5,16,128]{2,1,0:T(8,128)S(1)} %get-tuple-element.51.below_ref, f32[3,5,16,128]{3,2,1,0:T(8,128)S(1)} %collective-permute-done.11.ends_other_ref, f32[8,5,16,128]{3,2,1,0:T(8,128)S(1)} %get-tuple-element.53.cur_ref, ...), custom_call_target="tpu_custom_call" | custom-call | flops 1000000000 | bytes 1000000 | tf_op jit(solution)/shard_map/pallas_call | solution.py:26
  38.2 1.3 %collective-permute-done.12.pair_other_ref = f32[1,5,16,128]{3,2,1,0:T(8,128)S(1)} collective-permute-done((f32[1,5,16,128]{3,2,1,0:T(8,128)S(1)}, f32[1,5,16,128]{3,2,1,0:T(8,128)S(1)}, u32[]{:S(2)}, u32[]{:S(2)}) %collective-permute-start.12) | collective-permute-done | bytes 40992 | tf_op jit(solution)/shard_map/ppermute | solution.py:584
  39.5 1.1 %shard_map.108 = f32[8,5,16,128]{3,2,1,0:T(8,128)} custom-call(f32[16,128]{1,0:T(8,128)S(1)} %get-tuple-element.57.done_ref, f32[8,5,16,128]{3,2,1,0:T(8,128)S(1)} %get-tuple-element.53.cur_ref, f32[8,5,16,128]{3,2,1,0:T(8,128)S(1)} %get-tuple-element.58.s_ref, f32[8,5,5,16,128]{4,3,2,1,0:T(8,128)S(1)} %get-tuple-element.42.e_ref, ...), custom_call_target="tpu_custom_call" | custom-call | flops 1000000000 | bytes 1000000 | tf_op jit(solution)/shard_map/pallas_call | solution.py:26
  (4 shorter events, 0.1 us)
Async XLA Ops:
  0.6 7.1 %copy-start = (f32[1,8,5,5,16,128]{5,4,3,2,1,0:T(8,128)S(1)}, f32[1,8,5,5,16,128]{5,4,3,2,1,0:T(8,128)}, u32[]{:S(2)}) copy-start(f32[1,8,5,5,16,128]{5,4,3,2,1,0:T(8,128)} %param.13) | copy-start | bytes 4915204
  0.6 7.1 %copy-start.3 = (f32[1,8,5,5,16,128]{5,4,3,2,1,0:T(8,128)S(1)}, f32[1,8,5,5,16,128]{5,4,3,2,1,0:T(8,128)}, u32[]{:S(2)}) copy-start(f32[1,8,5,5,16,128]{5,4,3,2,1,0:T(8,128)} %param.11) | copy-start | bytes 4915204
  0.7 7.1 %copy-start.4 = (f32[1,8,5,5,16,128]{5,4,3,2,1,0:T(8,128)S(1)}, f32[1,8,5,5,16,128]{5,4,3,2,1,0:T(8,128)}, u32[]{:S(2)}) copy-start(f32[1,8,5,5,16,128]{5,4,3,2,1,0:T(8,128)} %param.12) | copy-start | bytes 4915204
  2.0 8.7 %collective-permute-start.2 = (f32[1,16,128]{2,1,0:T(8,128)S(1)}, f32[1,16,128]{2,1,0:T(8,128)S(1)}, u32[]{:S(2)}, u32[]{:S(2)}) collective-permute-start(f32[1,16,128]{2,1,0:T(8,128)S(1)} %get-tuple-element.31.tile_ref.own_ref), channel_id=1, source_target_pairs={{0,24},{4,28},{8,16},{12,20},{16,8},{20,12},{24,0},{28,4},{1,25},{... | collective-permute-start | bytes 24584 | tf_op jit(solution)/shard_map/ppermute | solution.py:606
  7.1 3.7 %collective-permute-start.1 = (f32[1,16,128]{2,1,0:T(8,128)S(1)}, f32[1,16,128]{2,1,0:T(8,128)S(1)}, u32[]{:S(2)}, u32[]{:S(2)}) collective-permute-start(f32[1,16,128]{2,1,0:T(8,128)S(1)} %get-tuple-element.31.tile_ref.own_ref), channel_id=1, source_target_pairs={{0,8},{4,12},{8,0},{12,4},{16,24},{20,28},{24,16},{28,20},{1,9},{5... | collective-permute-start | bytes 24584 | tf_op jit(solution)/shard_map/ppermute | solution.py:606
  7.1 4.5 %collective-permute-start = (f32[1,16,128]{2,1,0:T(8,128)S(1)}, f32[1,16,128]{2,1,0:T(8,128)S(1)}, u32[]{:S(2)}, u32[]{:S(2)}) collective-permute-start(f32[1,16,128]{2,1,0:T(8,128)S(1)} %get-tuple-element.31.tile_ref.own_ref), channel_id=1, source_target_pairs={{0,16},{4,20},{8,24},{12,28},{16,0},{20,4},{24,8},{28,12},{1,17},{... | collective-permute-start | bytes 24584 | tf_op jit(solution)/shard_map/ppermute | solution.py:606
  7.7 5.7 %copy-start.1 = (f32[1,8,5,5,16,128]{5,4,3,2,1,0:T(8,128)S(1)}, f32[1,8,5,5,16,128]{5,4,3,2,1,0:T(8,128)}, u32[]{:S(2)}) copy-start(f32[1,8,5,5,16,128]{5,4,3,2,1,0:T(8,128)} %param.10) | copy-start | bytes 4915204
  7.7 5.7 %copy-start.2 = (f32[1,8,5,16,128]{4,3,2,1,0:T(8,128)S(1)}, f32[1,8,5,16,128]{4,3,2,1,0:T(8,128)}, u32[]{:S(2)}) copy-start(f32[1,8,5,16,128]{4,3,2,1,0:T(8,128)} %param.8) | copy-start | bytes 983044
  7.7 5.7 %copy-start.5 = (f32[1,8,5,16,128]{4,3,2,1,0:T(8,128)S(1)}, f32[1,8,5,16,128]{4,3,2,1,0:T(8,128)}, u32[]{:S(2)}) copy-start(f32[1,8,5,16,128]{4,3,2,1,0:T(8,128)} %param.9) | copy-start | bytes 983044
  11.7 2.5 %collective-permute-start.3 = (f32[22,5,16,128]{3,2,1,0:T(8,128)S(1)}, f32[22,5,16,128]{3,2,1,0:T(8,128)S(1)}, u32[]{:S(2)}, u32[]{:S(2)}) collective-permute-start(f32[22,5,16,128]{3,2,1,0:T(8,128)S(1)} %get-tuple-element.36.mine_ref.mats_ref), channel_id=1, source_target_pairs={{0,1},{1,0},{2,3},{3,2},{4,5},{5,4},{6,7},{7,6},{8,9},{9,8},{10,11... | collective-permute-start | bytes 2703368 | tf_op jit(solution)/shard_map/ppermute | solution.py:584
  11.8 3.7 %collective-permute-start.4 = (f32[16,128]{1,0:T(8,128)S(1)}, f32[16,128]{1,0:T(8,128)S(1)}, u32[]{:S(2)}, u32[]{:S(2)}) collective-permute-start(f32[16,128]{1,0:T(8,128)S(1)} %get-tuple-element.41), channel_id=1, source_target_pairs={{0,4},{4,0},{8,12},{12,8},{16,20},{20,16},{24,28},{28,24},{1,5},{5... | collective-permute-start | bytes 24584 | tf_op jit(solution)/shard_map/ppermute | solution.py:606
  14.2 5.4 %collective-permute-start.7 = (f32[6,5,8,128]{3,2,1,0:T(8,128)S(1)}, f32[6,5,8,128]{3,2,1,0:T(8,128)S(1)}, u32[]{:S(2)}, u32[]{:S(2)}) collective-permute-start(f32[6,5,8,128]{3,2,1,0:T(8,128)S(1)} %shard_map.98.half_ref), channel_id=1, source_target_pairs={{0,3},{1,2},{2,1},{3,0},{4,7},{5,6},{6,5},{7,4},{8,11},{9,10},{10,... | collective-permute-start | bytes 368648 | tf_op jit(solution)/shard_map/ppermute | solution.py:584
  16.0 1.4 %collective-permute-start.5 = (f32[2,5,16,128]{3,2,1,0:T(8,128)S(1)}, f32[2,5,16,128]{3,2,1,0:T(8,128)S(1)}, u32[]{:S(2)}, u32[]{:S(2)}) collective-permute-start(f32[2,5,16,128]{3,2,1,0:T(8,128)S(1)} %get-tuple-element.46.ends_ref), channel_id=1, source_target_pairs={{0,1},{1,0},{2,3},{3,2},{4,5},{5,4},{6,7},{7,6},{8,9},{9,8},{10,11... | collective-permute-start | bytes 245768 | tf_op jit(solution)/shard_map/ppermute | solution.py:584
  17.4 3.5 %collective-permute-start.6 = (f32[1,5,16,128]{3,2,1,0:T(8,128)S(1)}, f32[1,5,16,128]{3,2,1,0:T(8,128)S(1)}, u32[]{:S(2)}, u32[]{:S(2)}) collective-permute-start(f32[1,5,16,128]{3,2,1,0:T(8,128)S(1)} %shard_map.102.pair_ref), channel_id=1, source_target_pairs={{0,3},{1,2},{2,1},{3,0},{4,7},{5,6},{6,5},{7,4},{8,11},{9,10},{10,... | collective-permute-start | bytes 122888 | tf_op jit(solution)/shard_map/ppermute | solution.py:584
  19.6 1.3 %collective-permute-start.8 = (f32[10,8,128]{2,1,0:T(8,128)S(1)}, f32[10,8,128]{2,1,0:T(8,128)S(1)}, u32[]{:S(2)}, u32[]{:S(2)}) collective-permute-start(f32[10,8,128]{2,1,0:T(8,128)S(1)} %get-tuple-element.48), channel_id=1, source_target_pairs={{0,1},{1,0},{2,3},{3,2},{4,5},{5,4},{6,7},{7,6},{8,9},{9,8},{10,11... | collective-permute-start | bytes 122888 | tf_op jit(solution)/shard_map/ppermute | solution.py:584
  19.8 1.3 %collective-permute-start.9 = (f32[10,8,128]{2,1,0:T(8,128)S(1)}, f32[10,8,128]{2,1,0:T(8,128)S(1)}, u32[]{:S(2)}, u32[]{:S(2)}) collective-permute-start(f32[10,8,128]{2,1,0:T(8,128)S(1)} %get-tuple-element.49), channel_id=1, source_target_pairs={{0,1},{1,0},{2,3},{3,2},{4,5},{5,4},{6,7},{7,6},{8,9},{9,8},{10,11... | collective-permute-start | bytes 122888 | tf_op jit(solution)/shard_map/ppermute | solution.py:584
  20.2 1.2 %collective-permute-start.10 = (f32[10,8,128]{2,1,0:T(8,128)S(1)}, f32[10,8,128]{2,1,0:T(8,128)S(1)}, u32[]{:S(2)}, u32[]{:S(2)}) collective-permute-start(f32[10,8,128]{2,1,0:T(8,128)S(1)} %get-tuple-element.50), channel_id=1, source_target_pairs={{0,1},{1,0},{2,3},{3,2},{4,5},{5,4},{6,7},{7,6},{8,9},{9,8},{10,11... | collective-permute-start | bytes 122888 | tf_op jit(solution)/shard_map/ppermute | solution.py:584
  34.4 1.4 %collective-permute-start.11 = (f32[3,5,16,128]{3,2,1,0:T(8,128)S(1)}, f32[3,5,16,128]{3,2,1,0:T(8,128)S(1)}, u32[]{:S(2)}, u32[]{:S(2)}) collective-permute-start(f32[3,5,16,128]{3,2,1,0:T(8,128)S(1)} %get-tuple-element.55.ends_ref), channel_id=1, source_target_pairs={{0,1},{1,0},{2,3},{3,2},{4,5},{5,4},{6,7},{7,6},{8,9},{9,8},{10,11... | collective-permute-start | bytes 368648 | tf_op jit(solution)/shard_map/ppermute | solution.py:584
  35.8 3.6 %collective-permute-start.12 = (f32[1,5,16,128]{3,2,1,0:T(8,128)S(1)}, f32[1,5,16,128]{3,2,1,0:T(8,128)S(1)}, u32[]{:S(2)}, u32[]{:S(2)}) collective-permute-start(f32[1,5,16,128]{3,2,1,0:T(8,128)S(1)} %shard_map.107.pair_ref), channel_id=1, source_target_pairs={{0,3},{1,2},{2,1},{3,0},{4,7},{5,6},{6,5},{7,4},{8,11},{9,10},{10,... | collective-permute-start | bytes 122888 | tf_op jit(solution)/shard_map/ppermute | solution.py:584

commit v18 on v17

--- a/solution.py
+++ b/solution.py
@@ -99,15 +99,7 @@
     return [jnp.where(live, x, 0.0) for x in values]
 
 
-def pack_kernel(flow_hbm, tile_ref, first_ref, last_ref, flow_ref, sems):
-    copies = [
-        pltpu.make_async_copy(flow_hbm.at[j], flow_ref.at[j], sems.at[j])
-        for j in range(flow_ref.shape[0])
-    ]
-    for copy in copies:
-        copy.start()
-    for copy in copies:
-        copy.wait()
+def pack_kernel(flow_ref, tile_ref, first_ref, last_ref):
     put(first_ref, cell(flow_ref, 0))
     put(last_ref, cell(flow_ref, flow_ref.shape[0] - 1))
     pack_faces(lambda j, v: flow_ref[j, v], flow_ref.shape[0], tile_ref)
@@ -584,11 +576,7 @@
         return lax.ppermute(x, "ja", [(p, p ^ bit) for p in range(parts)])
 
     tile, first, final = call(
-        pack_kernel,
-        [(1, *state[2:]), plane, plane],
-        work + [pltpu.SemaphoreType.DMA((planes,))],
-        flops=10**10,
-        far=(0,),
+        pack_kernel, [(1, *state[2:]), plane, plane], flops=10**10
     )(current)
     e, f, mats, live, pick, partner = call(
         matrix_kernel,

time: 40.7 us -> 40.5 us (level)
  Pallas kernels: 8.68 us -> 7.53 us
  local copies, waits for them, and re-layouts: 0.03 us -> 1 us
    pallas_call x14, Pallas kernels: 8.68 us -> 7.53 us  [run(): pl.pallas_call(kernel, out_shape=[jax.ShapeDtypeStruct(s, jnp.float32) fo...]
    unnamed x12 -> x14, local copies, waits for them, and re-layouts: 0.03 us -> 1 us
where the time goes in v18:
time: 40.5 us; the launch traced here: 40.3 us
  starting transfers between devices  12.5 us (31%)
  blocking collectives  11.7 us (29%)
  Pallas kernels  7.53 us (19%)
  waiting for transfers between devices  6.8 us (17%)
  local copies, waits for them, and re-layouts  1 us (2%)
  between operations  0.77 us (2%)
    all_to_all x1, blocking collectives, per_device(): got = lax.all_to_all(tile, 'zone', 0, 0, tiled=True)  11.7 us
    pallas_call x14, Pallas kernels, run(): pl.pallas_call(kernel, out_shape=[jax.ShapeDtypeStruct(s, jnp.float32) fo...  7.53 us
    ppermute x4, starting transfers between devices, exchange(): return lax.ppermute(x, 'zone', [(z, z ^ stride) for z in range(zones)])  7.29 us
    ppermute x9, waiting for transfers between devices, swap(): return lax.ppermute(x, 'ja', [(p, p ^ bit) for p in range(parts)])  5.8 us
    ppermute x9, starting transfers between devices, swap(): return lax.ppermute(x, 'ja', [(p, p ^ bit) for p in range(parts)])  5.23 us
    ppermute x4, waiting for transfers between devices, exchange(): return lax.ppermute(x, 'zone', [(z, z ^ stride) for z in range(zones)])  1.01 us
    unnamed x14, local copies, waits for them, and re-layouts  1 us
  transfers between devices with their start and end apart: 13, of which 10 were waited for; matrix products, arithmetic and copies ran while one was open for 0% of the time, Pallas kernels for 12%

profile of v18, /device:TPU:0, one launch (start us, length us, event | category | flops | bytes accessed | tf_op | source)
XLA Modules:
  0.0 40.3 jit_solution(17606486965109492305)
XLA Ops:
  0.6 0.0 copy-start.2
  0.6 1.0 %copy-done.2 = f32[1,8,5,16,128]{4,3,2,1,0:T(8,128)S(1)} copy-done((f32[1,8,5,16,128]{4,3,2,1,0:T(8,128)S(1)}, f32[1,8,5,16,128]{4,3,2,1,0:T(8,128)}, u32[]{:S(2)}) %copy-start.2) | copy-done | bytes 327704
  1.6 0.0 copy-start
  1.6 0.0 copy-start.4
  1.6 0.0 copy-start.5
  1.6 0.1 shard_map.95
  1.8 5.1 %collective-permute-start.2 = (f32[1,16,128]{2,1,0:T(8,128)S(1)}, f32[1,16,128]{2,1,0:T(8,128)S(1)}, u32[]{:S(2)}, u32[]{:S(2)}) collective-permute-start(f32[1,16,128]{2,1,0:T(8,128)S(1)} %get-tuple-element.31.tile_ref.own_ref), channel_id=1, source_target_pairs={{0,24},{4,28},{8,16},{12,20},{16,8},{20,12},{24,0},{28,4},{1,25},{... | collective-permute-start | bytes 24584 | tf_op jit(solution)/shard_map/ppermute | solution.py:594
  6.9 0.0 collective-permute-start.1
  6.9 0.6 %collective-permute-start = (f32[1,16,128]{2,1,0:T(8,128)S(1)}, f32[1,16,128]{2,1,0:T(8,128)S(1)}, u32[]{:S(2)}, u32[]{:S(2)}) collective-permute-start(f32[1,16,128]{2,1,0:T(8,128)S(1)} %get-tuple-element.31.tile_ref.own_ref), channel_id=1, source_target_pairs={{0,16},{4,20},{8,24},{12,28},{16,0},{20,4},{24,8},{28,12},{1,17},{... | collective-permute-start | bytes 24584 | tf_op jit(solution)/shard_map/ppermute | solution.py:594
  7.5 0.0 copy-done
  7.5 0.0 copy-done.4
  7.5 0.0 copy-done.5
  7.5 0.0 copy-start.1
  7.5 0.0 copy-start.3
  7.5 0.0 copy-start.6
  7.6 2.9 %shard_map.96 = (f32[8,5,5,16,128]{4,3,2,1,0:T(8,128)S(1)}, f32[8,5,5,16,128]{4,3,2,1,0:T(8,128)S(1)}, f32[20,5,16,128]{3,2,1,0:T(8,128)S(1)}, f32[16,128]{1,0:T...) custom-call(s32[8]{0:T(128)} %depth_hbm.1, s32[8]{0:T(128)} %east_hbm.1, ...), custom_call_target="tpu_custom_call" | custom-call | flops 5000000000 | bytes 5000000 | tf_op jit(solution)/shard_map/pallas_call | solution.py:26
  10.4 0.0 collective-permute-done.2.both_ref
  10.4 0.1 collective-permute-done.1.quarter_ref
  10.5 0.9 %collective-permute-done.half_ref = f32[1,16,128]{2,1,0:T(8,128)S(1)} collective-permute-done((f32[1,16,128]{2,1,0:T(8,128)S(1)}, f32[1,16,128]{2,1,0:T(8,128)S(1)}, u32[]{:S(2)}, u32[]{:S(2)}) %collective-permute-start) | collective-permute-done | bytes 8224 | tf_op jit(solution)/shard_map/ppermute | solution.py:594
  11.4 0.1 shard_map.97
  11.5 0.1 collective-permute-start.3
  11.6 0.1 shard_map.99
  11.7 1.5 %collective-permute-start.4 = (f32[16,128]{1,0:T(8,128)S(1)}, f32[16,128]{1,0:T(8,128)S(1)}, u32[]{:S(2)}, u32[]{:S(2)}) collective-permute-start(f32[16,128]{1,0:T(8,128)S(1)} %get-tuple-element.41), channel_id=1, source_target_pairs={{0,4},{4,0},{8,12},{12,8},{16,20},{20,16},{24,28},{28,24},{1,5},{5... | collective-permute-start | bytes 24584 | tf_op jit(solution)/shard_map/ppermute | solution.py:594
  13.2 0.0 copy-done.1
  13.2 0.0 copy-done.3
  13.2 0.0 copy-done.6
  13.2 0.6 %shard_map.100.s0_ref = f32[8,5,16,128]{3,2,1,0:T(8,128)S(1)} custom-call(f32[16,128]{1,0:T(8,128)S(1)} %get-tuple-element.40.tiles_ref.mine_ref, f32[16,128]{1,0:T(8,128)S(1)} %get-tuple-element.32.live_ref, f32[8,5,16,128]{3,2,1,0:T(8,128)S(1)} %bitcast.15, f32[8,5,16,128]{3,2,1,0:T(8,128)S(1)} %bitcast.22, f32[8,5,5,16,128]{4,3,2,1,0:T(8,128)S(1)} %bitcast.12, ...), custom_call_target="tpu_custom_call" | custom-call | flops 2000000000 | bytes 2000000 | tf_op jit(solution)/shard_map/pallas_call | solution.py:26
  13.8 0.2 collective-permute-done.3.other_ref.mats_other_ref
  14.0 1.3 %collective-permute-start.7 = (f32[6,5,8,128]{3,2,1,0:T(8,128)S(1)}, f32[6,5,8,128]{3,2,1,0:T(8,128)S(1)}, u32[]{:S(2)}, u32[]{:S(2)}) collective-permute-start(f32[6,5,8,128]{3,2,1,0:T(8,128)S(1)} %shard_map.98.half_ref), channel_id=1, source_target_pairs={{0,3},{1,2},{2,1},{3,0},{4,7},{5,6},{6,5},{7,4},{8,11},{9,10},{10,... | collective-permute-start | bytes 368648 | tf_op jit(solution)/shard_map/ppermute | solution.py:576
  15.4 0.0 collective-permute-done.4.got_ref
  15.4 0.4 %shard_map.101 = (f32[8,5,16,128]{3,2,1,0:T(8,128)S(1)}, f32[2,5,16,128]{3,2,1,0:T(8,128)S(1)}, f32[5,16,128]{2,1,0:T(8,128)S(1)}) custom-call(f32[6,5,8,128]{3,2,1,0:T(8,128)S(1)} %shard_map.98.half_ref, f32[22,5,16,128]{3,2,1,0:T(8,128)S(1)} %collective-permute-done.3.other_ref.mats_other_ref, f32[16,128]{1,0:T(8,128)S(1)} %get-tuple-element.32.live_ref, ...), custom_call_target="tpu_custom_call" | custom-call | flops 1000000000 | bytes 1000000 | tf_op jit(solution)/shard_map/pallas_call | solution.py:26
  15.8 0.4 %collective-permute-start.5 = (f32[2,5,16,128]{3,2,1,0:T(8,128)S(1)}, f32[2,5,16,128]{3,2,1,0:T(8,128)S(1)}, u32[]{:S(2)}, u32[]{:S(2)}) collective-permute-start(f32[2,5,16,128]{3,2,1,0:T(8,128)S(1)} %get-tuple-element.46.ends_ref), channel_id=1, source_target_pairs={{0,1},{1,0},{2,3},{3,2},{4,5},{5,4},{6,7},{7,6},{8,9},{9,8},{10,11... | collective-permute-start | bytes 245768 | tf_op jit(solution)/shard_map/ppermute | solution.py:576
  16.3 0.9 %collective-permute-done.5.ends_other_ref = f32[2,5,16,128]{3,2,1,0:T(8,128)S(1)} collective-permute-done((f32[2,5,16,128]{3,2,1,0:T(8,128)S(1)}, f32[2,5,16,128]{3,2,1,0:T(8,128)S(1)}, u32[]{:S(2)}, u32[]{:S(2)}) %collective-permute-start.5) | collective-permute-done | bytes 81952 | tf_op jit(solution)/shard_map/ppermute | solution.py:576
  17.2 1.2 %collective-permute-start.6 = (f32[1,5,16,128]{3,2,1,0:T(8,128)S(1)}, f32[1,5,16,128]{3,2,1,0:T(8,128)S(1)}, u32[]{:S(2)}, u32[]{:S(2)}) collective-permute-start(f32[1,5,16,128]{3,2,1,0:T(8,128)S(1)} %shard_map.102.pair_ref), channel_id=1, source_target_pairs={{0,3},{1,2},{2,1},{3,0},{4,7},{5,6},{6,5},{7,4},{8,11},{9,10},{10,... | collective-permute-start | bytes 122888 | tf_op jit(solution)/shard_map/ppermute | solution.py:576
  18.5 1.0 %collective-permute-done.7.half_ref = f32[6,5,8,128]{3,2,1,0:T(8,128)S(1)} collective-permute-done((f32[6,5,8,128]{3,2,1,0:T(8,128)S(1)}, f32[6,5,8,128]{3,2,1,0:T(8,128)S(1)}, u32[]{:S(2)}, u32[]{:S(2)}) %collective-permute-start.7) | collective-permute-done | bytes 122912 | tf_op jit(solution)/shard_map/ppermute | solution.py:576
  19.4 0.2 collective-permute-start.8
  19.6 0.4 collective-permute-start.9
  20.0 0.1 collective-permute-start.10
  20.1 0.6 %collective-permute-done.6.pair_other_ref = f32[1,5,16,128]{3,2,1,0:T(8,128)S(1)} collective-permute-done((f32[1,5,16,128]{3,2,1,0:T(8,128)S(1)}, f32[1,5,16,128]{3,2,1,0:T(8,128)S(1)}, u32[]{:S(2)}, u32[]{:S(2)}) %collective-permute-start.6) | collective-permute-done | bytes 40992 | tf_op jit(solution)/shard_map/ppermute | solution.py:576
  20.7 0.0 collective-permute-done.8.rest_0_
  20.7 0.2 collective-permute-done.9.rest_1_
  20.9 0.3 collective-permute-done.10.rest_2_
  21.2 0.5 %shard_map.104 = (f32[8,5,16,128]{3,2,1,0:T(8,128)S(1)}, f32[5,16,128]{2,1,0:T(8,128)S(1)}, f32[5,16,128]{2,1,0:T(8,128)S(1)}, f32[8,16,128]{2,1,0:T(8,128)S(1)}) custom-call(f32[16,128]{1,0:T(8,128)S(1)} %get-tuple-element.32.live_ref, f32[8,5,16,128]{3,2,1,0:T(8,128)S(1)} %bitcast.17, f32[5,16,128]{2,1,0:T(8,128)S(1)} %get-tuple-element.44.above_ref, ...), custom_call_target="tpu_custom_call" | custom-call | flops 1000000000 | bytes 1000000 | tf_op jit(solution)/shard_map/pallas_call | solution.py:26
  21.7 11.7 %all_to_all.5.tiles_ref = f32[8,16,128]{2,1,0:T(8,128)S(1)} all-to-all(f32[8,16,128]{2,1,0:T(8,128)S(1)} %get-tuple-element.52), channel_id=1, replica_groups=mesh['zone'=8,'ja'=4] {'zone'}, dimensions={0} | all-to-all | bytes 131072 | tf_op jit(solution)/shard_map/all_to_all | solution.py:631
  33.4 0.8 %shard_map.105 = (f32[8,5,16,128]{3,2,1,0:T(8,128)S(1)}, f32[8,5,16,128]{3,2,1,0:T(8,128)S(1)}, f32[3,5,16,128]{3,2,1,0:T(8,128)S(1)}) custom-call(f32[16,128]{1,0:T(8,128)S(1)} %get-tuple-element.32.live_ref, f32[2,8,16,128]{3,2,1,0:T(8,128)S(1)} %get-tuple-element.38.pick_ref, f32[8,16,128]{2,1,0:T(8,128)S(1)} %all_to_all.5.tiles_ref, ...), custom_call_target="tpu_custom_call" | custom-call | flops 1000000000 | bytes 1000000 | tf_op jit(solution)/shard_map/pallas_call | solution.py:26
  34.2 0.1 collective-permute-start.11
  34.3 1.3 %collective-permute-done.11.ends_other_ref = f32[3,5,16,128]{3,2,1,0:T(8,128)S(1)} collective-permute-done((f32[3,5,16,128]{3,2,1,0:T(8,128)S(1)}, f32[3,5,16,128]{3,2,1,0:T(8,128)S(1)}, u32[]{:S(2)}, u32[]{:S(2)}) %collective-permute-start.11) | collective-permute-done | bytes 122912 | tf_op jit(solution)/shard_map/ppermute | solution.py:576
  35.6 1.3 %collective-permute-start.12 = (f32[1,5,16,128]{3,2,1,0:T(8,128)S(1)}, f32[1,5,16,128]{3,2,1,0:T(8,128)S(1)}, u32[]{:S(2)}, u32[]{:S(2)}) collective-permute-start(f32[1,5,16,128]{3,2,1,0:T(8,128)S(1)} %shard_map.107.pair_ref), channel_id=1, source_target_pairs={{0,3},{1,2},{2,1},{3,0},{4,7},{5,6},{6,5},{7,4},{8,11},{9,10},{10,... | collective-permute-start | bytes 122888 | tf_op jit(solution)/shard_map/ppermute | solution.py:576
  37.0 1.0 %shard_map.106 = (f32[8,5,16,128]{3,2,1,0:T(8,128)}, f32[16,128]{1,0:T(8,128)S(1)}) custom-call(f32[16,128]{1,0:T(8,128)S(1)} %get-tuple-element.32.live_ref, f32[5,16,128]{2,1,0:T(8,128)S(1)} %get-tuple-element.51.below_ref, f32[3,5,16,128]{3,2,1,0:T(8,128)S(1)} %collective-permute-done.11.ends_other_ref, f32[8,5,16,128]{3,2,1,0:T(8,128)S(1)} %get-tuple-element.53.cur_ref, ...), custom_call_target="tpu_custom_call" | custom-call | flops 1000000000 | bytes 1000000 | tf_op jit(solution)/shard_map/pallas_call | solution.py:26
  38.0 1.3 %collective-permute-done.12.pair_other_ref = f32[1,5,16,128]{3,2,1,0:T(8,128)S(1)} collective-permute-done((f32[1,5,16,128]{3,2,1,0:T(8,128)S(1)}, f32[1,5,16,128]{3,2,1,0:T(8,128)S(1)}, u32[]{:S(2)}, u32[]{:S(2)}) %collective-permute-start.12) | collective-permute-done | bytes 40992 | tf_op jit(solution)/shard_map/ppermute | solution.py:576
  39.3 1.1 %shard_map.108 = f32[8,5,16,128]{3,2,1,0:T(8,128)} custom-call(f32[16,128]{1,0:T(8,128)S(1)} %get-tuple-element.57.done_ref, f32[8,5,16,128]{3,2,1,0:T(8,128)S(1)} %get-tuple-element.53.cur_ref, f32[8,5,16,128]{3,2,1,0:T(8,128)S(1)} %get-tuple-element.58.s_ref, f32[8,5,5,16,128]{4,3,2,1,0:T(8,128)S(1)} %get-tuple-element.42.e_ref, ...), custom_call_target="tpu_custom_call" | custom-call | flops 1000000000 | bytes 1000000 | tf_op jit(solution)/shard_map/pallas_call | solution.py:26
  (4 shorter events, 0.1 us)
Async XLA Ops:
  0.6 1.0 %copy-start.2 = (f32[1,8,5,16,128]{4,3,2,1,0:T(8,128)S(1)}, f32[1,8,5,16,128]{4,3,2,1,0:T(8,128)}, u32[]{:S(2)}) copy-start(f32[1,8,5,16,128]{4,3,2,1,0:T(8,128)} %param.8) | copy-start | bytes 983044
  1.6 5.9 %copy-start = (f32[1,8,5,5,16,128]{5,4,3,2,1,0:T(8,128)S(1)}, f32[1,8,5,5,16,128]{5,4,3,2,1,0:T(8,128)}, u32[]{:S(2)}) copy-start(f32[1,8,5,5,16,128]{5,4,3,2,1,0:T(8,128)} %param.13) | copy-start | bytes 4915204
  1.6 5.9 %copy-start.4 = (f32[1,8,5,5,16,128]{5,4,3,2,1,0:T(8,128)S(1)}, f32[1,8,5,5,16,128]{5,4,3,2,1,0:T(8,128)}, u32[]{:S(2)}) copy-start(f32[1,8,5,5,16,128]{5,4,3,2,1,0:T(8,128)} %param.11) | copy-start | bytes 4915204
  1.6 5.9 %copy-start.5 = (f32[1,8,5,5,16,128]{5,4,3,2,1,0:T(8,128)S(1)}, f32[1,8,5,5,16,128]{5,4,3,2,1,0:T(8,128)}, u32[]{:S(2)}) copy-start(f32[1,8,5,5,16,128]{5,4,3,2,1,0:T(8,128)} %param.12) | copy-start | bytes 4915204
  1.8 8.7 %collective-permute-start.2 = (f32[1,16,128]{2,1,0:T(8,128)S(1)}, f32[1,16,128]{2,1,0:T(8,128)S(1)}, u32[]{:S(2)}, u32[]{:S(2)}) collective-permute-start(f32[1,16,128]{2,1,0:T(8,128)S(1)} %get-tuple-element.31.tile_ref.own_ref), channel_id=1, source_target_pairs={{0,24},{4,28},{8,16},{12,20},{16,8},{20,12},{24,0},{28,4},{1,25},{... | collective-permute-start | bytes 24584 | tf_op jit(solution)/shard_map/ppermute | solution.py:594
  6.9 3.7 %collective-permute-start.1 = (f32[1,16,128]{2,1,0:T(8,128)S(1)}, f32[1,16,128]{2,1,0:T(8,128)S(1)}, u32[]{:S(2)}, u32[]{:S(2)}) collective-permute-start(f32[1,16,128]{2,1,0:T(8,128)S(1)} %get-tuple-element.31.tile_ref.own_ref), channel_id=1, source_target_pairs={{0,8},{4,12},{8,0},{12,4},{16,24},{20,28},{24,16},{28,20},{1,9},{5... | collective-permute-start | bytes 24584 | tf_op jit(solution)/shard_map/ppermute | solution.py:594
  6.9 4.5 %collective-permute-start = (f32[1,16,128]{2,1,0:T(8,128)S(1)}, f32[1,16,128]{2,1,0:T(8,128)S(1)}, u32[]{:S(2)}, u32[]{:S(2)}) collective-permute-start(f32[1,16,128]{2,1,0:T(8,128)S(1)} %get-tuple-element.31.tile_ref.own_ref), channel_id=1, source_target_pairs={{0,16},{4,20},{8,24},{12,28},{16,0},{20,4},{24,8},{28,12},{1,17},{... | collective-permute-start | bytes 24584 | tf_op jit(solution)/shard_map/ppermute | solution.py:594
  7.5 5.7 %copy-start.1 = (f32[1,8,5,5,16,128]{5,4,3,2,1,0:T(8,128)S(1)}, f32[1,8,5,5,16,128]{5,4,3,2,1,0:T(8,128)}, u32[]{:S(2)}) copy-start(f32[1,8,5,5,16,128]{5,4,3,2,1,0:T(8,128)} %param.10) | copy-start | bytes 4915204
  7.5 5.7 %copy-start.3 = (f32[1,8,5,16,128]{4,3,2,1,0:T(8,128)S(1)}, f32[1,8,5,16,128]{4,3,2,1,0:T(8,128)}, u32[]{:S(2)}) copy-start(f32[1,8,5,16,128]{4,3,2,1,0:T(8,128)} %param.8) | copy-start | bytes 983044
  7.5 5.7 %copy-start.6 = (f32[1,8,5,16,128]{4,3,2,1,0:T(8,128)S(1)}, f32[1,8,5,16,128]{4,3,2,1,0:T(8,128)}, u32[]{:S(2)}) copy-start(f32[1,8,5,16,128]{4,3,2,1,0:T(8,128)} %param.9) | copy-start | bytes 983044
  11.5 2.5 %collective-permute-start.3 = (f32[22,5,16,128]{3,2,1,0:T(8,128)S(1)}, f32[22,5,16,128]{3,2,1,0:T(8,128)S(1)}, u32[]{:S(2)}, u32[]{:S(2)}) collective-permute-start(f32[22,5,16,128]{3,2,1,0:T(8,128)S(1)} %get-tuple-element.36.mine_ref.mats_ref), channel_id=1, source_target_pairs={{0,1},{1,0},{2,3},{3,2},{4,5},{5,4},{6,7},{7,6},{8,9},{9,8},{10,11... | collective-permute-start | bytes 2703368 | tf_op jit(solution)/shard_map/ppermute | solution.py:576
  11.7 3.7 %collective-permute-start.4 = (f32[16,128]{1,0:T(8,128)S(1)}, f32[16,128]{1,0:T(8,128)S(1)}, u32[]{:S(2)}, u32[]{:S(2)}) collective-permute-start(f32[16,128]{1,0:T(8,128)S(1)} %get-tuple-element.41), channel_id=1, source_target_pairs={{0,4},{4,0},{8,12},{12,8},{16,20},{20,16},{24,28},{28,24},{1,5},{5... | collective-permute-start | bytes 24584 | tf_op jit(solution)/shard_map/ppermute | solution.py:594
  14.0 5.4 %collective-permute-start.7 = (f32[6,5,8,128]{3,2,1,0:T(8,128)S(1)}, f32[6,5,8,128]{3,2,1,0:T(8,128)S(1)}, u32[]{:S(2)}, u32[]{:S(2)}) collective-permute-start(f32[6,5,8,128]{3,2,1,0:T(8,128)S(1)} %shard_map.98.half_ref), channel_id=1, source_target_pairs={{0,3},{1,2},{2,1},{3,0},{4,7},{5,6},{6,5},{7,4},{8,11},{9,10},{10,... | collective-permute-start | bytes 368648 | tf_op jit(solution)/shard_map/ppermute | solution.py:576
  15.8 1.4 %collective-permute-start.5 = (f32[2,5,16,128]{3,2,1,0:T(8,128)S(1)}, f32[2,5,16,128]{3,2,1,0:T(8,128)S(1)}, u32[]{:S(2)}, u32[]{:S(2)}) collective-permute-start(f32[2,5,16,128]{3,2,1,0:T(8,128)S(1)} %get-tuple-element.46.ends_ref), channel_id=1, source_target_pairs={{0,1},{1,0},{2,3},{3,2},{4,5},{5,4},{6,7},{7,6},{8,9},{9,8},{10,11... | collective-permute-start | bytes 245768 | tf_op jit(solution)/shard_map/ppermute | solution.py:576
  17.2 3.5 %collective-permute-start.6 = (f32[1,5,16,128]{3,2,1,0:T(8,128)S(1)}, f32[1,5,16,128]{3,2,1,0:T(8,128)S(1)}, u32[]{:S(2)}, u32[]{:S(2)}) collective-permute-start(f32[1,5,16,128]{3,2,1,0:T(8,128)S(1)} %shard_map.102.pair_ref), channel_id=1, source_target_pairs={{0,3},{1,2},{2,1},{3,0},{4,7},{5,6},{6,5},{7,4},{8,11},{9,10},{10,... | collective-permute-start | bytes 122888 | tf_op jit(solution)/shard_map/ppermute | solution.py:576
  19.4 1.3 %collective-permute-start.8 = (f32[10,8,128]{2,1,0:T(8,128)S(1)}, f32[10,8,128]{2,1,0:T(8,128)S(1)}, u32[]{:S(2)}, u32[]{:S(2)}) collective-permute-start(f32[10,8,128]{2,1,0:T(8,128)S(1)} %get-tuple-element.48), channel_id=1, source_target_pairs={{0,1},{1,0},{2,3},{3,2},{4,5},{5,4},{6,7},{7,6},{8,9},{9,8},{10,11... | collective-permute-start | bytes 122888 | tf_op jit(solution)/shard_map/ppermute | solution.py:576
  19.6 1.3 %collective-permute-start.9 = (f32[10,8,128]{2,1,0:T(8,128)S(1)}, f32[10,8,128]{2,1,0:T(8,128)S(1)}, u32[]{:S(2)}, u32[]{:S(2)}) collective-permute-start(f32[10,8,128]{2,1,0:T(8,128)S(1)} %get-tuple-element.49), channel_id=1, source_target_pairs={{0,1},{1,0},{2,3},{3,2},{4,5},{5,4},{6,7},{7,6},{8,9},{9,8},{10,11... | collective-permute-start | bytes 122888 | tf_op jit(solution)/shard_map/ppermute | solution.py:576
  20.0 1.2 %collective-permute-start.10 = (f32[10,8,128]{2,1,0:T(8,128)S(1)}, f32[10,8,128]{2,1,0:T(8,128)S(1)}, u32[]{:S(2)}, u32[]{:S(2)}) collective-permute-start(f32[10,8,128]{2,1,0:T(8,128)S(1)} %get-tuple-element.50), channel_id=1, source_target_pairs={{0,1},{1,0},{2,3},{3,2},{4,5},{5,4},{6,7},{7,6},{8,9},{9,8},{10,11... | collective-permute-start | bytes 122888 | tf_op jit(solution)/shard_map/ppermute | solution.py:576
  34.2 1.4 %collective-permute-start.11 = (f32[3,5,16,128]{3,2,1,0:T(8,128)S(1)}, f32[3,5,16,128]{3,2,1,0:T(8,128)S(1)}, u32[]{:S(2)}, u32[]{:S(2)}) collective-permute-start(f32[3,5,16,128]{3,2,1,0:T(8,128)S(1)} %get-tuple-element.55.ends_ref), channel_id=1, source_target_pairs={{0,1},{1,0},{2,3},{3,2},{4,5},{5,4},{6,7},{7,6},{8,9},{9,8},{10,11... | collective-permute-start | bytes 368648 | tf_op jit(solution)/shard_map/ppermute | solution.py:576
  35.6 3.6 %collective-permute-start.12 = (f32[1,5,16,128]{3,2,1,0:T(8,128)S(1)}, f32[1,5,16,128]{3,2,1,0:T(8,128)S(1)}, u32[]{:S(2)}, u32[]{:S(2)}) collective-permute-start(f32[1,5,16,128]{3,2,1,0:T(8,128)S(1)} %shard_map.107.pair_ref), channel_id=1, source_target_pairs={{0,3},{1,2},{2,1},{3,0},{4,7},{5,6},{6,5},{7,4},{8,11},{9,10},{10,... | collective-permute-start | bytes 122888 | tf_op jit(solution)/shard_map/ppermute | solution.py:576
